TPU v7x, 128 devices: a whole 4x4x4 slice. The times are simulated.
128 devices in a mesh: grp: 4 (over y_hi, core), blk: 32 (over z, x, y_lo).
Axes of the slice: x: 4, y: 4 (y_hi: 2, y_lo: 2; y = y_hi * 2 + y_lo), z: 4, core: 2. Of those that a mesh axis runs over, the one named last changes fastest.
Arguments:
- embeds: bfloat16 [4, 32768, 1024], P('grp', 'blk')
- doc_ids: int32 [4, 32768], P('grp', 'blk'), may hold values from 0 to 32767, each once within a row
- prior_max: float32 [4, 32768], P('grp', 'blk'), may hold values from -0.2 to 0.6
- owned: bfloat16 [32768, 1024], P(('grp', 'blk')), may hold values from -6 to 6
- owned_ids: int32 [32768], P(('grp', 'blk')), may hold values from 0 to 32767, each once
- owner_dest: int32 [32768, 1], P(('grp', 'blk')), may hold values from 0 to 127; in each aligned block of 256 rows (0 to 255, 256 to 511, ...) at most 4 rows name the same one
Outputs:
- running_max: float32 [4, 32768], P('grp', 'blk')
- next_rows: bfloat16 [65536, 1024], P(('grp', 'blk'))
- next_ids: int32 [65536], P(('grp', 'blk'))
Inputs may be any that keep to these rules, and one draw needn't show every extreme that they name: `owner_dest`: among the 256 rows of one device no target is named more than 4 times, a bound that some block reaches.
All inputs are finite; a program needn't handle non-finite values.
Results may differ from a plain program's by a relative error of at most 0.0016.
Values may be sent and summed in bfloat16 or wider, within the bound.
No kernel may reach another device: no remote copies, remote signals or barrier semaphores. Data moves between devices by JAX's collectives and lax.ppermute only.
A program may use at most 64 MiB of HBM per device.

v0:
```python
import jax
import jax.numpy as jnp
from jax import lax
from jax.sharding import PartitionSpec as P

CYCLE = 3
CAP = 4


def passed_along(value, axis, steps):
    count = lax.axis_size(axis)
    pairs = [(source, (source + steps) % count) for source in range(count)]
    return lax.ppermute(value, axis, pairs)


def normalize(matrix):
    values = matrix.astype(jnp.float32)
    scale = lax.rsqrt(jnp.sum(values * values, axis=-1, keepdims=True) + 1e-06)
    return (values * scale).astype(jnp.bfloat16)


def tile_max(row_normed, row_ids, col_normed, col_ids):
    scores = lax.dot_general(
        row_normed, col_normed, (((1,), (1,)), ((), ())), preferred_element_type=jnp.float32
    )
    masked = jnp.where(col_ids[None, :] < row_ids[:, None], scores, jnp.float32(-2.0))
    return jnp.max(masked, axis=1)


def body(embeds, doc_ids, prior_max, owned, owned_ids, owner_dest):
    devices = lax.axis_size("grp") * lax.axis_size("blk")
    groups = lax.axis_size("grp")
    members = lax.axis_size("blk")
    owned_normed = normalize(owned)
    target = owner_dest[:, 0]
    onehot = (target[:, None] == jnp.arange(devices, dtype=jnp.int32)[None, :]).astype(jnp.int32)
    position = jnp.sum(jnp.cumsum(onehot, axis=0) * onehot, axis=1) - 1
    place = target * CAP + position
    width = owned.shape[1]
    outgoing = jnp.zeros((devices * CAP, width), jnp.bfloat16).at[place].set(owned_normed)
    outgoing_ids = jnp.full((devices * CAP,), -1, jnp.int32).at[place].set(owned_ids)
    arrived, arrived_ids = (
        lax.all_to_all(
            lax.all_to_all(
                outgoing.reshape(groups, members, CAP, width),
                "blk",
                split_axis=1,
                concat_axis=1,
                tiled=True,
            ),
            "grp",
            split_axis=0,
            concat_axis=0,
            tiled=True,
        ),
        lax.all_to_all(
            lax.all_to_all(
                outgoing_ids.reshape(groups, members, CAP),
                "blk",
                split_axis=1,
                concat_axis=1,
                tiled=True,
            ),
            "grp",
            split_axis=0,
            concat_axis=0,
            tiled=True,
        ),
    )
    next_rows = arrived.reshape(devices * CAP, width)
    next_ids = arrived_ids.reshape(devices * CAP)
    normed = normalize(embeds[0])
    numbers = doc_ids[0]
    running = jnp.maximum(prior_max[0], tile_max(normed, numbers, normed, numbers))
    for distance in range(1, CYCLE + 1):
        col_normed, col_ids = passed_along((normed, numbers), "blk", distance)
        running = jnp.maximum(running, tile_max(normed, numbers, col_normed, col_ids))
    return (running[None, :], next_rows, next_ids)


def solution(mesh):
    return jax.shard_map(
        body,
        mesh=mesh,
        in_specs=(
            P("grp", "blk", None),
            P("grp", "blk"),
            P("grp", "blk"),
            P(("grp", "blk"), None),
            P(("grp", "blk")),
            P(("grp", "blk"), None),
        ),
        out_specs=(P("grp", "blk"), P(("grp", "blk"), None), P(("grp", "blk"))),
        check_vma=False,
    )
```

profile of v0, /device:TPU:0, one launch (start us, length us, event | category | flops | bytes accessed | tf_op | source)
XLA Modules:
  0.0 177.4 jit_solution(1391676072860974057)
XLA Ops:
  0.6 0.0 copy-start
  0.6 2.2 %fusion.2 = f32[1024]{0:T(1024)S(1)} fusion(bf16[1,1024,1024]{2,1,0:T(8,128)(2,1)} %param.6), kind=kLoop, calls=%fused_computation.6 | loop fusion | flops 3144704 | bytes 2101248 | tf_op jit(solution)/shard_map/reduce_sum | solution.py:18
  2.9 0.0 copy-done
  2.9 0.0 copy-start.2
  2.9 0.0 copy-start.1
  2.9 1.8 fusion.3
  4.7 2.6 %collective-permute-start.5 = (bf16[1024,1024]{1,0:T(8,128)(2,1)}, bf16[1024,1024]{1,0:T(8,128)(2,1)}, u32[]{:S(2)}, u32[]{:S(2)}) collective-permute-start(bf16[1024,1024]{1,0:T(8,128)(2,1)} %fusion.3), channel_id=1, source_target_pairs={{0,3},{1,4},{2,5},{3,6},{4,7},{5,8},{6,9},{7,10},{8,11},{9,12},{10... | collective-permute-start | bytes 6291464 | tf_op jit(solution)/shard_map/ppermute | solution.py:13
  7.3 0.0 copy-done.2
  7.3 0.1 copy.25
  7.4 0.2 fusion.17
  7.7 0.2 fusion.18
  7.9 1.6 scatter_custom_fusion.1
  9.4 0.1 reshape.84
  9.5 0.7 copy.29
  10.2 8.6 %all-to-all-start.2 = ((s32[4,32,4]{2,0,1:T(4,128)}), s32[4,32,4]{2,0,1:T(4,128)S(1)}, u32[]{:S(2)}, u32[]{:S(2)}) async-start(s32[4,32,4]{2,0,1:T(4,128)} %copy.29), calls=%async_computation.2 | async-start | bytes 131072 | tf_op jit(solution)/shard_map/all_to_all | solution.py:57
  18.8 0.0 copy-done.1
  18.8 0.2 fusion.11
  19.0 2.5 %scatter_custom_fusion = bf16[512,1024]{1,0:T(8,128)(2,1)S(1)} fusion(s32[256]{0:T(256)S(1)} %bitcast.56, bf16[256,1024]{1,0:T(8,128)(2,1)} %param.9, f32[256]{0:T(256)S(1)} %add_rsqrt_fusion.1, bf16[]{:T(256)} %constant.4.clone.1), kind=kCustom, calls=%fused_computation.20 | custom fusion | flops 786432 | bytes 1573890 | tf_op jit(solution)/shard_map/scatter | solution.py:40
  21.5 1.2 reshape.82
  22.7 2.9 %copy.27 = bf16[4,32,4,1024]{3,2,0,1:T(4,128)(2,1)} copy(bf16[4,32,4,1024]{3,2,1,0:T(4,128)(2,1)} %reshape.82) | data formatting | bytes 2097152 | tf_op jit(solution)/shard_map/reshape | solution.py:45
  25.6 34.3 %all-to-all-done.2 = s32[4,32,4]{2,0,1:T(4,128)S(1)} async-done(((s32[4,32,4]{2,0,1:T(4,128)}), s32[4,32,4]{2,0,1:T(4,128)S(1)}, u32[]{:S(2)}, u32[]{:S(2)}) %all-to-all-start.2) | async-done | bytes 2080 | tf_op jit(solution)/shard_map/all_to_all | solution.py:57
  59.9 4.7 %all-to-all-start = ((bf16[4,32,4,1024]{3,2,0,1:T(4,128)(2,1)}), bf16[4,32,4,1024]{3,2,0,1:T(4,128)(2,1)S(1)}, u32[]{:S(2)}, u32[]{:S(2)}) async-start(bf16[4,32,4,1024]{3,2,0,1:T(4,128)(2,1)} %copy.27), calls=%async_computation | async-start | bytes 2097152 | tf_op jit(solution)/shard_map/all_to_all | solution.py:44
  64.5 1.9 %collective-permute-start.3 = (bf16[1024,1024]{1,0:T(8,128)(2,1)}, bf16[1024,1024]{1,0:T(8,128)(2,1)}, u32[]{:S(2)}, u32[]{:S(2)}) collective-permute-start(bf16[1024,1024]{1,0:T(8,128)(2,1)} %fusion.3), channel_id=1, source_target_pairs={{0,2},{1,3},{2,4},{3,5},{4,6},{5,7},{6,8},{7,9},{8,10},{9,11},{10,... | collective-permute-start | bytes 6291464 | tf_op jit(solution)/shard_map/ppermute | solution.py:13
  66.4 1.5 collective-permute-start.1
  67.8 0.1 copy.30
  67.9 0.7 reshape.107
  68.6 15.6 %all-to-all-done = bf16[4,32,4,1024]{3,2,0,1:T(4,128)(2,1)S(1)} async-done(((bf16[4,32,4,1024]{3,2,0,1:T(4,128)(2,1)}), bf16[4,32,4,1024]{3,2,0,1:T(4,128)(2,1)S(1)}, u32[]{:S(2)}, u32[]{:S(2)}) %all-to-all-start) | async-done | bytes 1048608 | tf_op jit(solution)/shard_map/all_to_all | solution.py:44
  84.2 4.5 %all-to-all-start.3 = ((s32[4,1,128]{2,1,0:T(1,128)}), s32[4,1,128]{2,1,0:T(1,128)S(1)}, u32[]{:S(2)}, u32[]{:S(2)}) async-start(s32[4,1,128]{2,1,0:T(1,128)} %reshape.107), calls=%async_computation.3 | async-start | bytes 4096 | tf_op jit(solution)/shard_map/all_to_all | solution.py:56
  88.7 0.0 copy-start.4
  88.7 1.4 copy.28
  90.1 34.0 %all-to-all-done.3 = s32[4,1,128]{2,1,0:T(1,128)S(1)} async-done(((s32[4,1,128]{2,1,0:T(1,128)}), s32[4,1,128]{2,1,0:T(1,128)S(1)}, u32[]{:S(2)}, u32[]{:S(2)}) %all-to-all-start.3) | async-done | bytes 2080 | tf_op jit(solution)/shard_map/all_to_all | solution.py:56
  124.1 3.5 %all-to-all-start.1 = ((bf16[4,32,4,1024]{3,2,1,0:T(4,128)(2,1)}), bf16[4,32,4,1024]{3,2,1,0:T(4,128)(2,1)S(1)}, u32[]{:S(2)}, u32[]{:S(2)}) async-start(bf16[4,32,4,1024]{3,2,1,0:T(4,128)(2,1)} %copy.28), calls=%async_computation.1 | async-start | bytes 2097152 | tf_op jit(solution)/shard_map/all_to_all | solution.py:43
  127.6 0.0 copy-done.4
  127.6 0.1 collective-permute-start
  127.7 1.1 collective-permute-start.2
  128.8 2.5 %select_reduce_fusion.3 = f32[1024]{0:T(1024)S(1)} fusion(s32[1024]{0:T(1024)S(1)} %bitcast.59, bf16[1,1024,1024]{2,1,0:T(8,128)(2,1)S(1)} %copy-done, f32[1024]{0:T(1024)S(1)} %add_rsqrt_fusion), kind=kOutput, calls=%fused_computation.12 | convolution fusion | flops 2153774080 | bytes 2109440 | tf_op jit(solution)/shard_map/dot_general | solution.py:23
  131.2 0.5 broadcast.65
  131.8 0.7 reduce
  132.4 0.1 reshape.108
  132.5 0.1 copy.31
  132.6 0.7 reshape.85
  133.3 10.3 %all-to-all-done.1 = bf16[4,32,4,1024]{3,2,1,0:T(4,128)(2,1)S(1)} async-done(((bf16[4,32,4,1024]{3,2,1,0:T(4,128)(2,1)}), bf16[4,32,4,1024]{3,2,1,0:T(4,128)(2,1)S(1)}, u32[]{:S(2)}, u32[]{:S(2)}) %all-to-all-start.1) | async-done | bytes 1048608 | tf_op jit(solution)/shard_map/all_to_all | solution.py:43
  143.6 1.1 reshape.83
  144.6 0.0 collective-permute-done.5
  144.6 0.0 collective-permute-start.4
  144.7 4.6 %fusion.24 = f32[1024,1024]{0,1:T(8,128)S(1)} fusion(bf16[1024,1024]{1,0:T(8,128)(2,1)} %fusion.3, bf16[1024,1024]{1,0:T(8,128)(2,1)} %collective-permute-done.5), kind=kOutput, calls=%fused_computation.40 | convolution fusion | flops 2147483648 | bytes 8388608 | tf_op jit(solution)/shard_map/dot_general | solution.py:23
  149.2 0.0 collective-permute-done.3
  149.3 4.6 %fusion.23 = f32[1024,1024]{0,1:T(8,128)S(1)} fusion(bf16[1024,1024]{1,0:T(8,128)(2,1)} %fusion.3, bf16[1024,1024]{1,0:T(8,128)(2,1)} %collective-permute-done.3), kind=kOutput, calls=%fused_computation.39 | convolution fusion | flops 2147483648 | bytes 8388608 | tf_op jit(solution)/shard_map/dot_general | solution.py:23
  153.9 0.0 copy-start.3
  153.9 17.5 %collective-permute-done = s32[1024]{0:T(1024)S(1)} collective-permute-done((s32[1024]{0:T(1024)S(1)}, s32[1024]{0:T(1024)S(1)}, u32[]{:S(2)}, u32[]{:S(2)}) %collective-permute-start) | collective-permute-done | bytes 4128 | tf_op jit(solution)/shard_map/ppermute | solution.py:13
  171.4 0.0 collective-permute-done.2
  171.4 0.3 collective-permute-done.4
  171.7 0.0 collective-permute-done.1
  171.7 5.1 %select_reduce_fusion.2 = (f32[1024]{0:T(1024)S(1)}, f32[1024]{0:T(1024)S(1)}, f32[1024]{0:T(1024)S(1)}) fusion(s32[1024]{0:T(1024)S(1)} %bitcast.61, s32[1024]{0:T(1024)S(1)} %collective-permute-done, f32[1024,1024]{0,1:T(8,128)S(1)} %fusion.23, s32[1024]{0:T(1024)S(1)} %collective-permute-done.2, f32[1024,1024]{0,1:T(8,128)S(1)} %fusion.24, ...), kind=kOutput, calls=%fused_computation.11 | convolution fusion | flops 2156917760 | bytes 12611584 | tf_op jit(solution)/shard_map/dot_general | solution.py:23
  176.8 0.0 copy-done.3
  176.8 0.6 maximum_maximum_fusion
  (10 shorter events, 0.1 us)
Async XLA Ops:
  0.6 2.2 %copy-start = (bf16[1,1024,1024]{2,1,0:T(8,128)(2,1)S(1)}, bf16[1,1024,1024]{2,1,0:T(8,128)(2,1)}, u32[]{:S(2)}) copy-start(bf16[1,1024,1024]{2,1,0:T(8,128)(2,1)} %param.6) | copy-start | bytes 6291460
  2.9 4.4 %copy-start.2 = (s32[256,1]{0,1:T(1,128)S(1)}, s32[256,1]{0,1:T(1,128)}, u32[]{:S(2)}) copy-start(s32[256,1]{0,1:T(1,128)} %param.11) | copy-start | bytes 3076
  2.9 15.9 %copy-start.1 = (bf16[256,1024]{1,0:T(8,128)(2,1)S(1)}, bf16[256,1024]{1,0:T(8,128)(2,1)}, u32[]{:S(2)}) copy-start(bf16[256,1024]{1,0:T(8,128)(2,1)} %param.9) | copy-start | bytes 1572868
  4.7 140.0 %collective-permute-start.5 = (bf16[1024,1024]{1,0:T(8,128)(2,1)}, bf16[1024,1024]{1,0:T(8,128)(2,1)}, u32[]{:S(2)}, u32[]{:S(2)}) collective-permute-start(bf16[1024,1024]{1,0:T(8,128)(2,1)} %fusion.3), channel_id=1, source_target_pairs={{0,3},{1,4},{2,5},{3,6},{4,7},{5,8},{6,9},{7,10},{8,11},{9,12},{10... | collective-permute-start | bytes 6291464 | tf_op jit(solution)/shard_map/ppermute | solution.py:13
  10.2 49.6 %all-to-all-start.2 = ((s32[4,32,4]{2,0,1:T(4,128)}), s32[4,32,4]{2,0,1:T(4,128)S(1)}, u32[]{:S(2)}, u32[]{:S(2)}) async-start(s32[4,32,4]{2,0,1:T(4,128)} %copy.29), calls=%async_computation.2 | async-start | bytes 131072 | tf_op jit(solution)/shard_map/all_to_all | solution.py:57
  59.9 24.3 %all-to-all-start = ((bf16[4,32,4,1024]{3,2,0,1:T(4,128)(2,1)}), bf16[4,32,4,1024]{3,2,0,1:T(4,128)(2,1)S(1)}, u32[]{:S(2)}, u32[]{:S(2)}) async-start(bf16[4,32,4,1024]{3,2,0,1:T(4,128)(2,1)} %copy.27), calls=%async_computation | async-start | bytes 2097152 | tf_op jit(solution)/shard_map/all_to_all | solution.py:44
  64.5 84.7 %collective-permute-start.3 = (bf16[1024,1024]{1,0:T(8,128)(2,1)}, bf16[1024,1024]{1,0:T(8,128)(2,1)}, u32[]{:S(2)}, u32[]{:S(2)}) collective-permute-start(bf16[1024,1024]{1,0:T(8,128)(2,1)} %fusion.3), channel_id=1, source_target_pairs={{0,2},{1,3},{2,4},{3,5},{4,6},{5,7},{6,8},{7,9},{8,10},{9,11},{10,... | collective-permute-start | bytes 6291464 | tf_op jit(solution)/shard_map/ppermute | solution.py:13
  66.4 105.3 %collective-permute-start.1 = (bf16[1024,1024]{1,0:T(8,128)(2,1)}, bf16[1024,1024]{1,0:T(8,128)(2,1)}, u32[]{:S(2)}, u32[]{:S(2)}) collective-permute-start(bf16[1024,1024]{1,0:T(8,128)(2,1)} %fusion.3), channel_id=1, source_target_pairs={{0,1},{1,2},{2,3},{3,4},{4,5},{5,6},{6,7},{7,8},{8,9},{9,10},{10,1... | collective-permute-start | bytes 6291464 | tf_op jit(solution)/shard_map/ppermute | solution.py:13
  84.2 39.9 %all-to-all-start.3 = ((s32[4,1,128]{2,1,0:T(1,128)}), s32[4,1,128]{2,1,0:T(1,128)S(1)}, u32[]{:S(2)}, u32[]{:S(2)}) async-start(s32[4,1,128]{2,1,0:T(1,128)} %reshape.107), calls=%async_computation.3 | async-start | bytes 4096 | tf_op jit(solution)/shard_map/all_to_all | solution.py:56
  88.7 38.9 %copy-start.4 = (s32[1,1024]{1,0:T(1,128)S(1)}, s32[1,1024]{1,0:T(1,128)}, u32[]{:S(2)}) copy-start(s32[1,1024]{1,0:T(1,128)} %param.7) | copy-start | bytes 12292
  124.1 19.5 %all-to-all-start.1 = ((bf16[4,32,4,1024]{3,2,1,0:T(4,128)(2,1)}), bf16[4,32,4,1024]{3,2,1,0:T(4,128)(2,1)S(1)}, u32[]{:S(2)}, u32[]{:S(2)}) async-start(bf16[4,32,4,1024]{3,2,1,0:T(4,128)(2,1)} %copy.28), calls=%async_computation.1 | async-start | bytes 2097152 | tf_op jit(solution)/shard_map/all_to_all | solution.py:43
  127.6 43.8 %collective-permute-start = (s32[1024]{0:T(1024)S(1)}, s32[1024]{0:T(1024)S(1)}, u32[]{:S(2)}, u32[]{:S(2)}) collective-permute-start(s32[1024]{0:T(1024)S(1)} %bitcast.57), channel_id=1, source_target_pairs={{0,1},{1,2},{2,3},{3,4},{4,5},{5,6},{6,7},{7,8},{8,9},{9,10},{10,1... | collective-permute-start | bytes 12296 | tf_op jit(solution)/shard_map/ppermute | solution.py:13
  127.7 43.7 %collective-permute-start.2 = (s32[1024]{0:T(1024)S(1)}, s32[1024]{0:T(1024)S(1)}, u32[]{:S(2)}, u32[]{:S(2)}) collective-permute-start(s32[1024]{0:T(1024)S(1)} %bitcast.58), channel_id=1, source_target_pairs={{0,2},{1,3},{2,4},{3,5},{4,6},{5,7},{6,8},{7,9},{8,10},{9,11},{10,... | collective-permute-start | bytes 12296 | tf_op jit(solution)/shard_map/ppermute | solution.py:13
  144.6 27.0 %collective-permute-start.4 = (s32[1024]{0:T(1024)S(1)}, s32[1024]{0:T(1024)S(1)}, u32[]{:S(2)}, u32[]{:S(2)}) collective-permute-start(s32[1024]{0:T(1024)S(1)} %bitcast.60), channel_id=1, source_target_pairs={{0,3},{1,4},{2,5},{3,6},{4,7},{5,8},{6,9},{7,10},{8,11},{9,12},{10... | collective-permute-start | bytes 12296 | tf_op jit(solution)/shard_map/ppermute | solution.py:13
  153.9 22.9 %copy-start.3 = (f32[1,1024]{1,0:T(1,128)S(1)}, f32[1,1024]{1,0:T(1,128)}, u32[]{:S(2)}) copy-start(f32[1,1024]{1,0:T(1,128)} %param.8) | copy-start | bytes 12292
where the time goes:
time: 178 us; the launch traced here: 177 us
  waiting for transfers between devices  112 us (63%)
  starting transfers between devices  28.3 us (16%)
  matrix products  16.7 us (9%)
  local copies, waits for them, and re-layouts  11.2 us (6%)
  other arithmetic  8.36 us (5%)
    all_to_all x1, waiting for transfers between devices, body(): lax.all_to_all(outgoing_ids.reshape(groups, members, CAP), 'blk', split_a...  34.3 us
    all_to_all x1, waiting for transfers between devices, body(): lax.all_to_all(lax.all_to_all(outgoing_ids.reshape(groups, members, CAP),...  34 us
    ppermute x6, waiting for transfers between devices, passed_along(): return lax.ppermute(value, axis, pairs)  17.8 us
    dot_general x4, matrix products, tile_max(): lax.dot_general(row_normed, col_normed, (((1,), (1,)), ((), ())), preferr...  16.7 us
    all_to_all x1, waiting for transfers between devices, body(): lax.all_to_all(outgoing.reshape(groups, members, CAP, width), 'blk', spli...  15.6 us
    all_to_all x1, waiting for transfers between devices, body(): lax.all_to_all(lax.all_to_all(outgoing.reshape(groups, members, CAP, widt...  10.3 us
    all_to_all x1, starting transfers between devices, body(): lax.all_to_all(outgoing_ids.reshape(groups, members, CAP), 'blk', split_a...  8.6 us
    ppermute x6, starting transfers between devices, passed_along(): return lax.ppermute(value, axis, pairs)  7.07 us
  transfers between devices with their start and end apart: 10, of which 6 were waited for; matrix products, arithmetic and copies ran while one was open for 15% of the time, Pallas kernels for 0%

commit v1 on v0

v1 whole, which is shorter than its diff:
```python
import jax
import jax.numpy as jnp
from jax import lax
from jax.experimental import pallas as pl
from jax.experimental.pallas import tpu as pltpu
from jax.sharding import PartitionSpec as P

CAP = 4
PARTS = 4
LOWEST = -2.0
BOTH = ("grp", "blk")


def normalize(matrix):
    values = matrix.astype(jnp.float32)
    scale = lax.rsqrt(jnp.sum(values * values, axis=-1, keepdims=True) + 1e-06)
    return (values * scale).astype(jnp.bfloat16)


def send(value, to):
    count = lax.axis_size("blk")
    pairs = [(s, to(s) % count) for s in range(count) if to(s) is not None]
    return lax.ppermute(value, "blk", pairs)


def params():
    return pltpu.CompilerParams(vmem_limit_bytes=48 * 1024 * 1024)


def vmem(n):
    return [pl.BlockSpec(memory_space=pltpu.VMEM)] * n


def down(row):
    return jnp.broadcast_to(row, (128, row.shape[1])).T


def best(rows, row_ids, cols, col_down):
    scores = lax.dot_general(cols, rows, (((1,), (1,)), ((), ())), preferred_element_type=jnp.float32)
    found = []
    for left in range(0, rows.shape[0], 128):
        keep = col_down < row_ids[:, left : left + 128]
        part = jnp.where(keep, scores[:, left : left + 128], jnp.float32(LOWEST))
        found.append(jnp.max(part, axis=0, keepdims=True))
    return jnp.concatenate(found, axis=1)


def norm_kernel(x_ref, out_ref):
    out_ref[...] = normalize(x_ref[...])


def norm_part(embeds, part):
    rows, width = embeds.shape
    size = rows // PARTS
    return pl.pallas_call(
        norm_kernel,
        grid=(1,),
        in_specs=[pl.BlockSpec((size, width), lambda i: (part, 0))],
        out_specs=pl.BlockSpec((size, width), lambda i: (0, 0)),
        out_shape=jax.ShapeDtypeStruct((size, width), jnp.bfloat16),
        compiler_params=params(),
        name=f"norm_{part}",
        cost_estimate=pl.CostEstimate(flops=4 * size * width, bytes_accessed=4 * size * width, transcendentals=size),
    )(embeds)


def place_kernel(rows_ref, target_ref, out_ref):
    count = rows_ref.shape[0]
    target = target_ref[...]
    across = jnp.broadcast_to(target, (count, count))
    earlier = lax.broadcasted_iota(jnp.int32, (count, count), 0) < lax.broadcasted_iota(
        jnp.int32, (count, count), 1
    )
    same = (across.T == across) & earlier
    position = jnp.sum(same.astype(jnp.float32), axis=0, keepdims=True).astype(jnp.int32)
    place = target * CAP + position
    slots = out_ref.shape[0] * out_ref.shape[1]
    pick = (lax.broadcasted_iota(jnp.int32, (slots, count), 0) == place).astype(jnp.float32).astype(jnp.bfloat16)
    placed = jnp.dot(pick, normalize(rows_ref[...]), preferred_element_type=jnp.float32)
    out_ref[...] = placed.astype(jnp.bfloat16).reshape(out_ref.shape)


def placed_rows(owned, target, devices):
    count, width = owned.shape
    return pl.pallas_call(
        place_kernel,
        in_specs=vmem(2),
        out_specs=pl.BlockSpec(memory_space=pltpu.VMEM),
        out_shape=jax.ShapeDtypeStruct((devices, CAP, width), jnp.bfloat16),
        compiler_params=params(),
        name="place",
        cost_estimate=pl.CostEstimate(
            flops=2 * devices * CAP * count * width, bytes_accessed=2 * (count + devices * CAP) * width, transcendentals=count
        ),
    )(owned, target)


def ids_kernel(numbers, me_ref, all_ref, out_ref):
    me = me_ref[0]
    count = numbers // 2
    ids = all_ref[:, :count].astype(jnp.float32)
    mine = all_ref[:, count:] == me
    ones = mine.astype(jnp.float32)
    earlier = (
        lax.broadcasted_iota(jnp.int32, (count, count), 0) < lax.broadcasted_iota(jnp.int32, (count, count), 1)
    ).astype(jnp.float32)
    position = jnp.dot(
        ones.astype(jnp.bfloat16), earlier.astype(jnp.bfloat16), preferred_element_type=jnp.float32
    )
    found = [
        jnp.sum(jnp.where(mine & (position == p), ids + 1.0, 0.0), axis=1, keepdims=True) - 1.0
        for p in range(CAP)
    ]
    out_ref[...] = jnp.concatenate(found, axis=1).astype(jnp.int32)


def self_kernel(*refs):
    parts, (ids_ref, prior_ref, out_ref, down_ref) = refs[:PARTS], refs[PARTS:]
    size = parts[0].shape[0]
    down_ref[...] = down(ids_ref[...])
    for r in range(PARTS):
        at = slice(r * size, (r + 1) * size)
        found = prior_ref[:, at]
        for c in range(PARTS):
            cols = down_ref[c * size : (c + 1) * size, :]
            found = jnp.maximum(found, best(parts[r][...], ids_ref[:, at], parts[c][...], cols))
        out_ref[:, at] = found


def main_kernel(*refs):
    own, other = refs[:PARTS], refs[PARTS : 2 * PARTS]
    (where_ref, before_ref, ids_ref, other_ids_ref, before_ids_ref, so_far_ref) = refs[2 * PARTS : 2 * PARTS + 6]
    own_out, other_out, before_out, down_ref = refs[2 * PARTS + 6 :]
    size = own[0].shape[0]
    before_out[...] = normalize(before_ref[...])
    down_ref[...] = down(before_ids_ref[...])
    for r in range(PARTS):
        at = slice(r * size, (r + 1) * size)
        found = best(own[r][...], ids_ref[:, at], before_out[...], down_ref[...])
        own_out[:, at] = jnp.maximum(so_far_ref[:, at], found)
    for r in range(PARTS):
        at = slice(r * size, (r + 1) * size)
        other_out[:, at] = best(other[r][...], other_ids_ref[:, at], before_out[...], down_ref[...])

    @pl.when(where_ref[0] == 0)
    def _():
        down_ref[...] = down(ids_ref[...])
        for r in range(PARTS):
            at = slice(r * size, (r + 1) * size)
            found = other_out[:, at]
            for c in range(PARTS):
                cols = down_ref[c * size : (c + 1) * size, :]
                found = jnp.maximum(found, best(other[r][...], other_ids_ref[:, at], own[c][...], cols))
            other_out[:, at] = found


def far_kernel(parts, *refs):
    rows, (where_ref, before_ref, row_ids_ref, before_ids_ref, out_ref, down_ref) = refs[:parts], refs[parts:]
    size = rows[0].shape[0]

    @pl.when(where_ref[0] == 1)
    def _():
        down_ref[...] = down(before_ids_ref[...])
        for r in range(parts):
            at = slice(r * size, (r + 1) * size)
            out_ref[:, at] = best(rows[r][...], row_ids_ref[:, at], before_ref[...], down_ref[...])

    @pl.when(where_ref[0] == 0)
    def _():
        out_ref[...] = jnp.full(out_ref.shape, LOWEST, jnp.float32)


def far(rows, where, before, row_ids, before_ids):
    parts = len(rows)
    size, width = rows[0].shape
    cols = before.shape[0]
    return pl.pallas_call(
        lambda *refs: far_kernel(parts, *refs),
        in_specs=vmem(parts) + [pl.BlockSpec(memory_space=pltpu.SMEM)] + vmem(3),
        out_specs=pl.BlockSpec(memory_space=pltpu.VMEM),
        out_shape=jax.ShapeDtypeStruct((1, parts * size), jnp.float32),
        scratch_shapes=[pltpu.VMEM((cols, 128), jnp.int32)],
        compiler_params=params(),
        name=f"far_{parts}",
        cost_estimate=pl.CostEstimate(
            flops=2 * parts * size * cols * width, bytes_accessed=2 * (parts * size + cols) * width, transcendentals=0
        ),
    )(*rows, where, before, row_ids, before_ids)


def body(embeds, doc_ids, prior_max, owned, owned_ids, owner_dest):
    members = lax.axis_size("blk")
    devices = lax.axis_size("grp") * members
    raw = embeds[0]
    rows, width = raw.shape
    size = rows // PARTS
    group, member = lax.axis_index("grp"), lax.axis_index("blk")
    where = (member % 2).astype(jnp.int32).reshape(1)

    before = send(raw, lambda s: s + 2)
    numbers = jnp.concatenate([doc_ids[0], owned_ids, owner_dest[:, 0]])
    everyone = lax.all_gather(numbers, BOTH)

    own, other, after = [], [], []
    for part in range(PARTS):
        own.append(norm_part(raw, part))
        other.append(send(own[part], lambda s: s ^ 1))
        after.append(send(other[part], lambda s: s - 2 if s % 2 else None))

    outgoing = placed_rows(owned, owner_dest.reshape(1, -1), devices)
    arrived = lax.all_to_all(outgoing, BOTH, split_axis=0, concat_axis=0, tiled=True)
    next_rows = arrived.reshape(devices * CAP, width)

    me = (group * members + member).astype(jnp.int32)
    owners = everyone[:, rows:]
    next_ids = pl.pallas_call(
        lambda *refs: ids_kernel(owners.shape[1], *refs),
        in_specs=[pl.BlockSpec(memory_space=pltpu.SMEM)] + vmem(1),
        out_specs=pl.BlockSpec(memory_space=pltpu.VMEM),
        out_shape=jax.ShapeDtypeStruct((devices, CAP), jnp.int32),
        compiler_params=params(),
        name="ids",
    )(me.reshape(1), owners).reshape(devices * CAP)

    def ids_of(number):
        return lax.dynamic_slice(everyone, (group * members + number % members, 0), (1, rows))

    other_ids = ids_of(member + 1 - 2 * (member % 2))
    before_ids = ids_of(member + members - 2)
    after_ids = ids_of(member + 1)

    mine = pl.pallas_call(
        self_kernel,
        in_specs=vmem(PARTS + 2),
        out_specs=pl.BlockSpec(memory_space=pltpu.VMEM),
        out_shape=jax.ShapeDtypeStruct((1, rows), jnp.float32),
        scratch_shapes=[pltpu.VMEM((rows, 128), jnp.int32)],
        compiler_params=params(),
        name="within",
        cost_estimate=pl.CostEstimate(flops=2 * rows * rows * width, bytes_accessed=2 * rows * width, transcendentals=0),
    )(*own, doc_ids, prior_max)

    mine, others, before_normed = pl.pallas_call(
        main_kernel,
        in_specs=vmem(2 * PARTS) + [pl.BlockSpec(memory_space=pltpu.SMEM)] + vmem(5),
        out_specs=vmem(3),
        out_shape=[
            jax.ShapeDtypeStruct((1, rows), jnp.float32),
            jax.ShapeDtypeStruct((1, rows), jnp.float32),
            jax.ShapeDtypeStruct((rows, width), jnp.bfloat16),
        ],
        scratch_shapes=[pltpu.VMEM((rows, 128), jnp.int32)],
        compiler_params=params(),
        name="across",
        cost_estimate=pl.CostEstimate(
            flops=6 * rows * rows * width, bytes_accessed=8 * rows * width, transcendentals=rows
        ),
    )(*own, *other, where, before, doc_ids, other_ids, before_ids, mine)
    from_other = send(others, lambda s: s ^ 1)

    early = far(after[: PARTS - 1], where, before_normed, after_ids[:, : rows - size], before_ids)
    late = far(after[PARTS - 1 :], where, before_normed, after_ids[:, rows - size :], before_ids)
    from_far = send(jnp.concatenate([early, late], axis=1), lambda s: s + 1 if s % 2 else None)
    from_far = jnp.where(where[0] == 0, from_far, jnp.float32(LOWEST))
    running = jnp.maximum(jnp.maximum(mine, from_other), from_far)
    return (running, next_rows, next_ids)


def solution(mesh):
    return jax.shard_map(
        body,
        mesh=mesh,
        in_specs=(
            P("grp", "blk", None),
            P("grp", "blk"),
            P("grp", "blk"),
            P(("grp", "blk"), None),
            P(("grp", "blk")),
            P(("grp", "blk"), None),
        ),
        out_specs=(P("grp", "blk"), P(("grp", "blk"), None), P(("grp", "blk"))),
        check_vma=False,
    )
```

time: 178 us -> 419 us (2.35)
  blocking collectives: 0 us -> 353 us
  waiting for transfers between devices: 112 us -> 1.05 us
  matrix products: 16.7 us -> 0 us
  Pallas kernels: 0 us -> 15.6 us
  starting transfers between devices: 28.3 us -> 40.9 us
  other arithmetic: 8.36 us -> 0.62 us
    all_gather x0 -> x1, blocking collectives: none -> 353 us  [body(): everyone = lax.all_gather(numbers, BOTH)]
    all_to_all x4 -> x1, waiting for transfers between devices: 94.1 us -> 0.01 us  [body(): lax.all_to_all(outgoing, BOTH, split_axis=0, concat_axis=0, tiled=True)]
    ppermute x6 -> x11, starting transfers between devices: 7.07 us -> 29.6 us  [send(): return lax.ppermute(value, 'blk', pairs)]
    ppermute x6 -> x11, waiting for transfers between devices: 17.8 us -> 1.05 us  [send(): return lax.ppermute(value, 'blk', pairs)]
    dot_general x4 -> x0, matrix products: 16.7 us -> none  [tile_max(): lax.dot_general(row_normed, col_normed, (((1,), (1,)), ((), ())), preferr...]
    pallas_call x0 -> x10, Pallas kernels: none -> 15.6 us  [the longest x1 10.5 us: body(): pl.pallas_call(main_kernel, in_specs=vmem(2 * PARTS) + [pl.BlockSpec(memo...]
    all_to_all x4 -> x1, starting transfers between devices: 21.3 us -> 11.3 us  [body(): lax.all_to_all(outgoing, BOTH, split_axis=0, concat_axis=0, tiled=True)]
    reshape x5 -> x1, local copies, waits for them, and re-layouts: 5.55 us -> 0.69 us  [body(): next_ids = pl.pallas_call(lambda *refs: ids_kernel(owners.shape[1], *refs...]
  transfers between devices with their start and end apart: 10 -> 12, of which waited for: 6 -> 1; matrix products, arithmetic and copies ran while one was open for 15% -> 1% of each run, Pallas kernels for 0% -> 4%
where the time goes in v1:
time: 419 us
  blocking collectives  353 us (84%)
  starting transfers between devices  40.9 us (10%)
  Pallas kernels  15.6 us (4%)
  local copies, waits for them, and re-layouts  7.04 us (2%)
    all_gather x1, blocking collectives, body(): everyone = lax.all_gather(numbers, BOTH)  353 us
    ppermute x11, starting transfers between devices, send(): return lax.ppermute(value, 'blk', pairs)  29.6 us
    all_to_all x1, starting transfers between devices, body(): lax.all_to_all(outgoing, BOTH, split_axis=0, concat_axis=0, tiled=True)  11.3 us
    pallas_call x1, Pallas kernels, body(): pl.pallas_call(main_kernel, in_specs=vmem(2 * PARTS) + [pl.BlockSpec(memo...  10.5 us
  transfers between devices with their start and end apart: 12, of which 1 were waited for; matrix products, arithmetic and copies ran while one was open for 1% of the time, Pallas kernels for 4%

profile of v1, /device:TPU:0, one launch (start us, length us, event | category | flops | bytes accessed | tf_op | source)
XLA Modules:
  0.0 418.7 jit_solution(16324340301296604395)
XLA Ops:
  0.6 1.6 collective-permute-start.4
  2.3 0.0 copy-start
  2.3 1.6 copy-done
  3.9 0.2 norm_0.1.refs_0_
  4.1 1.7 collective-permute-start
  5.7 0.2 norm_1.1.refs_1_
  5.9 0.0 copy-start.2
  6.0 0.0 copy-start.4
  6.0 0.5 collective-permute-start.1
  6.5 0.2 norm_2.1.refs_2_
  6.7 1.7 collective-permute-start.2
  8.3 0.2 norm_3.1.refs_3_
  8.5 0.0 copy-start.3
  8.5 0.0 copy-start.8
  8.6 0.5 collective-permute-start.3
  9.1 0.0 copy-done.2
  9.1 0.0 copy-done.4
  9.1 0.0 copy-start.5
  9.1 1.6 place.1
  10.7 11.3 %all-to-all-start = ((bf16[128,4,1024]{2,1,0:T(4,128)(2,1)}), bf16[128,4,1024]{2,1,0:T(4,128)(2,1)}, u32[]{:S(2)}, u32[]{:S(2)}) async-start(bf16[128,4,1024]{2,1,0:T(4,128)(2,1)} %place.1), calls=%async_computation | async-start | bytes 2097152 | tf_op jit(solution)/shard_map/all_to_all | solution.py:211
  22.1 0.0 copy-done.3
  22.1 0.0 copy-done.8
  22.1 352.6 %all-gather.1 = s32[128,1,1536]{2,1,0:T(1,128)S(1)} all-gather(s32[1,1,1536]{2,1,0:T(1,128)S(1)} %reshape.27), channel_id=2, replica_groups=mesh['grp'=4,'blk'=32] {'grp','blk'}, dimensions={0}, use_global_device_ids=true | all-gather | bytes 792576 | tf_op jit(solution)/shard_map/all_gather | solution.py:202
  374.7 0.0 copy-start.6
  374.7 0.9 copy-done.6
  375.6 0.0 copy-done.5
  375.6 2.4 within.1.refs_13_
  378.0 0.0 collective-permute-done.refs_4_
  378.0 0.7 collective-permute-start.6
  378.7 0.0 collective-permute-done.1.refs_5_
  378.7 0.7 collective-permute-start.7
  379.4 0.0 collective-permute-done.2.refs_6_
  379.4 0.7 collective-permute-start.8
  380.1 0.0 collective-permute-done.3.refs_7_
  380.1 0.7 collective-permute-start.9
  380.8 0.0 collective-permute-done.4.refs_9_
  380.8 10.5 %across.1 = (f32[1,1024]{1,0:T(1,128)S(1)}, f32[1,1024]{1,0:T(1,128)S(1)}, bf16[1024,1024]{1,0:T(8,128)(2,1)}) custom-call(bf16[256,1024]{1,0:T(8,128)(2,1)S(1)} %norm_0.1.refs_0_, bf16[256,1024]{1,0:T(8,128)(2,1)S(1)} %norm_1.1.refs_1_, bf16[256,1024]{1,0:T(8,128)(2,1)S(1)} %norm_2.1.refs_2_, bf16[256,1024]{1,0:T(8,128)(2,1)S(1)} %norm_3.1.refs_3_, ...), custom_call_target="tpu_custom_call" | custom-call | flops 6442450944 | bytes 8388608 | tf_op jit(solution)/shard_map/across/pallas_call | solution.py:243
  391.3 0.0 collective-permute-done.9.refs_0_
  391.3 0.0 copy-start.1
  391.3 1.6 copy-done.1
  392.9 0.0 copy-start.7
  392.9 0.0 collective-permute-done.6.refs_0_
  392.9 0.0 collective-permute-done.7.refs_1_
  392.9 0.0 collective-permute-done.8.refs_2_
  393.0 1.4 collective-permute-start.10
  394.4 19.4 %collective-permute-start.5 = (f32[1,1024]{1,0:T(1,128)S(1)}, f32[1,1024]{1,0:T(1,128)S(1)}, u32[]{:S(2)}, u32[]{:S(2)}) collective-permute-start(f32[1,1024]{1,0:T(1,128)S(1)} %get-tuple-element.7), channel_id=1, source_target_pairs={{0,1},{1,0},{2,3},{3,2},{4,5},{5,4},{6,7},{7,6},{8,9},{9,8},{10,11... | collective-permute-start | bytes 12296 | tf_op jit(solution)/shard_map/ppermute | solution.py:23
  413.9 0.0 copy-done.7
  413.9 0.1 copy.11
  413.9 0.3 ids.1
  414.3 0.7 reshape.25
  415.0 0.0 all-to-all-done
  415.0 2.1 reshape.23
  417.1 1.0 collective-permute-done.10
  418.1 0.0 collective-permute-done.5
  418.1 0.6 fusion
  (9 shorter events, 0.1 us)
Async XLA Ops:
  0.6 380.2 %collective-permute-start.4 = (bf16[1024,1024]{1,0:T(8,128)(2,1)}, bf16[1024,1024]{1,0:T(8,128)(2,1)}, u32[]{:S(2)}, u32[]{:S(2)}) collective-permute-start(bf16[1024,1024]{1,0:T(8,128)(2,1)} %bitcast.15), channel_id=1, source_target_pairs={{0,2},{1,3},{2,4},{3,5},{4,6},{5,7},{6,8},{7,9},{8,10},{9,11},{10,... | collective-permute-start | bytes 6291464 | tf_op jit(solution)/shard_map/ppermute | solution.py:23
  2.3 1.6 copy-start
  4.1 373.9 %collective-permute-start = (bf16[256,1024]{1,0:T(8,128)(2,1)S(1)}, bf16[256,1024]{1,0:T(8,128)(2,1)S(1)}, u32[]{:S(2)}, u32[]{:S(2)}) collective-permute-start(bf16[256,1024]{1,0:T(8,128)(2,1)S(1)} %norm_0.1.refs_0_), channel_id=1, source_target_pairs={{0,1},{1,0},{2,3},{3,2},{4,5},{5,4},{6,7},{7,6},{8,9},{9,8},{10,11... | collective-permute-start | bytes 1572872 | tf_op jit(solution)/shard_map/ppermute | solution.py:23
  5.9 3.1 copy-start.2
  6.0 3.1 copy-start.4
  6.0 372.7 %collective-permute-start.1 = (bf16[256,1024]{1,0:T(8,128)(2,1)S(1)}, bf16[256,1024]{1,0:T(8,128)(2,1)S(1)}, u32[]{:S(2)}, u32[]{:S(2)}) collective-permute-start(bf16[256,1024]{1,0:T(8,128)(2,1)S(1)} %norm_1.1.refs_1_), channel_id=1, source_target_pairs={{0,1},{1,0},{2,3},{3,2},{4,5},{5,4},{6,7},{7,6},{8,9},{9,8},{10,11... | collective-permute-start | bytes 1572872 | tf_op jit(solution)/shard_map/ppermute | solution.py:23
  6.7 372.7 %collective-permute-start.2 = (bf16[256,1024]{1,0:T(8,128)(2,1)S(1)}, bf16[256,1024]{1,0:T(8,128)(2,1)}, u32[]{:S(2)}, u32[]{:S(2)}) collective-permute-start(bf16[256,1024]{1,0:T(8,128)(2,1)S(1)} %norm_2.1.refs_2_), channel_id=1, source_target_pairs={{0,1},{1,0},{2,3},{3,2},{4,5},{5,4},{6,7},{7,6},{8,9},{9,8},{10,11... | collective-permute-start | bytes 1572872 | tf_op jit(solution)/shard_map/ppermute | solution.py:23
  8.5 13.5 %copy-start.3 = (s32[1,1024]{1,0:T(1,128)S(1)}, s32[1,1024]{1,0:T(1,128)}, u32[]{:S(2)}) copy-start(s32[1,1024]{1,0:T(1,128)} %refs_10_.1) | copy-start | bytes 12292
  8.5 13.5 %copy-start.8 = (s32[256]{0:T(256)S(1)}, s32[256]{0:T(256)}, u32[]{:S(2)}) copy-start(s32[256]{0:T(256)} %param.10) | copy-start | bytes 3076
  8.6 371.6 %collective-permute-start.3 = (bf16[256,1024]{1,0:T(8,128)(2,1)S(1)}, bf16[256,1024]{1,0:T(8,128)(2,1)}, u32[]{:S(2)}, u32[]{:S(2)}) collective-permute-start(bf16[256,1024]{1,0:T(8,128)(2,1)S(1)} %norm_3.1.refs_3_), channel_id=1, source_target_pairs={{0,1},{1,0},{2,3},{3,2},{4,5},{5,4},{6,7},{7,6},{8,9},{9,8},{10,11... | collective-permute-start | bytes 1572872 | tf_op jit(solution)/shard_map/ppermute | solution.py:23
  9.1 366.5 %copy-start.5 = (f32[1,1024]{1,0:T(1,128)S(1)}, f32[1,1024]{1,0:T(1,128)}, u32[]{:S(2)}) copy-start(f32[1,1024]{1,0:T(1,128)} %refs_5_.1) | copy-start | bytes 12292
  10.7 404.2 %all-to-all-start = ((bf16[128,4,1024]{2,1,0:T(4,128)(2,1)}), bf16[128,4,1024]{2,1,0:T(4,128)(2,1)}, u32[]{:S(2)}, u32[]{:S(2)}) async-start(bf16[128,4,1024]{2,1,0:T(4,128)(2,1)} %place.1), calls=%async_computation | async-start | bytes 2097152 | tf_op jit(solution)/shard_map/all_to_all | solution.py:211
  374.7 0.9 copy-start.6
  378.0 14.9 %collective-permute-start.6 = (bf16[256,1024]{1,0:T(8,128)(2,1)S(1)}, bf16[256,1024]{1,0:T(8,128)(2,1)S(1)}, u32[]{:S(2)}, u32[]{:S(2)}) collective-permute-start(bf16[256,1024]{1,0:T(8,128)(2,1)S(1)} %collective-permute-done.refs_4_), channel_id=1, source_target_pairs={{1,31},{3,1},{5,3},{7,5},{9,7},{11,9},{13,11},{15,13},{17,15},{19,... | collective-permute-start | bytes 1572872 | tf_op jit(solution)/shard_map/ppermute | solution.py:23
  378.7 14.2 %collective-permute-start.7 = (bf16[256,1024]{1,0:T(8,128)(2,1)S(1)}, bf16[256,1024]{1,0:T(8,128)(2,1)S(1)}, u32[]{:S(2)}, u32[]{:S(2)}) collective-permute-start(bf16[256,1024]{1,0:T(8,128)(2,1)S(1)} %collective-permute-done.1.refs_5_), channel_id=1, source_target_pairs={{1,31},{3,1},{5,3},{7,5},{9,7},{11,9},{13,11},{15,13},{17,15},{19,... | collective-permute-start | bytes 1572872 | tf_op jit(solution)/shard_map/ppermute | solution.py:23
  379.4 13.5 %collective-permute-start.8 = (bf16[256,1024]{1,0:T(8,128)(2,1)}, bf16[256,1024]{1,0:T(8,128)(2,1)S(1)}, u32[]{:S(2)}, u32[]{:S(2)}) collective-permute-start(bf16[256,1024]{1,0:T(8,128)(2,1)} %collective-permute-done.2.refs_6_), channel_id=1, source_target_pairs={{1,31},{3,1},{5,3},{7,5},{9,7},{11,9},{13,11},{15,13},{17,15},{19,... | collective-permute-start | bytes 1572872 | tf_op jit(solution)/shard_map/ppermute | solution.py:23
  380.1 11.2 %collective-permute-start.9 = (bf16[256,1024]{1,0:T(8,128)(2,1)}, bf16[256,1024]{1,0:T(8,128)(2,1)S(1)}, u32[]{:S(2)}, u32[]{:S(2)}) collective-permute-start(bf16[256,1024]{1,0:T(8,128)(2,1)} %collective-permute-done.3.refs_7_), channel_id=1, source_target_pairs={{1,31},{3,1},{5,3},{7,5},{9,7},{11,9},{13,11},{15,13},{17,15},{19,... | collective-permute-start | bytes 1572872 | tf_op jit(solution)/shard_map/ppermute | solution.py:23
  391.3 1.6 copy-start.1
  392.9 20.9 %copy-start.7 = (s32[128,1,1536]{2,1,0:T(1,128)S(1)}, s32[128,1,1536]{2,1,0:T(1,128)}, u32[]{:S(2)}) copy-start(s32[128,1,1536]{2,1,0:T(1,128)} %copy-done.6) | copy-start | bytes 2359300
  393.0 25.1 %collective-permute-start.10 = (f32[1,1024]{1,0:T(1,128)S(1)}, f32[1,1024]{1,0:T(1,128)S(1)}, u32[]{:S(2)}, u32[]{:S(2)}) collective-permute-start(f32[1,1024]{1,0:T(1,128)S(1)} %pad_maximum_fusion), channel_id=1, source_target_pairs={{1,2},{3,4},{5,6},{7,8},{9,10},{11,12},{13,14},{15,16},{17,18},{19... | collective-permute-start | bytes 12296 | tf_op jit(solution)/shard_map/ppermute | solution.py:23
  394.4 23.7 %collective-permute-start.5 = (f32[1,1024]{1,0:T(1,128)S(1)}, f32[1,1024]{1,0:T(1,128)S(1)}, u32[]{:S(2)}, u32[]{:S(2)}) collective-permute-start(f32[1,1024]{1,0:T(1,128)S(1)} %get-tuple-element.7), channel_id=1, source_target_pairs={{0,1},{1,0},{2,3},{3,2},{4,5},{5,4},{6,7},{7,6},{8,9},{9,8},{10,11... | collective-permute-start | bytes 12296 | tf_op jit(solution)/shard_map/ppermute | solution.py:23

commit v2 on v0

v2 whole, which is shorter than its diff:
```python
import jax
import jax.numpy as jnp
from jax import lax
from jax.experimental import pallas as pl
from jax.experimental.pallas import tpu as pltpu
from jax.sharding import PartitionSpec as P

CAP = 4
PARTS = 4
LOWEST = -2.0
EXTRA = 16
BOTH = ("grp", "blk")


def normalize(matrix):
    values = matrix.astype(jnp.float32)
    scale = lax.rsqrt(jnp.sum(values * values, axis=-1, keepdims=True) + 1e-06)
    return (values * scale).astype(jnp.bfloat16)


def send(value, to):
    count = lax.axis_size("blk")
    pairs = [(s, to(s) % count) for s in range(count) if to(s) is not None]
    return lax.ppermute(value, "blk", pairs)


def params():
    return pltpu.CompilerParams(vmem_limit_bytes=48 * 1024 * 1024)


def vmem(n):
    return [pl.BlockSpec(memory_space=pltpu.VMEM)] * n


def down(row):
    return jnp.broadcast_to(row, (128, row.shape[1])).T


def best(rows, row_ids, cols, col_down):
    scores = lax.dot_general(cols, rows, (((1,), (1,)), ((), ())), preferred_element_type=jnp.float32)
    found = []
    for left in range(0, rows.shape[0], 128):
        keep = col_down < row_ids[:, left : left + 128]
        part = jnp.where(keep, scores[:, left : left + 128], jnp.float32(LOWEST))
        found.append(jnp.max(part, axis=0, keepdims=True))
    return jnp.concatenate(found, axis=1)


def halves(numbers):
    numbers = numbers.astype(jnp.int32)
    return (numbers >> 7).astype(jnp.float32), (numbers & 127).astype(jnp.float32)


def number_rows(ref):
    tail = ref[ref.shape[0] - EXTRA :, :].astype(jnp.float32)
    return (tail[0:1, :] * 128.0 + tail[1:2, :]).astype(jnp.int32)


def tail_rows(ids, width):
    ids = jnp.concatenate([ids, jnp.zeros((1, width - ids.shape[1]), jnp.int32)], axis=1) if ids.shape[1] < width else ids
    high, low = halves(ids)
    row = lax.broadcasted_iota(jnp.int32, (EXTRA, width), 0)
    return jnp.where(row == 0, high, jnp.where(row == 1, low, 0.0)).astype(jnp.bfloat16)


def first_kernel(x_ref, ids_ref, out_ref):
    size, width = x_ref.shape
    out_ref[:size, :] = normalize(x_ref[...])
    out_ref[size:, :] = tail_rows(ids_ref[:, :size], width)


def rest_kernel(x_ref, ids_ref, first_ref, *outs):
    whole_ref = outs[-1]
    rows, width = x_ref.shape
    size = rows // PARTS
    whole_ref[:size, :] = first_ref[:size, :]
    for part in range(1, PARTS):
        at = slice(part * size, (part + 1) * size)
        normed = normalize(x_ref[at, :])
        outs[part - 1][:size, :] = normed
        outs[part - 1][size:, :] = tail_rows(ids_ref[:, at], width)
        whole_ref[at, :] = normed
    whole_ref[rows:, :] = tail_rows(ids_ref[...], width)


def norm_parts(embeds, ids):
    rows, width = embeds.shape
    size = rows // PARTS

    def cost(part):
        return pl.CostEstimate(flops=4 * part * width, bytes_accessed=4 * part * width, transcendentals=part)

    def shape(part):
        return jax.ShapeDtypeStruct((part, width), jnp.bfloat16)

    first = pl.pallas_call(
        first_kernel,
        grid=(1,),
        in_specs=[
            pl.BlockSpec((size, width), lambda i: (0, 0)),
            pl.BlockSpec((1, rows), lambda i: (0, 0)),
        ],
        out_specs=pl.BlockSpec((size + EXTRA, width), lambda i: (0, 0)),
        out_shape=shape(size + EXTRA),
        compiler_params=params(),
        name="norm_first",
        cost_estimate=cost(size),
    )(embeds, ids)
    rest = pl.pallas_call(
        rest_kernel,
        in_specs=vmem(3),
        out_specs=vmem(PARTS),
        out_shape=[shape(size + EXTRA)] * (PARTS - 1) + [shape(rows + EXTRA)],
        compiler_params=params(),
        name="norm_rest",
        cost_estimate=cost(rows),
    )(embeds, ids, first)
    return [first, *rest[:-1]], rest[-1]


def place_kernel(rows_ref, target_ref, ids_ref, out_ref):
    count, width = rows_ref.shape
    target = target_ref[...]
    across = jnp.broadcast_to(target, (count, count))
    earlier = lax.broadcasted_iota(jnp.int32, (count, count), 0) < lax.broadcasted_iota(
        jnp.int32, (count, count), 1
    )
    same = (across.T == across) & earlier
    position = jnp.sum(same.astype(jnp.float32), axis=0, keepdims=True).astype(jnp.int32)
    place = target * CAP + position
    devices = out_ref.shape[0]
    slots = devices * CAP
    pick = (lax.broadcasted_iota(jnp.int32, (slots, count), 0) == place).astype(jnp.float32).astype(jnp.bfloat16)
    placed = jnp.dot(pick, normalize(rows_ref[...]), preferred_element_type=jnp.float32)
    out_ref[:, :, :width] = placed.astype(jnp.bfloat16).reshape(devices, CAP, width)
    high, low = halves(down(ids_ref[...]))
    lane = lax.broadcasted_iota(jnp.int32, high.shape, 1)
    pair = jnp.where(lane < 64, high + 1.0, low).astype(jnp.bfloat16)
    tail = jnp.dot(pick, pair, preferred_element_type=jnp.float32)
    out_ref[:, :, width:] = tail.astype(jnp.bfloat16).reshape(devices, CAP, 128)


def placed_rows(owned, target, ids, devices):
    count, width = owned.shape
    return pl.pallas_call(
        place_kernel,
        in_specs=vmem(3),
        out_specs=pl.BlockSpec(memory_space=pltpu.VMEM),
        out_shape=jax.ShapeDtypeStruct((devices, CAP, width + 128), jnp.bfloat16),
        compiler_params=params(),
        name="place",
        cost_estimate=pl.CostEstimate(
            flops=2 * devices * CAP * count * width, bytes_accessed=2 * (count + devices * CAP) * width, transcendentals=count
        ),
    )(owned, target, ids)


def split_kernel(in_ref, rows_ref, ids_ref):
    slots, width = rows_ref.shape
    rows_ref[...] = in_ref[:, :, :width].reshape(slots, width)
    tail = in_ref[:, :, width:].reshape(slots, 128).astype(jnp.float32).T
    high, low = tail[0:1, :], tail[64:65, :]
    ids_ref[...] = jnp.where(high == 0.0, -1.0, (high - 1.0) * 128.0 + low).astype(jnp.int32)


def split_rows(arrived):
    devices, cap, wide = arrived.shape
    slots, width = devices * cap, wide - 128
    return pl.pallas_call(
        split_kernel,
        in_specs=vmem(1),
        out_specs=vmem(2),
        out_shape=[
            jax.ShapeDtypeStruct((slots, width), jnp.bfloat16),
            jax.ShapeDtypeStruct((1, slots), jnp.int32),
        ],
        compiler_params=params(),
        name="split",
        cost_estimate=pl.CostEstimate(flops=0, bytes_accessed=4 * slots * width, transcendentals=0),
    )(arrived)


def self_kernel(whole_ref, ids_ref, prior_ref, out_ref, down_ref):
    rows = ids_ref.shape[1]
    size = rows // PARTS
    down_ref[...] = down(ids_ref[...])
    out_ref[...] = prior_ref[...]
    parts = [whole_ref.at[r * size : (r + 1) * size, :] for r in range(PARTS)]
    against(parts, ids_ref[...], whole_ref[:rows, :], down_ref, out_ref)


def against(row_refs, row_ids, cols, down_ref, out_ref):
    size = out_ref.shape[1] // len(row_refs)
    for r, rows in enumerate(row_refs):
        at = slice(r * size, (r + 1) * size)
        found = best(rows[:size, :], row_ids[:, at], cols, down_ref[...])
        out_ref[:, at] = jnp.maximum(out_ref[:, at], found)


def main_kernel(*refs):
    own, other = refs[:PARTS], refs[PARTS : 2 * PARTS]
    whole_ref, before_ref, where_ref, ids_ref, so_far_ref, own_out, other_out, down_ref = refs[2 * PARTS :]
    rows = ids_ref.shape[1]
    size = rows // PARTS
    other_ids = jnp.concatenate([number_rows(part)[:, :size] for part in other], axis=1)
    down_ref[...] = down(number_rows(before_ref))
    own_out[...] = so_far_ref[...]
    other_out[...] = jnp.full(other_out.shape, LOWEST, jnp.float32)
    against(own, ids_ref[...], before_ref[:rows, :], down_ref, own_out)
    against(other, other_ids, before_ref[:rows, :], down_ref, other_out)

    @pl.when(where_ref[0] == 0)
    def _():
        down_ref[...] = down(ids_ref[...])
        against(other, other_ids, whole_ref[:rows, :], down_ref, other_out)


def far_kernel(part, rows_ref, before_ref, where_ref, so_far_ref, out_ref, down_ref):
    rows = out_ref.shape[1]
    size = rows // PARTS
    out_ref[...] = so_far_ref[...]

    @pl.when(where_ref[0] == 1)
    def _():
        down_ref[...] = down(number_rows(before_ref))
        at = slice(part * size, (part + 1) * size)
        against([rows_ref], number_rows(rows_ref)[:, :size], before_ref[:rows, :], down_ref, out_ref.at[:, at])


def far(after, where, before):
    size, width = after[0].shape
    rows = PARTS * (size - EXTRA)
    found = jnp.full((1, rows), LOWEST, jnp.float32)
    for part in range(PARTS):
        found = pl.pallas_call(
            lambda *refs, part=part: far_kernel(part, *refs),
            in_specs=vmem(2) + [pl.BlockSpec(memory_space=pltpu.SMEM)] + vmem(1),
            out_specs=pl.BlockSpec(memory_space=pltpu.VMEM),
            out_shape=jax.ShapeDtypeStruct((1, rows), jnp.float32),
            scratch_shapes=[pltpu.VMEM((rows, 128), jnp.int32)],
            compiler_params=params(),
            name=f"far_{part}",
            cost_estimate=pl.CostEstimate(
                flops=2 * size * rows * width, bytes_accessed=2 * (size + rows) * width, transcendentals=0
            ),
        )(after[part], before, where, found)
    return found


def body(embeds, doc_ids, prior_max, owned, owned_ids, owner_dest):
    members = lax.axis_size("blk")
    devices = lax.axis_size("grp") * members
    raw = embeds[0]
    rows, width = raw.shape
    where = (lax.axis_index("blk") & 1).astype(jnp.int32).reshape(1)

    own, whole = norm_parts(raw, doc_ids)
    other = [send(part, lambda s: s ^ 1) for part in own]
    before = send(whole, lambda s: s + 2)
    after = [send(part, lambda s: s - 2 if s % 2 else None) for part in other]

    outgoing = placed_rows(owned, owner_dest.reshape(1, -1), owned_ids.reshape(1, -1), devices)
    next_rows, next_ids = split_rows(lax.all_to_all(outgoing, BOTH, split_axis=0, concat_axis=0, tiled=True))

    mine = pl.pallas_call(
        self_kernel,
        in_specs=vmem(3),
        out_specs=pl.BlockSpec(memory_space=pltpu.VMEM),
        out_shape=jax.ShapeDtypeStruct((1, rows), jnp.float32),
        scratch_shapes=[pltpu.VMEM((rows, 128), jnp.int32)],
        compiler_params=params(),
        name="within",
        cost_estimate=pl.CostEstimate(flops=2 * rows * rows * width, bytes_accessed=2 * rows * width, transcendentals=0),
    )(whole, doc_ids, prior_max)

    mine, others = pl.pallas_call(
        main_kernel,
        in_specs=vmem(2 * PARTS + 2) + [pl.BlockSpec(memory_space=pltpu.SMEM)] + vmem(2),
        out_specs=vmem(2),
        out_shape=[jax.ShapeDtypeStruct((1, rows), jnp.float32)] * 2,
        scratch_shapes=[pltpu.VMEM((rows, 128), jnp.int32)],
        compiler_params=params(),
        name="across",
        cost_estimate=pl.CostEstimate(flops=6 * rows * rows * width, bytes_accessed=6 * rows * width, transcendentals=0),
    )(*own, *other, whole, before, where, doc_ids, mine)
    from_other = send(others, lambda s: s ^ 1)

    from_far = send(far(after, where, before), lambda s: s + 1 if s % 2 else None)
    from_far = jnp.where(where[0] == 0, from_far, jnp.float32(LOWEST))
    running = jnp.maximum(jnp.maximum(mine, from_other), from_far)
    return (running, next_rows, next_ids.reshape(-1))


def solution(mesh):
    return jax.shard_map(
        body,
        mesh=mesh,
        in_specs=(
            P("grp", "blk", None),
            P("grp", "blk"),
            P("grp", "blk"),
            P(("grp", "blk"), None),
            P(("grp", "blk")),
            P(("grp", "blk"), None),
        ),
        out_specs=(P("grp", "blk"), P(("grp", "blk"), None), P(("grp", "blk"))),
        check_vma=False,
    )
```

time: 178 us -> 102 us (0.57)
  waiting for transfers between devices: 112 us -> 43.7 us
  Pallas kernels: 0 us -> 19.1 us
  matrix products: 16.7 us -> 0 us
  other arithmetic: 8.36 us -> 0.6 us
    all_to_all x4 -> x1, waiting for transfers between devices: 94.1 us -> 0.01 us  [body(): lax.all_to_all(outgoing, BOTH, split_axis=0, concat_axis=0, tiled=True)]
    ppermute x6 -> x11, waiting for transfers between devices: 17.8 us -> 43.7 us  [send(): return lax.ppermute(value, 'blk', pairs)]
    pallas_call x0 -> x10, Pallas kernels: none -> 19.2 us  [the longest x1 10.5 us: body(): pl.pallas_call(main_kernel, in_specs=vmem(2 * PARTS + 2) + [pl.BlockSpec(...]
    dot_general x4 -> x0, matrix products: 16.7 us -> none  [tile_max(): lax.dot_general(row_normed, col_normed, (((1,), (1,)), ((), ())), preferr...]
    all_to_all x4 -> x1, starting transfers between devices: 21.3 us -> 10.8 us  [body(): lax.all_to_all(outgoing, BOTH, split_axis=0, concat_axis=0, tiled=True)]
    ppermute x6 -> x11, starting transfers between devices: 7.07 us -> 17.4 us  [send(): return lax.ppermute(value, 'blk', pairs)]
    unnamed x13 -> x24, local copies, waits for them, and re-layouts: 0.79 us -> 9.44 us
    reshape x6 -> x0, local copies, waits for them, and re-layouts: 6.63 us -> none  [the longest x2 4.07 us: body(): outgoing.reshape(groups, members, CAP, width)]
  transfers between devices with their start and end apart: 10 -> 12, of which waited for: 6 -> 5; matrix products, arithmetic and copies ran while one was open for 15% -> 0% of each run, Pallas kernels for 0% -> 14%
where the time goes in v2:
time: 102 us
  waiting for transfers between devices  43.7 us (43%)
  starting transfers between devices  28.1 us (28%)
  Pallas kernels  19.1 us (19%)
  local copies, waits for them, and re-layouts  9.44 us (9%)
    ppermute x11, waiting for transfers between devices, send(): return lax.ppermute(value, 'blk', pairs)  43.7 us
    ppermute x11, starting transfers between devices, send(): return lax.ppermute(value, 'blk', pairs)  17.4 us
    all_to_all x1, starting transfers between devices, body(): lax.all_to_all(outgoing, BOTH, split_axis=0, concat_axis=0, tiled=True)  10.8 us
    pallas_call x1, Pallas kernels, body(): pl.pallas_call(main_kernel, in_specs=vmem(2 * PARTS + 2) + [pl.BlockSpec(...  10.5 us
    unnamed x24, local copies, waits for them, and re-layouts  9.44 us
    pallas_call x1, Pallas kernels, norm_parts(): pl.pallas_call(rest_kernel, in_specs=vmem(3), out_specs=vmem(PARTS), out_...  3.43 us
    pallas_call x1, Pallas kernels, body(): pl.pallas_call(self_kernel, in_specs=vmem(3), out_specs=pl.BlockSpec(memo...  2.37 us
  transfers between devices with their start and end apart: 12, of which 5 were waited for; matrix products, arithmetic and copies ran while one was open for 0% of the time, Pallas kernels for 14%

profile of v2, /device:TPU:0, one launch (start us, length us, event | category | flops | bytes accessed | tf_op | source)
XLA Modules:
  0.0 101.8 jit_solution(3152851050107635869)
XLA Ops:
  0.6 0.0 copy-start.3
  0.6 1.6 %copy-done.3 = bf16[1,1024,1024]{2,1,0:T(8,128)(2,1)S(1)} copy-done((bf16[1,1024,1024]{2,1,0:T(8,128)(2,1)S(1)}, bf16[1,1024,1024]{2,1,0:T(8,128)(2,1)}, u32[]{:S(2)}) %copy-start.3) | copy-done | bytes 2097176
  2.2 0.0 copy-start.6
  2.2 0.7 copy-done.6
  2.9 0.0 copy-start.7
  2.9 0.0 copy-start.5
  2.9 0.0 copy-start.8
  2.9 0.0 copy-start.9
  2.9 1.0 norm_first.1.first_ref.refs_0_
  3.9 0.0 copy-done.7
  3.9 3.4 %norm_rest.1 = (bf16[272,1024]{1,0:T(8,128)(2,1)}, bf16[272,1024]{1,0:T(8,128)(2,1)}, bf16[272,1024]{1,0:T(8,128)(2,1)}, bf16[1040,1024]{1,0:T(8,128)(2,1)}) custom-call(bf16[1024,1024]{1,0:T(8,128)(2,1)S(1)} %bitcast.6, s32[1,1024]{1,0:T(1,128)S(1)} %copy-done.7, bf16[272,1024]{1,0:T(8,128)(2,1)} %norm_first.1.first_ref.refs_0_), custom_call_target="tpu_custom_call" | custom-call | flops 4194304 | bytes 4194304 | tf_op jit(solution)/shard_map/norm_rest/pallas_call | solution.py:109
  7.3 0.0 copy-start.11
  7.3 1.6 %collective-permute-start.4 = (bf16[1040,1024]{1,0:T(8,128)(2,1)}, bf16[1040,1024]{1,0:T(8,128)(2,1)S(1)}, u32[]{:S(2)}, u32[]{:S(2)}) collective-permute-start(bf16[1040,1024]{1,0:T(8,128)(2,1)} %get-tuple-element.14.whole_ref.refs_8_), channel_id=1, source_target_pairs={{0,2},{1,3},{2,4},{3,5},{4,6},{5,7},{6,8},{7,9},{8,10},{9,11},{10,... | collective-permute-start | bytes 6389768 | tf_op jit(solution)/shard_map/ppermute | solution.py:24
  8.9 1.6 %collective-permute-start = (bf16[272,1024]{1,0:T(8,128)(2,1)}, bf16[272,1024]{1,0:T(8,128)(2,1)}, u32[]{:S(2)}, u32[]{:S(2)}) collective-permute-start(bf16[272,1024]{1,0:T(8,128)(2,1)} %norm_first.1.first_ref.refs_0_), channel_id=1, source_target_pairs={{0,1},{1,0},{2,3},{3,2},{4,5},{5,4},{6,7},{7,6},{8,9},{9,8},{10,11... | collective-permute-start | bytes 1671176 | tf_op jit(solution)/shard_map/ppermute | solution.py:24
  10.5 0.4 collective-permute-start.1
  10.9 1.6 %collective-permute-start.2 = (bf16[272,1024]{1,0:T(8,128)(2,1)}, bf16[272,1024]{1,0:T(8,128)(2,1)}, u32[]{:S(2)}, u32[]{:S(2)}) collective-permute-start(bf16[272,1024]{1,0:T(8,128)(2,1)} %get-tuple-element.12.refs_2_), channel_id=1, source_target_pairs={{0,1},{1,0},{2,3},{3,2},{4,5},{5,4},{6,7},{7,6},{8,9},{9,8},{10,11... | collective-permute-start | bytes 1671176 | tf_op jit(solution)/shard_map/ppermute | solution.py:24
  12.5 0.4 collective-permute-start.3
  13.0 0.0 copy-done.5
  13.0 0.0 copy-done.8
  13.0 0.0 copy-done.9
  13.0 0.7 place.1
  13.7 0.0 copy-start.4
  13.7 1.0 %copy-done.4 = bf16[128,4,1152]{2,1,0:T(4,128)(2,1)} copy-done((bf16[128,4,1152]{2,1,0:T(4,128)(2,1)}, bf16[128,4,1152]{2,1,0:T(4,128)(2,1)S(1)}, u32[]{:S(2)}) %copy-start.4) | copy-done | bytes 1179672
  14.8 10.8 %all-to-all-start = ((bf16[128,4,1152]{2,1,0:T(4,128)(2,1)}), bf16[128,4,1152]{2,1,0:T(4,128)(2,1)S(1)}, u32[]{:S(2)}, u32[]{:S(2)}) async-start(bf16[128,4,1152]{2,1,0:T(4,128)(2,1)} %copy-done.4), calls=%async_computation | async-start | bytes 2359296 | tf_op jit(solution)/shard_map/all_to_all | solution.py:263
  25.5 0.0 copy-done.11
  25.6 0.0 copy-start.10
  25.6 1.6 %copy-done.10 = bf16[1040,1024]{1,0:T(8,128)(2,1)S(1)} copy-done((bf16[1040,1024]{1,0:T(8,128)(2,1)S(1)}, bf16[1040,1024]{1,0:T(8,128)(2,1)}, u32[]{:S(2)}) %copy-start.10) | copy-done | bytes 2129944
  27.2 2.4 %within.1.refs_12_ = f32[1,1024]{1,0:T(1,128)S(1)} custom-call(bf16[1040,1024]{1,0:T(8,128)(2,1)S(1)} %copy-done.10, s32[1,1024]{1,0:T(1,128)S(1)} %copy-done.7, f32[1,1024]{1,0:T(1,128)S(1)} %copy-done.11), custom_call_target="tpu_custom_call" | custom-call | flops 2147483648 | bytes 2097152 | tf_op jit(solution)/shard_map/within/pallas_call | solution.py:265
  29.5 0.0 collective-permute-done.refs_4_
  29.5 0.7 collective-permute-start.9
  30.2 9.4 %collective-permute-done.1.refs_5_ = bf16[272,1024]{1,0:T(8,128)(2,1)} collective-permute-done((bf16[272,1024]{1,0:T(8,128)(2,1)}, bf16[272,1024]{1,0:T(8,128)(2,1)}, u32[]{:S(2)}, u32[]{:S(2)}) %collective-permute-start.1) | collective-permute-done | bytes 557088 | tf_op jit(solution)/shard_map/ppermute | solution.py:24
  39.7 0.7 collective-permute-start.8
  40.4 11.4 %collective-permute-done.2.refs_6_ = bf16[272,1024]{1,0:T(8,128)(2,1)} collective-permute-done((bf16[272,1024]{1,0:T(8,128)(2,1)}, bf16[272,1024]{1,0:T(8,128)(2,1)}, u32[]{:S(2)}, u32[]{:S(2)}) %collective-permute-start.2) | collective-permute-done | bytes 557088 | tf_op jit(solution)/shard_map/ppermute | solution.py:24
  51.8 0.7 collective-permute-start.7
  52.5 13.0 %collective-permute-done.3.refs_7_ = bf16[272,1024]{1,0:T(8,128)(2,1)} collective-permute-done((bf16[272,1024]{1,0:T(8,128)(2,1)}, bf16[272,1024]{1,0:T(8,128)(2,1)}, u32[]{:S(2)}, u32[]{:S(2)}) %collective-permute-start.3) | collective-permute-done | bytes 557088 | tf_op jit(solution)/shard_map/ppermute | solution.py:24
  65.6 0.7 collective-permute-start.6
  66.3 2.3 %collective-permute-done.4.refs_9_.refs_1_ = bf16[1040,1024]{1,0:T(8,128)(2,1)S(1)} collective-permute-done((bf16[1040,1024]{1,0:T(8,128)(2,1)}, bf16[1040,1024]{1,0:T(8,128)(2,1)S(1)}, u32[]{:S(2)}, u32[]{:S(2)}) %collective-permute-start.4) | collective-permute-done | bytes 2129952 | tf_op jit(solution)/shard_map/ppermute | solution.py:24
  68.6 0.0 copy-start
  68.6 1.3 %copy-done = bf16[1040,1024]{1,0:T(8,128)(2,1)} copy-done((bf16[1040,1024]{1,0:T(8,128)(2,1)}, bf16[1040,1024]{1,0:T(8,128)(2,1)S(1)}, u32[]{:S(2)}) %copy-start) | copy-done | bytes 2129944
  69.9 10.5 %across.1 = (f32[1,1024]{1,0:T(1,128)S(1)}, f32[1,1024]{1,0:T(1,128)S(1)}) custom-call(bf16[272,1024]{1,0:T(8,128)(2,1)} %norm_first.1.first_ref.refs_0_, bf16[272,1024]{1,0:T(8,128)(2,1)} %get-tuple-element.11.refs_1_, bf16[272,1024]{1,0:T(8,128)(2,1)} %get-tuple-element.12.refs_2_, bf16[272,1024]{1,0:T(8,128)(2,1)} %get-tuple-element.13.refs_3_, ...), custom_call_target="tpu_custom_call" | custom-call | flops 6442450944 | bytes 6291456 | tf_op jit(solution)/shard_map/across/pallas_call | solution.py:276
  80.4 7.7 %collective-permute-start.5 = (f32[1,1024]{1,0:T(1,128)S(1)}, f32[1,1024]{1,0:T(1,128)S(1)}, u32[]{:S(2)}, u32[]{:S(2)}) collective-permute-start(f32[1,1024]{1,0:T(1,128)S(1)} %get-tuple-element.16), channel_id=1, source_target_pairs={{0,1},{1,0},{2,3},{3,2},{4,5},{5,4},{6,7},{7,6},{8,9},{9,8},{10,11... | collective-permute-start | bytes 12296 | tf_op jit(solution)/shard_map/ppermute | solution.py:24
  88.1 0.0 collective-permute-done.9.refs_0_
  88.1 0.0 copy-start.1
  88.1 1.6 %copy-done.1 = bf16[1040,1024]{1,0:T(8,128)(2,1)S(1)} copy-done((bf16[1040,1024]{1,0:T(8,128)(2,1)S(1)}, bf16[1040,1024]{1,0:T(8,128)(2,1)}, u32[]{:S(2)}) %copy-start.1) | copy-done | bytes 2129944
  89.7 0.0 copy-start.2
  89.7 0.0 collective-permute-done.8.refs_0_
  89.7 1.6 %copy-done.2 = bf16[1040,1024]{1,0:T(8,128)(2,1)S(1)} copy-done((bf16[1040,1024]{1,0:T(8,128)(2,1)S(1)}, bf16[1040,1024]{1,0:T(8,128)(2,1)}, u32[]{:S(2)}) %copy-start.2) | copy-done | bytes 2129944
  91.3 0.0 collective-permute-done.7.refs_0_
  91.3 0.0 collective-permute-done.6.refs_0_
  91.3 1.3 %collective-permute-start.10 = (f32[1,1024]{1,0:T(1,128)S(1)}, f32[1,1024]{1,0:T(1,128)S(1)}, u32[]{:S(2)}, u32[]{:S(2)}) collective-permute-start(f32[1,1024]{1,0:T(1,128)S(1)} %far_3.1), channel_id=1, source_target_pairs={{1,2},{3,4},{5,6},{7,8},{9,10},{11,12},{13,14},{15,16},{17,18},{19... | collective-permute-start | bytes 12296 | tf_op jit(solution)/shard_map/ppermute | solution.py:24
  92.6 0.0 all-to-all-done.in_ref
  92.6 1.1 %split.1 = (bf16[512,1024]{1,0:T(8,128)(2,1)}, s32[1,512]{1,0:T(1,128)}) custom-call(bf16[128,4,1152]{2,1,0:T(4,128)(2,1)S(1)} %all-to-all-done.in_ref), custom_call_target="tpu_custom_call" | custom-call | bytes 2097152 | tf_op jit(solution)/shard_map/split/pallas_call | solution.py:169
  93.8 0.0 collective-permute-done.5
  93.8 7.5 %collective-permute-done.10 = f32[1,1024]{1,0:T(1,128)S(1)} collective-permute-done((f32[1,1024]{1,0:T(1,128)S(1)}, f32[1,1024]{1,0:T(1,128)S(1)}, u32[]{:S(2)}, u32[]{:S(2)}) %collective-permute-start.10) | collective-permute-done | bytes 4128 | tf_op jit(solution)/shard_map/ppermute | solution.py:24
  101.2 0.6 fusion
  (5 shorter events, 0.0 us)
Async XLA Ops:
  0.6 1.6 %copy-start.3 = (bf16[1,1024,1024]{2,1,0:T(8,128)(2,1)S(1)}, bf16[1,1024,1024]{2,1,0:T(8,128)(2,1)}, u32[]{:S(2)}) copy-start(bf16[1,1024,1024]{2,1,0:T(8,128)(2,1)} %param.6) | copy-start | bytes 6291460
  2.2 0.7 copy-start.6
  2.9 1.0 copy-start.7
  2.9 10.1 %copy-start.5 = (bf16[256,1024]{1,0:T(8,128)(2,1)S(1)}, bf16[256,1024]{1,0:T(8,128)(2,1)}, u32[]{:S(2)}) copy-start(bf16[256,1024]{1,0:T(8,128)(2,1)} %rows_ref.1) | copy-start | bytes 1572868
  2.9 10.1 %copy-start.8 = (s32[256,1]{0,1:T(1,128)S(1)}, s32[256,1]{0,1:T(1,128)}, u32[]{:S(2)}) copy-start(s32[256,1]{0,1:T(1,128)} %param.11) | copy-start | bytes 3076
  2.9 10.1 %copy-start.9 = (s32[256]{0:T(256)S(1)}, s32[256]{0:T(256)}, u32[]{:S(2)}) copy-start(s32[256]{0:T(256)} %param.10) | copy-start | bytes 3076
  7.3 18.2 %copy-start.11 = (f32[1,1024]{1,0:T(1,128)S(1)}, f32[1,1024]{1,0:T(1,128)}, u32[]{:S(2)}) copy-start(f32[1,1024]{1,0:T(1,128)} %prior_ref.1) | copy-start | bytes 12292
  7.3 61.2 %collective-permute-start.4 = (bf16[1040,1024]{1,0:T(8,128)(2,1)}, bf16[1040,1024]{1,0:T(8,128)(2,1)S(1)}, u32[]{:S(2)}, u32[]{:S(2)}) collective-permute-start(bf16[1040,1024]{1,0:T(8,128)(2,1)} %get-tuple-element.14.whole_ref.refs_8_), channel_id=1, source_target_pairs={{0,2},{1,3},{2,4},{3,5},{4,6},{5,7},{6,8},{7,9},{8,10},{9,11},{10,... | collective-permute-start | bytes 6389768 | tf_op jit(solution)/shard_map/ppermute | solution.py:24
  8.9 20.6 %collective-permute-start = (bf16[272,1024]{1,0:T(8,128)(2,1)}, bf16[272,1024]{1,0:T(8,128)(2,1)}, u32[]{:S(2)}, u32[]{:S(2)}) collective-permute-start(bf16[272,1024]{1,0:T(8,128)(2,1)} %norm_first.1.first_ref.refs_0_), channel_id=1, source_target_pairs={{0,1},{1,0},{2,3},{3,2},{4,5},{5,4},{6,7},{7,6},{8,9},{9,8},{10,11... | collective-permute-start | bytes 1671176 | tf_op jit(solution)/shard_map/ppermute | solution.py:24
  10.5 29.2 %collective-permute-start.1 = (bf16[272,1024]{1,0:T(8,128)(2,1)}, bf16[272,1024]{1,0:T(8,128)(2,1)}, u32[]{:S(2)}, u32[]{:S(2)}) collective-permute-start(bf16[272,1024]{1,0:T(8,128)(2,1)} %get-tuple-element.11.refs_1_), channel_id=1, source_target_pairs={{0,1},{1,0},{2,3},{3,2},{4,5},{5,4},{6,7},{7,6},{8,9},{9,8},{10,11... | collective-permute-start | bytes 1671176 | tf_op jit(solution)/shard_map/ppermute | solution.py:24
  10.9 40.9 %collective-permute-start.2 = (bf16[272,1024]{1,0:T(8,128)(2,1)}, bf16[272,1024]{1,0:T(8,128)(2,1)}, u32[]{:S(2)}, u32[]{:S(2)}) collective-permute-start(bf16[272,1024]{1,0:T(8,128)(2,1)} %get-tuple-element.12.refs_2_), channel_id=1, source_target_pairs={{0,1},{1,0},{2,3},{3,2},{4,5},{5,4},{6,7},{7,6},{8,9},{9,8},{10,11... | collective-permute-start | bytes 1671176 | tf_op jit(solution)/shard_map/ppermute | solution.py:24
  12.5 53.0 %collective-permute-start.3 = (bf16[272,1024]{1,0:T(8,128)(2,1)}, bf16[272,1024]{1,0:T(8,128)(2,1)}, u32[]{:S(2)}, u32[]{:S(2)}) collective-permute-start(bf16[272,1024]{1,0:T(8,128)(2,1)} %get-tuple-element.13.refs_3_), channel_id=1, source_target_pairs={{0,1},{1,0},{2,3},{3,2},{4,5},{5,4},{6,7},{7,6},{8,9},{9,8},{10,11... | collective-permute-start | bytes 1671176 | tf_op jit(solution)/shard_map/ppermute | solution.py:24
  13.7 1.1 %copy-start.4 = (bf16[128,4,1152]{2,1,0:T(4,128)(2,1)}, bf16[128,4,1152]{2,1,0:T(4,128)(2,1)S(1)}, u32[]{:S(2)}) copy-start(bf16[128,4,1152]{2,1,0:T(4,128)(2,1)S(1)} %place.1) | copy-start | bytes 3538948
  14.8 77.9 %all-to-all-start = ((bf16[128,4,1152]{2,1,0:T(4,128)(2,1)}), bf16[128,4,1152]{2,1,0:T(4,128)(2,1)S(1)}, u32[]{:S(2)}, u32[]{:S(2)}) async-start(bf16[128,4,1152]{2,1,0:T(4,128)(2,1)} %copy-done.4), calls=%async_computation | async-start | bytes 2359296 | tf_op jit(solution)/shard_map/all_to_all | solution.py:263
  25.6 1.6 %copy-start.10 = (bf16[1040,1024]{1,0:T(8,128)(2,1)S(1)}, bf16[1040,1024]{1,0:T(8,128)(2,1)}, u32[]{:S(2)}) copy-start(bf16[1040,1024]{1,0:T(8,128)(2,1)} %get-tuple-element.14.whole_ref.refs_8_) | copy-start | bytes 6389764
  29.5 58.5 %collective-permute-start.9 = (bf16[272,1024]{1,0:T(8,128)(2,1)}, bf16[272,1024]{1,0:T(8,128)(2,1)S(1)}, u32[]{:S(2)}, u32[]{:S(2)}) collective-permute-start(bf16[272,1024]{1,0:T(8,128)(2,1)} %collective-permute-done.refs_4_), channel_id=1, source_target_pairs={{1,31},{3,1},{5,3},{7,5},{9,7},{11,9},{13,11},{15,13},{17,15},{19,... | collective-permute-start | bytes 1671176 | tf_op jit(solution)/shard_map/ppermute | solution.py:24
  39.7 50.0 %collective-permute-start.8 = (bf16[272,1024]{1,0:T(8,128)(2,1)}, bf16[272,1024]{1,0:T(8,128)(2,1)S(1)}, u32[]{:S(2)}, u32[]{:S(2)}) collective-permute-start(bf16[272,1024]{1,0:T(8,128)(2,1)} %collective-permute-done.1.refs_5_), channel_id=1, source_target_pairs={{1,31},{3,1},{5,3},{7,5},{9,7},{11,9},{13,11},{15,13},{17,15},{19,... | collective-permute-start | bytes 1671176 | tf_op jit(solution)/shard_map/ppermute | solution.py:24
  51.8 39.5 %collective-permute-start.7 = (bf16[272,1024]{1,0:T(8,128)(2,1)}, bf16[272,1024]{1,0:T(8,128)(2,1)S(1)}, u32[]{:S(2)}, u32[]{:S(2)}) collective-permute-start(bf16[272,1024]{1,0:T(8,128)(2,1)} %collective-permute-done.2.refs_6_), channel_id=1, source_target_pairs={{1,31},{3,1},{5,3},{7,5},{9,7},{11,9},{13,11},{15,13},{17,15},{19,... | collective-permute-start | bytes 1671176 | tf_op jit(solution)/shard_map/ppermute | solution.py:24
  65.6 25.7 %collective-permute-start.6 = (bf16[272,1024]{1,0:T(8,128)(2,1)}, bf16[272,1024]{1,0:T(8,128)(2,1)S(1)}, u32[]{:S(2)}, u32[]{:S(2)}) collective-permute-start(bf16[272,1024]{1,0:T(8,128)(2,1)} %collective-permute-done.3.refs_7_), channel_id=1, source_target_pairs={{1,31},{3,1},{5,3},{7,5},{9,7},{11,9},{13,11},{15,13},{17,15},{19,... | collective-permute-start | bytes 1671176 | tf_op jit(solution)/shard_map/ppermute | solution.py:24
  68.6 1.3 %copy-start = (bf16[1040,1024]{1,0:T(8,128)(2,1)}, bf16[1040,1024]{1,0:T(8,128)(2,1)S(1)}, u32[]{:S(2)}) copy-start(bf16[1040,1024]{1,0:T(8,128)(2,1)S(1)} %collective-permute-done.4.refs_9_.refs_1_) | copy-start | bytes 6389764
  80.4 13.4 %collective-permute-start.5 = (f32[1,1024]{1,0:T(1,128)S(1)}, f32[1,1024]{1,0:T(1,128)S(1)}, u32[]{:S(2)}, u32[]{:S(2)}) collective-permute-start(f32[1,1024]{1,0:T(1,128)S(1)} %get-tuple-element.16), channel_id=1, source_target_pairs={{0,1},{1,0},{2,3},{3,2},{4,5},{5,4},{6,7},{7,6},{8,9},{9,8},{10,11... | collective-permute-start | bytes 12296 | tf_op jit(solution)/shard_map/ppermute | solution.py:24
  88.1 1.6 %copy-start.1 = (bf16[1040,1024]{1,0:T(8,128)(2,1)S(1)}, bf16[1040,1024]{1,0:T(8,128)(2,1)}, u32[]{:S(2)}) copy-start(bf16[1040,1024]{1,0:T(8,128)(2,1)} %copy-done) | copy-start | bytes 6389764
  89.7 1.6 %copy-start.2 = (bf16[1040,1024]{1,0:T(8,128)(2,1)S(1)}, bf16[1040,1024]{1,0:T(8,128)(2,1)}, u32[]{:S(2)}) copy-start(bf16[1040,1024]{1,0:T(8,128)(2,1)} %copy-done) | copy-start | bytes 6389764
  91.3 9.9 %collective-permute-start.10 = (f32[1,1024]{1,0:T(1,128)S(1)}, f32[1,1024]{1,0:T(1,128)S(1)}, u32[]{:S(2)}, u32[]{:S(2)}) collective-permute-start(f32[1,1024]{1,0:T(1,128)S(1)} %far_3.1), channel_id=1, source_target_pairs={{1,2},{3,4},{5,6},{7,8},{9,10},{11,12},{13,14},{15,16},{17,18},{19... | collective-permute-start | bytes 12296 | tf_op jit(solution)/shard_map/ppermute | solution.py:24

commit v3 on v2

v3 whole, which is shorter than its diff:
```python
import jax
import jax.numpy as jnp
from jax import lax
from jax.experimental import pallas as pl
from jax.experimental.pallas import tpu as pltpu
from jax.sharding import PartitionSpec as P

CAP = 4
LOWEST = -2.0
EXTRA = 16
BOTH = ("grp", "blk")
OWN, PARTNER, NEAR, NEAR_PARTNER, FAR_PARTNER = range(5)


def normalize(matrix):
    values = matrix.astype(jnp.float32)
    scale = lax.rsqrt(jnp.sum(values * values, axis=-1, keepdims=True) + 1e-06)
    return (values * scale).astype(jnp.bfloat16)


def send(value, to):
    groups, members = lax.axis_size("grp"), lax.axis_size("blk")
    pairs = []
    for group in range(groups):
        for block in range(members):
            core = group % 2
            target = to(core, (block + core) % 2 == 1, block)
            if target is not None:
                pairs.append((group * members + block, group * members + target % members))
    return lax.ppermute(value, BOTH, pairs)


def params():
    return pltpu.CompilerParams(vmem_limit_bytes=56 * 1024 * 1024)


def vmem(n):
    return [pl.BlockSpec(memory_space=pltpu.VMEM)] * n


def smem():
    return [pl.BlockSpec(memory_space=pltpu.SMEM)]


def down(row):
    return jnp.broadcast_to(row, (128, row.shape[1])).T


def halves(numbers):
    numbers = numbers.astype(jnp.int32)
    return (numbers >> 7).astype(jnp.float32), (numbers & 127).astype(jnp.float32)


def numbers_of(ref):
    size = ref.shape[0] - EXTRA
    tail = ref[size:, :size].astype(jnp.float32)
    return (tail[0:1, :] * 128.0 + tail[1:2, :]).astype(jnp.int32)


def best(rows, row_ids, cols, col_down):
    scores = lax.dot_general(cols, rows, (((1,), (1,)), ((), ())), preferred_element_type=jnp.float32)
    found = []
    for left in range(0, rows.shape[0], 128):
        keep = col_down < row_ids[:, left : left + 128]
        part = jnp.where(keep, scores[:, left : left + 128], jnp.float32(LOWEST))
        found.append(jnp.max(part, axis=0, keepdims=True))
    return jnp.concatenate(found, axis=1)


def update(acc_ref, at_row, rows, cols):
    for _, col_ref in cols:
        size = col_ref.shape[0] - EXTRA
        col_down = down(numbers_of(col_ref))
        for half, row_ref in rows:
            row_ids = numbers_of(row_ref)
            for top in range(0, size, 256):
                found = best(row_ref[top : top + 256, :], row_ids[:, top : top + 256], col_ref[:size, :], col_down)
                at = slice(half * size + top, half * size + top + 256)
                acc_ref[at_row : at_row + 1, at] = jnp.maximum(acc_ref[at_row : at_row + 1, at], found)


def compare(where_ref, heavy, acc_ref, pairs):
    for core in (0, 1):

        @pl.when((where_ref[0] == core) & (where_ref[1] == heavy))
        def _():
            for (first, first_refs), (second, second_refs) in pairs:
                if core == 0:
                    update(acc_ref, first, first_refs, second_refs)
                else:
                    update(acc_ref, second, second_refs, first_refs)


def norm_kernel(x_ref, ids_ref, out_ref):
    size, width = x_ref.shape
    out_ref[:size, :] = normalize(x_ref[...])
    ids = jnp.concatenate([ids_ref[...], jnp.zeros((1, width - size), jnp.int32)], axis=1)
    high, low = halves(ids)
    row = lax.broadcasted_iota(jnp.int32, (EXTRA, width), 0)
    out_ref[size:, :] = jnp.where(row == 0, high, jnp.where(row == 1, low, 0.0)).astype(jnp.bfloat16)


def norm_half(embeds, ids, half):
    rows, width = embeds.shape
    size = rows // 2
    return pl.pallas_call(
        norm_kernel,
        grid=(1,),
        in_specs=[
            pl.BlockSpec((size, width), lambda i: (half, 0)),
            pl.BlockSpec((1, size), lambda i: (0, half)),
        ],
        out_specs=pl.BlockSpec((size + EXTRA, width), lambda i: (0, 0)),
        out_shape=jax.ShapeDtypeStruct((size + EXTRA, width), jnp.bfloat16),
        compiler_params=params(),
        name=f"norm_{half}",
        cost_estimate=pl.CostEstimate(flops=4 * size * width, bytes_accessed=4 * size * width, transcendentals=size),
    )(embeds, ids)


def place_kernel(rows_ref, target_ref, ids_ref, out_ref):
    count, width = rows_ref.shape
    target = target_ref[...]
    across = jnp.broadcast_to(target, (count, count))
    earlier = lax.broadcasted_iota(jnp.int32, (count, count), 0) < lax.broadcasted_iota(
        jnp.int32, (count, count), 1
    )
    same = (across.T == across) & earlier
    position = jnp.sum(same.astype(jnp.float32), axis=0, keepdims=True).astype(jnp.int32)
    place = target * CAP + position
    devices = out_ref.shape[0]
    slots = devices * CAP
    pick = (lax.broadcasted_iota(jnp.int32, (slots, count), 0) == place).astype(jnp.float32).astype(jnp.bfloat16)
    placed = jnp.dot(pick, normalize(rows_ref[...]), preferred_element_type=jnp.float32)
    out_ref[:, :, :width] = placed.astype(jnp.bfloat16).reshape(devices, CAP, width)
    high, low = halves(down(ids_ref[...]))
    lane = lax.broadcasted_iota(jnp.int32, high.shape, 1)
    pair = jnp.where(lane < 64, high + 1.0, low).astype(jnp.bfloat16)
    tail = jnp.dot(pick, pair, preferred_element_type=jnp.float32)
    out_ref[:, :, width:] = tail.astype(jnp.bfloat16).reshape(devices, CAP, 128)


def placed_rows(owned, target, ids, devices):
    count, width = owned.shape
    return pl.pallas_call(
        place_kernel,
        in_specs=vmem(3),
        out_specs=pl.BlockSpec(memory_space=pltpu.VMEM),
        out_shape=jax.ShapeDtypeStruct((devices, CAP, width + 128), jnp.bfloat16),
        compiler_params=params(),
        name="place",
        cost_estimate=pl.CostEstimate(
            flops=2 * devices * CAP * count * width, bytes_accessed=2 * (count + devices * CAP) * width, transcendentals=count
        ),
    )(owned, target, ids)


def split_kernel(in_ref, rows_ref, ids_ref):
    slots, width = rows_ref.shape
    rows_ref[...] = in_ref[:, :, :width].reshape(slots, width)
    tail = in_ref[:, :, width:].reshape(slots, 128).astype(jnp.float32).T
    high, low = tail[0:1, :], tail[64:65, :]
    ids_ref[...] = jnp.where(high == 0.0, -1.0, (high - 1.0) * 128.0 + low).astype(jnp.int32)


def split_rows(arrived):
    devices, cap, wide = arrived.shape
    slots, width = devices * cap, wide - 128
    return pl.pallas_call(
        split_kernel,
        in_specs=vmem(1),
        out_specs=vmem(2),
        out_shape=[
            jax.ShapeDtypeStruct((slots, width), jnp.bfloat16),
            jax.ShapeDtypeStruct((1, slots), jnp.int32),
        ],
        compiler_params=params(),
        name="split",
        cost_estimate=pl.CostEstimate(flops=0, bytes_accessed=4 * slots * width, transcendentals=0),
    )(arrived)


def within_kernel(own0, own1, prior_ref, acc_ref):
    acc_ref[...] = jnp.full(acc_ref.shape, LOWEST, jnp.float32)
    acc_ref[OWN : OWN + 1, :] = prior_ref[...]
    own = [(0, own0), (1, own1)]
    update(acc_ref, OWN, own, own)


def near_kernel(own0, own1, partner0, partner1, near0, near1, where_ref, so_far_ref, acc_ref):
    acc_ref[...] = so_far_ref[...]
    own = (OWN, [(0, own0), (1, own1)])
    partner = (PARTNER, [(0, partner0), (1, partner1)])
    near = (NEAR, [(0, near0), (1, near1)])
    compare(where_ref, 1, acc_ref, [(own, partner), (own, near), (partner, near)])
    compare(where_ref, 0, acc_ref, [(own, (NEAR_PARTNER, [(1, near1)]))])


def middle_kernel(
    own0, own1, partner0, partner1, near0, near1, near_partner0, far0, where_ref, so_far_ref, acc_ref, partner_out
):
    acc_ref[...] = so_far_ref[...]
    own = (OWN, [(0, own0), (1, own1)])
    partner = (PARTNER, [(0, partner0), (1, partner1)])
    near = (NEAR, [(0, near0), (1, near1)])
    near_partner = (NEAR_PARTNER, [(0, near_partner0)])
    far = (FAR_PARTNER, [(0, far0)])
    compare(where_ref, 1, acc_ref, [(own, near_partner), (partner, near_partner), (far, near)])
    partner_out[...] = acc_ref[PARTNER : PARTNER + 1, :]


def last_kernel(
    own0, own1, near0, near1, near_partner1, far1, where_ref, so_far_ref, own_out, far_out, side_out, acc_ref
):
    acc_ref[...] = so_far_ref[...]
    own = (OWN, [(0, own0), (1, own1)])
    near = (NEAR, [(0, near0), (1, near1)])
    near_partner = (NEAR_PARTNER, [(1, near_partner1)])
    far = (FAR_PARTNER, [(1, far1)])
    compare(where_ref, 1, acc_ref, [(own, near_partner), (far, near)])
    own_out[...] = acc_ref[OWN : OWN + 1, :]
    near_partner_row = acc_ref[NEAR_PARTNER : NEAR_PARTNER + 1, :]
    far_out[...] = jnp.where(where_ref[0] == 0, acc_ref[FAR_PARTNER : FAR_PARTNER + 1, :], near_partner_row)
    side_out[...] = jnp.where(where_ref[1] == 1, acc_ref[NEAR : NEAR + 1, :], near_partner_row)


def body(embeds, doc_ids, prior_max, owned, owned_ids, owner_dest):
    devices = lax.axis_size("grp") * lax.axis_size("blk")
    raw = embeds[0]
    rows, width = raw.shape
    core = lax.axis_index("grp") & 1
    heavy = (lax.axis_index("blk") + core) & 1
    where = jnp.stack([core, heavy]).astype(jnp.int32)

    def step(core):
        return 2 - 4 * core

    def to_heavy(core, heavy, block):
        return None if heavy else block ^ 1

    def to_light(core, heavy, block):
        return block ^ 1 if heavy else None

    def ahead(core, heavy, block):
        return block + step(core)

    def heavy_ahead(core, heavy, block):
        return block + step(core) if heavy else None

    def heavy_back(core, heavy, block):
        return block - step(core) if heavy else None

    own = [norm_half(raw, doc_ids, half) for half in range(2)]
    partner = [send(own[half], to_heavy) for half in range(2)]
    near1 = send(own[1], ahead)
    near0 = send(own[0], heavy_ahead)
    far = [send(partner[half], heavy_back) for half in range(2)]
    near_partner0 = send(partner[0], heavy_ahead)
    near_partner1 = send(near1, to_heavy)

    outgoing = placed_rows(owned, owner_dest.reshape(1, -1), owned_ids.reshape(1, -1), devices)
    next_rows, next_ids = split_rows(lax.all_to_all(outgoing, BOTH, split_axis=0, concat_axis=0, tiled=True))

    line = jax.ShapeDtypeStruct((1, rows), jnp.float32)
    acc = jax.ShapeDtypeStruct((8, rows), jnp.float32)

    def cost(products, blocks):
        return pl.CostEstimate(
            flops=int(2 * products * rows * rows * width), bytes_accessed=2 * blocks * rows * width, transcendentals=0
        )

    found = pl.pallas_call(
        within_kernel,
        in_specs=vmem(3),
        out_specs=pl.BlockSpec(memory_space=pltpu.VMEM),
        out_shape=acc,
        compiler_params=params(),
        name="within",
        cost_estimate=cost(1, 1),
    )(*own, prior_max)
    found = pl.pallas_call(
        near_kernel,
        in_specs=vmem(6) + smem() + vmem(1),
        out_specs=pl.BlockSpec(memory_space=pltpu.VMEM),
        out_shape=acc,
        compiler_params=params(),
        name="near",
        cost_estimate=cost(3, 3),
    )(*own, *partner, near0, near1, where, found)
    found, for_partner = pl.pallas_call(
        middle_kernel,
        in_specs=vmem(8) + smem() + vmem(1),
        out_specs=vmem(2),
        out_shape=[acc, line],
        compiler_params=params(),
        name="cross_middle",
        cost_estimate=cost(1.5, 4),
    )(*own, *partner, near0, near1, near_partner0, far[0], where, found)
    from_partner = send(for_partner, to_light)
    mine, for_far, for_side = pl.pallas_call(
        last_kernel,
        in_specs=vmem(6) + smem() + vmem(1),
        out_specs=vmem(3),
        out_shape=[line] * 3,
        scratch_shapes=[pltpu.VMEM((8, rows), jnp.float32)],
        compiler_params=params(),
        name="cross_last",
        cost_estimate=cost(1, 3),
    )(*own, near0, near1, near_partner1, far[1], where, found)
    from_far = send(for_far, lambda core, heavy, block: block + 1 + 2 * core if heavy else None)
    from_side = send(for_side, lambda core, heavy, block: block + 2 if core else None)
    lowest = jnp.float32(LOWEST)
    running = jnp.maximum(mine, jnp.where(heavy == 0, jnp.maximum(from_partner, from_far), lowest))
    running = jnp.maximum(running, jnp.where(core == 1, from_side, lowest))
    return (running, next_rows, next_ids.reshape(-1))


def solution(mesh):
    return jax.shard_map(
        body,
        mesh=mesh,
        in_specs=(
            P("grp", "blk", None),
            P("grp", "blk"),
            P("grp", "blk"),
            P(("grp", "blk"), None),
            P(("grp", "blk")),
            P(("grp", "blk"), None),
        ),
        out_specs=(P("grp", "blk"), P(("grp", "blk"), None), P(("grp", "blk"))),
        check_vma=False,
    )
```

time: 102 us -> 89.6 us (0.88)
  the two profiles are of different devices: /device:TPU:0 before, /device:TPU:9 now
where the time goes in v3:
time: 89.6 us; the launch traced here: 89.1 us
  starting transfers between devices  42.9 us (48%)
  Pallas kernels  27.7 us (31%)
  waiting for transfers between devices  15.3 us (17%)
  other arithmetic  1.25 us (1%)
  local copies, waits for them, and re-layouts  1.05 us (1%)
    ppermute x11, starting transfers between devices, send(): return lax.ppermute(value, BOTH, pairs)  26.9 us
    all_to_all x1, starting transfers between devices, body(): lax.all_to_all(outgoing, BOTH, split_axis=0, concat_axis=0, tiled=True)  16 us
    ppermute x11, waiting for transfers between devices, send(): return lax.ppermute(value, BOTH, pairs)  15.3 us
    pallas_call x2, Pallas kernels, norm_half(): pl.pallas_call(norm_kernel, grid=(1,), in_specs=[pl.BlockSpec((size, widt...  5.08 us
    pallas_call x1, Pallas kernels, body(): pl.pallas_call(near_kernel, in_specs=vmem(6) + smem() + vmem(1), out_spec...  5.03 us
    pallas_call x1, Pallas kernels, body(): pl.pallas_call(within_kernel, in_specs=vmem(3), out_specs=pl.BlockSpec(me...  4.55 us
    pallas_call x1, Pallas kernels, body(): pl.pallas_call(middle_kernel, in_specs=vmem(8) + smem() + vmem(1), out_sp...  4.35 us
    pallas_call x1, Pallas kernels, body(): pl.pallas_call(last_kernel, in_specs=vmem(6) + smem() + vmem(1), out_spec...  3.5 us
  transfers between devices with their start and end apart: 12, of which 2 were waited for; matrix products, arithmetic and copies ran while one was open for 1% of the time, Pallas kernels for 28%

profile of v3, /device:TPU:9, one launch (start us, length us, event | category | flops | bytes accessed | tf_op | source)
XLA Modules:
  0.0 89.1 jit_solution(1798376012919797898)
XLA Ops:
  0.6 2.5 %norm_0.1.own0 = bf16[528,1024]{1,0:T(8,128)(2,1)} custom-call(bf16[1024,1024]{1,0:T(8,128)(2,1)} %bitcast.6, s32[1,1024]{1,0:T(1,128)} %ids_ref.3), custom_call_target="tpu_custom_call" | custom-call | flops 2097152 | bytes 2097152 | tf_op jit(solution)/shard_map/norm_0/pallas_call | solution.py:106
  3.2 0.0 copy-start.1
  3.2 2.4 %collective-permute-start.5 = (bf16[528,1024]{1,0:T(8,128)(2,1)}, bf16[528,1024]{1,0:T(8,128)(2,1)}, u32[]{:S(2)}, u32[]{:S(2)}) collective-permute-start(bf16[528,1024]{1,0:T(8,128)(2,1)} %norm_0.1.own0), channel_id=1, source_target_pairs={{0,1},{2,3},{4,5},{6,7},{8,9},{10,11},{12,13},{14,15},{16,17},{18,... | collective-permute-start | bytes 3244040 | tf_op jit(solution)/shard_map/ppermute | solution.py:30
  5.6 2.6 %norm_1.1.own1 = bf16[528,1024]{1,0:T(8,128)(2,1)} custom-call(bf16[1024,1024]{1,0:T(8,128)(2,1)} %bitcast.7, s32[1,1024]{1,0:T(1,128)} %ids_ref.3), custom_call_target="tpu_custom_call" | custom-call | flops 2097152 | bytes 2097152 | tf_op jit(solution)/shard_map/norm_1/pallas_call | solution.py:106
  8.1 6.7 %collective-permute-start.1 = (bf16[528,1024]{1,0:T(8,128)(2,1)}, bf16[528,1024]{1,0:T(8,128)(2,1)S(1)}, u32[]{:S(2)}, u32[]{:S(2)}) collective-permute-start(bf16[528,1024]{1,0:T(8,128)(2,1)} %norm_1.1.own1), channel_id=1, source_target_pairs={{0,2},{1,3},{2,4},{3,5},{4,6},{5,7},{6,8},{7,9},{8,10},{9,11},{10,... | collective-permute-start | bytes 3244040 | tf_op jit(solution)/shard_map/ppermute | solution.py:30
  14.9 2.4 %collective-permute-start.3 = (bf16[528,1024]{1,0:T(8,128)(2,1)}, bf16[528,1024]{1,0:T(8,128)(2,1)}, u32[]{:S(2)}, u32[]{:S(2)}) collective-permute-start(bf16[528,1024]{1,0:T(8,128)(2,1)} %norm_1.1.own1), channel_id=1, source_target_pairs={{0,1},{2,3},{4,5},{6,7},{8,9},{10,11},{12,13},{14,15},{16,17},{18,... | collective-permute-start | bytes 3244040 | tf_op jit(solution)/shard_map/ppermute | solution.py:30
  17.3 0.0 copy-done.1
  17.3 1.6 %collective-permute-start = (bf16[528,1024]{1,0:T(8,128)(2,1)S(1)}, bf16[528,1024]{1,0:T(8,128)(2,1)}, u32[]{:S(2)}, u32[]{:S(2)}) collective-permute-start(bf16[528,1024]{1,0:T(8,128)(2,1)S(1)} %copy-done.1), channel_id=1, source_target_pairs={{1,3},{3,5},{5,7},{7,9},{9,11},{11,13},{13,15},{15,17},{17,19},{19... | collective-permute-start | bytes 3244040 | tf_op jit(solution)/shard_map/ppermute | solution.py:30
  18.9 0.0 collective-permute-done.5.partner0
  18.9 1.6 %collective-permute-start.6 = (bf16[528,1024]{1,0:T(8,128)(2,1)}, bf16[528,1024]{1,0:T(8,128)(2,1)}, u32[]{:S(2)}, u32[]{:S(2)}) collective-permute-start(bf16[528,1024]{1,0:T(8,128)(2,1)} %collective-permute-done.5.partner0), channel_id=1, source_target_pairs={{1,3},{3,5},{5,7},{7,9},{9,11},{11,13},{13,15},{15,17},{17,19},{19... | collective-permute-start | bytes 3244040 | tf_op jit(solution)/shard_map/ppermute | solution.py:30
  20.5 1.6 %collective-permute-start.7 = (bf16[528,1024]{1,0:T(8,128)(2,1)}, bf16[528,1024]{1,0:T(8,128)(2,1)}, u32[]{:S(2)}, u32[]{:S(2)}) collective-permute-start(bf16[528,1024]{1,0:T(8,128)(2,1)} %collective-permute-done.5.partner0), channel_id=1, source_target_pairs={{1,31},{3,1},{5,3},{7,5},{9,7},{11,9},{13,11},{15,13},{17,15},{19,... | collective-permute-start | bytes 3244040 | tf_op jit(solution)/shard_map/ppermute | solution.py:30
  22.2 2.8 %place.1 = bf16[128,4,1152]{2,1,0:T(4,128)(2,1)} custom-call(bf16[256,1024]{1,0:T(8,128)(2,1)} %rows_ref.1, s32[1,256]{1,0:T(1,128)} %bitcast.8, s32[1,256]{1,0:T(1,128)} %bitcast.9), custom_call_target="tpu_custom_call" | custom-call | flops 268435456 | bytes 1572864 | tf_op jit(solution)/shard_map/place/pallas_call | solution.py:145
  25.0 16.0 %all-to-all-start = ((bf16[128,4,1152]{2,1,0:T(4,128)(2,1)}), bf16[128,4,1152]{2,1,0:T(4,128)(2,1)S(1)}, u32[]{:S(2)}, u32[]{:S(2)}) async-start(bf16[128,4,1152]{2,1,0:T(4,128)(2,1)} %place.1), calls=%async_computation | async-start | bytes 2359296 | tf_op jit(solution)/shard_map/all_to_all | solution.py:262
  41.1 0.0 collective-permute-done.1.near1
  41.1 0.0 copy-start.3
  41.1 3.0 %collective-permute-start.2 = (bf16[528,1024]{1,0:T(8,128)(2,1)S(1)}, bf16[528,1024]{1,0:T(8,128)(2,1)}, u32[]{:S(2)}, u32[]{:S(2)}) collective-permute-start(bf16[528,1024]{1,0:T(8,128)(2,1)S(1)} %collective-permute-done.1.near1), channel_id=1, source_target_pairs={{0,1},{2,3},{4,5},{6,7},{8,9},{10,11},{12,13},{14,15},{16,17},{18,... | collective-permute-start | bytes 3244040 | tf_op jit(solution)/shard_map/ppermute | solution.py:30
  44.1 0.0 collective-permute-done.3.partner1
  44.1 1.6 %collective-permute-start.4 = (bf16[528,1024]{1,0:T(8,128)(2,1)}, bf16[528,1024]{1,0:T(8,128)(2,1)}, u32[]{:S(2)}, u32[]{:S(2)}) collective-permute-start(bf16[528,1024]{1,0:T(8,128)(2,1)} %collective-permute-done.3.partner1), channel_id=1, source_target_pairs={{1,31},{3,1},{5,3},{7,5},{9,7},{11,9},{13,11},{15,13},{17,15},{19,... | collective-permute-start | bytes 3244040 | tf_op jit(solution)/shard_map/ppermute | solution.py:30
  45.7 4.6 %within.1.so_far_ref = f32[8,1024]{1,0:T(8,128)} custom-call(bf16[528,1024]{1,0:T(8,128)(2,1)} %norm_0.1.own0, bf16[528,1024]{1,0:T(8,128)(2,1)} %norm_1.1.own1, f32[1,1024]{1,0:T(1,128)} %prior_ref.1), custom_call_target="tpu_custom_call" | custom-call | flops 2147483648 | bytes 2097152 | tf_op jit(solution)/shard_map/within/pallas_call | solution.py:272
  50.3 0.0 copy-done.3
  50.3 0.6 pad_add_fusion.where_ref
  50.9 0.0 collective-permute-done.near0
  50.9 5.0 %near.1.so_far_ref = f32[8,1024]{1,0:T(8,128)} custom-call(bf16[528,1024]{1,0:T(8,128)(2,1)} %norm_0.1.own0, bf16[528,1024]{1,0:T(8,128)(2,1)} %norm_1.1.own1, bf16[528,1024]{1,0:T(8,128)(2,1)} %collective-permute-done.5.partner0, bf16[528,1024]{1,0:T(8,128)(2,1)} %collective-permute-done.3.partner1, bf16[528,1024]{1,0:T(8,128)(2,1)} %collective-permute-done.near0, ...), custom_call_target="tpu_custom_call" | custom-call | flops 6442450944 | bytes 6291456 | tf_op jit(solution)/shard_map/near/pallas_call | solution.py:281
  56.0 0.0 collective-permute-done.6.near_partner0
  56.0 0.0 collective-permute-done.7.far0
  56.0 4.4 %cross_middle.1 = (f32[8,1024]{1,0:T(8,128)}, f32[1,1024]{1,0:T(1,128)}) custom-call(bf16[528,1024]{1,0:T(8,128)(2,1)} %norm_0.1.own0, bf16[528,1024]{1,0:T(8,128)(2,1)} %norm_1.1.own1, bf16[528,1024]{1,0:T(8,128)(2,1)} %collective-permute-done.5.partner0, bf16[528,1024]{1,0:T(8,128)(2,1)} %collective-permute-done.3.partner1, ...), custom_call_target="tpu_custom_call" | custom-call | flops 3221225472 | bytes 8388608 | tf_op jit(solution)/shard_map/cross_middle/pallas_call | solution.py:290
  60.3 4.8 %collective-permute-done.2.near_partner1 = bf16[528,1024]{1,0:T(8,128)(2,1)} collective-permute-done((bf16[528,1024]{1,0:T(8,128)(2,1)S(1)}, bf16[528,1024]{1,0:T(8,128)(2,1)}, u32[]{:S(2)}, u32[]{:S(2)}) %collective-permute-start.2) | collective-permute-done | bytes 1081376 | tf_op jit(solution)/shard_map/ppermute | solution.py:30
  65.1 0.0 collective-permute-done.4.far1
  65.1 0.0 copy-start.4
  65.1 3.5 %cross_last.1 = (f32[1,1024]{1,0:T(1,128)}, f32[1,1024]{1,0:T(1,128)}, f32[1,1024]{1,0:T(1,128)}) custom-call(bf16[528,1024]{1,0:T(8,128)(2,1)} %norm_0.1.own0, bf16[528,1024]{1,0:T(8,128)(2,1)} %norm_1.1.own1, bf16[528,1024]{1,0:T(8,128)(2,1)} %collective-permute-done.near0, bf16[528,1024]{1,0:T(8,128)(2,1)} %copy-done.3, ...), custom_call_target="tpu_custom_call" | custom-call | flops 2147483648 | bytes 6291456 | tf_op jit(solution)/shard_map/cross_last/pallas_call | solution.py:300
  68.6 0.0 copy-start.2
  68.6 3.2 %collective-permute-start.10 = (f32[1,1024]{1,0:T(1,128)}, f32[1,1024]{1,0:T(1,128)S(1)}, u32[]{:S(2)}, u32[]{:S(2)}) collective-permute-start(f32[1,1024]{1,0:T(1,128)} %get-tuple-element.14), channel_id=1, source_target_pairs={{32,34},{33,35},{34,36},{35,37},{36,38},{37,39},{38,40},{39,41},{4... | collective-permute-start | bytes 12296 | tf_op jit(solution)/shard_map/ppermute | solution.py:30
  71.9 1.3 %collective-permute-start.9 = (f32[1,1024]{1,0:T(1,128)}, f32[1,1024]{1,0:T(1,128)S(1)}, u32[]{:S(2)}, u32[]{:S(2)}) collective-permute-start(f32[1,1024]{1,0:T(1,128)} %get-tuple-element.13), channel_id=1, source_target_pairs={{1,2},{3,4},{5,6},{7,8},{9,10},{11,12},{13,14},{15,16},{17,18},{19... | collective-permute-start | bytes 12296 | tf_op jit(solution)/shard_map/ppermute | solution.py:30
  73.2 0.0 copy-done.4
  73.2 1.3 %collective-permute-start.8 = (f32[1,1024]{1,0:T(1,128)S(1)}, f32[1,1024]{1,0:T(1,128)S(1)}, u32[]{:S(2)}, u32[]{:S(2)}) collective-permute-start(f32[1,1024]{1,0:T(1,128)S(1)} %copy-done.4), channel_id=1, source_target_pairs={{1,0},{3,2},{5,4},{7,6},{9,8},{11,10},{13,12},{15,14},{17,16},{19,... | collective-permute-start | bytes 12296 | tf_op jit(solution)/shard_map/ppermute | solution.py:30
  74.5 0.0 all-to-all-done.in_ref
  74.5 0.0 copy-start
  74.5 1.0 %copy-done = bf16[128,4,1152]{2,1,0:T(4,128)(2,1)} copy-done((bf16[128,4,1152]{2,1,0:T(4,128)(2,1)}, bf16[128,4,1152]{2,1,0:T(4,128)(2,1)S(1)}, u32[]{:S(2)}) %copy-start) | copy-done | bytes 1179672
  75.5 2.4 %split.1 = (bf16[512,1024]{1,0:T(8,128)(2,1)}, s32[1,512]{1,0:T(1,128)}) custom-call(bf16[128,4,1152]{2,1,0:T(4,128)(2,1)} %copy-done), custom_call_target="tpu_custom_call" | custom-call | bytes 2097152 | tf_op jit(solution)/shard_map/split/pallas_call | solution.py:169
  77.9 0.0 collective-permute-done.10
  77.9 10.5 %collective-permute-done.9 = f32[1,1024]{1,0:T(1,128)S(1)} collective-permute-done((f32[1,1024]{1,0:T(1,128)}, f32[1,1024]{1,0:T(1,128)S(1)}, u32[]{:S(2)}, u32[]{:S(2)}) %collective-permute-start.9) | collective-permute-done | bytes 4128 | tf_op jit(solution)/shard_map/ppermute | solution.py:30
  88.5 0.0 collective-permute-done.8
  88.5 0.0 copy-done.2
  88.5 0.6 fusion.1
Async XLA Ops:
  3.2 14.1 %copy-start.1 = (bf16[528,1024]{1,0:T(8,128)(2,1)S(1)}, bf16[528,1024]{1,0:T(8,128)(2,1)}, u32[]{:S(2)}) copy-start(bf16[528,1024]{1,0:T(8,128)(2,1)} %norm_0.1.own0) | copy-start | bytes 3244036
  3.2 15.7 %collective-permute-start.5 = (bf16[528,1024]{1,0:T(8,128)(2,1)}, bf16[528,1024]{1,0:T(8,128)(2,1)}, u32[]{:S(2)}, u32[]{:S(2)}) collective-permute-start(bf16[528,1024]{1,0:T(8,128)(2,1)} %norm_0.1.own0), channel_id=1, source_target_pairs={{0,1},{2,3},{4,5},{6,7},{8,9},{10,11},{12,13},{14,15},{16,17},{18,... | collective-permute-start | bytes 3244040 | tf_op jit(solution)/shard_map/ppermute | solution.py:30
  8.1 32.9 %collective-permute-start.1 = (bf16[528,1024]{1,0:T(8,128)(2,1)}, bf16[528,1024]{1,0:T(8,128)(2,1)S(1)}, u32[]{:S(2)}, u32[]{:S(2)}) collective-permute-start(bf16[528,1024]{1,0:T(8,128)(2,1)} %norm_1.1.own1), channel_id=1, source_target_pairs={{0,2},{1,3},{2,4},{3,5},{4,6},{5,7},{6,8},{7,9},{8,10},{9,11},{10,... | collective-permute-start | bytes 3244040 | tf_op jit(solution)/shard_map/ppermute | solution.py:30
  14.9 29.2 %collective-permute-start.3 = (bf16[528,1024]{1,0:T(8,128)(2,1)}, bf16[528,1024]{1,0:T(8,128)(2,1)}, u32[]{:S(2)}, u32[]{:S(2)}) collective-permute-start(bf16[528,1024]{1,0:T(8,128)(2,1)} %norm_1.1.own1), channel_id=1, source_target_pairs={{0,1},{2,3},{4,5},{6,7},{8,9},{10,11},{12,13},{14,15},{16,17},{18,... | collective-permute-start | bytes 3244040 | tf_op jit(solution)/shard_map/ppermute | solution.py:30
  17.3 33.7 %collective-permute-start = (bf16[528,1024]{1,0:T(8,128)(2,1)S(1)}, bf16[528,1024]{1,0:T(8,128)(2,1)}, u32[]{:S(2)}, u32[]{:S(2)}) collective-permute-start(bf16[528,1024]{1,0:T(8,128)(2,1)S(1)} %copy-done.1), channel_id=1, source_target_pairs={{1,3},{3,5},{5,7},{7,9},{9,11},{11,13},{13,15},{15,17},{17,19},{19... | collective-permute-start | bytes 3244040 | tf_op jit(solution)/shard_map/ppermute | solution.py:30
  18.9 37.1 %collective-permute-start.6 = (bf16[528,1024]{1,0:T(8,128)(2,1)}, bf16[528,1024]{1,0:T(8,128)(2,1)}, u32[]{:S(2)}, u32[]{:S(2)}) collective-permute-start(bf16[528,1024]{1,0:T(8,128)(2,1)} %collective-permute-done.5.partner0), channel_id=1, source_target_pairs={{1,3},{3,5},{5,7},{7,9},{9,11},{11,13},{13,15},{15,17},{17,19},{19... | collective-permute-start | bytes 3244040 | tf_op jit(solution)/shard_map/ppermute | solution.py:30
  20.5 35.4 %collective-permute-start.7 = (bf16[528,1024]{1,0:T(8,128)(2,1)}, bf16[528,1024]{1,0:T(8,128)(2,1)}, u32[]{:S(2)}, u32[]{:S(2)}) collective-permute-start(bf16[528,1024]{1,0:T(8,128)(2,1)} %collective-permute-done.5.partner0), channel_id=1, source_target_pairs={{1,31},{3,1},{5,3},{7,5},{9,7},{11,9},{13,11},{15,13},{17,15},{19,... | collective-permute-start | bytes 3244040 | tf_op jit(solution)/shard_map/ppermute | solution.py:30
  25.0 49.5 %all-to-all-start = ((bf16[128,4,1152]{2,1,0:T(4,128)(2,1)}), bf16[128,4,1152]{2,1,0:T(4,128)(2,1)S(1)}, u32[]{:S(2)}, u32[]{:S(2)}) async-start(bf16[128,4,1152]{2,1,0:T(4,128)(2,1)} %place.1), calls=%async_computation | async-start | bytes 2359296 | tf_op jit(solution)/shard_map/all_to_all | solution.py:262
  41.1 9.2 %copy-start.3 = (bf16[528,1024]{1,0:T(8,128)(2,1)}, bf16[528,1024]{1,0:T(8,128)(2,1)S(1)}, u32[]{:S(2)}) copy-start(bf16[528,1024]{1,0:T(8,128)(2,1)S(1)} %collective-permute-done.1.near1) | copy-start | bytes 3244036
  41.1 24.1 %collective-permute-start.2 = (bf16[528,1024]{1,0:T(8,128)(2,1)S(1)}, bf16[528,1024]{1,0:T(8,128)(2,1)}, u32[]{:S(2)}, u32[]{:S(2)}) collective-permute-start(bf16[528,1024]{1,0:T(8,128)(2,1)S(1)} %collective-permute-done.1.near1), channel_id=1, source_target_pairs={{0,1},{2,3},{4,5},{6,7},{8,9},{10,11},{12,13},{14,15},{16,17},{18,... | collective-permute-start | bytes 3244040 | tf_op jit(solution)/shard_map/ppermute | solution.py:30
  44.1 21.1 %collective-permute-start.4 = (bf16[528,1024]{1,0:T(8,128)(2,1)}, bf16[528,1024]{1,0:T(8,128)(2,1)}, u32[]{:S(2)}, u32[]{:S(2)}) collective-permute-start(bf16[528,1024]{1,0:T(8,128)(2,1)} %collective-permute-done.3.partner1), channel_id=1, source_target_pairs={{1,31},{3,1},{5,3},{7,5},{9,7},{11,9},{13,11},{15,13},{17,15},{19,... | collective-permute-start | bytes 3244040 | tf_op jit(solution)/shard_map/ppermute | solution.py:30
  65.1 8.0 %copy-start.4 = (f32[1,1024]{1,0:T(1,128)S(1)}, f32[1,1024]{1,0:T(1,128)}, u32[]{:S(2)}) copy-start(f32[1,1024]{1,0:T(1,128)} %get-tuple-element.12) | copy-start | bytes 12292
  68.6 19.8 %copy-start.2 = (f32[1,1024]{1,0:T(1,128)S(1)}, f32[1,1024]{1,0:T(1,128)}, u32[]{:S(2)}) copy-start(f32[1,1024]{1,0:T(1,128)} %get-tuple-element.11) | copy-start | bytes 12292
  68.6 9.3 %collective-permute-start.10 = (f32[1,1024]{1,0:T(1,128)}, f32[1,1024]{1,0:T(1,128)S(1)}, u32[]{:S(2)}, u32[]{:S(2)}) collective-permute-start(f32[1,1024]{1,0:T(1,128)} %get-tuple-element.14), channel_id=1, source_target_pairs={{32,34},{33,35},{34,36},{35,37},{36,38},{37,39},{38,40},{39,41},{4... | collective-permute-start | bytes 12296 | tf_op jit(solution)/shard_map/ppermute | solution.py:30
  71.9 16.6 %collective-permute-start.9 = (f32[1,1024]{1,0:T(1,128)}, f32[1,1024]{1,0:T(1,128)S(1)}, u32[]{:S(2)}, u32[]{:S(2)}) collective-permute-start(f32[1,1024]{1,0:T(1,128)} %get-tuple-element.13), channel_id=1, source_target_pairs={{1,2},{3,4},{5,6},{7,8},{9,10},{11,12},{13,14},{15,16},{17,18},{19... | collective-permute-start | bytes 12296 | tf_op jit(solution)/shard_map/ppermute | solution.py:30
  73.2 15.3 %collective-permute-start.8 = (f32[1,1024]{1,0:T(1,128)S(1)}, f32[1,1024]{1,0:T(1,128)S(1)}, u32[]{:S(2)}, u32[]{:S(2)}) collective-permute-start(f32[1,1024]{1,0:T(1,128)S(1)} %copy-done.4), channel_id=1, source_target_pairs={{1,0},{3,2},{5,4},{7,6},{9,8},{11,10},{13,12},{15,14},{17,16},{19,... | collective-permute-start | bytes 12296 | tf_op jit(solution)/shard_map/ppermute | solution.py:30
  74.5 1.0 %copy-start = (bf16[128,4,1152]{2,1,0:T(4,128)(2,1)}, bf16[128,4,1152]{2,1,0:T(4,128)(2,1)S(1)}, u32[]{:S(2)}) copy-start(bf16[128,4,1152]{2,1,0:T(4,128)(2,1)S(1)} %all-to-all-done.in_ref) | copy-start | bytes 3538948

commit v4 on v3

--- a/solution.py
+++ b/solution.py
@@ -31,7 +31,7 @@
 
 
 def params():
-    return pltpu.CompilerParams(vmem_limit_bytes=56 * 1024 * 1024)
+    return pltpu.CompilerParams(vmem_limit_bytes=24 * 1024 * 1024)
 
 
 def vmem(n):
@@ -187,7 +187,8 @@
     update(acc_ref, OWN, own, own)
 
 
-def near_kernel(own0, own1, partner0, partner1, near0, near1, where_ref, so_far_ref, acc_ref):
+def near_kernel(own0, own1, partner0, partner1, near0, near1, where_ref, so_far_ref, after_ref, acc_ref):
+    del after_ref
     acc_ref[...] = so_far_ref[...]
     own = (OWN, [(0, own0), (1, own1)])
     partner = (PARTNER, [(0, partner0), (1, partner1)])
@@ -210,7 +211,7 @@
 
 
 def last_kernel(
-    own0, own1, near0, near1, near_partner1, far1, where_ref, so_far_ref, own_out, far_out, side_out, acc_ref
+    own0, own1, near0, near1, near_partner1, far1, where_ref, so_far_ref, from_partner_ref, own_out, far_out, side_out, acc_ref
 ):
     acc_ref[...] = so_far_ref[...]
     own = (OWN, [(0, own0), (1, own1)])
@@ -218,7 +219,8 @@
     near_partner = (NEAR_PARTNER, [(1, near_partner1)])
     far = (FAR_PARTNER, [(1, far1)])
     compare(where_ref, 1, acc_ref, [(own, near_partner), (far, near)])
-    own_out[...] = acc_ref[OWN : OWN + 1, :]
+    own_row = acc_ref[OWN : OWN + 1, :]
+    own_out[...] = jnp.where(where_ref[1] == 0, jnp.maximum(own_row, from_partner_ref[...]), own_row)
     near_partner_row = acc_ref[NEAR_PARTNER : NEAR_PARTNER + 1, :]
     far_out[...] = jnp.where(where_ref[0] == 0, acc_ref[FAR_PARTNER : FAR_PARTNER + 1, :], near_partner_row)
     side_out[...] = jnp.where(where_ref[1] == 1, acc_ref[NEAR : NEAR + 1, :], near_partner_row)
@@ -280,13 +282,13 @@
     )(*own, prior_max)
     found = pl.pallas_call(
         near_kernel,
-        in_specs=vmem(6) + smem() + vmem(1),
+        in_specs=vmem(6) + smem() + vmem(1) + [pl.BlockSpec(memory_space=pl.ANY)],
         out_specs=pl.BlockSpec(memory_space=pltpu.VMEM),
         out_shape=acc,
         compiler_params=params(),
         name="near",
         cost_estimate=cost(3, 3),
-    )(*own, *partner, near0, near1, where, found)
+    )(*own, *partner, near0, near1, where, found, next_ids)
     found, for_partner = pl.pallas_call(
         middle_kernel,
         in_specs=vmem(8) + smem() + vmem(1),
@@ -299,18 +301,18 @@
     from_partner = send(for_partner, to_light)
     mine, for_far, for_side = pl.pallas_call(
         last_kernel,
-        in_specs=vmem(6) + smem() + vmem(1),
+        in_specs=vmem(6) + smem() + vmem(2),
         out_specs=vmem(3),
         out_shape=[line] * 3,
         scratch_shapes=[pltpu.VMEM((8, rows), jnp.float32)],
         compiler_params=params(),
         name="cross_last",
         cost_estimate=cost(1, 3),
-    )(*own, near0, near1, near_partner1, far[1], where, found)
+    )(*own, near0, near1, near_partner1, far[1], where, found, from_partner)
     from_far = send(for_far, lambda core, heavy, block: block + 1 + 2 * core if heavy else None)
     from_side = send(for_side, lambda core, heavy, block: block + 2 if core else None)
     lowest = jnp.float32(LOWEST)
-    running = jnp.maximum(mine, jnp.where(heavy == 0, jnp.maximum(from_partner, from_far), lowest))
+    running = jnp.maximum(mine, jnp.where(heavy == 0, from_far, lowest))
     running = jnp.maximum(running, jnp.where(core == 1, from_side, lowest))
     return (running, next_rows, next_ids.reshape(-1))
 

time: 89.6 us -> 91.6 us (1.022)
  the two profiles are of different devices: /device:TPU:9 before, /device:TPU:0 now
where the time goes in v4:
time: 91.6 us; the launch traced here: 91.1 us
  starting transfers between devices  40.4 us (44%)
  waiting for transfers between devices  31.3 us (34%)
  Pallas kernels  15 us (16%)
  local copies, waits for them, and re-layouts  2.98 us (3%)
    ppermute x11, starting transfers between devices, send(): return lax.ppermute(value, BOTH, pairs)  29.9 us
    ppermute x11, waiting for transfers between devices, send(): return lax.ppermute(value, BOTH, pairs)  26.7 us
    all_to_all x1, starting transfers between devices, body(): lax.all_to_all(outgoing, BOTH, split_axis=0, concat_axis=0, tiled=True)  10.5 us
    all_to_all x1, waiting for transfers between devices, body(): lax.all_to_all(outgoing, BOTH, split_axis=0, concat_axis=0, tiled=True)  4.52 us
    pallas_call x1, Pallas kernels, body(): pl.pallas_call(near_kernel, in_specs=vmem(6) + smem() + vmem(1) + [pl.Blo...  3.72 us
    pallas_call x1, Pallas kernels, body(): pl.pallas_call(middle_kernel, in_specs=vmem(8) + smem() + vmem(1), out_sp...  3.16 us
    unnamed x14, local copies, waits for them, and re-layouts  2.98 us
    pallas_call x1, Pallas kernels, body(): pl.pallas_call(within_kernel, in_specs=vmem(3), out_specs=pl.BlockSpec(me...  2.38 us
  transfers between devices with their start and end apart: 12, of which 4 were waited for; matrix products, arithmetic and copies ran while one was open for 0% of the time, Pallas kernels for 14%

profile of v4, /device:TPU:0, one launch (start us, length us, event | category | flops | bytes accessed | tf_op | source)
XLA Modules:
  0.0 91.1 jit_solution(17763870675214335741)
XLA Ops:
  0.6 0.0 copy-start
  0.6 1.6 %copy-done = bf16[1,1024,1024]{2,1,0:T(8,128)(2,1)S(1)} copy-done((bf16[1,1024,1024]{2,1,0:T(8,128)(2,1)S(1)}, bf16[1,1024,1024]{2,1,0:T(8,128)(2,1)}, u32[]{:S(2)}) %copy-start) | copy-done | bytes 2097176
  2.2 0.0 copy-start.2
  2.2 0.7 copy-done.2
  2.9 0.3 norm_0.1.own0
  3.2 0.0 copy-start.1
  3.3 0.0 copy-start.3
  3.3 0.0 copy-start.4
  3.3 4.7 %collective-permute-start.5 = (bf16[528,1024]{1,0:T(8,128)(2,1)S(1)}, bf16[528,1024]{1,0:T(8,128)(2,1)}, u32[]{:S(2)}, u32[]{:S(2)}) collective-permute-start(bf16[528,1024]{1,0:T(8,128)(2,1)S(1)} %norm_0.1.own0), channel_id=1, source_target_pairs={{0,1},{2,3},{4,5},{6,7},{8,9},{10,11},{12,13},{14,15},{16,17},{18,... | collective-permute-start | bytes 3244040 | tf_op jit(solution)/shard_map/ppermute | solution.py:30
  8.0 0.3 norm_1.1.own1
  8.3 1.6 %collective-permute-start.1 = (bf16[528,1024]{1,0:T(8,128)(2,1)S(1)}, bf16[528,1024]{1,0:T(8,128)(2,1)}, u32[]{:S(2)}, u32[]{:S(2)}) collective-permute-start(bf16[528,1024]{1,0:T(8,128)(2,1)S(1)} %norm_1.1.own1), channel_id=1, source_target_pairs={{0,2},{1,3},{2,4},{3,5},{4,6},{5,7},{6,8},{7,9},{8,10},{9,11},{10,... | collective-permute-start | bytes 3244040 | tf_op jit(solution)/shard_map/ppermute | solution.py:30
  9.9 2.3 %collective-permute-start.3 = (bf16[528,1024]{1,0:T(8,128)(2,1)S(1)}, bf16[528,1024]{1,0:T(8,128)(2,1)}, u32[]{:S(2)}, u32[]{:S(2)}) collective-permute-start(bf16[528,1024]{1,0:T(8,128)(2,1)S(1)} %norm_1.1.own1), channel_id=1, source_target_pairs={{0,1},{2,3},{4,5},{6,7},{8,9},{10,11},{12,13},{14,15},{16,17},{18,... | collective-permute-start | bytes 3244040 | tf_op jit(solution)/shard_map/ppermute | solution.py:30
  12.2 0.0 copy-done.1
  12.2 0.0 copy-done.3
  12.2 0.0 copy-done.4
  12.2 1.8 %place.1 = bf16[128,4,1152]{2,1,0:T(4,128)(2,1)} custom-call(bf16[256,1024]{1,0:T(8,128)(2,1)S(1)} %copy-done.1, s32[1,256]{1,0:T(1,128)S(1)} %bitcast.8, s32[1,256]{1,0:T(1,128)S(1)} %bitcast.9), custom_call_target="tpu_custom_call" | custom-call | flops 268435456 | bytes 1572864 | tf_op jit(solution)/shard_map/place/pallas_call | solution.py:145
  13.9 0.0 copy-start.5
  13.9 10.5 %all-to-all-start = ((bf16[128,4,1152]{2,1,0:T(4,128)(2,1)}), bf16[128,4,1152]{2,1,0:T(4,128)(2,1)S(1)}, u32[]{:S(2)}, u32[]{:S(2)}) async-start(bf16[128,4,1152]{2,1,0:T(4,128)(2,1)} %place.1), calls=%async_computation | async-start | bytes 2359296 | tf_op jit(solution)/shard_map/all_to_all | solution.py:264
  24.4 1.7 %collective-permute-start = (bf16[528,1024]{1,0:T(8,128)(2,1)S(1)}, bf16[528,1024]{1,0:T(8,128)(2,1)}, u32[]{:S(2)}, u32[]{:S(2)}) collective-permute-start(bf16[528,1024]{1,0:T(8,128)(2,1)S(1)} %norm_0.1.own0), channel_id=1, source_target_pairs={{1,3},{3,5},{5,7},{7,9},{9,11},{11,13},{13,15},{15,17},{17,19},{19... | collective-permute-start | bytes 3244040 | tf_op jit(solution)/shard_map/ppermute | solution.py:30
  26.1 0.0 collective-permute-done.5.partner0
  26.1 1.7 %collective-permute-start.6 = (bf16[528,1024]{1,0:T(8,128)(2,1)}, bf16[528,1024]{1,0:T(8,128)(2,1)}, u32[]{:S(2)}, u32[]{:S(2)}) collective-permute-start(bf16[528,1024]{1,0:T(8,128)(2,1)} %collective-permute-done.5.partner0), channel_id=1, source_target_pairs={{1,3},{3,5},{5,7},{7,9},{9,11},{11,13},{13,15},{15,17},{17,19},{19... | collective-permute-start | bytes 3244040 | tf_op jit(solution)/shard_map/ppermute | solution.py:30
  27.8 1.6 %collective-permute-start.7 = (bf16[528,1024]{1,0:T(8,128)(2,1)}, bf16[528,1024]{1,0:T(8,128)(2,1)}, u32[]{:S(2)}, u32[]{:S(2)}) collective-permute-start(bf16[528,1024]{1,0:T(8,128)(2,1)} %collective-permute-done.5.partner0), channel_id=1, source_target_pairs={{1,31},{3,1},{5,3},{7,5},{9,7},{11,9},{13,11},{15,13},{17,15},{19,... | collective-permute-start | bytes 3244040 | tf_op jit(solution)/shard_map/ppermute | solution.py:30
  29.5 0.1 pad_add_fusion.where_ref
  29.6 0.0 collective-permute-done.1.near1
  29.6 11.4 %collective-permute-start.2 = (bf16[528,1024]{1,0:T(8,128)(2,1)}, bf16[528,1024]{1,0:T(8,128)(2,1)}, u32[]{:S(2)}, u32[]{:S(2)}) collective-permute-start(bf16[528,1024]{1,0:T(8,128)(2,1)} %collective-permute-done.1.near1), channel_id=1, source_target_pairs={{0,1},{2,3},{4,5},{6,7},{8,9},{10,11},{12,13},{14,15},{16,17},{18,... | collective-permute-start | bytes 3244040 | tf_op jit(solution)/shard_map/ppermute | solution.py:30
  41.0 1.3 %collective-permute-done.3.partner1 = bf16[528,1024]{1,0:T(8,128)(2,1)} collective-permute-done((bf16[528,1024]{1,0:T(8,128)(2,1)S(1)}, bf16[528,1024]{1,0:T(8,128)(2,1)}, u32[]{:S(2)}, u32[]{:S(2)}) %collective-permute-start.3) | collective-permute-done | bytes 1081376 | tf_op jit(solution)/shard_map/ppermute | solution.py:30
  42.3 1.7 %collective-permute-start.4 = (bf16[528,1024]{1,0:T(8,128)(2,1)}, bf16[528,1024]{1,0:T(8,128)(2,1)}, u32[]{:S(2)}, u32[]{:S(2)}) collective-permute-start(bf16[528,1024]{1,0:T(8,128)(2,1)} %collective-permute-done.3.partner1), channel_id=1, source_target_pairs={{1,31},{3,1},{5,3},{7,5},{9,7},{11,9},{13,11},{15,13},{17,15},{19,... | collective-permute-start | bytes 3244040 | tf_op jit(solution)/shard_map/ppermute | solution.py:30
  43.9 0.0 copy-done.5
  43.9 2.4 %within.1.so_far_ref = f32[8,1024]{1,0:T(8,128)S(1)} custom-call(bf16[528,1024]{1,0:T(8,128)(2,1)S(1)} %norm_0.1.own0, bf16[528,1024]{1,0:T(8,128)(2,1)S(1)} %norm_1.1.own1, f32[1,1024]{1,0:T(1,128)S(1)} %copy-done.5), custom_call_target="tpu_custom_call" | custom-call | flops 2147483648 | bytes 2097152 | tf_op jit(solution)/shard_map/within/pallas_call | solution.py:274
  46.3 4.5 %all-to-all-done.in_ref = bf16[128,4,1152]{2,1,0:T(4,128)(2,1)S(1)} async-done(((bf16[128,4,1152]{2,1,0:T(4,128)(2,1)}), bf16[128,4,1152]{2,1,0:T(4,128)(2,1)S(1)}, u32[]{:S(2)}, u32[]{:S(2)}) %all-to-all-start) | async-done | bytes 1179680 | tf_op jit(solution)/shard_map/all_to_all | solution.py:264
  50.8 1.1 %split.1 = (bf16[512,1024]{1,0:T(8,128)(2,1)}, s32[1,512]{1,0:T(1,128)}) custom-call(bf16[128,4,1152]{2,1,0:T(4,128)(2,1)S(1)} %all-to-all-done.in_ref), custom_call_target="tpu_custom_call" | custom-call | bytes 2097152 | tf_op jit(solution)/shard_map/split/pallas_call | solution.py:169
  52.0 0.0 collective-permute-done.near0
  52.0 0.0 copy-start.6
  52.0 0.7 copy-done.6
  52.6 3.7 %near.1.so_far_ref = f32[8,1024]{1,0:T(8,128)S(1)} custom-call(bf16[528,1024]{1,0:T(8,128)(2,1)S(1)} %norm_0.1.own0, bf16[528,1024]{1,0:T(8,128)(2,1)S(1)} %norm_1.1.own1, bf16[528,1024]{1,0:T(8,128)(2,1)} %collective-permute-done.5.partner0, bf16[528,1024]{1,0:T(8,128)(2,1)} %collective-permute-done.3.partner1, ...), custom_call_target="tpu_custom_call" | custom-call | flops 6442450944 | bytes 6291456 | tf_op jit(solution)/shard_map/near/pallas_call | solution.py:283
  56.4 0.0 collective-permute-done.6.near_partner0
  56.4 0.0 collective-permute-done.7.far0
  56.4 3.2 %cross_middle.1 = (f32[8,1024]{1,0:T(8,128)S(1)}, f32[1,1024]{1,0:T(1,128)S(1)}) custom-call(bf16[528,1024]{1,0:T(8,128)(2,1)S(1)} %norm_0.1.own0, bf16[528,1024]{1,0:T(8,128)(2,1)S(1)} %norm_1.1.own1, bf16[528,1024]{1,0:T(8,128)(2,1)} %collective-permute-done.5.partner0, bf16[528,1024]{1,0:T(8,128)(2,1)} %collective-permute-done.3.partner1, ...), custom_call_target="tpu_custom_call" | custom-call | flops 3221225472 | bytes 8388608 | tf_op jit(solution)/shard_map/cross_middle/pallas_call | solution.py:292
  59.6 1.3 %collective-permute-start.8 = (f32[1,1024]{1,0:T(1,128)S(1)}, f32[1,1024]{1,0:T(1,128)S(1)}, u32[]{:S(2)}, u32[]{:S(2)}) collective-permute-start(f32[1,1024]{1,0:T(1,128)S(1)} %get-tuple-element.12), channel_id=1, source_target_pairs={{1,0},{3,2},{5,4},{7,6},{9,8},{11,10},{13,12},{15,14},{17,16},{19,... | collective-permute-start | bytes 12296 | tf_op jit(solution)/shard_map/ppermute | solution.py:30
  60.9 0.0 collective-permute-done.2.near_partner1
  60.9 0.0 collective-permute-done.4.far1
  60.9 17.0 %collective-permute-done.8.from_partner_ref = f32[1,1024]{1,0:T(1,128)S(1)} collective-permute-done((f32[1,1024]{1,0:T(1,128)S(1)}, f32[1,1024]{1,0:T(1,128)S(1)}, u32[]{:S(2)}, u32[]{:S(2)}) %collective-permute-start.8) | collective-permute-done | bytes 4128 | tf_op jit(solution)/shard_map/ppermute | solution.py:30
  77.9 2.2 %cross_last.1 = (f32[1,1024]{1,0:T(1,128)S(1)}, f32[1,1024]{1,0:T(1,128)S(1)}, f32[1,1024]{1,0:T(1,128)S(1)}) custom-call(bf16[528,1024]{1,0:T(8,128)(2,1)S(1)} %norm_0.1.own0, bf16[528,1024]{1,0:T(8,128)(2,1)S(1)} %norm_1.1.own1, bf16[528,1024]{1,0:T(8,128)(2,1)} %collective-permute-done.near0, bf16[528,1024]{1,0:T(8,128)(2,1)} %collective-permute-done.1.near1, ...), custom_call_target="tpu_custom_call" | custom-call | flops 2147483648 | bytes 6291456 | tf_op jit(solution)/shard_map/cross_last/pallas_call | solution.py:302
  80.1 0.7 collective-permute-start.10
  80.8 1.3 %collective-permute-start.9 = (f32[1,1024]{1,0:T(1,128)S(1)}, f32[1,1024]{1,0:T(1,128)S(1)}, u32[]{:S(2)}, u32[]{:S(2)}) collective-permute-start(f32[1,1024]{1,0:T(1,128)S(1)} %get-tuple-element.14), channel_id=1, source_target_pairs={{1,2},{3,4},{5,6},{7,8},{9,10},{11,12},{13,14},{15,16},{17,18},{19... | collective-permute-start | bytes 12296 | tf_op jit(solution)/shard_map/ppermute | solution.py:30
  82.1 0.0 collective-permute-done.10
  82.1 8.4 %collective-permute-done.9 = f32[1,1024]{1,0:T(1,128)S(1)} collective-permute-done((f32[1,1024]{1,0:T(1,128)S(1)}, f32[1,1024]{1,0:T(1,128)S(1)}, u32[]{:S(2)}, u32[]{:S(2)}) %collective-permute-start.9) | collective-permute-done | bytes 4128 | tf_op jit(solution)/shard_map/ppermute | solution.py:30
  90.5 0.6 fusion.1
Async XLA Ops:
  0.6 1.6 %copy-start = (bf16[1,1024,1024]{2,1,0:T(8,128)(2,1)S(1)}, bf16[1,1024,1024]{2,1,0:T(8,128)(2,1)}, u32[]{:S(2)}) copy-start(bf16[1,1024,1024]{2,1,0:T(8,128)(2,1)} %param.6) | copy-start | bytes 6291460
  2.2 0.7 copy-start.2
  3.2 8.9 %copy-start.1 = (bf16[256,1024]{1,0:T(8,128)(2,1)S(1)}, bf16[256,1024]{1,0:T(8,128)(2,1)}, u32[]{:S(2)}) copy-start(bf16[256,1024]{1,0:T(8,128)(2,1)} %rows_ref.1) | copy-start | bytes 1572868
  3.3 8.9 %copy-start.3 = (s32[256,1]{0,1:T(1,128)S(1)}, s32[256,1]{0,1:T(1,128)}, u32[]{:S(2)}) copy-start(s32[256,1]{0,1:T(1,128)} %param.11) | copy-start | bytes 3076
  3.3 8.9 %copy-start.4 = (s32[256]{0:T(256)S(1)}, s32[256]{0:T(256)}, u32[]{:S(2)}) copy-start(s32[256]{0:T(256)} %param.10) | copy-start | bytes 3076
  3.3 22.8 %collective-permute-start.5 = (bf16[528,1024]{1,0:T(8,128)(2,1)S(1)}, bf16[528,1024]{1,0:T(8,128)(2,1)}, u32[]{:S(2)}, u32[]{:S(2)}) collective-permute-start(bf16[528,1024]{1,0:T(8,128)(2,1)S(1)} %norm_0.1.own0), channel_id=1, source_target_pairs={{0,1},{2,3},{4,5},{6,7},{8,9},{10,11},{12,13},{14,15},{16,17},{18,... | collective-permute-start | bytes 3244040 | tf_op jit(solution)/shard_map/ppermute | solution.py:30
  8.3 21.2 %collective-permute-start.1 = (bf16[528,1024]{1,0:T(8,128)(2,1)S(1)}, bf16[528,1024]{1,0:T(8,128)(2,1)}, u32[]{:S(2)}, u32[]{:S(2)}) collective-permute-start(bf16[528,1024]{1,0:T(8,128)(2,1)S(1)} %norm_1.1.own1), channel_id=1, source_target_pairs={{0,2},{1,3},{2,4},{3,5},{4,6},{5,7},{6,8},{7,9},{8,10},{9,11},{10,... | collective-permute-start | bytes 3244040 | tf_op jit(solution)/shard_map/ppermute | solution.py:30
  9.9 32.4 %collective-permute-start.3 = (bf16[528,1024]{1,0:T(8,128)(2,1)S(1)}, bf16[528,1024]{1,0:T(8,128)(2,1)}, u32[]{:S(2)}, u32[]{:S(2)}) collective-permute-start(bf16[528,1024]{1,0:T(8,128)(2,1)S(1)} %norm_1.1.own1), channel_id=1, source_target_pairs={{0,1},{2,3},{4,5},{6,7},{8,9},{10,11},{12,13},{14,15},{16,17},{18,... | collective-permute-start | bytes 3244040 | tf_op jit(solution)/shard_map/ppermute | solution.py:30
  13.9 30.0 %copy-start.5 = (f32[1,1024]{1,0:T(1,128)S(1)}, f32[1,1024]{1,0:T(1,128)}, u32[]{:S(2)}) copy-start(f32[1,1024]{1,0:T(1,128)} %prior_ref.1) | copy-start | bytes 12292
  13.9 36.9 %all-to-all-start = ((bf16[128,4,1152]{2,1,0:T(4,128)(2,1)}), bf16[128,4,1152]{2,1,0:T(4,128)(2,1)S(1)}, u32[]{:S(2)}, u32[]{:S(2)}) async-start(bf16[128,4,1152]{2,1,0:T(4,128)(2,1)} %place.1), calls=%async_computation | async-start | bytes 2359296 | tf_op jit(solution)/shard_map/all_to_all | solution.py:264
  24.4 27.5 %collective-permute-start = (bf16[528,1024]{1,0:T(8,128)(2,1)S(1)}, bf16[528,1024]{1,0:T(8,128)(2,1)}, u32[]{:S(2)}, u32[]{:S(2)}) collective-permute-start(bf16[528,1024]{1,0:T(8,128)(2,1)S(1)} %norm_0.1.own0), channel_id=1, source_target_pairs={{1,3},{3,5},{5,7},{7,9},{9,11},{11,13},{13,15},{15,17},{17,19},{19... | collective-permute-start | bytes 3244040 | tf_op jit(solution)/shard_map/ppermute | solution.py:30
  26.1 30.3 %collective-permute-start.6 = (bf16[528,1024]{1,0:T(8,128)(2,1)}, bf16[528,1024]{1,0:T(8,128)(2,1)}, u32[]{:S(2)}, u32[]{:S(2)}) collective-permute-start(bf16[528,1024]{1,0:T(8,128)(2,1)} %collective-permute-done.5.partner0), channel_id=1, source_target_pairs={{1,3},{3,5},{5,7},{7,9},{9,11},{11,13},{13,15},{15,17},{17,19},{19... | collective-permute-start | bytes 3244040 | tf_op jit(solution)/shard_map/ppermute | solution.py:30
  27.8 28.5 %collective-permute-start.7 = (bf16[528,1024]{1,0:T(8,128)(2,1)}, bf16[528,1024]{1,0:T(8,128)(2,1)}, u32[]{:S(2)}, u32[]{:S(2)}) collective-permute-start(bf16[528,1024]{1,0:T(8,128)(2,1)} %collective-permute-done.5.partner0), channel_id=1, source_target_pairs={{1,31},{3,1},{5,3},{7,5},{9,7},{11,9},{13,11},{15,13},{17,15},{19,... | collective-permute-start | bytes 3244040 | tf_op jit(solution)/shard_map/ppermute | solution.py:30
  29.6 31.3 %collective-permute-start.2 = (bf16[528,1024]{1,0:T(8,128)(2,1)}, bf16[528,1024]{1,0:T(8,128)(2,1)}, u32[]{:S(2)}, u32[]{:S(2)}) collective-permute-start(bf16[528,1024]{1,0:T(8,128)(2,1)} %collective-permute-done.1.near1), channel_id=1, source_target_pairs={{0,1},{2,3},{4,5},{6,7},{8,9},{10,11},{12,13},{14,15},{16,17},{18,... | collective-permute-start | bytes 3244040 | tf_op jit(solution)/shard_map/ppermute | solution.py:30
  42.3 18.6 %collective-permute-start.4 = (bf16[528,1024]{1,0:T(8,128)(2,1)}, bf16[528,1024]{1,0:T(8,128)(2,1)}, u32[]{:S(2)}, u32[]{:S(2)}) collective-permute-start(bf16[528,1024]{1,0:T(8,128)(2,1)} %collective-permute-done.3.partner1), channel_id=1, source_target_pairs={{1,31},{3,1},{5,3},{7,5},{9,7},{11,9},{13,11},{15,13},{17,15},{19,... | collective-permute-start | bytes 3244040 | tf_op jit(solution)/shard_map/ppermute | solution.py:30
  52.0 0.7 copy-start.6
  59.6 18.3 %collective-permute-start.8 = (f32[1,1024]{1,0:T(1,128)S(1)}, f32[1,1024]{1,0:T(1,128)S(1)}, u32[]{:S(2)}, u32[]{:S(2)}) collective-permute-start(f32[1,1024]{1,0:T(1,128)S(1)} %get-tuple-element.12), channel_id=1, source_target_pairs={{1,0},{3,2},{5,4},{7,6},{9,8},{11,10},{13,12},{15,14},{17,16},{19,... | collective-permute-start | bytes 12296 | tf_op jit(solution)/shard_map/ppermute | solution.py:30
  80.1 2.0 %collective-permute-start.10 = (f32[1,1024]{1,0:T(1,128)S(1)}, f32[1,1024]{1,0:T(1,128)S(1)}, u32[]{:S(2)}, u32[]{:S(2)}) collective-permute-start(f32[1,1024]{1,0:T(1,128)S(1)} %get-tuple-element.15), channel_id=1, source_target_pairs={{32,34},{33,35},{34,36},{35,37},{36,38},{37,39},{38,40},{39,41},{4... | collective-permute-start | bytes 12296 | tf_op jit(solution)/shard_map/ppermute | solution.py:30
  80.8 9.7 %collective-permute-start.9 = (f32[1,1024]{1,0:T(1,128)S(1)}, f32[1,1024]{1,0:T(1,128)S(1)}, u32[]{:S(2)}, u32[]{:S(2)}) collective-permute-start(f32[1,1024]{1,0:T(1,128)S(1)} %get-tuple-element.14), channel_id=1, source_target_pairs={{1,2},{3,4},{5,6},{7,8},{9,10},{11,12},{13,14},{15,16},{17,18},{19... | collective-permute-start | bytes 12296 | tf_op jit(solution)/shard_map/ppermute | solution.py:30

commit v5 on v4

--- a/solution.py
+++ b/solution.py
@@ -8,6 +8,7 @@
 CAP = 4
 LOWEST = -2.0
 EXTRA = 16
+TIES = True
 BOTH = ("grp", "blk")
 OWN, PARTNER, NEAR, NEAR_PARTNER, FAR_PARTNER = range(5)
 
@@ -67,11 +68,13 @@
     return jnp.concatenate(found, axis=1)
 
 
-def update(acc_ref, at_row, rows, cols):
-    for _, col_ref in cols:
+def update(acc_ref, at_row, rows, cols, arrive):
+    for _, col in cols:
+        col_ref = arrive(col)
         size = col_ref.shape[0] - EXTRA
         col_down = down(numbers_of(col_ref))
-        for half, row_ref in rows:
+        for half, row in rows:
+            row_ref = arrive(row)
             row_ids = numbers_of(row_ref)
             for top in range(0, size, 256):
                 found = best(row_ref[top : top + 256, :], row_ids[:, top : top + 256], col_ref[:size, :], col_down)
@@ -79,16 +82,35 @@
                 acc_ref[at_row : at_row + 1, at] = jnp.maximum(acc_ref[at_row : at_row + 1, at], found)
 
 
-def compare(where_ref, heavy, acc_ref, pairs):
+def compare(where_ref, heavy, acc_ref, names, refs, buffers, sems, pairs):
+    needed = [name for name in names if any(name == n for p in pairs for side in p for _, n in side[1])]
+
+    def run(core):
+        copies = {
+            name: pltpu.make_async_copy(refs[names.index(name)], buffers.at[k], sems.at[k])
+            for k, name in enumerate(needed)
+        }
+        for copy in copies.values():
+            copy.start()
+        there = set()
+
+        def arrive(name):
+            if name not in there:
+                copies[name].wait()
+                there.add(name)
+            return buffers.at[needed.index(name)]
+
+        for (first, first_halves), (second, second_halves) in pairs:
+            if core == 0:
+                update(acc_ref, first, first_halves, second_halves, arrive)
+            else:
+                update(acc_ref, second, second_halves, first_halves, arrive)
+
     for core in (0, 1):
 
         @pl.when((where_ref[0] == core) & (where_ref[1] == heavy))
         def _():
-            for (first, first_refs), (second, second_refs) in pairs:
-                if core == 0:
-                    update(acc_ref, first, first_refs, second_refs)
-                else:
-                    update(acc_ref, second, second_refs, first_refs)
+            run(core)
 
 
 def norm_kernel(x_ref, ids_ref, out_ref):
@@ -176,54 +198,73 @@
         ],
         compiler_params=params(),
         name="split",
-        cost_estimate=pl.CostEstimate(flops=0, bytes_accessed=4 * slots * width, transcendentals=0),
+        cost_estimate=pl.CostEstimate(flops=20 * 10**9, bytes_accessed=4 * slots * width, transcendentals=0),
     )(arrived)
 
 
 def within_kernel(own0, own1, prior_ref, acc_ref):
     acc_ref[...] = jnp.full(acc_ref.shape, LOWEST, jnp.float32)
     acc_ref[OWN : OWN + 1, :] = prior_ref[...]
-    own = [(0, own0), (1, own1)]
-    update(acc_ref, OWN, own, own)
-
-
-def near_kernel(own0, own1, partner0, partner1, near0, near1, where_ref, so_far_ref, after_ref, acc_ref):
-    del after_ref
-    acc_ref[...] = so_far_ref[...]
-    own = (OWN, [(0, own0), (1, own1)])
-    partner = (PARTNER, [(0, partner0), (1, partner1)])
-    near = (NEAR, [(0, near0), (1, near1)])
-    compare(where_ref, 1, acc_ref, [(own, partner), (own, near), (partner, near)])
-    compare(where_ref, 0, acc_ref, [(own, (NEAR_PARTNER, [(1, near1)]))])
-
-
-def middle_kernel(
-    own0, own1, partner0, partner1, near0, near1, near_partner0, far0, where_ref, so_far_ref, acc_ref, partner_out
-):
-    acc_ref[...] = so_far_ref[...]
-    own = (OWN, [(0, own0), (1, own1)])
-    partner = (PARTNER, [(0, partner0), (1, partner1)])
-    near = (NEAR, [(0, near0), (1, near1)])
-    near_partner = (NEAR_PARTNER, [(0, near_partner0)])
-    far = (FAR_PARTNER, [(0, far0)])
-    compare(where_ref, 1, acc_ref, [(own, near_partner), (partner, near_partner), (far, near)])
-    partner_out[...] = acc_ref[PARTNER : PARTNER + 1, :]
-
-
-def last_kernel(
-    own0, own1, near0, near1, near_partner1, far1, where_ref, so_far_ref, from_partner_ref, own_out, far_out, side_out, acc_ref
-):
-    acc_ref[...] = so_far_ref[...]
-    own = (OWN, [(0, own0), (1, own1)])
-    near = (NEAR, [(0, near0), (1, near1)])
-    near_partner = (NEAR_PARTNER, [(1, near_partner1)])
-    far = (FAR_PARTNER, [(1, far1)])
-    compare(where_ref, 1, acc_ref, [(own, near_partner), (far, near)])
-    own_row = acc_ref[OWN : OWN + 1, :]
+    own = [(0, 0), (1, 1)]
+    update(acc_ref, OWN, own, own, lambda half: (own0, own1)[half])
+
+
+def stage(name, arrays, heavy_pairs, light_pairs, where, found, after=()):
+    names = list(arrays)
+    size, width = arrays[names[0]].shape
+    rows = found.shape[1]
+
+    def run(*refs):
+        inputs, where_ref, so_far_ref = refs[: len(names)], refs[len(names)], refs[len(names) + 1]
+        acc_ref, buffers, sems = refs[-3:]
+        acc_ref[...] = so_far_ref[...]
+        compare(where_ref, 1, acc_ref, names, inputs, buffers, sems, heavy_pairs)
+        if light_pairs:
+            compare(where_ref, 0, acc_ref, names, inputs, buffers, sems, light_pairs)
+
+    products = sum(len(a[1]) * len(b[1]) for a, b in heavy_pairs) / 4
+    return pl.pallas_call(
+        run,
+        in_specs=[pl.BlockSpec(memory_space=pltpu.HBM)] * len(names)
+        + smem()
+        + vmem(1)
+        + vmem(len(after)),
+        out_specs=pl.BlockSpec(memory_space=pltpu.VMEM),
+        out_shape=jax.ShapeDtypeStruct(found.shape, jnp.float32),
+        scratch_shapes=[pltpu.VMEM((len(names), size, width), jnp.bfloat16), pltpu.SemaphoreType.DMA((len(names),))],
+        compiler_params=params(),
+        name=name,
+        cost_estimate=pl.CostEstimate(
+            flops=int(2 * products * rows * rows * width),
+            bytes_accessed=2 * len(names) * size * width,
+            transcendentals=0,
+        ),
+    )(*arrays.values(), where, found, *after)
+
+
+def tie_kernel(array_ref, after_ref, out_ref):
+    del array_ref, after_ref, out_ref
+
+
+def tie(array, after):
+    return pl.pallas_call(
+        tie_kernel,
+        in_specs=[pl.BlockSpec(memory_space=pltpu.HBM)] + vmem(1),
+        out_specs=pl.BlockSpec(memory_space=pltpu.HBM),
+        out_shape=jax.ShapeDtypeStruct(array.shape, array.dtype),
+        input_output_aliases={0: 0},
+        compiler_params=params(),
+        name="tie",
+        cost_estimate=pl.CostEstimate(flops=0, bytes_accessed=0, transcendentals=0),
+    )(array, after)
+
+
+def results_kernel(where_ref, so_far_ref, from_partner_ref, own_out, far_out, side_out):
+    own_row = so_far_ref[OWN : OWN + 1, :]
     own_out[...] = jnp.where(where_ref[1] == 0, jnp.maximum(own_row, from_partner_ref[...]), own_row)
-    near_partner_row = acc_ref[NEAR_PARTNER : NEAR_PARTNER + 1, :]
-    far_out[...] = jnp.where(where_ref[0] == 0, acc_ref[FAR_PARTNER : FAR_PARTNER + 1, :], near_partner_row)
-    side_out[...] = jnp.where(where_ref[1] == 1, acc_ref[NEAR : NEAR + 1, :], near_partner_row)
+    near_partner_row = so_far_ref[NEAR_PARTNER : NEAR_PARTNER + 1, :]
+    far_out[...] = jnp.where(where_ref[0] == 0, so_far_ref[FAR_PARTNER : FAR_PARTNER + 1, :], near_partner_row)
+    side_out[...] = jnp.where(where_ref[1] == 1, so_far_ref[NEAR : NEAR + 1, :], near_partner_row)
 
 
 def body(embeds, doc_ids, prior_max, owned, owned_ids, owner_dest):
@@ -252,63 +293,112 @@
     def heavy_back(core, heavy, block):
         return block - step(core) if heavy else None
 
-    own = [norm_half(raw, doc_ids, half) for half in range(2)]
-    partner = [send(own[half], to_heavy) for half in range(2)]
-    near1 = send(own[1], ahead)
-    near0 = send(own[0], heavy_ahead)
-    far = [send(partner[half], heavy_back) for half in range(2)]
-    near_partner0 = send(partner[0], heavy_ahead)
-    near_partner1 = send(near1, to_heavy)
-
     outgoing = placed_rows(owned, owner_dest.reshape(1, -1), owned_ids.reshape(1, -1), devices)
     next_rows, next_ids = split_rows(lax.all_to_all(outgoing, BOTH, split_axis=0, concat_axis=0, tiled=True))
 
     line = jax.ShapeDtypeStruct((1, rows), jnp.float32)
-    acc = jax.ShapeDtypeStruct((8, rows), jnp.float32)
-
-    def cost(products, blocks):
-        return pl.CostEstimate(
-            flops=int(2 * products * rows * rows * width), bytes_accessed=2 * blocks * rows * width, transcendentals=0
-        )
+    own0, own1 = (norm_half(raw, doc_ids, half) for half in range(2))
+    partner0 = send(own0, to_heavy)
+    near1 = send(own1, ahead)
+    partner1 = send(own1, to_heavy)
+    near0 = send(own0, heavy_ahead)
 
     found = pl.pallas_call(
         within_kernel,
         in_specs=vmem(3),
         out_specs=pl.BlockSpec(memory_space=pltpu.VMEM),
-        out_shape=acc,
+        out_shape=jax.ShapeDtypeStruct((8, rows), jnp.float32),
         compiler_params=params(),
         name="within",
-        cost_estimate=cost(1, 1),
-    )(*own, prior_max)
-    found = pl.pallas_call(
-        near_kernel,
-        in_specs=vmem(6) + smem() + vmem(1) + [pl.BlockSpec(memory_space=pl.ANY)],
-        out_specs=pl.BlockSpec(memory_space=pltpu.VMEM),
-        out_shape=acc,
-        compiler_params=params(),
-        name="near",
-        cost_estimate=cost(3, 3),
-    )(*own, *partner, near0, near1, where, found, next_ids)
-    found, for_partner = pl.pallas_call(
-        middle_kernel,
-        in_specs=vmem(8) + smem() + vmem(1),
-        out_specs=vmem(2),
-        out_shape=[acc, line],
-        compiler_params=params(),
-        name="cross_middle",
-        cost_estimate=cost(1.5, 4),
-    )(*own, *partner, near0, near1, near_partner0, far[0], where, found)
-    from_partner = send(for_partner, to_light)
+        cost_estimate=pl.CostEstimate(
+            flops=2 * rows * rows * width, bytes_accessed=2 * rows * width, transcendentals=0
+        ),
+    )(own0, own1, prior_max)
+    if TIES:
+        partner0 = tie(partner0, found)
+    far0 = send(partner0, heavy_back)
+    near_partner0 = send(partner0, heavy_ahead)
+    near_partner1 = send(near1, to_heavy)
+
+    own = (OWN, [(0, "own0"), (1, "own1")])
+    found = stage(
+        "cross_a",
+        {"own0": own0, "own1": own1, "partner0": partner0, "near1": near1},
+        [
+            (own, (PARTNER, [(0, "partner0")])),
+            (own, (NEAR, [(1, "near1")])),
+            ((PARTNER, [(0, "partner0")]), (NEAR, [(1, "near1")])),
+        ],
+        [(own, (NEAR_PARTNER, [(1, "near1")]))],
+        where,
+        found,
+        (next_ids,),
+    )
+    if TIES:
+        partner1 = tie(partner1, found)
+    far1 = send(partner1, heavy_back)
+    found = stage(
+        "cross_b",
+        {"own0": own0, "own1": own1, "partner1": partner1, "near0": near0, "partner0": partner0, "near1": near1},
+        [
+            (own, (PARTNER, [(1, "partner1")])),
+            (own, (NEAR, [(0, "near0")])),
+            ((PARTNER, [(0, "partner0"), (1, "partner1")]), (NEAR, [(0, "near0")])),
+            ((PARTNER, [(1, "partner1")]), (NEAR, [(1, "near1")])),
+        ],
+        [],
+        where,
+        found,
+    )
+    near_both = (NEAR, [(0, "near0"), (1, "near1")])
+    found = stage(
+        "cross_c",
+        {
+            "own0": own0,
+            "near_partner0": near_partner0,
+            "own1": own1,
+            "partner0": partner0,
+            "partner1": partner1,
+            "near0": near0,
+            "far0": far0,
+            "near1": near1,
+        },
+        [
+            (own, (NEAR_PARTNER, [(0, "near_partner0")])),
+            ((PARTNER, [(0, "partner0"), (1, "partner1")]), (NEAR_PARTNER, [(0, "near_partner0")])),
+            ((FAR_PARTNER, [(0, "far0")]), near_both),
+        ],
+        [],
+        where,
+        found,
+    )
+    from_partner = send(found[PARTNER : PARTNER + 1], to_light)
+    found = stage(
+        "cross_d",
+        {
+            "own0": own0,
+            "near_partner1": near_partner1,
+            "own1": own1,
+            "near0": near0,
+            "far1": far1,
+            "near1": near1,
+        },
+        [
+            (own, (NEAR_PARTNER, [(1, "near_partner1")])),
+            ((FAR_PARTNER, [(1, "far1")]), near_both),
+        ],
+        [],
+        where,
+        found,
+    )
     mine, for_far, for_side = pl.pallas_call(
-        last_kernel,
-        in_specs=vmem(6) + smem() + vmem(2),
+        results_kernel,
+        in_specs=smem() + vmem(2),
         out_specs=vmem(3),
         out_shape=[line] * 3,
-        scratch_shapes=[pltpu.VMEM((8, rows), jnp.float32)],
-        compiler_params=params(),
-        name="cross_last",
-        cost_estimate=cost(1, 3),
-    )(*own, near0, near1, near_partner1, far[1], where, found, from_partner)
+        compiler_params=params(),
+        name="results",
+    )(where, found, from_partner)
     from_far = send(for_far, lambda core, heavy, block: block + 1 + 2 * core if heavy else None)
     from_side = send(for_side, lambda core, heavy, block: block + 2 if core else None)
     lowest = jnp.float32(LOWEST)

time: 91.6 us -> 95.8 us (1.046)
  the two profiles are of different devices: /device:TPU:0 before, /device:TPU:9 now
where the time goes in v5:
time: 95.8 us; the launch traced here: 95.3 us
  starting transfers between devices  41.5 us (43%)
  waiting for transfers between devices  32.7 us (34%)
  Pallas kernels  16.5 us (17%)
  local copies, waits for them, and re-layouts  3.09 us (3%)
    ppermute x11, waiting for transfers between devices, send(): return lax.ppermute(value, BOTH, pairs)  32.7 us
    ppermute x11, starting transfers between devices, send(): return lax.ppermute(value, BOTH, pairs)  30.7 us
    all_to_all x1, starting transfers between devices, body(): lax.all_to_all(outgoing, BOTH, split_axis=0, concat_axis=0, tiled=True)  10.8 us
    pallas_call x4, Pallas kernels, stage(): pl.pallas_call(run, in_specs=[pl.BlockSpec(memory_space=pltpu.HBM)] * len...  6.52 us
    pallas_call x1, Pallas kernels, body(): pl.pallas_call(within_kernel, in_specs=vmem(3), out_specs=pl.BlockSpec(me...  3.94 us
    unnamed x14, local copies, waits for them, and re-layouts  3.08 us
    pallas_call x2, Pallas kernels, norm_half(): pl.pallas_call(norm_kernel, grid=(1,), in_specs=[pl.BlockSpec((size, widt...  2.62 us
  transfers between devices with their start and end apart: 12, of which 5 were waited for; matrix products, arithmetic and copies ran while one was open for 0% of the time, Pallas kernels for 15%

profile of v5, /device:TPU:9, one launch (start us, length us, event | category | flops | bytes accessed | tf_op | source)
XLA Modules:
  0.0 95.3 jit_solution(5929072790105664966)
XLA Ops:
  0.6 0.0 copy-start.1
  0.6 1.0 %copy-done.1 = bf16[256,1024]{1,0:T(8,128)(2,1)S(1)} copy-done((bf16[256,1024]{1,0:T(8,128)(2,1)S(1)}, bf16[256,1024]{1,0:T(8,128)(2,1)}, u32[]{:S(2)}) %copy-start.1) | copy-done | bytes 524312
  1.7 0.0 copy-start.3
  1.7 0.7 copy-done.3
  2.4 0.0 copy-start.4
  2.4 0.7 copy-done.4
  3.0 1.8 %place.1 = bf16[128,4,1152]{2,1,0:T(4,128)(2,1)} custom-call(bf16[256,1024]{1,0:T(8,128)(2,1)S(1)} %copy-done.1, s32[1,256]{1,0:T(1,128)S(1)} %bitcast.8, s32[1,256]{1,0:T(1,128)S(1)} %bitcast.9), custom_call_target="tpu_custom_call" | custom-call | flops 268435456 | bytes 1572864 | tf_op jit(solution)/shard_map/place/pallas_call | solution.py:167
  4.8 0.0 copy-start
  4.8 0.0 copy-start.2
  4.8 10.8 %all-to-all-start = ((bf16[128,4,1152]{2,1,0:T(4,128)(2,1)}), bf16[128,4,1152]{2,1,0:T(4,128)(2,1)S(1)}, u32[]{:S(2)}, u32[]{:S(2)}) async-start(bf16[128,4,1152]{2,1,0:T(4,128)(2,1)} %place.1), calls=%async_computation | async-start | bytes 2359296 | tf_op jit(solution)/shard_map/all_to_all | solution.py:297
  15.6 0.0 copy-done
  15.6 0.0 copy-done.2
  15.6 1.3 %norm_0.1.own0.refs_0_ = bf16[528,1024]{1,0:T(8,128)(2,1)} custom-call(bf16[1024,1024]{1,0:T(8,128)(2,1)S(1)} %bitcast.6, s32[1,1024]{1,0:T(1,128)S(1)} %copy-done.2), custom_call_target="tpu_custom_call" | custom-call | flops 2097152 | bytes 2097152 | tf_op jit(solution)/shard_map/norm_0/pallas_call | solution.py:128
  16.9 0.0 copy-start.5
  16.9 3.1 %collective-permute-start.4 = (bf16[528,1024]{1,0:T(8,128)(2,1)}, bf16[528,1024]{1,0:T(8,128)(2,1)}, u32[]{:S(2)}, u32[]{:S(2)}) collective-permute-start(bf16[528,1024]{1,0:T(8,128)(2,1)} %norm_0.1.own0.refs_0_), channel_id=1, source_target_pairs={{0,1},{2,3},{4,5},{6,7},{8,9},{10,11},{12,13},{14,15},{16,17},{18,... | collective-permute-start | bytes 3244040 | tf_op jit(solution)/shard_map/ppermute | solution.py:31
  20.0 1.3 %norm_1.1.own1.refs_1_.refs_2_ = bf16[528,1024]{1,0:T(8,128)(2,1)} custom-call(bf16[1024,1024]{1,0:T(8,128)(2,1)S(1)} %bitcast.7, s32[1,1024]{1,0:T(1,128)S(1)} %copy-done.2), custom_call_target="tpu_custom_call" | custom-call | flops 2097152 | bytes 2097152 | tf_op jit(solution)/shard_map/norm_1/pallas_call | solution.py:128
  21.3 5.4 %collective-permute-start = (bf16[528,1024]{1,0:T(8,128)(2,1)}, bf16[528,1024]{1,0:T(8,128)(2,1)}, u32[]{:S(2)}, u32[]{:S(2)}) collective-permute-start(bf16[528,1024]{1,0:T(8,128)(2,1)} %norm_1.1.own1.refs_1_.refs_2_), channel_id=1, source_target_pairs={{0,2},{1,3},{2,4},{3,5},{4,6},{5,7},{6,8},{7,9},{8,10},{9,11},{10,... | collective-permute-start | bytes 3244040 | tf_op jit(solution)/shard_map/ppermute | solution.py:31
  26.7 1.3 %collective-permute-start.3 = (bf16[528,1024]{1,0:T(8,128)(2,1)}, bf16[528,1024]{1,0:T(8,128)(2,1)S(1)}, u32[]{:S(2)}, u32[]{:S(2)}) collective-permute-start(bf16[528,1024]{1,0:T(8,128)(2,1)} %norm_1.1.own1.refs_1_.refs_2_), channel_id=1, source_target_pairs={{0,1},{2,3},{4,5},{6,7},{8,9},{10,11},{12,13},{14,15},{16,17},{18,... | collective-permute-start | bytes 3244040 | tf_op jit(solution)/shard_map/ppermute | solution.py:31
  28.1 1.7 %collective-permute-start.2 = (bf16[528,1024]{1,0:T(8,128)(2,1)}, bf16[528,1024]{1,0:T(8,128)(2,1)}, u32[]{:S(2)}, u32[]{:S(2)}) collective-permute-start(bf16[528,1024]{1,0:T(8,128)(2,1)} %norm_0.1.own0.refs_0_), channel_id=1, source_target_pairs={{1,3},{3,5},{5,7},{7,9},{9,11},{11,13},{13,15},{15,17},{17,19},{19... | collective-permute-start | bytes 3244040 | tf_op jit(solution)/shard_map/ppermute | solution.py:31
  29.8 0.1 pad_add_fusion.refs_4_.refs_6_.refs_8_.where_ref
  29.9 0.0 copy-done.5
  29.9 3.9 %within.1.after_ref.refs_5_ = f32[8,1024]{1,0:T(8,128)S(1)} custom-call(bf16[528,1024]{1,0:T(8,128)(2,1)} %norm_0.1.own0.refs_0_, bf16[528,1024]{1,0:T(8,128)(2,1)} %norm_1.1.own1.refs_1_.refs_2_, f32[1,1024]{1,0:T(1,128)S(1)} %copy-done.5), custom_call_target="tpu_custom_call" | custom-call | flops 2147483648 | bytes 2097152 | tf_op jit(solution)/shard_map/within/pallas_call | solution.py:306
  33.8 5.9 %collective-permute-done.4.array_ref = bf16[528,1024]{1,0:T(8,128)(2,1)} collective-permute-done((bf16[528,1024]{1,0:T(8,128)(2,1)}, bf16[528,1024]{1,0:T(8,128)(2,1)}, u32[]{:S(2)}, u32[]{:S(2)}) %collective-permute-start.4) | collective-permute-done | bytes 1081376 | tf_op jit(solution)/shard_map/ppermute | solution.py:31
  39.7 1.7 %collective-permute-start.6 = (bf16[528,1024]{1,0:T(8,128)(2,1)}, bf16[528,1024]{1,0:T(8,128)(2,1)}, u32[]{:S(2)}, u32[]{:S(2)}) collective-permute-start(bf16[528,1024]{1,0:T(8,128)(2,1)} %tie.2.refs_2_.refs_4_.refs_3_), channel_id=1, source_target_pairs={{1,3},{3,5},{5,7},{7,9},{9,11},{11,13},{13,15},{15,17},{17,19},{19... | collective-permute-start | bytes 3244040 | tf_op jit(solution)/shard_map/ppermute | solution.py:31
  41.5 1.6 %collective-permute-start.7 = (bf16[528,1024]{1,0:T(8,128)(2,1)}, bf16[528,1024]{1,0:T(8,128)(2,1)}, u32[]{:S(2)}, u32[]{:S(2)}) collective-permute-start(bf16[528,1024]{1,0:T(8,128)(2,1)} %tie.2.refs_2_.refs_4_.refs_3_), channel_id=1, source_target_pairs={{1,31},{3,1},{5,3},{7,5},{9,7},{11,9},{13,11},{15,13},{17,15},{19,... | collective-permute-start | bytes 3244040 | tf_op jit(solution)/shard_map/ppermute | solution.py:31
  43.1 0.0 collective-permute-done.refs_3_.refs_5_.refs_7_
  43.1 10.5 %collective-permute-start.1 = (bf16[528,1024]{1,0:T(8,128)(2,1)}, bf16[528,1024]{1,0:T(8,128)(2,1)}, u32[]{:S(2)}, u32[]{:S(2)}) collective-permute-start(bf16[528,1024]{1,0:T(8,128)(2,1)} %collective-permute-done.refs_3_.refs_5_.refs_7_), channel_id=1, source_target_pairs={{0,1},{2,3},{4,5},{6,7},{8,9},{10,11},{12,13},{14,15},{16,17},{18,... | collective-permute-start | bytes 3244040 | tf_op jit(solution)/shard_map/ppermute | solution.py:31
  53.7 0.0 all-to-all-done.in_ref
  53.7 1.1 %split.1 = (bf16[512,1024]{1,0:T(8,128)(2,1)}, s32[1,512]{1,0:T(1,128)}) custom-call(bf16[128,4,1152]{2,1,0:T(4,128)(2,1)S(1)} %all-to-all-done.in_ref), custom_call_target="tpu_custom_call" | custom-call | flops 20000000000 | bytes 2097152 | tf_op jit(solution)/shard_map/split/pallas_call | solution.py:191
  54.8 0.0 copy-start.6
  54.8 0.7 copy-done.6
  55.5 4.2 %cross_a.1.after_ref.refs_7_ = f32[8,1024]{1,0:T(8,128)S(1)} custom-call(bf16[528,1024]{1,0:T(8,128)(2,1)} %norm_0.1.own0.refs_0_, bf16[528,1024]{1,0:T(8,128)(2,1)} %norm_1.1.own1.refs_1_.refs_2_, bf16[528,1024]{1,0:T(8,128)(2,1)} %tie.2.refs_2_.refs_4_.refs_3_, bf16[528,1024]{1,0:T(8,128)(2,1)} %collective-permute-done.refs_3_.refs_5_.refs_7_, ...), custom_call_target="tpu_custom_call" | custom-call | flops 2684354560 | bytes 4325376 | tf_op jit(solution)/shard_map/cross_a/pallas_call | solution.py:226
  59.6 0.0 collective-permute-done.3.array_ref
  59.7 0.7 collective-permute-start.5
  60.4 0.0 collective-permute-done.2.refs_3_.refs_5_
  60.4 0.6 cross_b.1.refs_9_
  61.0 0.0 collective-permute-done.6.refs_1_
  61.0 0.0 collective-permute-done.7.refs_6_
  61.1 0.9 cross_c.1.refs_7_
  61.9 1.3 %collective-permute-start.8 = (f32[1,1024]{1,0:T(1,128)S(1)}, f32[1,1024]{1,0:T(1,128)S(1)}, u32[]{:S(2)}, u32[]{:S(2)}) collective-permute-start(f32[1,1024]{1,0:T(1,128)S(1)} %slice.4), channel_id=1, source_target_pairs={{1,0},{3,2},{5,4},{7,6},{9,8},{11,10},{13,12},{15,14},{17,16},{19,... | collective-permute-start | bytes 12296 | tf_op jit(solution)/shard_map/ppermute | solution.py:31
  63.2 1.8 %collective-permute-done.1.refs_1_ = bf16[528,1024]{1,0:T(8,128)(2,1)} collective-permute-done((bf16[528,1024]{1,0:T(8,128)(2,1)}, bf16[528,1024]{1,0:T(8,128)(2,1)}, u32[]{:S(2)}, u32[]{:S(2)}) %collective-permute-start.1) | collective-permute-done | bytes 1081376 | tf_op jit(solution)/shard_map/ppermute | solution.py:31
  65.0 0.0 collective-permute-done.5.refs_4_
  65.0 0.9 cross_d.1.so_far_ref
  65.9 12.2 %collective-permute-done.8.from_partner_ref = f32[1,1024]{1,0:T(1,128)S(1)} collective-permute-done((f32[1,1024]{1,0:T(1,128)S(1)}, f32[1,1024]{1,0:T(1,128)S(1)}, u32[]{:S(2)}, u32[]{:S(2)}) %collective-permute-start.8) | collective-permute-done | bytes 4128 | tf_op jit(solution)/shard_map/ppermute | solution.py:31
  78.1 0.5 results.1
  78.6 1.9 %collective-permute-start.10 = (f32[1,1024]{1,0:T(1,128)S(1)}, f32[1,1024]{1,0:T(1,128)S(1)}, u32[]{:S(2)}, u32[]{:S(2)}) collective-permute-start(f32[1,1024]{1,0:T(1,128)S(1)} %get-tuple-element.11), channel_id=1, source_target_pairs={{32,34},{33,35},{34,36},{35,37},{36,38},{37,39},{38,40},{39,41},{4... | collective-permute-start | bytes 12296 | tf_op jit(solution)/shard_map/ppermute | solution.py:31
  80.6 1.3 %collective-permute-start.9 = (f32[1,1024]{1,0:T(1,128)S(1)}, f32[1,1024]{1,0:T(1,128)S(1)}, u32[]{:S(2)}, u32[]{:S(2)}) collective-permute-start(f32[1,1024]{1,0:T(1,128)S(1)} %get-tuple-element.10), channel_id=1, source_target_pairs={{1,2},{3,4},{5,6},{7,8},{9,10},{11,12},{13,14},{15,16},{17,18},{19... | collective-permute-start | bytes 12296 | tf_op jit(solution)/shard_map/ppermute | solution.py:31
  81.9 4.4 %collective-permute-done.10 = f32[1,1024]{1,0:T(1,128)S(1)} collective-permute-done((f32[1,1024]{1,0:T(1,128)S(1)}, f32[1,1024]{1,0:T(1,128)S(1)}, u32[]{:S(2)}, u32[]{:S(2)}) %collective-permute-start.10) | collective-permute-done | bytes 4128 | tf_op jit(solution)/shard_map/ppermute | solution.py:31
  86.3 8.3 %collective-permute-done.9 = f32[1,1024]{1,0:T(1,128)S(1)} collective-permute-done((f32[1,1024]{1,0:T(1,128)S(1)}, f32[1,1024]{1,0:T(1,128)S(1)}, u32[]{:S(2)}, u32[]{:S(2)}) %collective-permute-start.9) | collective-permute-done | bytes 4128 | tf_op jit(solution)/shard_map/ppermute | solution.py:31
  94.7 0.6 fusion.1
  (3 shorter events, 0.0 us)
Async XLA Ops:
  0.6 1.0 %copy-start.1 = (bf16[256,1024]{1,0:T(8,128)(2,1)S(1)}, bf16[256,1024]{1,0:T(8,128)(2,1)}, u32[]{:S(2)}) copy-start(bf16[256,1024]{1,0:T(8,128)(2,1)} %rows_ref.1) | copy-start | bytes 1572868
  1.7 0.7 copy-start.3
  2.4 0.7 copy-start.4
  4.8 10.8 %copy-start = (bf16[1,1024,1024]{2,1,0:T(8,128)(2,1)S(1)}, bf16[1,1024,1024]{2,1,0:T(8,128)(2,1)}, u32[]{:S(2)}) copy-start(bf16[1,1024,1024]{2,1,0:T(8,128)(2,1)} %param.6) | copy-start | bytes 6291460
  4.8 10.8 %copy-start.2 = (s32[1,1024]{1,0:T(1,128)S(1)}, s32[1,1024]{1,0:T(1,128)}, u32[]{:S(2)}) copy-start(s32[1,1024]{1,0:T(1,128)} %ids_ref.3) | copy-start | bytes 12292
  4.8 48.9 %all-to-all-start = ((bf16[128,4,1152]{2,1,0:T(4,128)(2,1)}), bf16[128,4,1152]{2,1,0:T(4,128)(2,1)S(1)}, u32[]{:S(2)}, u32[]{:S(2)}) async-start(bf16[128,4,1152]{2,1,0:T(4,128)(2,1)} %place.1), calls=%async_computation | async-start | bytes 2359296 | tf_op jit(solution)/shard_map/all_to_all | solution.py:297
  16.9 13.0 %copy-start.5 = (f32[1,1024]{1,0:T(1,128)S(1)}, f32[1,1024]{1,0:T(1,128)}, u32[]{:S(2)}) copy-start(f32[1,1024]{1,0:T(1,128)} %prior_ref.1) | copy-start | bytes 12292
  16.9 22.9 %collective-permute-start.4 = (bf16[528,1024]{1,0:T(8,128)(2,1)}, bf16[528,1024]{1,0:T(8,128)(2,1)}, u32[]{:S(2)}, u32[]{:S(2)}) collective-permute-start(bf16[528,1024]{1,0:T(8,128)(2,1)} %norm_0.1.own0.refs_0_), channel_id=1, source_target_pairs={{0,1},{2,3},{4,5},{6,7},{8,9},{10,11},{12,13},{14,15},{16,17},{18,... | collective-permute-start | bytes 3244040 | tf_op jit(solution)/shard_map/ppermute | solution.py:31
  21.3 21.8 %collective-permute-start = (bf16[528,1024]{1,0:T(8,128)(2,1)}, bf16[528,1024]{1,0:T(8,128)(2,1)}, u32[]{:S(2)}, u32[]{:S(2)}) collective-permute-start(bf16[528,1024]{1,0:T(8,128)(2,1)} %norm_1.1.own1.refs_1_.refs_2_), channel_id=1, source_target_pairs={{0,2},{1,3},{2,4},{3,5},{4,6},{5,7},{6,8},{7,9},{8,10},{9,11},{10,... | collective-permute-start | bytes 3244040 | tf_op jit(solution)/shard_map/ppermute | solution.py:31
  26.7 32.9 %collective-permute-start.3 = (bf16[528,1024]{1,0:T(8,128)(2,1)}, bf16[528,1024]{1,0:T(8,128)(2,1)S(1)}, u32[]{:S(2)}, u32[]{:S(2)}) collective-permute-start(bf16[528,1024]{1,0:T(8,128)(2,1)} %norm_1.1.own1.refs_1_.refs_2_), channel_id=1, source_target_pairs={{0,1},{2,3},{4,5},{6,7},{8,9},{10,11},{12,13},{14,15},{16,17},{18,... | collective-permute-start | bytes 3244040 | tf_op jit(solution)/shard_map/ppermute | solution.py:31
  28.1 32.3 %collective-permute-start.2 = (bf16[528,1024]{1,0:T(8,128)(2,1)}, bf16[528,1024]{1,0:T(8,128)(2,1)}, u32[]{:S(2)}, u32[]{:S(2)}) collective-permute-start(bf16[528,1024]{1,0:T(8,128)(2,1)} %norm_0.1.own0.refs_0_), channel_id=1, source_target_pairs={{1,3},{3,5},{5,7},{7,9},{9,11},{11,13},{13,15},{15,17},{17,19},{19... | collective-permute-start | bytes 3244040 | tf_op jit(solution)/shard_map/ppermute | solution.py:31
  39.7 21.3 %collective-permute-start.6 = (bf16[528,1024]{1,0:T(8,128)(2,1)}, bf16[528,1024]{1,0:T(8,128)(2,1)}, u32[]{:S(2)}, u32[]{:S(2)}) collective-permute-start(bf16[528,1024]{1,0:T(8,128)(2,1)} %tie.2.refs_2_.refs_4_.refs_3_), channel_id=1, source_target_pairs={{1,3},{3,5},{5,7},{7,9},{9,11},{11,13},{13,15},{15,17},{17,19},{19... | collective-permute-start | bytes 3244040 | tf_op jit(solution)/shard_map/ppermute | solution.py:31
  41.5 19.6 %collective-permute-start.7 = (bf16[528,1024]{1,0:T(8,128)(2,1)}, bf16[528,1024]{1,0:T(8,128)(2,1)}, u32[]{:S(2)}, u32[]{:S(2)}) collective-permute-start(bf16[528,1024]{1,0:T(8,128)(2,1)} %tie.2.refs_2_.refs_4_.refs_3_), channel_id=1, source_target_pairs={{1,31},{3,1},{5,3},{7,5},{9,7},{11,9},{13,11},{15,13},{17,15},{19,... | collective-permute-start | bytes 3244040 | tf_op jit(solution)/shard_map/ppermute | solution.py:31
  43.1 21.9 %collective-permute-start.1 = (bf16[528,1024]{1,0:T(8,128)(2,1)}, bf16[528,1024]{1,0:T(8,128)(2,1)}, u32[]{:S(2)}, u32[]{:S(2)}) collective-permute-start(bf16[528,1024]{1,0:T(8,128)(2,1)} %collective-permute-done.refs_3_.refs_5_.refs_7_), channel_id=1, source_target_pairs={{0,1},{2,3},{4,5},{6,7},{8,9},{10,11},{12,13},{14,15},{16,17},{18,... | collective-permute-start | bytes 3244040 | tf_op jit(solution)/shard_map/ppermute | solution.py:31
  54.8 0.7 copy-start.6
  59.7 5.4 %collective-permute-start.5 = (bf16[528,1024]{1,0:T(8,128)(2,1)S(1)}, bf16[528,1024]{1,0:T(8,128)(2,1)S(1)}, u32[]{:S(2)}, u32[]{:S(2)}) collective-permute-start(bf16[528,1024]{1,0:T(8,128)(2,1)S(1)} %tie.3.refs_2_.refs_4_), channel_id=1, source_target_pairs={{1,31},{3,1},{5,3},{7,5},{9,7},{11,9},{13,11},{15,13},{17,15},{19,... | collective-permute-start | bytes 3244040 | tf_op jit(solution)/shard_map/ppermute | solution.py:31
  61.9 16.1 %collective-permute-start.8 = (f32[1,1024]{1,0:T(1,128)S(1)}, f32[1,1024]{1,0:T(1,128)S(1)}, u32[]{:S(2)}, u32[]{:S(2)}) collective-permute-start(f32[1,1024]{1,0:T(1,128)S(1)} %slice.4), channel_id=1, source_target_pairs={{1,0},{3,2},{5,4},{7,6},{9,8},{11,10},{13,12},{15,14},{17,16},{19,... | collective-permute-start | bytes 12296 | tf_op jit(solution)/shard_map/ppermute | solution.py:31
  78.6 7.7 %collective-permute-start.10 = (f32[1,1024]{1,0:T(1,128)S(1)}, f32[1,1024]{1,0:T(1,128)S(1)}, u32[]{:S(2)}, u32[]{:S(2)}) collective-permute-start(f32[1,1024]{1,0:T(1,128)S(1)} %get-tuple-element.11), channel_id=1, source_target_pairs={{32,34},{33,35},{34,36},{35,37},{36,38},{37,39},{38,40},{39,41},{4... | collective-permute-start | bytes 12296 | tf_op jit(solution)/shard_map/ppermute | solution.py:31
  80.6 14.1 %collective-permute-start.9 = (f32[1,1024]{1,0:T(1,128)S(1)}, f32[1,1024]{1,0:T(1,128)S(1)}, u32[]{:S(2)}, u32[]{:S(2)}) collective-permute-start(f32[1,1024]{1,0:T(1,128)S(1)} %get-tuple-element.10), channel_id=1, source_target_pairs={{1,2},{3,4},{5,6},{7,8},{9,10},{11,12},{13,14},{15,16},{17,18},{19... | collective-permute-start | bytes 12296 | tf_op jit(solution)/shard_map/ppermute | solution.py:31

commit v6 on v5

--- a/solution.py
+++ b/solution.py
@@ -8,7 +8,7 @@
 CAP = 4
 LOWEST = -2.0
 EXTRA = 16
-TIES = True
+AHEAD = 1
 BOTH = ("grp", "blk")
 OWN, PARTNER, NEAR, NEAR_PARTNER, FAR_PARTNER = range(5)
 
@@ -82,7 +82,7 @@
                 acc_ref[at_row : at_row + 1, at] = jnp.maximum(acc_ref[at_row : at_row + 1, at], found)
 
 
-def compare(where_ref, heavy, acc_ref, names, refs, buffers, sems, pairs):
+def compare(where_ref, heavy, acc_ref, held, names, refs, buffers, sems, pairs):
     needed = [name for name in names if any(name == n for p in pairs for side in p for _, n in side[1])]
 
     def run(core):
@@ -90,12 +90,16 @@
             name: pltpu.make_async_copy(refs[names.index(name)], buffers.at[k], sems.at[k])
             for k, name in enumerate(needed)
         }
-        for copy in copies.values():
-            copy.start()
-        there = set()
+        started, there = set(), set()
 
         def arrive(name):
+            if name in held:
+                return held[name]
             if name not in there:
+                for k, other in enumerate(needed):
+                    if other not in started and k <= needed.index(name) + AHEAD:
+                        copies[other].start()
+                        started.add(other)
                 copies[name].wait()
                 there.add(name)
             return buffers.at[needed.index(name)]
@@ -198,7 +202,7 @@
         ],
         compiler_params=params(),
         name="split",
-        cost_estimate=pl.CostEstimate(flops=20 * 10**9, bytes_accessed=4 * slots * width, transcendentals=0),
+        cost_estimate=pl.CostEstimate(flops=0, bytes_accessed=4 * slots * width, transcendentals=0),
     )(arrived)
 
 
@@ -209,23 +213,25 @@
     update(acc_ref, OWN, own, own, lambda half: (own0, own1)[half])
 
 
-def stage(name, arrays, heavy_pairs, light_pairs, where, found, after=()):
+def stage(name, own, arrays, heavy_pairs, light_pairs, where, found, after=()):
     names = list(arrays)
     size, width = arrays[names[0]].shape
     rows = found.shape[1]
 
     def run(*refs):
+        held, refs = {"own0": refs[0], "own1": refs[1]}, refs[2:]
         inputs, where_ref, so_far_ref = refs[: len(names)], refs[len(names)], refs[len(names) + 1]
         acc_ref, buffers, sems = refs[-3:]
         acc_ref[...] = so_far_ref[...]
-        compare(where_ref, 1, acc_ref, names, inputs, buffers, sems, heavy_pairs)
+        compare(where_ref, 1, acc_ref, held, names, inputs, buffers, sems, heavy_pairs)
         if light_pairs:
-            compare(where_ref, 0, acc_ref, names, inputs, buffers, sems, light_pairs)
+            compare(where_ref, 0, acc_ref, held, names, inputs, buffers, sems, light_pairs)
 
     products = sum(len(a[1]) * len(b[1]) for a, b in heavy_pairs) / 4
     return pl.pallas_call(
         run,
-        in_specs=[pl.BlockSpec(memory_space=pltpu.HBM)] * len(names)
+        in_specs=vmem(2)
+        + [pl.BlockSpec(memory_space=pl.ANY)] * len(names)
         + smem()
         + vmem(1)
         + vmem(len(after)),
@@ -239,7 +245,7 @@
             bytes_accessed=2 * len(names) * size * width,
             transcendentals=0,
         ),
-    )(*arrays.values(), where, found, *after)
+    )(*own, *arrays.values(), where, found, *after)
 
 
 def tie_kernel(array_ref, after_ref, out_ref):
@@ -249,8 +255,8 @@
 def tie(array, after):
     return pl.pallas_call(
         tie_kernel,
-        in_specs=[pl.BlockSpec(memory_space=pltpu.HBM)] + vmem(1),
-        out_specs=pl.BlockSpec(memory_space=pltpu.HBM),
+        in_specs=[pl.BlockSpec(memory_space=pl.ANY)] + vmem(1),
+        out_specs=pl.BlockSpec(memory_space=pl.ANY),
         out_shape=jax.ShapeDtypeStruct(array.shape, array.dtype),
         input_output_aliases={0: 0},
         compiler_params=params(),
@@ -314,16 +320,17 @@
             flops=2 * rows * rows * width, bytes_accessed=2 * rows * width, transcendentals=0
         ),
     )(own0, own1, prior_max)
-    if TIES:
-        partner0 = tie(partner0, found)
     far0 = send(partner0, heavy_back)
     near_partner0 = send(partner0, heavy_ahead)
     near_partner1 = send(near1, to_heavy)
 
     own = (OWN, [(0, "own0"), (1, "own1")])
+    partner_both = (PARTNER, [(0, "partner0"), (1, "partner1")])
+    near_both = (NEAR, [(0, "near0"), (1, "near1")])
     found = stage(
         "cross_a",
-        {"own0": own0, "own1": own1, "partner0": partner0, "near1": near1},
+        (own0, own1),
+        {"partner0": partner0, "near1": near1},
         [
             (own, (PARTNER, [(0, "partner0")])),
             (own, (NEAR, [(1, "near1")])),
@@ -332,57 +339,39 @@
         [(own, (NEAR_PARTNER, [(1, "near1")]))],
         where,
         found,
-        (next_ids,),
     )
-    if TIES:
-        partner1 = tie(partner1, found)
+    partner1 = tie(partner1, found)
     far1 = send(partner1, heavy_back)
     found = stage(
         "cross_b",
-        {"own0": own0, "own1": own1, "partner1": partner1, "near0": near0, "partner0": partner0, "near1": near1},
+        (own0, own1),
+        {
+            "partner1": partner1,
+            "near0": near0,
+            "near_partner0": near_partner0,
+            "partner0": partner0,
+            "near1": near1,
+            "far0": far0,
+        },
         [
             (own, (PARTNER, [(1, "partner1")])),
             (own, (NEAR, [(0, "near0")])),
-            ((PARTNER, [(0, "partner0"), (1, "partner1")]), (NEAR, [(0, "near0")])),
+            (own, (NEAR_PARTNER, [(0, "near_partner0")])),
+            (partner_both, (NEAR_PARTNER, [(0, "near_partner0")])),
+            (partner_both, (NEAR, [(0, "near0")])),
             ((PARTNER, [(1, "partner1")]), (NEAR, [(1, "near1")])),
-        ],
-        [],
-        where,
-        found,
-    )
-    near_both = (NEAR, [(0, "near0"), (1, "near1")])
-    found = stage(
-        "cross_c",
-        {
-            "own0": own0,
-            "near_partner0": near_partner0,
-            "own1": own1,
-            "partner0": partner0,
-            "partner1": partner1,
-            "near0": near0,
-            "far0": far0,
-            "near1": near1,
-        },
-        [
-            (own, (NEAR_PARTNER, [(0, "near_partner0")])),
-            ((PARTNER, [(0, "partner0"), (1, "partner1")]), (NEAR_PARTNER, [(0, "near_partner0")])),
             ((FAR_PARTNER, [(0, "far0")]), near_both),
         ],
         [],
         where,
         found,
+        (next_ids,),
     )
     from_partner = send(found[PARTNER : PARTNER + 1], to_light)
     found = stage(
-        "cross_d",
-        {
-            "own0": own0,
-            "near_partner1": near_partner1,
-            "own1": own1,
-            "near0": near0,
-            "far1": far1,
-            "near1": near1,
-        },
+        "cross_c",
+        (own0, own1),
+        {"near_partner1": near_partner1, "far1": far1, "near0": near0, "near1": near1},
         [
             (own, (NEAR_PARTNER, [(1, "near_partner1")])),
             ((FAR_PARTNER, [(1, "far1")]), near_both),
@@ -390,6 +379,7 @@
         [],
         where,
         found,
+        (),
     )
     mine, for_far, for_side = pl.pallas_call(
         results_kernel,

time: 95.8 us -> 94.8 us (0.990)
  the two profiles are of different devices: /device:TPU:9 before, /device:TPU:0 now
where the time goes in v6:
time: 94.8 us; the launch traced here: 94.2 us
  starting transfers between devices  41 us (43%)
  waiting for transfers between devices  37.6 us (40%)
  Pallas kernels  11.2 us (12%)
  local copies, waits for them, and re-layouts  2.98 us (3%)
    ppermute x11, waiting for transfers between devices, send(): return lax.ppermute(value, BOTH, pairs)  37.6 us
    ppermute x11, starting transfers between devices, send(): return lax.ppermute(value, BOTH, pairs)  30.5 us
    all_to_all x1, starting transfers between devices, body(): lax.all_to_all(outgoing, BOTH, split_axis=0, concat_axis=0, tiled=True)  10.5 us
    pallas_call x3, Pallas kernels, stage(): pl.pallas_call(run, in_specs=vmem(2) + [pl.BlockSpec(memory_space=pl.ANY)...  4.72 us
    unnamed x14, local copies, waits for them, and re-layouts  2.97 us
    pallas_call x1, Pallas kernels, body(): pl.pallas_call(within_kernel, in_specs=vmem(3), out_specs=pl.BlockSpec(me...  2.38 us
  transfers between devices with their start and end apart: 12, of which 4 were waited for; matrix products, arithmetic and copies ran while one was open for 0% of the time, Pallas kernels for 11%

profile of v6, /device:TPU:0, one launch (start us, length us, event | category | flops | bytes accessed | tf_op | source)
XLA Modules:
  0.0 94.2 jit_solution(6036477272472802708)
XLA Ops:
  0.6 0.0 copy-start
  0.6 1.6 %copy-done = bf16[1,1024,1024]{2,1,0:T(8,128)(2,1)S(1)} copy-done((bf16[1,1024,1024]{2,1,0:T(8,128)(2,1)S(1)}, bf16[1,1024,1024]{2,1,0:T(8,128)(2,1)}, u32[]{:S(2)}) %copy-start) | copy-done | bytes 2097176
  2.2 0.0 copy-start.2
  2.2 0.7 copy-done.2
  2.9 0.3 norm_0.1.own0.refs_0_
  3.2 0.0 copy-start.1
  3.3 0.0 copy-start.3
  3.3 0.0 copy-start.4
  3.3 4.7 %collective-permute-start.3 = (bf16[528,1024]{1,0:T(8,128)(2,1)S(1)}, bf16[528,1024]{1,0:T(8,128)(2,1)}, u32[]{:S(2)}, u32[]{:S(2)}) collective-permute-start(bf16[528,1024]{1,0:T(8,128)(2,1)S(1)} %norm_0.1.own0.refs_0_), channel_id=1, source_target_pairs={{0,1},{2,3},{4,5},{6,7},{8,9},{10,11},{12,13},{14,15},{16,17},{18,... | collective-permute-start | bytes 3244040 | tf_op jit(solution)/shard_map/ppermute | solution.py:31
  8.0 0.3 norm_1.1.own1.refs_1_
  8.3 1.6 %collective-permute-start = (bf16[528,1024]{1,0:T(8,128)(2,1)S(1)}, bf16[528,1024]{1,0:T(8,128)(2,1)}, u32[]{:S(2)}, u32[]{:S(2)}) collective-permute-start(bf16[528,1024]{1,0:T(8,128)(2,1)S(1)} %norm_1.1.own1.refs_1_), channel_id=1, source_target_pairs={{0,2},{1,3},{2,4},{3,5},{4,6},{5,7},{6,8},{7,9},{8,10},{9,11},{10,... | collective-permute-start | bytes 3244040 | tf_op jit(solution)/shard_map/ppermute | solution.py:31
  9.9 2.3 %collective-permute-start.2 = (bf16[528,1024]{1,0:T(8,128)(2,1)S(1)}, bf16[528,1024]{1,0:T(8,128)(2,1)}, u32[]{:S(2)}, u32[]{:S(2)}) collective-permute-start(bf16[528,1024]{1,0:T(8,128)(2,1)S(1)} %norm_1.1.own1.refs_1_), channel_id=1, source_target_pairs={{0,1},{2,3},{4,5},{6,7},{8,9},{10,11},{12,13},{14,15},{16,17},{18,... | collective-permute-start | bytes 3244040 | tf_op jit(solution)/shard_map/ppermute | solution.py:31
  12.1 0.0 copy-done.1
  12.1 0.0 copy-done.3
  12.1 0.0 copy-done.4
  12.1 1.8 %place.1 = bf16[128,4,1152]{2,1,0:T(4,128)(2,1)} custom-call(bf16[256,1024]{1,0:T(8,128)(2,1)S(1)} %copy-done.1, s32[1,256]{1,0:T(1,128)S(1)} %bitcast.8, s32[1,256]{1,0:T(1,128)S(1)} %bitcast.9), custom_call_target="tpu_custom_call" | custom-call | flops 268435456 | bytes 1572864 | tf_op jit(solution)/shard_map/place/pallas_call | solution.py:171
  13.9 0.0 copy-start.5
  13.9 10.5 %all-to-all-start = ((bf16[128,4,1152]{2,1,0:T(4,128)(2,1)}), bf16[128,4,1152]{2,1,0:T(4,128)(2,1)S(1)}, u32[]{:S(2)}, u32[]{:S(2)}) async-start(bf16[128,4,1152]{2,1,0:T(4,128)(2,1)} %place.1), calls=%async_computation | async-start | bytes 2359296 | tf_op jit(solution)/shard_map/all_to_all | solution.py:303
  24.4 1.7 %collective-permute-start.5 = (bf16[528,1024]{1,0:T(8,128)(2,1)S(1)}, bf16[528,1024]{1,0:T(8,128)(2,1)}, u32[]{:S(2)}, u32[]{:S(2)}) collective-permute-start(bf16[528,1024]{1,0:T(8,128)(2,1)S(1)} %norm_0.1.own0.refs_0_), channel_id=1, source_target_pairs={{1,3},{3,5},{5,7},{7,9},{9,11},{11,13},{13,15},{15,17},{17,19},{19... | collective-permute-start | bytes 3244040 | tf_op jit(solution)/shard_map/ppermute | solution.py:31
  26.0 0.0 collective-permute-done.3.refs_2_.refs_5_
  26.1 1.6 %collective-permute-start.6 = (bf16[528,1024]{1,0:T(8,128)(2,1)}, bf16[528,1024]{1,0:T(8,128)(2,1)}, u32[]{:S(2)}, u32[]{:S(2)}) collective-permute-start(bf16[528,1024]{1,0:T(8,128)(2,1)} %collective-permute-done.3.refs_2_.refs_5_), channel_id=1, source_target_pairs={{1,3},{3,5},{5,7},{7,9},{9,11},{11,13},{13,15},{15,17},{17,19},{19... | collective-permute-start | bytes 3244040 | tf_op jit(solution)/shard_map/ppermute | solution.py:31
  27.7 1.7 %collective-permute-start.7 = (bf16[528,1024]{1,0:T(8,128)(2,1)}, bf16[528,1024]{1,0:T(8,128)(2,1)}, u32[]{:S(2)}, u32[]{:S(2)}) collective-permute-start(bf16[528,1024]{1,0:T(8,128)(2,1)} %collective-permute-done.3.refs_2_.refs_5_), channel_id=1, source_target_pairs={{1,31},{3,1},{5,3},{7,5},{9,7},{11,9},{13,11},{15,13},{17,15},{19,... | collective-permute-start | bytes 3244040 | tf_op jit(solution)/shard_map/ppermute | solution.py:31
  29.4 0.1 pad_add_fusion.refs_4_.refs_8_.refs_6_.where_ref
  29.5 0.0 copy-done.5
  29.5 2.4 %within.1.refs_5_ = f32[8,1024]{1,0:T(8,128)S(1)} custom-call(bf16[528,1024]{1,0:T(8,128)(2,1)S(1)} %norm_0.1.own0.refs_0_, bf16[528,1024]{1,0:T(8,128)(2,1)S(1)} %norm_1.1.own1.refs_1_, f32[1,1024]{1,0:T(1,128)S(1)} %copy-done.5), custom_call_target="tpu_custom_call" | custom-call | flops 2147483648 | bytes 2097152 | tf_op jit(solution)/shard_map/within/pallas_call | solution.py:312
  31.9 0.0 collective-permute-done.refs_3_.refs_6_.refs_5_
  31.9 3.3 %cross_a.1.after_ref.refs_9_ = f32[8,1024]{1,0:T(8,128)S(1)} custom-call(bf16[528,1024]{1,0:T(8,128)(2,1)S(1)} %norm_0.1.own0.refs_0_, bf16[528,1024]{1,0:T(8,128)(2,1)S(1)} %norm_1.1.own1.refs_1_, bf16[528,1024]{1,0:T(8,128)(2,1)} %collective-permute-done.3.refs_2_.refs_5_, bf16[528,1024]{1,0:T(8,128)(2,1)} %collective-permute-done.refs_3_.refs_6_.refs_5_, ...), custom_call_target="tpu_custom_call" | custom-call | flops 2684354560 | bytes 2162688 | tf_op jit(solution)/shard_map/cross_a/pallas_call | solution.py:231
  35.2 7.1 %collective-permute-done.2.array_ref = bf16[528,1024]{1,0:T(8,128)(2,1)} collective-permute-done((bf16[528,1024]{1,0:T(8,128)(2,1)S(1)}, bf16[528,1024]{1,0:T(8,128)(2,1)}, u32[]{:S(2)}, u32[]{:S(2)}) %collective-permute-start.2) | collective-permute-done | bytes 1081376 | tf_op jit(solution)/shard_map/ppermute | solution.py:31
  42.3 1.7 %collective-permute-start.4 = (bf16[528,1024]{1,0:T(8,128)(2,1)}, bf16[528,1024]{1,0:T(8,128)(2,1)}, u32[]{:S(2)}, u32[]{:S(2)}) collective-permute-start(bf16[528,1024]{1,0:T(8,128)(2,1)} %tie.1.refs_2_), channel_id=1, source_target_pairs={{1,31},{3,1},{5,3},{7,5},{9,7},{11,9},{13,11},{15,13},{17,15},{19,... | collective-permute-start | bytes 3244040 | tf_op jit(solution)/shard_map/ppermute | solution.py:31
  44.0 12.0 %collective-permute-start.1 = (bf16[528,1024]{1,0:T(8,128)(2,1)}, bf16[528,1024]{1,0:T(8,128)(2,1)}, u32[]{:S(2)}, u32[]{:S(2)}) collective-permute-start(bf16[528,1024]{1,0:T(8,128)(2,1)} %collective-permute-done.refs_3_.refs_6_.refs_5_), channel_id=1, source_target_pairs={{0,1},{2,3},{4,5},{6,7},{8,9},{10,11},{12,13},{14,15},{16,17},{18,... | collective-permute-start | bytes 3244040 | tf_op jit(solution)/shard_map/ppermute | solution.py:31
  56.0 0.0 all-to-all-done.in_ref
  56.0 1.1 %split.1 = (bf16[512,1024]{1,0:T(8,128)(2,1)}, s32[1,512]{1,0:T(1,128)}) custom-call(bf16[128,4,1152]{2,1,0:T(4,128)(2,1)S(1)} %all-to-all-done.in_ref), custom_call_target="tpu_custom_call" | custom-call | bytes 2097152 | tf_op jit(solution)/shard_map/split/pallas_call | solution.py:195
  57.1 0.0 collective-permute-done.5.refs_3_.refs_4_
  57.1 0.0 collective-permute-done.6.refs_4_
  57.1 0.0 collective-permute-done.7.refs_7_
  57.1 0.0 copy-start.6
  57.1 0.7 copy-done.6
  57.8 0.8 cross_b.1.refs_7_
  58.6 1.3 %collective-permute-start.8 = (f32[1,1024]{1,0:T(1,128)S(1)}, f32[1,1024]{1,0:T(1,128)S(1)}, u32[]{:S(2)}, u32[]{:S(2)}) collective-permute-start(f32[1,1024]{1,0:T(1,128)S(1)} %slice.4), channel_id=1, source_target_pairs={{1,0},{3,2},{5,4},{7,6},{9,8},{11,10},{13,12},{15,14},{17,16},{19,... | collective-permute-start | bytes 12296 | tf_op jit(solution)/shard_map/ppermute | solution.py:31
  59.9 0.0 collective-permute-done.4.refs_3_
  59.9 7.9 %collective-permute-done.1.refs_2_ = bf16[528,1024]{1,0:T(8,128)(2,1)} collective-permute-done((bf16[528,1024]{1,0:T(8,128)(2,1)}, bf16[528,1024]{1,0:T(8,128)(2,1)}, u32[]{:S(2)}, u32[]{:S(2)}) %collective-permute-start.1) | collective-permute-done | bytes 1081376 | tf_op jit(solution)/shard_map/ppermute | solution.py:31
  67.9 0.6 cross_c.1.so_far_ref
  68.5 14.2 %collective-permute-done.8.from_partner_ref = f32[1,1024]{1,0:T(1,128)S(1)} collective-permute-done((f32[1,1024]{1,0:T(1,128)S(1)}, f32[1,1024]{1,0:T(1,128)S(1)}, u32[]{:S(2)}, u32[]{:S(2)}) %collective-permute-start.8) | collective-permute-done | bytes 4128 | tf_op jit(solution)/shard_map/ppermute | solution.py:31
  82.7 0.5 results.1
  83.2 0.7 collective-permute-start.10
  83.9 1.3 %collective-permute-start.9 = (f32[1,1024]{1,0:T(1,128)S(1)}, f32[1,1024]{1,0:T(1,128)S(1)}, u32[]{:S(2)}, u32[]{:S(2)}) collective-permute-start(f32[1,1024]{1,0:T(1,128)S(1)} %get-tuple-element.10), channel_id=1, source_target_pairs={{1,2},{3,4},{5,6},{7,8},{9,10},{11,12},{13,14},{15,16},{17,18},{19... | collective-permute-start | bytes 12296 | tf_op jit(solution)/shard_map/ppermute | solution.py:31
  85.2 0.0 collective-permute-done.10
  85.2 8.4 %collective-permute-done.9 = f32[1,1024]{1,0:T(1,128)S(1)} collective-permute-done((f32[1,1024]{1,0:T(1,128)S(1)}, f32[1,1024]{1,0:T(1,128)S(1)}, u32[]{:S(2)}, u32[]{:S(2)}) %collective-permute-start.9) | collective-permute-done | bytes 4128 | tf_op jit(solution)/shard_map/ppermute | solution.py:31
  93.6 0.6 fusion.1
  (2 shorter events, 0.0 us)
Async XLA Ops:
  0.6 1.6 %copy-start = (bf16[1,1024,1024]{2,1,0:T(8,128)(2,1)S(1)}, bf16[1,1024,1024]{2,1,0:T(8,128)(2,1)}, u32[]{:S(2)}) copy-start(bf16[1,1024,1024]{2,1,0:T(8,128)(2,1)} %param.6) | copy-start | bytes 6291460
  2.2 0.7 copy-start.2
  3.2 8.9 %copy-start.1 = (bf16[256,1024]{1,0:T(8,128)(2,1)S(1)}, bf16[256,1024]{1,0:T(8,128)(2,1)}, u32[]{:S(2)}) copy-start(bf16[256,1024]{1,0:T(8,128)(2,1)} %rows_ref.1) | copy-start | bytes 1572868
  3.3 8.9 %copy-start.3 = (s32[256,1]{0,1:T(1,128)S(1)}, s32[256,1]{0,1:T(1,128)}, u32[]{:S(2)}) copy-start(s32[256,1]{0,1:T(1,128)} %param.11) | copy-start | bytes 3076
  3.3 8.9 %copy-start.4 = (s32[256]{0:T(256)S(1)}, s32[256]{0:T(256)}, u32[]{:S(2)}) copy-start(s32[256]{0:T(256)} %param.10) | copy-start | bytes 3076
  3.3 22.8 %collective-permute-start.3 = (bf16[528,1024]{1,0:T(8,128)(2,1)S(1)}, bf16[528,1024]{1,0:T(8,128)(2,1)}, u32[]{:S(2)}, u32[]{:S(2)}) collective-permute-start(bf16[528,1024]{1,0:T(8,128)(2,1)S(1)} %norm_0.1.own0.refs_0_), channel_id=1, source_target_pairs={{0,1},{2,3},{4,5},{6,7},{8,9},{10,11},{12,13},{14,15},{16,17},{18,... | collective-permute-start | bytes 3244040 | tf_op jit(solution)/shard_map/ppermute | solution.py:31
  8.3 23.6 %collective-permute-start = (bf16[528,1024]{1,0:T(8,128)(2,1)S(1)}, bf16[528,1024]{1,0:T(8,128)(2,1)}, u32[]{:S(2)}, u32[]{:S(2)}) collective-permute-start(bf16[528,1024]{1,0:T(8,128)(2,1)S(1)} %norm_1.1.own1.refs_1_), channel_id=1, source_target_pairs={{0,2},{1,3},{2,4},{3,5},{4,6},{5,7},{6,8},{7,9},{8,10},{9,11},{10,... | collective-permute-start | bytes 3244040 | tf_op jit(solution)/shard_map/ppermute | solution.py:31
  9.9 32.4 %collective-permute-start.2 = (bf16[528,1024]{1,0:T(8,128)(2,1)S(1)}, bf16[528,1024]{1,0:T(8,128)(2,1)}, u32[]{:S(2)}, u32[]{:S(2)}) collective-permute-start(bf16[528,1024]{1,0:T(8,128)(2,1)S(1)} %norm_1.1.own1.refs_1_), channel_id=1, source_target_pairs={{0,1},{2,3},{4,5},{6,7},{8,9},{10,11},{12,13},{14,15},{16,17},{18,... | collective-permute-start | bytes 3244040 | tf_op jit(solution)/shard_map/ppermute | solution.py:31
  13.9 15.6 %copy-start.5 = (f32[1,1024]{1,0:T(1,128)S(1)}, f32[1,1024]{1,0:T(1,128)}, u32[]{:S(2)}) copy-start(f32[1,1024]{1,0:T(1,128)} %prior_ref.1) | copy-start | bytes 12292
  13.9 42.0 %all-to-all-start = ((bf16[128,4,1152]{2,1,0:T(4,128)(2,1)}), bf16[128,4,1152]{2,1,0:T(4,128)(2,1)S(1)}, u32[]{:S(2)}, u32[]{:S(2)}) async-start(bf16[128,4,1152]{2,1,0:T(4,128)(2,1)} %place.1), calls=%async_computation | async-start | bytes 2359296 | tf_op jit(solution)/shard_map/all_to_all | solution.py:303
  24.4 32.7 %collective-permute-start.5 = (bf16[528,1024]{1,0:T(8,128)(2,1)S(1)}, bf16[528,1024]{1,0:T(8,128)(2,1)}, u32[]{:S(2)}, u32[]{:S(2)}) collective-permute-start(bf16[528,1024]{1,0:T(8,128)(2,1)S(1)} %norm_0.1.own0.refs_0_), channel_id=1, source_target_pairs={{1,3},{3,5},{5,7},{7,9},{9,11},{11,13},{13,15},{15,17},{17,19},{19... | collective-permute-start | bytes 3244040 | tf_op jit(solution)/shard_map/ppermute | solution.py:31
  26.1 31.0 %collective-permute-start.6 = (bf16[528,1024]{1,0:T(8,128)(2,1)}, bf16[528,1024]{1,0:T(8,128)(2,1)}, u32[]{:S(2)}, u32[]{:S(2)}) collective-permute-start(bf16[528,1024]{1,0:T(8,128)(2,1)} %collective-permute-done.3.refs_2_.refs_5_), channel_id=1, source_target_pairs={{1,3},{3,5},{5,7},{7,9},{9,11},{11,13},{13,15},{15,17},{17,19},{19... | collective-permute-start | bytes 3244040 | tf_op jit(solution)/shard_map/ppermute | solution.py:31
  27.7 29.4 %collective-permute-start.7 = (bf16[528,1024]{1,0:T(8,128)(2,1)}, bf16[528,1024]{1,0:T(8,128)(2,1)}, u32[]{:S(2)}, u32[]{:S(2)}) collective-permute-start(bf16[528,1024]{1,0:T(8,128)(2,1)} %collective-permute-done.3.refs_2_.refs_5_), channel_id=1, source_target_pairs={{1,31},{3,1},{5,3},{7,5},{9,7},{11,9},{13,11},{15,13},{17,15},{19,... | collective-permute-start | bytes 3244040 | tf_op jit(solution)/shard_map/ppermute | solution.py:31
  42.3 17.7 %collective-permute-start.4 = (bf16[528,1024]{1,0:T(8,128)(2,1)}, bf16[528,1024]{1,0:T(8,128)(2,1)}, u32[]{:S(2)}, u32[]{:S(2)}) collective-permute-start(bf16[528,1024]{1,0:T(8,128)(2,1)} %tie.1.refs_2_), channel_id=1, source_target_pairs={{1,31},{3,1},{5,3},{7,5},{9,7},{11,9},{13,11},{15,13},{17,15},{19,... | collective-permute-start | bytes 3244040 | tf_op jit(solution)/shard_map/ppermute | solution.py:31
  44.0 23.9 %collective-permute-start.1 = (bf16[528,1024]{1,0:T(8,128)(2,1)}, bf16[528,1024]{1,0:T(8,128)(2,1)}, u32[]{:S(2)}, u32[]{:S(2)}) collective-permute-start(bf16[528,1024]{1,0:T(8,128)(2,1)} %collective-permute-done.refs_3_.refs_6_.refs_5_), channel_id=1, source_target_pairs={{0,1},{2,3},{4,5},{6,7},{8,9},{10,11},{12,13},{14,15},{16,17},{18,... | collective-permute-start | bytes 3244040 | tf_op jit(solution)/shard_map/ppermute | solution.py:31
  57.1 0.7 copy-start.6
  58.6 24.0 %collective-permute-start.8 = (f32[1,1024]{1,0:T(1,128)S(1)}, f32[1,1024]{1,0:T(1,128)S(1)}, u32[]{:S(2)}, u32[]{:S(2)}) collective-permute-start(f32[1,1024]{1,0:T(1,128)S(1)} %slice.4), channel_id=1, source_target_pairs={{1,0},{3,2},{5,4},{7,6},{9,8},{11,10},{13,12},{15,14},{17,16},{19,... | collective-permute-start | bytes 12296 | tf_op jit(solution)/shard_map/ppermute | solution.py:31
  83.2 2.0 %collective-permute-start.10 = (f32[1,1024]{1,0:T(1,128)S(1)}, f32[1,1024]{1,0:T(1,128)S(1)}, u32[]{:S(2)}, u32[]{:S(2)}) collective-permute-start(f32[1,1024]{1,0:T(1,128)S(1)} %get-tuple-element.11), channel_id=1, source_target_pairs={{32,34},{33,35},{34,36},{35,37},{36,38},{37,39},{38,40},{39,41},{4... | collective-permute-start | bytes 12296 | tf_op jit(solution)/shard_map/ppermute | solution.py:31
  83.9 9.7 %collective-permute-start.9 = (f32[1,1024]{1,0:T(1,128)S(1)}, f32[1,1024]{1,0:T(1,128)S(1)}, u32[]{:S(2)}, u32[]{:S(2)}) collective-permute-start(f32[1,1024]{1,0:T(1,128)S(1)} %get-tuple-element.10), channel_id=1, source_target_pairs={{1,2},{3,4},{5,6},{7,8},{9,10},{11,12},{13,14},{15,16},{17,18},{19... | collective-permute-start | bytes 12296 | tf_op jit(solution)/shard_map/ppermute | solution.py:31

commit v7 on v6

--- a/solution.py
+++ b/solution.py
@@ -8,7 +8,7 @@
 CAP = 4
 LOWEST = -2.0
 EXTRA = 16
-AHEAD = 1
+AHEAD = 3
 BOTH = ("grp", "blk")
 OWN, PARTNER, NEAR, NEAR_PARTNER, FAR_PARTNER = range(5)
 
@@ -144,7 +144,8 @@
     )(embeds, ids)
 
 
-def place_kernel(rows_ref, target_ref, ids_ref, out_ref):
+def place_kernel(rows_ref, target_ref, ids_ref, after_ref, out_ref):
+    del after_ref
     count, width = rows_ref.shape
     target = target_ref[...]
     across = jnp.broadcast_to(target, (count, count))
@@ -166,11 +167,11 @@
     out_ref[:, :, width:] = tail.astype(jnp.bfloat16).reshape(devices, CAP, 128)
 
 
-def placed_rows(owned, target, ids, devices):
+def placed_rows(owned, target, ids, devices, after):
     count, width = owned.shape
     return pl.pallas_call(
         place_kernel,
-        in_specs=vmem(3),
+        in_specs=vmem(4),
         out_specs=pl.BlockSpec(memory_space=pltpu.VMEM),
         out_shape=jax.ShapeDtypeStruct((devices, CAP, width + 128), jnp.bfloat16),
         compiler_params=params(),
@@ -178,7 +179,7 @@
         cost_estimate=pl.CostEstimate(
             flops=2 * devices * CAP * count * width, bytes_accessed=2 * (count + devices * CAP) * width, transcendentals=count
         ),
-    )(owned, target, ids)
+    )(owned, target, ids, after)
 
 
 def split_kernel(in_ref, rows_ref, ids_ref):
@@ -213,7 +214,7 @@
     update(acc_ref, OWN, own, own, lambda half: (own0, own1)[half])
 
 
-def stage(name, own, arrays, heavy_pairs, light_pairs, where, found, after=()):
+def stage(name, own, arrays, heavy_pairs, light_pairs, where, found, after=(), last=False):
     names = list(arrays)
     size, width = arrays[names[0]].shape
     rows = found.shape[1]
@@ -221,11 +222,19 @@
     def run(*refs):
         held, refs = {"own0": refs[0], "own1": refs[1]}, refs[2:]
         inputs, where_ref, so_far_ref = refs[: len(names)], refs[len(names)], refs[len(names) + 1]
-        acc_ref, buffers, sems = refs[-3:]
+        outs, (buffers, sems) = refs[len(names) + 2 + len(after) : -2], refs[-2:]
+        acc_ref = outs[-1]
         acc_ref[...] = so_far_ref[...]
         compare(where_ref, 1, acc_ref, held, names, inputs, buffers, sems, heavy_pairs)
         if light_pairs:
             compare(where_ref, 0, acc_ref, held, names, inputs, buffers, sems, light_pairs)
+        if last:
+            own_out, far_out, side_out = outs[:3]
+            own_row, from_partner = acc_ref[OWN : OWN + 1, :], refs[len(names) + 2][...]
+            own_out[...] = jnp.where(where_ref[1] == 0, jnp.maximum(own_row, from_partner), own_row)
+            near_partner_row = acc_ref[NEAR_PARTNER : NEAR_PARTNER + 1, :]
+            far_out[...] = jnp.where(where_ref[0] == 0, acc_ref[FAR_PARTNER : FAR_PARTNER + 1, :], near_partner_row)
+            side_out[...] = jnp.where(where_ref[1] == 1, acc_ref[NEAR : NEAR + 1, :], near_partner_row)
 
     products = sum(len(a[1]) * len(b[1]) for a, b in heavy_pairs) / 4
     return pl.pallas_call(
@@ -235,8 +244,9 @@
         + smem()
         + vmem(1)
         + vmem(len(after)),
-        out_specs=pl.BlockSpec(memory_space=pltpu.VMEM),
-        out_shape=jax.ShapeDtypeStruct(found.shape, jnp.float32),
+        out_specs=vmem(4 if last else 1),
+        out_shape=[jax.ShapeDtypeStruct((1, rows), jnp.float32)] * (3 if last else 0)
+        + [jax.ShapeDtypeStruct(found.shape, jnp.float32)],
         scratch_shapes=[pltpu.VMEM((len(names), size, width), jnp.bfloat16), pltpu.SemaphoreType.DMA((len(names),))],
         compiler_params=params(),
         name=name,
@@ -248,31 +258,6 @@
     )(*own, *arrays.values(), where, found, *after)
 
 
-def tie_kernel(array_ref, after_ref, out_ref):
-    del array_ref, after_ref, out_ref
-
-
-def tie(array, after):
-    return pl.pallas_call(
-        tie_kernel,
-        in_specs=[pl.BlockSpec(memory_space=pl.ANY)] + vmem(1),
-        out_specs=pl.BlockSpec(memory_space=pl.ANY),
-        out_shape=jax.ShapeDtypeStruct(array.shape, array.dtype),
-        input_output_aliases={0: 0},
-        compiler_params=params(),
-        name="tie",
-        cost_estimate=pl.CostEstimate(flops=0, bytes_accessed=0, transcendentals=0),
-    )(array, after)
-
-
-def results_kernel(where_ref, so_far_ref, from_partner_ref, own_out, far_out, side_out):
-    own_row = so_far_ref[OWN : OWN + 1, :]
-    own_out[...] = jnp.where(where_ref[1] == 0, jnp.maximum(own_row, from_partner_ref[...]), own_row)
-    near_partner_row = so_far_ref[NEAR_PARTNER : NEAR_PARTNER + 1, :]
-    far_out[...] = jnp.where(where_ref[0] == 0, so_far_ref[FAR_PARTNER : FAR_PARTNER + 1, :], near_partner_row)
-    side_out[...] = jnp.where(where_ref[1] == 1, so_far_ref[NEAR : NEAR + 1, :], near_partner_row)
-
-
 def body(embeds, doc_ids, prior_max, owned, owned_ids, owner_dest):
     devices = lax.axis_size("grp") * lax.axis_size("blk")
     raw = embeds[0]
@@ -299,10 +284,6 @@
     def heavy_back(core, heavy, block):
         return block - step(core) if heavy else None
 
-    outgoing = placed_rows(owned, owner_dest.reshape(1, -1), owned_ids.reshape(1, -1), devices)
-    next_rows, next_ids = split_rows(lax.all_to_all(outgoing, BOTH, split_axis=0, concat_axis=0, tiled=True))
-
-    line = jax.ShapeDtypeStruct((1, rows), jnp.float32)
     own0, own1 = (norm_half(raw, doc_ids, half) for half in range(2))
     partner0 = send(own0, to_heavy)
     near1 = send(own1, ahead)
@@ -320,6 +301,9 @@
             flops=2 * rows * rows * width, bytes_accessed=2 * rows * width, transcendentals=0
         ),
     )(own0, own1, prior_max)
+    outgoing = placed_rows(owned, owner_dest.reshape(1, -1), owned_ids.reshape(1, -1), devices, found)
+    next_rows, next_ids = split_rows(lax.all_to_all(outgoing, BOTH, split_axis=0, concat_axis=0, tiled=True))
+
     far0 = send(partner0, heavy_back)
     near_partner0 = send(partner0, heavy_ahead)
     near_partner1 = send(near1, to_heavy)
@@ -327,40 +311,37 @@
     own = (OWN, [(0, "own0"), (1, "own1")])
     partner_both = (PARTNER, [(0, "partner0"), (1, "partner1")])
     near_both = (NEAR, [(0, "near0"), (1, "near1")])
-    found = stage(
+    (found,) = stage(
         "cross_a",
         (own0, own1),
-        {"partner0": partner0, "near1": near1},
+        {"partner0": partner0, "near1": near1, "near0": near0},
         [
             (own, (PARTNER, [(0, "partner0")])),
-            (own, (NEAR, [(1, "near1")])),
-            ((PARTNER, [(0, "partner0")]), (NEAR, [(1, "near1")])),
+            (own, (NEAR, [(1, "near1"), (0, "near0")])),
+            ((PARTNER, [(0, "partner0")]), near_both),
         ],
         [(own, (NEAR_PARTNER, [(1, "near1")]))],
         where,
         found,
     )
-    partner1 = tie(partner1, found)
     far1 = send(partner1, heavy_back)
-    found = stage(
+    (found,) = stage(
         "cross_b",
         (own0, own1),
         {
             "partner1": partner1,
+            "near1": near1,
             "near0": near0,
+            "far0": far0,
             "near_partner0": near_partner0,
             "partner0": partner0,
-            "near1": near1,
-            "far0": far0,
         },
         [
             (own, (PARTNER, [(1, "partner1")])),
-            (own, (NEAR, [(0, "near0")])),
+            ((PARTNER, [(1, "partner1")]), near_both),
+            ((FAR_PARTNER, [(0, "far0")]), near_both),
             (own, (NEAR_PARTNER, [(0, "near_partner0")])),
             (partner_both, (NEAR_PARTNER, [(0, "near_partner0")])),
-            (partner_both, (NEAR, [(0, "near0")])),
-            ((PARTNER, [(1, "partner1")]), (NEAR, [(1, "near1")])),
-            ((FAR_PARTNER, [(0, "far0")]), near_both),
         ],
         [],
         where,
@@ -368,7 +349,7 @@
         (next_ids,),
     )
     from_partner = send(found[PARTNER : PARTNER + 1], to_light)
-    found = stage(
+    mine, for_far, for_side, _ = stage(
         "cross_c",
         (own0, own1),
         {"near_partner1": near_partner1, "far1": far1, "near0": near0, "near1": near1},
@@ -379,16 +360,9 @@
         [],
         where,
         found,
-        (),
-    )
-    mine, for_far, for_side = pl.pallas_call(
-        results_kernel,
-        in_specs=smem() + vmem(2),
-        out_specs=vmem(3),
-        out_shape=[line] * 3,
-        compiler_params=params(),
-        name="results",
-    )(where, found, from_partner)
+        (from_partner,),
+        last=True,
+    )
     from_far = send(for_far, lambda core, heavy, block: block + 1 + 2 * core if heavy else None)
     from_side = send(for_side, lambda core, heavy, block: block + 2 if core else None)
     lowest = jnp.float32(LOWEST)

time: 94.8 us -> 87.4 us (0.922)
  waiting for transfers between devices: 37.6 us -> 32.5 us
  starting transfers between devices: 41 us -> 38.7 us
    ppermute x11, waiting for transfers between devices: 37.6 us -> 25.2 us  [send(): return lax.ppermute(value, BOTH, pairs)]
    all_to_all x1, waiting for transfers between devices: 0.01 us -> 7.27 us  [body(): lax.all_to_all(outgoing, BOTH, split_axis=0, concat_axis=0, tiled=True)]
    ppermute x11, starting transfers between devices: 30.5 us -> 28.3 us  [send(): return lax.ppermute(value, BOTH, pairs)]
    pallas_call x3 -> x1, Pallas kernels: 2.31 us -> 1.76 us  [placed_rows(): pl.pallas_call(place_kernel, in_specs=vmem(4), out_specs=pl.BlockSpec(mem...]
  transfers between devices with their start and end apart: 12 -> 12, of which waited for: 4 -> 3; matrix products, arithmetic and copies ran while one was open for 0% -> 0% of each run, Pallas kernels for 11% -> 11%
where the time goes in v7:
time: 87.4 us; the launch traced here: 87 us
  starting transfers between devices  38.7 us (44%)
  waiting for transfers between devices  32.5 us (37%)
  Pallas kernels  11.3 us (13%)
  local copies, waits for them, and re-layouts  2.98 us (3%)
    ppermute x11, starting transfers between devices, send(): return lax.ppermute(value, BOTH, pairs)  28.3 us
    ppermute x11, waiting for transfers between devices, send(): return lax.ppermute(value, BOTH, pairs)  25.2 us
    all_to_all x1, starting transfers between devices, body(): lax.all_to_all(outgoing, BOTH, split_axis=0, concat_axis=0, tiled=True)  10.5 us
    all_to_all x1, waiting for transfers between devices, body(): lax.all_to_all(outgoing, BOTH, split_axis=0, concat_axis=0, tiled=True)  7.27 us
    pallas_call x3, Pallas kernels, stage(): pl.pallas_call(run, in_specs=vmem(2) + [pl.BlockSpec(memory_space=pl.ANY)...  5.33 us
    unnamed x14, local copies, waits for them, and re-layouts  2.97 us
    pallas_call x1, Pallas kernels, body(): pl.pallas_call(within_kernel, in_specs=vmem(3), out_specs=pl.BlockSpec(me...  2.38 us
    pallas_call x1, Pallas kernels, placed_rows(): pl.pallas_call(place_kernel, in_specs=vmem(4), out_specs=pl.BlockSpec(mem...  1.76 us
  transfers between devices with their start and end apart: 12, of which 3 were waited for; matrix products, arithmetic and copies ran while one was open for 0% of the time, Pallas kernels for 11%

profile of v7, /device:TPU:0, one launch (start us, length us, event | category | flops | bytes accessed | tf_op | source)
XLA Modules:
  0.0 87.0 jit_solution(15565786507163224794)
XLA Ops:
  0.6 0.0 copy-start
  0.6 1.6 %copy-done = bf16[1,1024,1024]{2,1,0:T(8,128)(2,1)S(1)} copy-done((bf16[1,1024,1024]{2,1,0:T(8,128)(2,1)S(1)}, bf16[1,1024,1024]{2,1,0:T(8,128)(2,1)}, u32[]{:S(2)}) %copy-start) | copy-done | bytes 2097176
  2.2 0.0 copy-start.2
  2.2 0.7 copy-done.2
  2.9 0.3 norm_0.1.own0.refs_0_
  3.2 0.0 copy-start.5
  3.3 4.6 %collective-permute-start.5 = (bf16[528,1024]{1,0:T(8,128)(2,1)S(1)}, bf16[528,1024]{1,0:T(8,128)(2,1)}, u32[]{:S(2)}, u32[]{:S(2)}) collective-permute-start(bf16[528,1024]{1,0:T(8,128)(2,1)S(1)} %norm_0.1.own0.refs_0_), channel_id=1, source_target_pairs={{0,1},{2,3},{4,5},{6,7},{8,9},{10,11},{12,13},{14,15},{16,17},{18,... | collective-permute-start | bytes 3244040 | tf_op jit(solution)/shard_map/ppermute | solution.py:31
  7.8 0.3 norm_1.1.own1.refs_1_
  8.1 0.0 copy-start.1
  8.1 0.0 copy-start.3
  8.2 0.0 copy-start.4
  8.2 1.6 %collective-permute-start = (bf16[528,1024]{1,0:T(8,128)(2,1)S(1)}, bf16[528,1024]{1,0:T(8,128)(2,1)}, u32[]{:S(2)}, u32[]{:S(2)}) collective-permute-start(bf16[528,1024]{1,0:T(8,128)(2,1)S(1)} %norm_1.1.own1.refs_1_), channel_id=1, source_target_pairs={{0,2},{1,3},{2,4},{3,5},{4,6},{5,7},{6,8},{7,9},{8,10},{9,11},{10,... | collective-permute-start | bytes 3244040 | tf_op jit(solution)/shard_map/ppermute | solution.py:31
  9.7 2.3 %collective-permute-start.2 = (bf16[528,1024]{1,0:T(8,128)(2,1)S(1)}, bf16[528,1024]{1,0:T(8,128)(2,1)}, u32[]{:S(2)}, u32[]{:S(2)}) collective-permute-start(bf16[528,1024]{1,0:T(8,128)(2,1)S(1)} %norm_1.1.own1.refs_1_), channel_id=1, source_target_pairs={{0,1},{2,3},{4,5},{6,7},{8,9},{10,11},{12,13},{14,15},{16,17},{18,... | collective-permute-start | bytes 3244040 | tf_op jit(solution)/shard_map/ppermute | solution.py:31
  12.0 1.7 %collective-permute-start.4 = (bf16[528,1024]{1,0:T(8,128)(2,1)S(1)}, bf16[528,1024]{1,0:T(8,128)(2,1)}, u32[]{:S(2)}, u32[]{:S(2)}) collective-permute-start(bf16[528,1024]{1,0:T(8,128)(2,1)S(1)} %norm_0.1.own0.refs_0_), channel_id=1, source_target_pairs={{1,3},{3,5},{5,7},{7,9},{9,11},{11,13},{13,15},{15,17},{17,19},{19... | collective-permute-start | bytes 3244040 | tf_op jit(solution)/shard_map/ppermute | solution.py:31
  13.7 0.0 copy-done.5
  13.7 2.4 %within.1.refs_6_.after_ref = f32[8,1024]{1,0:T(8,128)S(1)} custom-call(bf16[528,1024]{1,0:T(8,128)(2,1)S(1)} %norm_0.1.own0.refs_0_, bf16[528,1024]{1,0:T(8,128)(2,1)S(1)} %norm_1.1.own1.refs_1_, f32[1,1024]{1,0:T(1,128)S(1)} %copy-done.5), custom_call_target="tpu_custom_call" | custom-call | flops 2147483648 | bytes 2097152 | tf_op jit(solution)/shard_map/within/pallas_call | solution.py:293
  16.0 0.0 copy-done.1
  16.1 0.0 copy-done.3
  16.1 0.0 copy-done.4
  16.1 1.8 %place.1 = bf16[128,4,1152]{2,1,0:T(4,128)(2,1)} custom-call(bf16[256,1024]{1,0:T(8,128)(2,1)S(1)} %copy-done.1, s32[1,256]{1,0:T(1,128)S(1)} %bitcast.8, s32[1,256]{1,0:T(1,128)S(1)} %bitcast.9, f32[8,1024]{1,0:T(8,128)S(1)} %within.1.refs_6_.after_ref), custom_call_target="tpu_custom_call" | custom-call | flops 268435456 | bytes 1572864 | tf_op jit(solution)/shard_map/place/pallas_call | solution.py:172
  17.8 10.5 %all-to-all-start = ((bf16[128,4,1152]{2,1,0:T(4,128)(2,1)}), bf16[128,4,1152]{2,1,0:T(4,128)(2,1)S(1)}, u32[]{:S(2)}, u32[]{:S(2)}) async-start(bf16[128,4,1152]{2,1,0:T(4,128)(2,1)} %place.1), calls=%async_computation | async-start | bytes 2359296 | tf_op jit(solution)/shard_map/all_to_all | solution.py:305
  28.3 0.0 collective-permute-done.5.refs_2_.refs_7_
  28.3 1.8 %collective-permute-start.6 = (bf16[528,1024]{1,0:T(8,128)(2,1)}, bf16[528,1024]{1,0:T(8,128)(2,1)}, u32[]{:S(2)}, u32[]{:S(2)}) collective-permute-start(bf16[528,1024]{1,0:T(8,128)(2,1)} %collective-permute-done.5.refs_2_.refs_7_), channel_id=1, source_target_pairs={{1,31},{3,1},{5,3},{7,5},{9,7},{11,9},{13,11},{15,13},{17,15},{19,... | collective-permute-start | bytes 3244040 | tf_op jit(solution)/shard_map/ppermute | solution.py:31
  30.1 1.6 %collective-permute-start.7 = (bf16[528,1024]{1,0:T(8,128)(2,1)}, bf16[528,1024]{1,0:T(8,128)(2,1)}, u32[]{:S(2)}, u32[]{:S(2)}) collective-permute-start(bf16[528,1024]{1,0:T(8,128)(2,1)} %collective-permute-done.5.refs_2_.refs_7_), channel_id=1, source_target_pairs={{1,3},{3,5},{5,7},{7,9},{9,11},{11,13},{13,15},{15,17},{17,19},{19... | collective-permute-start | bytes 3244040 | tf_op jit(solution)/shard_map/ppermute | solution.py:31
  31.7 0.0 collective-permute-done.refs_3_.refs_5_
  31.7 9.9 %collective-permute-start.1 = (bf16[528,1024]{1,0:T(8,128)(2,1)}, bf16[528,1024]{1,0:T(8,128)(2,1)}, u32[]{:S(2)}, u32[]{:S(2)}) collective-permute-start(bf16[528,1024]{1,0:T(8,128)(2,1)} %collective-permute-done.refs_3_.refs_5_), channel_id=1, source_target_pairs={{0,1},{2,3},{4,5},{6,7},{8,9},{10,11},{12,13},{14,15},{16,17},{18,... | collective-permute-start | bytes 3244040 | tf_op jit(solution)/shard_map/ppermute | solution.py:31
  41.6 0.0 collective-permute-done.2.refs_2_
  41.7 1.7 %collective-permute-start.3 = (bf16[528,1024]{1,0:T(8,128)(2,1)}, bf16[528,1024]{1,0:T(8,128)(2,1)}, u32[]{:S(2)}, u32[]{:S(2)}) collective-permute-start(bf16[528,1024]{1,0:T(8,128)(2,1)} %collective-permute-done.2.refs_2_), channel_id=1, source_target_pairs={{1,31},{3,1},{5,3},{7,5},{9,7},{11,9},{13,11},{15,13},{17,15},{19,... | collective-permute-start | bytes 3244040 | tf_op jit(solution)/shard_map/ppermute | solution.py:31
  43.3 0.1 pad_add_fusion.refs_5_.refs_8_.refs_6_
  43.4 0.0 collective-permute-done.4.refs_4_
  43.4 3.3 %cross_a.1.refs_9_ = f32[8,1024]{1,0:T(8,128)S(1)} custom-call(bf16[528,1024]{1,0:T(8,128)(2,1)S(1)} %norm_0.1.own0.refs_0_, bf16[528,1024]{1,0:T(8,128)(2,1)S(1)} %norm_1.1.own1.refs_1_, bf16[528,1024]{1,0:T(8,128)(2,1)} %collective-permute-done.5.refs_2_.refs_7_, bf16[528,1024]{1,0:T(8,128)(2,1)} %collective-permute-done.refs_3_.refs_5_, ...), custom_call_target="tpu_custom_call" | custom-call | flops 4294967296 | bytes 3244032 | tf_op jit(solution)/shard_map/cross_a/pallas_call | solution.py:240
  46.7 7.3 %all-to-all-done.in_ref = bf16[128,4,1152]{2,1,0:T(4,128)(2,1)S(1)} async-done(((bf16[128,4,1152]{2,1,0:T(4,128)(2,1)}), bf16[128,4,1152]{2,1,0:T(4,128)(2,1)S(1)}, u32[]{:S(2)}, u32[]{:S(2)}) %all-to-all-start) | async-done | bytes 1179680 | tf_op jit(solution)/shard_map/all_to_all | solution.py:305
  54.0 1.1 %split.1 = (bf16[512,1024]{1,0:T(8,128)(2,1)}, s32[1,512]{1,0:T(1,128)}) custom-call(bf16[128,4,1152]{2,1,0:T(4,128)(2,1)S(1)} %all-to-all-done.in_ref), custom_call_target="tpu_custom_call" | custom-call | bytes 2097152 | tf_op jit(solution)/shard_map/split/pallas_call | solution.py:196
  55.1 0.0 collective-permute-done.6.refs_5_
  55.1 0.0 collective-permute-done.7.refs_6_
  55.1 0.0 copy-start.6
  55.1 0.7 copy-done.6
  55.8 0.8 cross_b.1.refs_7_
  56.7 1.3 %collective-permute-start.8 = (f32[1,1024]{1,0:T(1,128)S(1)}, f32[1,1024]{1,0:T(1,128)S(1)}, u32[]{:S(2)}, u32[]{:S(2)}) collective-permute-start(f32[1,1024]{1,0:T(1,128)S(1)} %slice.4), channel_id=1, source_target_pairs={{1,0},{3,2},{5,4},{7,6},{9,8},{11,10},{13,12},{15,14},{17,16},{19,... | collective-permute-start | bytes 12296 | tf_op jit(solution)/shard_map/ppermute | solution.py:31
  58.0 0.0 collective-permute-done.1.refs_2_
  58.0 0.0 collective-permute-done.3.refs_3_
  58.0 16.8 %collective-permute-done.8.refs_8_ = f32[1,1024]{1,0:T(1,128)S(1)} collective-permute-done((f32[1,1024]{1,0:T(1,128)S(1)}, f32[1,1024]{1,0:T(1,128)S(1)}, u32[]{:S(2)}, u32[]{:S(2)}) %collective-permute-start.8) | collective-permute-done | bytes 4128 | tf_op jit(solution)/shard_map/ppermute | solution.py:31
  74.8 1.2 %cross_c.1 = (f32[1,1024]{1,0:T(1,128)S(1)}, f32[1,1024]{1,0:T(1,128)S(1)}, f32[1,1024]{1,0:T(1,128)S(1)}, f32[8,1024]{1,0:T(8,128)}) custom-call(bf16[528,1024]{1,0:T(8,128)(2,1)S(1)} %norm_0.1.own0.refs_0_, bf16[528,1024]{1,0:T(8,128)(2,1)S(1)} %norm_1.1.own1.refs_1_, bf16[528,1024]{1,0:T(8,128)(2,1)} %collective-permute-done.1.refs_2_, ...), custom_call_target="tpu_custom_call" | custom-call | flops 2147483648 | bytes 4325376 | tf_op jit(solution)/shard_map/cross_c/pallas_call | solution.py:240
  76.0 0.7 collective-permute-start.10
  76.6 1.3 %collective-permute-start.9 = (f32[1,1024]{1,0:T(1,128)S(1)}, f32[1,1024]{1,0:T(1,128)S(1)}, u32[]{:S(2)}, u32[]{:S(2)}) collective-permute-start(f32[1,1024]{1,0:T(1,128)S(1)} %get-tuple-element.10), channel_id=1, source_target_pairs={{1,2},{3,4},{5,6},{7,8},{9,10},{11,12},{13,14},{15,16},{17,18},{19... | collective-permute-start | bytes 12296 | tf_op jit(solution)/shard_map/ppermute | solution.py:31
  77.9 0.0 collective-permute-done.10
  77.9 8.4 %collective-permute-done.9 = f32[1,1024]{1,0:T(1,128)S(1)} collective-permute-done((f32[1,1024]{1,0:T(1,128)S(1)}, f32[1,1024]{1,0:T(1,128)S(1)}, u32[]{:S(2)}, u32[]{:S(2)}) %collective-permute-start.9) | collective-permute-done | bytes 4128 | tf_op jit(solution)/shard_map/ppermute | solution.py:31
  86.4 0.6 fusion.1
  (1 shorter events, 0.0 us)
Async XLA Ops:
  0.6 1.6 %copy-start = (bf16[1,1024,1024]{2,1,0:T(8,128)(2,1)S(1)}, bf16[1,1024,1024]{2,1,0:T(8,128)(2,1)}, u32[]{:S(2)}) copy-start(bf16[1,1024,1024]{2,1,0:T(8,128)(2,1)} %param.6) | copy-start | bytes 6291460
  2.2 0.7 copy-start.2
  3.2 10.4 %copy-start.5 = (f32[1,1024]{1,0:T(1,128)S(1)}, f32[1,1024]{1,0:T(1,128)}, u32[]{:S(2)}) copy-start(f32[1,1024]{1,0:T(1,128)} %prior_ref.1) | copy-start | bytes 12292
  3.3 25.1 %collective-permute-start.5 = (bf16[528,1024]{1,0:T(8,128)(2,1)S(1)}, bf16[528,1024]{1,0:T(8,128)(2,1)}, u32[]{:S(2)}, u32[]{:S(2)}) collective-permute-start(bf16[528,1024]{1,0:T(8,128)(2,1)S(1)} %norm_0.1.own0.refs_0_), channel_id=1, source_target_pairs={{0,1},{2,3},{4,5},{6,7},{8,9},{10,11},{12,13},{14,15},{16,17},{18,... | collective-permute-start | bytes 3244040 | tf_op jit(solution)/shard_map/ppermute | solution.py:31
  8.1 7.9 %copy-start.1 = (bf16[256,1024]{1,0:T(8,128)(2,1)S(1)}, bf16[256,1024]{1,0:T(8,128)(2,1)}, u32[]{:S(2)}) copy-start(bf16[256,1024]{1,0:T(8,128)(2,1)} %rows_ref.1) | copy-start | bytes 1572868
  8.1 7.9 %copy-start.3 = (s32[256,1]{0,1:T(1,128)S(1)}, s32[256,1]{0,1:T(1,128)}, u32[]{:S(2)}) copy-start(s32[256,1]{0,1:T(1,128)} %param.11) | copy-start | bytes 3076
  8.2 7.9 %copy-start.4 = (s32[256]{0:T(256)S(1)}, s32[256]{0:T(256)}, u32[]{:S(2)}) copy-start(s32[256]{0:T(256)} %param.10) | copy-start | bytes 3076
  8.2 23.6 %collective-permute-start = (bf16[528,1024]{1,0:T(8,128)(2,1)S(1)}, bf16[528,1024]{1,0:T(8,128)(2,1)}, u32[]{:S(2)}, u32[]{:S(2)}) collective-permute-start(bf16[528,1024]{1,0:T(8,128)(2,1)S(1)} %norm_1.1.own1.refs_1_), channel_id=1, source_target_pairs={{0,2},{1,3},{2,4},{3,5},{4,6},{5,7},{6,8},{7,9},{8,10},{9,11},{10,... | collective-permute-start | bytes 3244040 | tf_op jit(solution)/shard_map/ppermute | solution.py:31
  9.7 31.9 %collective-permute-start.2 = (bf16[528,1024]{1,0:T(8,128)(2,1)S(1)}, bf16[528,1024]{1,0:T(8,128)(2,1)}, u32[]{:S(2)}, u32[]{:S(2)}) collective-permute-start(bf16[528,1024]{1,0:T(8,128)(2,1)S(1)} %norm_1.1.own1.refs_1_), channel_id=1, source_target_pairs={{0,1},{2,3},{4,5},{6,7},{8,9},{10,11},{12,13},{14,15},{16,17},{18,... | collective-permute-start | bytes 3244040 | tf_op jit(solution)/shard_map/ppermute | solution.py:31
  12.0 31.4 %collective-permute-start.4 = (bf16[528,1024]{1,0:T(8,128)(2,1)S(1)}, bf16[528,1024]{1,0:T(8,128)(2,1)}, u32[]{:S(2)}, u32[]{:S(2)}) collective-permute-start(bf16[528,1024]{1,0:T(8,128)(2,1)S(1)} %norm_0.1.own0.refs_0_), channel_id=1, source_target_pairs={{1,3},{3,5},{5,7},{7,9},{9,11},{11,13},{13,15},{15,17},{17,19},{19... | collective-permute-start | bytes 3244040 | tf_op jit(solution)/shard_map/ppermute | solution.py:31
  17.8 36.1 %all-to-all-start = ((bf16[128,4,1152]{2,1,0:T(4,128)(2,1)}), bf16[128,4,1152]{2,1,0:T(4,128)(2,1)S(1)}, u32[]{:S(2)}, u32[]{:S(2)}) async-start(bf16[128,4,1152]{2,1,0:T(4,128)(2,1)} %place.1), calls=%async_computation | async-start | bytes 2359296 | tf_op jit(solution)/shard_map/all_to_all | solution.py:305
  28.3 26.8 %collective-permute-start.6 = (bf16[528,1024]{1,0:T(8,128)(2,1)}, bf16[528,1024]{1,0:T(8,128)(2,1)}, u32[]{:S(2)}, u32[]{:S(2)}) collective-permute-start(bf16[528,1024]{1,0:T(8,128)(2,1)} %collective-permute-done.5.refs_2_.refs_7_), channel_id=1, source_target_pairs={{1,31},{3,1},{5,3},{7,5},{9,7},{11,9},{13,11},{15,13},{17,15},{19,... | collective-permute-start | bytes 3244040 | tf_op jit(solution)/shard_map/ppermute | solution.py:31
  30.1 25.0 %collective-permute-start.7 = (bf16[528,1024]{1,0:T(8,128)(2,1)}, bf16[528,1024]{1,0:T(8,128)(2,1)}, u32[]{:S(2)}, u32[]{:S(2)}) collective-permute-start(bf16[528,1024]{1,0:T(8,128)(2,1)} %collective-permute-done.5.refs_2_.refs_7_), channel_id=1, source_target_pairs={{1,3},{3,5},{5,7},{7,9},{9,11},{11,13},{13,15},{15,17},{17,19},{19... | collective-permute-start | bytes 3244040 | tf_op jit(solution)/shard_map/ppermute | solution.py:31
  31.7 26.2 %collective-permute-start.1 = (bf16[528,1024]{1,0:T(8,128)(2,1)}, bf16[528,1024]{1,0:T(8,128)(2,1)}, u32[]{:S(2)}, u32[]{:S(2)}) collective-permute-start(bf16[528,1024]{1,0:T(8,128)(2,1)} %collective-permute-done.refs_3_.refs_5_), channel_id=1, source_target_pairs={{0,1},{2,3},{4,5},{6,7},{8,9},{10,11},{12,13},{14,15},{16,17},{18,... | collective-permute-start | bytes 3244040 | tf_op jit(solution)/shard_map/ppermute | solution.py:31
  41.7 16.3 %collective-permute-start.3 = (bf16[528,1024]{1,0:T(8,128)(2,1)}, bf16[528,1024]{1,0:T(8,128)(2,1)}, u32[]{:S(2)}, u32[]{:S(2)}) collective-permute-start(bf16[528,1024]{1,0:T(8,128)(2,1)} %collective-permute-done.2.refs_2_), channel_id=1, source_target_pairs={{1,31},{3,1},{5,3},{7,5},{9,7},{11,9},{13,11},{15,13},{17,15},{19,... | collective-permute-start | bytes 3244040 | tf_op jit(solution)/shard_map/ppermute | solution.py:31
  55.1 0.7 copy-start.6
  56.7 18.1 %collective-permute-start.8 = (f32[1,1024]{1,0:T(1,128)S(1)}, f32[1,1024]{1,0:T(1,128)S(1)}, u32[]{:S(2)}, u32[]{:S(2)}) collective-permute-start(f32[1,1024]{1,0:T(1,128)S(1)} %slice.4), channel_id=1, source_target_pairs={{1,0},{3,2},{5,4},{7,6},{9,8},{11,10},{13,12},{15,14},{17,16},{19,... | collective-permute-start | bytes 12296 | tf_op jit(solution)/shard_map/ppermute | solution.py:31
  76.0 2.0 %collective-permute-start.10 = (f32[1,1024]{1,0:T(1,128)S(1)}, f32[1,1024]{1,0:T(1,128)S(1)}, u32[]{:S(2)}, u32[]{:S(2)}) collective-permute-start(f32[1,1024]{1,0:T(1,128)S(1)} %get-tuple-element.11), channel_id=1, source_target_pairs={{32,34},{33,35},{34,36},{35,37},{36,38},{37,39},{38,40},{39,41},{4... | collective-permute-start | bytes 12296 | tf_op jit(solution)/shard_map/ppermute | solution.py:31
  76.6 9.7 %collective-permute-start.9 = (f32[1,1024]{1,0:T(1,128)S(1)}, f32[1,1024]{1,0:T(1,128)S(1)}, u32[]{:S(2)}, u32[]{:S(2)}) collective-permute-start(f32[1,1024]{1,0:T(1,128)S(1)} %get-tuple-element.10), channel_id=1, source_target_pairs={{1,2},{3,4},{5,6},{7,8},{9,10},{11,12},{13,14},{15,16},{17,18},{19... | collective-permute-start | bytes 12296 | tf_op jit(solution)/shard_map/ppermute | solution.py:31

commit v8 on v7

--- a/solution.py
+++ b/solution.py
@@ -229,9 +229,9 @@
         if light_pairs:
             compare(where_ref, 0, acc_ref, held, names, inputs, buffers, sems, light_pairs)
         if last:
-            own_out, far_out, side_out = outs[:3]
-            own_row, from_partner = acc_ref[OWN : OWN + 1, :], refs[len(names) + 2][...]
-            own_out[...] = jnp.where(where_ref[1] == 0, jnp.maximum(own_row, from_partner), own_row)
+            own_out, partner_out, far_out, side_out = outs[:4]
+            own_out[...] = acc_ref[OWN : OWN + 1, :]
+            partner_out[...] = acc_ref[PARTNER : PARTNER + 1, :]
             near_partner_row = acc_ref[NEAR_PARTNER : NEAR_PARTNER + 1, :]
             far_out[...] = jnp.where(where_ref[0] == 0, acc_ref[FAR_PARTNER : FAR_PARTNER + 1, :], near_partner_row)
             side_out[...] = jnp.where(where_ref[1] == 1, acc_ref[NEAR : NEAR + 1, :], near_partner_row)
@@ -244,8 +244,8 @@
         + smem()
         + vmem(1)
         + vmem(len(after)),
-        out_specs=vmem(4 if last else 1),
-        out_shape=[jax.ShapeDtypeStruct((1, rows), jnp.float32)] * (3 if last else 0)
+        out_specs=vmem(5 if last else 1),
+        out_shape=[jax.ShapeDtypeStruct((1, rows), jnp.float32)] * (4 if last else 0)
         + [jax.ShapeDtypeStruct(found.shape, jnp.float32)],
         scratch_shapes=[pltpu.VMEM((len(names), size, width), jnp.bfloat16), pltpu.SemaphoreType.DMA((len(names),))],
         compiler_params=params(),
@@ -307,6 +307,7 @@
     far0 = send(partner0, heavy_back)
     near_partner0 = send(partner0, heavy_ahead)
     near_partner1 = send(near1, to_heavy)
+    far1 = send(partner1, heavy_back)
 
     own = (OWN, [(0, "own0"), (1, "own1")])
     partner_both = (PARTNER, [(0, "partner0"), (1, "partner1")])
@@ -314,59 +315,48 @@
     (found,) = stage(
         "cross_a",
         (own0, own1),
-        {"partner0": partner0, "near1": near1, "near0": near0},
+        {"partner0": partner0, "near1": near1, "near0": near0, "partner1": partner1},
         [
             (own, (PARTNER, [(0, "partner0")])),
-            (own, (NEAR, [(1, "near1"), (0, "near0")])),
+            (own, near_both),
             ((PARTNER, [(0, "partner0")]), near_both),
+            (own, (PARTNER, [(1, "partner1")])),
+            ((PARTNER, [(1, "partner1")]), near_both),
         ],
         [(own, (NEAR_PARTNER, [(1, "near1")]))],
         where,
         found,
     )
-    far1 = send(partner1, heavy_back)
-    (found,) = stage(
+    mine, for_partner, for_far, for_side, _ = stage(
         "cross_b",
         (own0, own1),
         {
-            "partner1": partner1,
-            "near1": near1,
+            "near_partner0": near_partner0,
+            "near_partner1": near_partner1,
             "near0": near0,
             "far0": far0,
-            "near_partner0": near_partner0,
+            "near1": near1,
+            "far1": far1,
             "partner0": partner0,
+            "partner1": partner1,
         },
         [
-            (own, (PARTNER, [(1, "partner1")])),
-            ((PARTNER, [(1, "partner1")]), near_both),
+            (own, (NEAR_PARTNER, [(0, "near_partner0"), (1, "near_partner1")])),
             ((FAR_PARTNER, [(0, "far0")]), near_both),
-            (own, (NEAR_PARTNER, [(0, "near_partner0")])),
+            ((FAR_PARTNER, [(1, "far1")]), near_both),
             (partner_both, (NEAR_PARTNER, [(0, "near_partner0")])),
         ],
         [],
         where,
         found,
         (next_ids,),
-    )
-    from_partner = send(found[PARTNER : PARTNER + 1], to_light)
-    mine, for_far, for_side, _ = stage(
-        "cross_c",
-        (own0, own1),
-        {"near_partner1": near_partner1, "far1": far1, "near0": near0, "near1": near1},
-        [
-            (own, (NEAR_PARTNER, [(1, "near_partner1")])),
-            ((FAR_PARTNER, [(1, "far1")]), near_both),
-        ],
-        [],
-        where,
-        found,
-        (from_partner,),
         last=True,
     )
+    from_partner = send(for_partner, to_light)
     from_far = send(for_far, lambda core, heavy, block: block + 1 + 2 * core if heavy else None)
     from_side = send(for_side, lambda core, heavy, block: block + 2 if core else None)
     lowest = jnp.float32(LOWEST)
-    running = jnp.maximum(mine, jnp.where(heavy == 0, from_far, lowest))
+    running = jnp.maximum(mine, jnp.where(heavy == 0, jnp.maximum(from_partner, from_far), lowest))
     running = jnp.maximum(running, jnp.where(core == 1, from_side, lowest))
     return (running, next_rows, next_ids.reshape(-1))
 

time: 87.4 us -> 93.4 us (1.069)
  the two profiles are of different devices: /device:TPU:0 before, /device:TPU:9 now
where the time goes in v8:
time: 93.4 us; the launch traced here: 93 us
  waiting for transfers between devices  39.3 us (42%)
  starting transfers between devices  38.6 us (41%)
  Pallas kernels  10.7 us (11%)
  local copies, waits for them, and re-layouts  2.98 us (3%)
    ppermute x11, waiting for transfers between devices, send(): return lax.ppermute(value, BOTH, pairs)  34.1 us
    ppermute x11, starting transfers between devices, send(): return lax.ppermute(value, BOTH, pairs)  31.4 us
    all_to_all x1, starting transfers between devices, body(): lax.all_to_all(outgoing, BOTH, split_axis=0, concat_axis=0, tiled=True)  7.12 us
    all_to_all x1, waiting for transfers between devices, body(): lax.all_to_all(outgoing, BOTH, split_axis=0, concat_axis=0, tiled=True)  5.15 us
    pallas_call x2, Pallas kernels, stage(): pl.pallas_call(run, in_specs=vmem(2) + [pl.BlockSpec(memory_space=pl.ANY)...  4.77 us
    unnamed x14, local copies, waits for them, and re-layouts  2.98 us
    pallas_call x1, Pallas kernels, body(): pl.pallas_call(within_kernel, in_specs=vmem(3), out_specs=pl.BlockSpec(me...  2.38 us
  transfers between devices with their start and end apart: 12, of which 5 were waited for; matrix products, arithmetic and copies ran while one was open for 0% of the time, Pallas kernels for 10%

profile of v8, /device:TPU:9, one launch (start us, length us, event | category | flops | bytes accessed | tf_op | source)
XLA Modules:
  0.0 93.0 jit_solution(4386652134996886372)
XLA Ops:
  0.6 0.0 copy-start
  0.6 1.6 %copy-done = bf16[1,1024,1024]{2,1,0:T(8,128)(2,1)S(1)} copy-done((bf16[1,1024,1024]{2,1,0:T(8,128)(2,1)S(1)}, bf16[1,1024,1024]{2,1,0:T(8,128)(2,1)}, u32[]{:S(2)}) %copy-start) | copy-done | bytes 2097176
  2.2 0.0 copy-start.2
  2.2 0.7 copy-done.2
  2.9 0.3 norm_0.1.own0.refs_0_
  3.2 0.0 copy-start.5
  3.3 2.3 %collective-permute-start = (bf16[528,1024]{1,0:T(8,128)(2,1)S(1)}, bf16[528,1024]{1,0:T(8,128)(2,1)}, u32[]{:S(2)}, u32[]{:S(2)}) collective-permute-start(bf16[528,1024]{1,0:T(8,128)(2,1)S(1)} %norm_0.1.own0.refs_0_), channel_id=1, source_target_pairs={{0,1},{2,3},{4,5},{6,7},{8,9},{10,11},{12,13},{14,15},{16,17},{18,... | collective-permute-start | bytes 3244040 | tf_op jit(solution)/shard_map/ppermute | solution.py:31
  5.5 0.3 norm_1.1.own1.refs_1_
  5.9 0.0 copy-start.1
  5.9 0.0 copy-start.3
  5.9 0.0 copy-start.4
  5.9 6.8 %collective-permute-start.2 = (bf16[528,1024]{1,0:T(8,128)(2,1)S(1)}, bf16[528,1024]{1,0:T(8,128)(2,1)}, u32[]{:S(2)}, u32[]{:S(2)}) collective-permute-start(bf16[528,1024]{1,0:T(8,128)(2,1)S(1)} %norm_1.1.own1.refs_1_), channel_id=1, source_target_pairs={{0,2},{1,3},{2,4},{3,5},{4,6},{5,7},{6,8},{7,9},{8,10},{9,11},{10,... | collective-permute-start | bytes 3244040 | tf_op jit(solution)/shard_map/ppermute | solution.py:31
  12.7 2.3 %collective-permute-start.6 = (bf16[528,1024]{1,0:T(8,128)(2,1)S(1)}, bf16[528,1024]{1,0:T(8,128)(2,1)}, u32[]{:S(2)}, u32[]{:S(2)}) collective-permute-start(bf16[528,1024]{1,0:T(8,128)(2,1)S(1)} %norm_1.1.own1.refs_1_), channel_id=1, source_target_pairs={{0,1},{2,3},{4,5},{6,7},{8,9},{10,11},{12,13},{14,15},{16,17},{18,... | collective-permute-start | bytes 3244040 | tf_op jit(solution)/shard_map/ppermute | solution.py:31
  15.0 1.6 %collective-permute-start.4 = (bf16[528,1024]{1,0:T(8,128)(2,1)S(1)}, bf16[528,1024]{1,0:T(8,128)(2,1)}, u32[]{:S(2)}, u32[]{:S(2)}) collective-permute-start(bf16[528,1024]{1,0:T(8,128)(2,1)S(1)} %norm_0.1.own0.refs_0_), channel_id=1, source_target_pairs={{1,3},{3,5},{5,7},{7,9},{9,11},{11,13},{13,15},{15,17},{17,19},{19... | collective-permute-start | bytes 3244040 | tf_op jit(solution)/shard_map/ppermute | solution.py:31
  16.7 0.0 copy-done.5
  16.7 2.4 %within.1.refs_7_.after_ref = f32[8,1024]{1,0:T(8,128)S(1)} custom-call(bf16[528,1024]{1,0:T(8,128)(2,1)S(1)} %norm_0.1.own0.refs_0_, bf16[528,1024]{1,0:T(8,128)(2,1)S(1)} %norm_1.1.own1.refs_1_, f32[1,1024]{1,0:T(1,128)S(1)} %copy-done.5), custom_call_target="tpu_custom_call" | custom-call | flops 2147483648 | bytes 2097152 | tf_op jit(solution)/shard_map/within/pallas_call | solution.py:293
  19.0 0.0 copy-done.1
  19.1 0.0 copy-done.3
  19.1 0.0 copy-done.4
  19.1 1.8 %place.1 = bf16[128,4,1152]{2,1,0:T(4,128)(2,1)} custom-call(bf16[256,1024]{1,0:T(8,128)(2,1)S(1)} %copy-done.1, s32[1,256]{1,0:T(1,128)S(1)} %bitcast.8, s32[1,256]{1,0:T(1,128)S(1)} %bitcast.9, f32[8,1024]{1,0:T(8,128)S(1)} %within.1.refs_7_.after_ref), custom_call_target="tpu_custom_call" | custom-call | flops 268435456 | bytes 1572864 | tf_op jit(solution)/shard_map/place/pallas_call | solution.py:172
  20.8 7.1 %all-to-all-start = ((bf16[128,4,1152]{2,1,0:T(4,128)(2,1)}), bf16[128,4,1152]{2,1,0:T(4,128)(2,1)S(1)}, u32[]{:S(2)}, u32[]{:S(2)}) async-start(bf16[128,4,1152]{2,1,0:T(4,128)(2,1)} %place.1), calls=%async_computation | async-start | bytes 2359296 | tf_op jit(solution)/shard_map/all_to_all | solution.py:305
  28.0 0.0 collective-permute-done.refs_2_.refs_8_
  28.0 1.7 %collective-permute-start.1 = (bf16[528,1024]{1,0:T(8,128)(2,1)}, bf16[528,1024]{1,0:T(8,128)(2,1)}, u32[]{:S(2)}, u32[]{:S(2)}) collective-permute-start(bf16[528,1024]{1,0:T(8,128)(2,1)} %collective-permute-done.refs_2_.refs_8_), channel_id=1, source_target_pairs={{1,3},{3,5},{5,7},{7,9},{9,11},{11,13},{13,15},{15,17},{17,19},{19... | collective-permute-start | bytes 3244040 | tf_op jit(solution)/shard_map/ppermute | solution.py:31
  29.7 1.7 %collective-permute-start.5 = (bf16[528,1024]{1,0:T(8,128)(2,1)}, bf16[528,1024]{1,0:T(8,128)(2,1)}, u32[]{:S(2)}, u32[]{:S(2)}) collective-permute-start(bf16[528,1024]{1,0:T(8,128)(2,1)} %collective-permute-done.refs_2_.refs_8_), channel_id=1, source_target_pairs={{1,31},{3,1},{5,3},{7,5},{9,7},{11,9},{13,11},{15,13},{17,15},{19,... | collective-permute-start | bytes 3244040 | tf_op jit(solution)/shard_map/ppermute | solution.py:31
  31.4 0.0 collective-permute-done.2.refs_3_.refs_6_
  31.4 8.8 %collective-permute-start.3 = (bf16[528,1024]{1,0:T(8,128)(2,1)}, bf16[528,1024]{1,0:T(8,128)(2,1)}, u32[]{:S(2)}, u32[]{:S(2)}) collective-permute-start(bf16[528,1024]{1,0:T(8,128)(2,1)} %collective-permute-done.2.refs_3_.refs_6_), channel_id=1, source_target_pairs={{0,1},{2,3},{4,5},{6,7},{8,9},{10,11},{12,13},{14,15},{16,17},{18,... | collective-permute-start | bytes 3244040 | tf_op jit(solution)/shard_map/ppermute | solution.py:31
  40.2 0.0 collective-permute-done.6.refs_5_.refs_9_
  40.2 1.6 %collective-permute-start.7 = (bf16[528,1024]{1,0:T(8,128)(2,1)}, bf16[528,1024]{1,0:T(8,128)(2,1)}, u32[]{:S(2)}, u32[]{:S(2)}) collective-permute-start(bf16[528,1024]{1,0:T(8,128)(2,1)} %collective-permute-done.6.refs_5_.refs_9_), channel_id=1, source_target_pairs={{1,31},{3,1},{5,3},{7,5},{9,7},{11,9},{13,11},{15,13},{17,15},{19,... | collective-permute-start | bytes 3244040 | tf_op jit(solution)/shard_map/ppermute | solution.py:31
  41.9 0.1 pad_add_fusion.refs_6_.refs_10_
  41.9 0.0 collective-permute-done.4.refs_4_
  42.0 3.3 %cross_a.1.refs_11_ = f32[8,1024]{1,0:T(8,128)S(1)} custom-call(bf16[528,1024]{1,0:T(8,128)(2,1)S(1)} %norm_0.1.own0.refs_0_, bf16[528,1024]{1,0:T(8,128)(2,1)S(1)} %norm_1.1.own1.refs_1_, bf16[528,1024]{1,0:T(8,128)(2,1)} %collective-permute-done.refs_2_.refs_8_, bf16[528,1024]{1,0:T(8,128)(2,1)} %collective-permute-done.2.refs_3_.refs_6_, ...), custom_call_target="tpu_custom_call" | custom-call | flops 6442450944 | bytes 4325376 | tf_op jit(solution)/shard_map/cross_a/pallas_call | solution.py:240
  45.3 5.2 %all-to-all-done.in_ref = bf16[128,4,1152]{2,1,0:T(4,128)(2,1)S(1)} async-done(((bf16[128,4,1152]{2,1,0:T(4,128)(2,1)}), bf16[128,4,1152]{2,1,0:T(4,128)(2,1)S(1)}, u32[]{:S(2)}, u32[]{:S(2)}) %all-to-all-start) | async-done | bytes 1179680 | tf_op jit(solution)/shard_map/all_to_all | solution.py:305
  50.4 1.1 %split.1 = (bf16[512,1024]{1,0:T(8,128)(2,1)}, s32[1,512]{1,0:T(1,128)}) custom-call(bf16[128,4,1152]{2,1,0:T(4,128)(2,1)S(1)} %all-to-all-done.in_ref), custom_call_target="tpu_custom_call" | custom-call | bytes 2097152 | tf_op jit(solution)/shard_map/split/pallas_call | solution.py:196
  51.6 0.0 collective-permute-done.1.refs_2_
  51.6 0.0 collective-permute-done.5.refs_5_
  51.6 3.5 %collective-permute-done.3.refs_3_ = bf16[528,1024]{1,0:T(8,128)(2,1)} collective-permute-done((bf16[528,1024]{1,0:T(8,128)(2,1)}, bf16[528,1024]{1,0:T(8,128)(2,1)}, u32[]{:S(2)}, u32[]{:S(2)}) %collective-permute-start.3) | collective-permute-done | bytes 1081376 | tf_op jit(solution)/shard_map/ppermute | solution.py:31
  55.0 0.0 collective-permute-done.7.refs_7_
  55.0 0.0 copy-start.6
  55.0 0.7 copy-done.6
  55.7 1.5 %cross_b.1 = (f32[1,1024]{1,0:T(1,128)S(1)}, f32[1,1024]{1,0:T(1,128)S(1)}, f32[1,1024]{1,0:T(1,128)S(1)}, f32[1,1024]{1,0:T(1,128)S(1)}, f32[8,1024]{1,0:T(8,128)}) custom-call(bf16[528,1024]{1,0:T(8,128)(2,1)S(1)} %norm_0.1.own0.refs_0_, bf16[528,1024]{1,0:T(8,128)(2,1)S(1)} %norm_1.1.own1.refs_1_, bf16[528,1024]{1,0:T(8,128)(2,1)} %collective-permute-done.1.refs_2_, ...), custom_call_target="tpu_custom_call" | custom-call | flops 5368709120 | bytes 8650752 | tf_op jit(solution)/shard_map/cross_b/pallas_call | solution.py:240
  57.2 1.9 %collective-permute-start.10 = (f32[1,1024]{1,0:T(1,128)S(1)}, f32[1,1024]{1,0:T(1,128)S(1)}, u32[]{:S(2)}, u32[]{:S(2)}) collective-permute-start(f32[1,1024]{1,0:T(1,128)S(1)} %get-tuple-element.13), channel_id=1, source_target_pairs={{32,34},{33,35},{34,36},{35,37},{36,38},{37,39},{38,40},{39,41},{4... | collective-permute-start | bytes 12296 | tf_op jit(solution)/shard_map/ppermute | solution.py:31
  59.1 1.3 %collective-permute-start.8 = (f32[1,1024]{1,0:T(1,128)S(1)}, f32[1,1024]{1,0:T(1,128)S(1)}, u32[]{:S(2)}, u32[]{:S(2)}) collective-permute-start(f32[1,1024]{1,0:T(1,128)S(1)} %get-tuple-element.11), channel_id=1, source_target_pairs={{1,0},{3,2},{5,4},{7,6},{9,8},{11,10},{13,12},{15,14},{17,16},{19,... | collective-permute-start | bytes 12296 | tf_op jit(solution)/shard_map/ppermute | solution.py:31
  60.4 1.3 %collective-permute-start.9 = (f32[1,1024]{1,0:T(1,128)S(1)}, f32[1,1024]{1,0:T(1,128)S(1)}, u32[]{:S(2)}, u32[]{:S(2)}) collective-permute-start(f32[1,1024]{1,0:T(1,128)S(1)} %get-tuple-element.12), channel_id=1, source_target_pairs={{1,2},{3,4},{5,6},{7,8},{9,10},{11,12},{13,14},{15,16},{17,18},{19... | collective-permute-start | bytes 12296 | tf_op jit(solution)/shard_map/ppermute | solution.py:31
  61.7 3.1 %collective-permute-done.10 = f32[1,1024]{1,0:T(1,128)S(1)} collective-permute-done((f32[1,1024]{1,0:T(1,128)S(1)}, f32[1,1024]{1,0:T(1,128)S(1)}, u32[]{:S(2)}, u32[]{:S(2)}) %collective-permute-start.10) | collective-permute-done | bytes 4128 | tf_op jit(solution)/shard_map/ppermute | solution.py:31
  64.8 21.7 %collective-permute-done.8 = f32[1,1024]{1,0:T(1,128)S(1)} collective-permute-done((f32[1,1024]{1,0:T(1,128)S(1)}, f32[1,1024]{1,0:T(1,128)S(1)}, u32[]{:S(2)}, u32[]{:S(2)}) %collective-permute-start.8) | collective-permute-done | bytes 4128 | tf_op jit(solution)/shard_map/ppermute | solution.py:31
  86.6 5.8 %collective-permute-done.9 = f32[1,1024]{1,0:T(1,128)S(1)} collective-permute-done((f32[1,1024]{1,0:T(1,128)S(1)}, f32[1,1024]{1,0:T(1,128)S(1)}, u32[]{:S(2)}, u32[]{:S(2)}) %collective-permute-start.9) | collective-permute-done | bytes 4128 | tf_op jit(solution)/shard_map/ppermute | solution.py:31
  92.4 0.6 fusion.1
Async XLA Ops:
  0.6 1.6 %copy-start = (bf16[1,1024,1024]{2,1,0:T(8,128)(2,1)S(1)}, bf16[1,1024,1024]{2,1,0:T(8,128)(2,1)}, u32[]{:S(2)}) copy-start(bf16[1,1024,1024]{2,1,0:T(8,128)(2,1)} %param.6) | copy-start | bytes 6291460
  2.2 0.7 copy-start.2
  3.2 13.4 %copy-start.5 = (f32[1,1024]{1,0:T(1,128)S(1)}, f32[1,1024]{1,0:T(1,128)}, u32[]{:S(2)}) copy-start(f32[1,1024]{1,0:T(1,128)} %prior_ref.1) | copy-start | bytes 12292
  3.3 24.7 %collective-permute-start = (bf16[528,1024]{1,0:T(8,128)(2,1)S(1)}, bf16[528,1024]{1,0:T(8,128)(2,1)}, u32[]{:S(2)}, u32[]{:S(2)}) collective-permute-start(bf16[528,1024]{1,0:T(8,128)(2,1)S(1)} %norm_0.1.own0.refs_0_), channel_id=1, source_target_pairs={{0,1},{2,3},{4,5},{6,7},{8,9},{10,11},{12,13},{14,15},{16,17},{18,... | collective-permute-start | bytes 3244040 | tf_op jit(solution)/shard_map/ppermute | solution.py:31
  5.9 13.2 %copy-start.1 = (bf16[256,1024]{1,0:T(8,128)(2,1)S(1)}, bf16[256,1024]{1,0:T(8,128)(2,1)}, u32[]{:S(2)}) copy-start(bf16[256,1024]{1,0:T(8,128)(2,1)} %rows_ref.1) | copy-start | bytes 1572868
  5.9 13.2 %copy-start.3 = (s32[256,1]{0,1:T(1,128)S(1)}, s32[256,1]{0,1:T(1,128)}, u32[]{:S(2)}) copy-start(s32[256,1]{0,1:T(1,128)} %param.11) | copy-start | bytes 3076
  5.9 13.2 %copy-start.4 = (s32[256]{0:T(256)S(1)}, s32[256]{0:T(256)}, u32[]{:S(2)}) copy-start(s32[256]{0:T(256)} %param.10) | copy-start | bytes 3076
  5.9 25.5 %collective-permute-start.2 = (bf16[528,1024]{1,0:T(8,128)(2,1)S(1)}, bf16[528,1024]{1,0:T(8,128)(2,1)}, u32[]{:S(2)}, u32[]{:S(2)}) collective-permute-start(bf16[528,1024]{1,0:T(8,128)(2,1)S(1)} %norm_1.1.own1.refs_1_), channel_id=1, source_target_pairs={{0,2},{1,3},{2,4},{3,5},{4,6},{5,7},{6,8},{7,9},{8,10},{9,11},{10,... | collective-permute-start | bytes 3244040 | tf_op jit(solution)/shard_map/ppermute | solution.py:31
  12.7 27.5 %collective-permute-start.6 = (bf16[528,1024]{1,0:T(8,128)(2,1)S(1)}, bf16[528,1024]{1,0:T(8,128)(2,1)}, u32[]{:S(2)}, u32[]{:S(2)}) collective-permute-start(bf16[528,1024]{1,0:T(8,128)(2,1)S(1)} %norm_1.1.own1.refs_1_), channel_id=1, source_target_pairs={{0,1},{2,3},{4,5},{6,7},{8,9},{10,11},{12,13},{14,15},{16,17},{18,... | collective-permute-start | bytes 3244040 | tf_op jit(solution)/shard_map/ppermute | solution.py:31
  15.0 26.9 %collective-permute-start.4 = (bf16[528,1024]{1,0:T(8,128)(2,1)S(1)}, bf16[528,1024]{1,0:T(8,128)(2,1)}, u32[]{:S(2)}, u32[]{:S(2)}) collective-permute-start(bf16[528,1024]{1,0:T(8,128)(2,1)S(1)} %norm_0.1.own0.refs_0_), channel_id=1, source_target_pairs={{1,3},{3,5},{5,7},{7,9},{9,11},{11,13},{13,15},{15,17},{17,19},{19... | collective-permute-start | bytes 3244040 | tf_op jit(solution)/shard_map/ppermute | solution.py:31
  20.8 29.6 %all-to-all-start = ((bf16[128,4,1152]{2,1,0:T(4,128)(2,1)}), bf16[128,4,1152]{2,1,0:T(4,128)(2,1)S(1)}, u32[]{:S(2)}, u32[]{:S(2)}) async-start(bf16[128,4,1152]{2,1,0:T(4,128)(2,1)} %place.1), calls=%async_computation | async-start | bytes 2359296 | tf_op jit(solution)/shard_map/all_to_all | solution.py:305
  28.0 23.6 %collective-permute-start.1 = (bf16[528,1024]{1,0:T(8,128)(2,1)}, bf16[528,1024]{1,0:T(8,128)(2,1)}, u32[]{:S(2)}, u32[]{:S(2)}) collective-permute-start(bf16[528,1024]{1,0:T(8,128)(2,1)} %collective-permute-done.refs_2_.refs_8_), channel_id=1, source_target_pairs={{1,3},{3,5},{5,7},{7,9},{9,11},{11,13},{13,15},{15,17},{17,19},{19... | collective-permute-start | bytes 3244040 | tf_op jit(solution)/shard_map/ppermute | solution.py:31
  29.7 21.9 %collective-permute-start.5 = (bf16[528,1024]{1,0:T(8,128)(2,1)}, bf16[528,1024]{1,0:T(8,128)(2,1)}, u32[]{:S(2)}, u32[]{:S(2)}) collective-permute-start(bf16[528,1024]{1,0:T(8,128)(2,1)} %collective-permute-done.refs_2_.refs_8_), channel_id=1, source_target_pairs={{1,31},{3,1},{5,3},{7,5},{9,7},{11,9},{13,11},{15,13},{17,15},{19,... | collective-permute-start | bytes 3244040 | tf_op jit(solution)/shard_map/ppermute | solution.py:31
  31.4 23.6 %collective-permute-start.3 = (bf16[528,1024]{1,0:T(8,128)(2,1)}, bf16[528,1024]{1,0:T(8,128)(2,1)}, u32[]{:S(2)}, u32[]{:S(2)}) collective-permute-start(bf16[528,1024]{1,0:T(8,128)(2,1)} %collective-permute-done.2.refs_3_.refs_6_), channel_id=1, source_target_pairs={{0,1},{2,3},{4,5},{6,7},{8,9},{10,11},{12,13},{14,15},{16,17},{18,... | collective-permute-start | bytes 3244040 | tf_op jit(solution)/shard_map/ppermute | solution.py:31
  40.2 14.8 %collective-permute-start.7 = (bf16[528,1024]{1,0:T(8,128)(2,1)}, bf16[528,1024]{1,0:T(8,128)(2,1)}, u32[]{:S(2)}, u32[]{:S(2)}) collective-permute-start(bf16[528,1024]{1,0:T(8,128)(2,1)} %collective-permute-done.6.refs_5_.refs_9_), channel_id=1, source_target_pairs={{1,31},{3,1},{5,3},{7,5},{9,7},{11,9},{13,11},{15,13},{17,15},{19,... | collective-permute-start | bytes 3244040 | tf_op jit(solution)/shard_map/ppermute | solution.py:31
  55.0 0.7 copy-start.6
  57.2 7.7 %collective-permute-start.10 = (f32[1,1024]{1,0:T(1,128)S(1)}, f32[1,1024]{1,0:T(1,128)S(1)}, u32[]{:S(2)}, u32[]{:S(2)}) collective-permute-start(f32[1,1024]{1,0:T(1,128)S(1)} %get-tuple-element.13), channel_id=1, source_target_pairs={{32,34},{33,35},{34,36},{35,37},{36,38},{37,39},{38,40},{39,41},{4... | collective-permute-start | bytes 12296 | tf_op jit(solution)/shard_map/ppermute | solution.py:31
  59.1 27.5 %collective-permute-start.8 = (f32[1,1024]{1,0:T(1,128)S(1)}, f32[1,1024]{1,0:T(1,128)S(1)}, u32[]{:S(2)}, u32[]{:S(2)}) collective-permute-start(f32[1,1024]{1,0:T(1,128)S(1)} %get-tuple-element.11), channel_id=1, source_target_pairs={{1,0},{3,2},{5,4},{7,6},{9,8},{11,10},{13,12},{15,14},{17,16},{19,... | collective-permute-start | bytes 12296 | tf_op jit(solution)/shard_map/ppermute | solution.py:31
  60.4 32.0 %collective-permute-start.9 = (f32[1,1024]{1,0:T(1,128)S(1)}, f32[1,1024]{1,0:T(1,128)S(1)}, u32[]{:S(2)}, u32[]{:S(2)}) collective-permute-start(f32[1,1024]{1,0:T(1,128)S(1)} %get-tuple-element.12), channel_id=1, source_target_pairs={{1,2},{3,4},{5,6},{7,8},{9,10},{11,12},{13,14},{15,16},{17,18},{19... | collective-permute-start | bytes 12296 | tf_op jit(solution)/shard_map/ppermute | solution.py:31

commit v9 on v7

--- a/solution.py
+++ b/solution.py
@@ -220,7 +220,7 @@
     rows = found.shape[1]
 
     def run(*refs):
-        held, refs = {"own0": refs[0], "own1": refs[1]}, refs[2:]
+        held, refs = dict(zip(("own0", "own1"), refs[: len(own)])), refs[len(own) :]
         inputs, where_ref, so_far_ref = refs[: len(names)], refs[len(names)], refs[len(names) + 1]
         outs, (buffers, sems) = refs[len(names) + 2 + len(after) : -2], refs[-2:]
         acc_ref = outs[-1]
@@ -239,11 +239,11 @@
     products = sum(len(a[1]) * len(b[1]) for a, b in heavy_pairs) / 4
     return pl.pallas_call(
         run,
-        in_specs=vmem(2)
+        in_specs=vmem(len(own))
         + [pl.BlockSpec(memory_space=pl.ANY)] * len(names)
         + smem()
         + vmem(1)
-        + vmem(len(after)),
+        + ([pl.BlockSpec(memory_space=pltpu.VMEM if last else pltpu.HBM)] * len(after)),
         out_specs=vmem(4 if last else 1),
         out_shape=[jax.ShapeDtypeStruct((1, rows), jnp.float32)] * (3 if last else 0)
         + [jax.ShapeDtypeStruct(found.shape, jnp.float32)],
@@ -307,6 +307,7 @@
     far0 = send(partner0, heavy_back)
     near_partner0 = send(partner0, heavy_ahead)
     near_partner1 = send(near1, to_heavy)
+    far1 = send(partner1, heavy_back)
 
     own = (OWN, [(0, "own0"), (1, "own1")])
     partner_both = (PARTNER, [(0, "partner0"), (1, "partner1")])
@@ -314,33 +315,33 @@
     (found,) = stage(
         "cross_a",
         (own0, own1),
-        {"partner0": partner0, "near1": near1, "near0": near0},
+        {"partner0": partner0, "near1": near1, "near0": near0, "partner1": partner1},
         [
             (own, (PARTNER, [(0, "partner0")])),
-            (own, (NEAR, [(1, "near1"), (0, "near0")])),
+            (own, near_both),
             ((PARTNER, [(0, "partner0")]), near_both),
+            (own, (PARTNER, [(1, "partner1")])),
+            ((PARTNER, [(1, "partner1")]), near_both),
         ],
         [(own, (NEAR_PARTNER, [(1, "near1")]))],
         where,
         found,
     )
-    far1 = send(partner1, heavy_back)
     (found,) = stage(
         "cross_b",
         (own0, own1),
         {
-            "partner1": partner1,
-            "near1": near1,
             "near0": near0,
             "far0": far0,
+            "near1": near1,
             "near_partner0": near_partner0,
+            "near_partner1": near_partner1,
             "partner0": partner0,
+            "partner1": partner1,
         },
         [
-            (own, (PARTNER, [(1, "partner1")])),
-            ((PARTNER, [(1, "partner1")]), near_both),
             ((FAR_PARTNER, [(0, "far0")]), near_both),
-            (own, (NEAR_PARTNER, [(0, "near_partner0")])),
+            (own, (NEAR_PARTNER, [(0, "near_partner0"), (1, "near_partner1")])),
             (partner_both, (NEAR_PARTNER, [(0, "near_partner0")])),
         ],
         [],
@@ -351,12 +352,9 @@
     from_partner = send(found[PARTNER : PARTNER + 1], to_light)
     mine, for_far, for_side, _ = stage(
         "cross_c",
-        (own0, own1),
-        {"near_partner1": near_partner1, "far1": far1, "near0": near0, "near1": near1},
-        [
-            (own, (NEAR_PARTNER, [(1, "near_partner1")])),
-            ((FAR_PARTNER, [(1, "far1")]), near_both),
-        ],
+        (),
+        {"far1": far1, "near0": near0, "near1": near1},
+        [((FAR_PARTNER, [(1, "far1")]), near_both)],
         [],
         where,
         found,

time: 87.4 us -> 86.7 us (level)
  transfers between devices with their start and end apart: 12 -> 12, of which waited for: 3 -> 4; matrix products, arithmetic and copies ran while one was open for 0% -> 0% of each run, Pallas kernels for 11% -> 11%
where the time goes in v9:
time: 86.7 us; the launch traced here: 86.2 us
  starting transfers between devices  38.8 us (45%)
  waiting for transfers between devices  31.7 us (37%)
  Pallas kernels  11.3 us (13%)
  local copies, waits for them, and re-layouts  2.98 us (3%)
    ppermute x11, starting transfers between devices, send(): return lax.ppermute(value, BOTH, pairs)  28.3 us
    ppermute x11, waiting for transfers between devices, send(): return lax.ppermute(value, BOTH, pairs)  24.5 us
    all_to_all x1, starting transfers between devices, body(): lax.all_to_all(outgoing, BOTH, split_axis=0, concat_axis=0, tiled=True)  10.5 us
    all_to_all x1, waiting for transfers between devices, body(): lax.all_to_all(outgoing, BOTH, split_axis=0, concat_axis=0, tiled=True)  7.25 us
    pallas_call x3, Pallas kernels, stage(): pl.pallas_call(run, in_specs=vmem(len(own)) + [pl.BlockSpec(memory_space=...  5.34 us
    unnamed x14, local copies, waits for them, and re-layouts  2.98 us
    pallas_call x1, Pallas kernels, body(): pl.pallas_call(within_kernel, in_specs=vmem(3), out_specs=pl.BlockSpec(me...  2.38 us
    pallas_call x1, Pallas kernels, placed_rows(): pl.pallas_call(place_kernel, in_specs=vmem(4), out_specs=pl.BlockSpec(mem...  1.76 us
  transfers between devices with their start and end apart: 12, of which 4 were waited for; matrix products, arithmetic and copies ran while one was open for 0% of the time, Pallas kernels for 11%

profile of v9, /device:TPU:0, one launch (start us, length us, event | category | flops | bytes accessed | tf_op | source)
XLA Modules:
  0.0 86.2 jit_solution(18374661094232706757)
XLA Ops:
  0.6 0.0 copy-start
  0.6 1.6 %copy-done = bf16[1,1024,1024]{2,1,0:T(8,128)(2,1)S(1)} copy-done((bf16[1,1024,1024]{2,1,0:T(8,128)(2,1)S(1)}, bf16[1,1024,1024]{2,1,0:T(8,128)(2,1)}, u32[]{:S(2)}) %copy-start) | copy-done | bytes 2097176
  2.2 0.0 copy-start.2
  2.2 0.7 copy-done.2
  2.9 0.3 norm_0.1.own0.refs_0_
  3.2 0.0 copy-start.5
  3.3 4.6 %collective-permute-start.4 = (bf16[528,1024]{1,0:T(8,128)(2,1)S(1)}, bf16[528,1024]{1,0:T(8,128)(2,1)}, u32[]{:S(2)}, u32[]{:S(2)}) collective-permute-start(bf16[528,1024]{1,0:T(8,128)(2,1)S(1)} %norm_0.1.own0.refs_0_), channel_id=1, source_target_pairs={{0,1},{2,3},{4,5},{6,7},{8,9},{10,11},{12,13},{14,15},{16,17},{18,... | collective-permute-start | bytes 3244040 | tf_op jit(solution)/shard_map/ppermute | solution.py:31
  7.9 0.3 norm_1.1.own1.refs_1_
  8.2 0.0 copy-start.1
  8.2 0.0 copy-start.3
  8.2 0.0 copy-start.4
  8.2 1.6 %collective-permute-start.3 = (bf16[528,1024]{1,0:T(8,128)(2,1)S(1)}, bf16[528,1024]{1,0:T(8,128)(2,1)}, u32[]{:S(2)}, u32[]{:S(2)}) collective-permute-start(bf16[528,1024]{1,0:T(8,128)(2,1)S(1)} %norm_1.1.own1.refs_1_), channel_id=1, source_target_pairs={{0,2},{1,3},{2,4},{3,5},{4,6},{5,7},{6,8},{7,9},{8,10},{9,11},{10,... | collective-permute-start | bytes 3244040 | tf_op jit(solution)/shard_map/ppermute | solution.py:31
  9.8 2.3 %collective-permute-start = (bf16[528,1024]{1,0:T(8,128)(2,1)S(1)}, bf16[528,1024]{1,0:T(8,128)(2,1)}, u32[]{:S(2)}, u32[]{:S(2)}) collective-permute-start(bf16[528,1024]{1,0:T(8,128)(2,1)S(1)} %norm_1.1.own1.refs_1_), channel_id=1, source_target_pairs={{0,1},{2,3},{4,5},{6,7},{8,9},{10,11},{12,13},{14,15},{16,17},{18,... | collective-permute-start | bytes 3244040 | tf_op jit(solution)/shard_map/ppermute | solution.py:31
  12.1 1.7 %collective-permute-start.2 = (bf16[528,1024]{1,0:T(8,128)(2,1)S(1)}, bf16[528,1024]{1,0:T(8,128)(2,1)}, u32[]{:S(2)}, u32[]{:S(2)}) collective-permute-start(bf16[528,1024]{1,0:T(8,128)(2,1)S(1)} %norm_0.1.own0.refs_0_), channel_id=1, source_target_pairs={{1,3},{3,5},{5,7},{7,9},{9,11},{11,13},{13,15},{15,17},{17,19},{19... | collective-permute-start | bytes 3244040 | tf_op jit(solution)/shard_map/ppermute | solution.py:31
  13.7 0.0 copy-done.5
  13.7 2.4 %within.1.refs_7_.after_ref = f32[8,1024]{1,0:T(8,128)S(1)} custom-call(bf16[528,1024]{1,0:T(8,128)(2,1)S(1)} %norm_0.1.own0.refs_0_, bf16[528,1024]{1,0:T(8,128)(2,1)S(1)} %norm_1.1.own1.refs_1_, f32[1,1024]{1,0:T(1,128)S(1)} %copy-done.5), custom_call_target="tpu_custom_call" | custom-call | flops 2147483648 | bytes 2097152 | tf_op jit(solution)/shard_map/within/pallas_call | solution.py:293
  16.1 0.0 copy-done.1
  16.1 0.0 copy-done.3
  16.1 0.0 copy-done.4
  16.1 1.8 %place.1 = bf16[128,4,1152]{2,1,0:T(4,128)(2,1)} custom-call(bf16[256,1024]{1,0:T(8,128)(2,1)S(1)} %copy-done.1, s32[1,256]{1,0:T(1,128)S(1)} %bitcast.8, s32[1,256]{1,0:T(1,128)S(1)} %bitcast.9, f32[8,1024]{1,0:T(8,128)S(1)} %within.1.refs_7_.after_ref), custom_call_target="tpu_custom_call" | custom-call | flops 268435456 | bytes 1572864 | tf_op jit(solution)/shard_map/place/pallas_call | solution.py:172
  17.9 10.5 %all-to-all-start = ((bf16[128,4,1152]{2,1,0:T(4,128)(2,1)}), bf16[128,4,1152]{2,1,0:T(4,128)(2,1)S(1)}, u32[]{:S(2)}, u32[]{:S(2)}) async-start(bf16[128,4,1152]{2,1,0:T(4,128)(2,1)} %place.1), calls=%async_computation | async-start | bytes 2359296 | tf_op jit(solution)/shard_map/all_to_all | solution.py:305
  28.4 0.0 collective-permute-done.4.refs_2_.refs_7_
  28.4 1.7 %collective-permute-start.5 = (bf16[528,1024]{1,0:T(8,128)(2,1)}, bf16[528,1024]{1,0:T(8,128)(2,1)}, u32[]{:S(2)}, u32[]{:S(2)}) collective-permute-start(bf16[528,1024]{1,0:T(8,128)(2,1)} %collective-permute-done.4.refs_2_.refs_7_), channel_id=1, source_target_pairs={{1,31},{3,1},{5,3},{7,5},{9,7},{11,9},{13,11},{15,13},{17,15},{19,... | collective-permute-start | bytes 3244040 | tf_op jit(solution)/shard_map/ppermute | solution.py:31
  30.0 1.7 %collective-permute-start.6 = (bf16[528,1024]{1,0:T(8,128)(2,1)}, bf16[528,1024]{1,0:T(8,128)(2,1)}, u32[]{:S(2)}, u32[]{:S(2)}) collective-permute-start(bf16[528,1024]{1,0:T(8,128)(2,1)} %collective-permute-done.4.refs_2_.refs_7_), channel_id=1, source_target_pairs={{1,3},{3,5},{5,7},{7,9},{9,11},{11,13},{13,15},{15,17},{17,19},{19... | collective-permute-start | bytes 3244040 | tf_op jit(solution)/shard_map/ppermute | solution.py:31
  31.8 0.0 collective-permute-done.3.refs_3_.refs_4_.refs_2_
  31.8 9.9 %collective-permute-start.7 = (bf16[528,1024]{1,0:T(8,128)(2,1)}, bf16[528,1024]{1,0:T(8,128)(2,1)}, u32[]{:S(2)}, u32[]{:S(2)}) collective-permute-start(bf16[528,1024]{1,0:T(8,128)(2,1)} %collective-permute-done.3.refs_3_.refs_4_.refs_2_), channel_id=1, source_target_pairs={{0,1},{2,3},{4,5},{6,7},{8,9},{10,11},{12,13},{14,15},{16,17},{18,... | collective-permute-start | bytes 3244040 | tf_op jit(solution)/shard_map/ppermute | solution.py:31
  41.7 0.0 collective-permute-done.refs_5_.refs_8_
  41.7 1.7 %collective-permute-start.1 = (bf16[528,1024]{1,0:T(8,128)(2,1)}, bf16[528,1024]{1,0:T(8,128)(2,1)}, u32[]{:S(2)}, u32[]{:S(2)}) collective-permute-start(bf16[528,1024]{1,0:T(8,128)(2,1)} %collective-permute-done.refs_5_.refs_8_), channel_id=1, source_target_pairs={{1,31},{3,1},{5,3},{7,5},{9,7},{11,9},{13,11},{15,13},{17,15},{19,... | collective-permute-start | bytes 3244040 | tf_op jit(solution)/shard_map/ppermute | solution.py:31
  43.3 0.1 pad_add_fusion.refs_6_.refs_9_.refs_3_
  43.4 0.0 collective-permute-done.2.refs_4_.refs_2_.refs_1_
  43.4 3.3 %cross_a.1.refs_10_ = f32[8,1024]{1,0:T(8,128)S(1)} custom-call(bf16[528,1024]{1,0:T(8,128)(2,1)S(1)} %norm_0.1.own0.refs_0_, bf16[528,1024]{1,0:T(8,128)(2,1)S(1)} %norm_1.1.own1.refs_1_, bf16[528,1024]{1,0:T(8,128)(2,1)} %collective-permute-done.4.refs_2_.refs_7_, bf16[528,1024]{1,0:T(8,128)(2,1)} %collective-permute-done.3.refs_3_.refs_4_.refs_2_, ...), custom_call_target="tpu_custom_call" | custom-call | flops 6442450944 | bytes 4325376 | tf_op jit(solution)/shard_map/cross_a/pallas_call | solution.py:240
  46.7 7.2 %all-to-all-done.in_ref = bf16[128,4,1152]{2,1,0:T(4,128)(2,1)S(1)} async-done(((bf16[128,4,1152]{2,1,0:T(4,128)(2,1)}), bf16[128,4,1152]{2,1,0:T(4,128)(2,1)S(1)}, u32[]{:S(2)}, u32[]{:S(2)}) %all-to-all-start) | async-done | bytes 1179680 | tf_op jit(solution)/shard_map/all_to_all | solution.py:305
  54.0 1.1 %split.1 = (bf16[512,1024]{1,0:T(8,128)(2,1)}, s32[1,512]{1,0:T(1,128)}) custom-call(bf16[128,4,1152]{2,1,0:T(4,128)(2,1)S(1)} %all-to-all-done.in_ref), custom_call_target="tpu_custom_call" | custom-call | bytes 2097152 | tf_op jit(solution)/shard_map/split/pallas_call | solution.py:196
  55.1 0.0 collective-permute-done.5.refs_3_
  55.1 0.0 collective-permute-done.6.refs_5_
  55.1 0.3 collective-permute-done.7.refs_6_
  55.4 0.0 copy-start.6
  55.4 0.7 copy-done.6
  56.1 0.8 cross_b.1.refs_4_
  56.9 1.3 %collective-permute-start.8 = (f32[1,1024]{1,0:T(1,128)S(1)}, f32[1,1024]{1,0:T(1,128)S(1)}, u32[]{:S(2)}, u32[]{:S(2)}) collective-permute-start(f32[1,1024]{1,0:T(1,128)S(1)} %slice.4), channel_id=1, source_target_pairs={{1,0},{3,2},{5,4},{7,6},{9,8},{11,10},{13,12},{15,14},{17,16},{19,... | collective-permute-start | bytes 12296 | tf_op jit(solution)/shard_map/ppermute | solution.py:31
  58.2 0.0 collective-permute-done.1.refs_0_
  58.2 15.8 %collective-permute-done.8.refs_5_ = f32[1,1024]{1,0:T(1,128)S(1)} collective-permute-done((f32[1,1024]{1,0:T(1,128)S(1)}, f32[1,1024]{1,0:T(1,128)S(1)}, u32[]{:S(2)}, u32[]{:S(2)}) %collective-permute-start.8) | collective-permute-done | bytes 4128 | tf_op jit(solution)/shard_map/ppermute | solution.py:31
  74.0 1.2 %cross_c.1 = (f32[1,1024]{1,0:T(1,128)S(1)}, f32[1,1024]{1,0:T(1,128)S(1)}, f32[1,1024]{1,0:T(1,128)S(1)}, f32[8,1024]{1,0:T(8,128)}) custom-call(bf16[528,1024]{1,0:T(8,128)(2,1)} %collective-permute-done.1.refs_0_, bf16[528,1024]{1,0:T(8,128)(2,1)} %collective-permute-done.2.refs_4_.refs_2_.refs_1_, ...), custom_call_target="tpu_custom_call" | custom-call | flops 1073741824 | bytes 3244032 | tf_op jit(solution)/shard_map/cross_c/pallas_call | solution.py:240
  75.2 0.7 collective-permute-start.10
  75.9 1.3 %collective-permute-start.9 = (f32[1,1024]{1,0:T(1,128)S(1)}, f32[1,1024]{1,0:T(1,128)S(1)}, u32[]{:S(2)}, u32[]{:S(2)}) collective-permute-start(f32[1,1024]{1,0:T(1,128)S(1)} %get-tuple-element.10), channel_id=1, source_target_pairs={{1,2},{3,4},{5,6},{7,8},{9,10},{11,12},{13,14},{15,16},{17,18},{19... | collective-permute-start | bytes 12296 | tf_op jit(solution)/shard_map/ppermute | solution.py:31
  77.2 0.0 collective-permute-done.10
  77.2 8.4 %collective-permute-done.9 = f32[1,1024]{1,0:T(1,128)S(1)} collective-permute-done((f32[1,1024]{1,0:T(1,128)S(1)}, f32[1,1024]{1,0:T(1,128)S(1)}, u32[]{:S(2)}, u32[]{:S(2)}) %collective-permute-start.9) | collective-permute-done | bytes 4128 | tf_op jit(solution)/shard_map/ppermute | solution.py:31
  85.6 0.6 fusion.1
  (1 shorter events, 0.0 us)
Async XLA Ops:
  0.6 1.6 %copy-start = (bf16[1,1024,1024]{2,1,0:T(8,128)(2,1)S(1)}, bf16[1,1024,1024]{2,1,0:T(8,128)(2,1)}, u32[]{:S(2)}) copy-start(bf16[1,1024,1024]{2,1,0:T(8,128)(2,1)} %param.6) | copy-start | bytes 6291460
  2.2 0.7 copy-start.2
  3.2 10.5 %copy-start.5 = (f32[1,1024]{1,0:T(1,128)S(1)}, f32[1,1024]{1,0:T(1,128)}, u32[]{:S(2)}) copy-start(f32[1,1024]{1,0:T(1,128)} %prior_ref.1) | copy-start | bytes 12292
  3.3 25.1 %collective-permute-start.4 = (bf16[528,1024]{1,0:T(8,128)(2,1)S(1)}, bf16[528,1024]{1,0:T(8,128)(2,1)}, u32[]{:S(2)}, u32[]{:S(2)}) collective-permute-start(bf16[528,1024]{1,0:T(8,128)(2,1)S(1)} %norm_0.1.own0.refs_0_), channel_id=1, source_target_pairs={{0,1},{2,3},{4,5},{6,7},{8,9},{10,11},{12,13},{14,15},{16,17},{18,... | collective-permute-start | bytes 3244040 | tf_op jit(solution)/shard_map/ppermute | solution.py:31
  8.2 7.9 %copy-start.1 = (bf16[256,1024]{1,0:T(8,128)(2,1)S(1)}, bf16[256,1024]{1,0:T(8,128)(2,1)}, u32[]{:S(2)}) copy-start(bf16[256,1024]{1,0:T(8,128)(2,1)} %rows_ref.1) | copy-start | bytes 1572868
  8.2 7.9 %copy-start.3 = (s32[256,1]{0,1:T(1,128)S(1)}, s32[256,1]{0,1:T(1,128)}, u32[]{:S(2)}) copy-start(s32[256,1]{0,1:T(1,128)} %param.11) | copy-start | bytes 3076
  8.2 7.9 %copy-start.4 = (s32[256]{0:T(256)S(1)}, s32[256]{0:T(256)}, u32[]{:S(2)}) copy-start(s32[256]{0:T(256)} %param.10) | copy-start | bytes 3076
  8.2 23.6 %collective-permute-start.3 = (bf16[528,1024]{1,0:T(8,128)(2,1)S(1)}, bf16[528,1024]{1,0:T(8,128)(2,1)}, u32[]{:S(2)}, u32[]{:S(2)}) collective-permute-start(bf16[528,1024]{1,0:T(8,128)(2,1)S(1)} %norm_1.1.own1.refs_1_), channel_id=1, source_target_pairs={{0,2},{1,3},{2,4},{3,5},{4,6},{5,7},{6,8},{7,9},{8,10},{9,11},{10,... | collective-permute-start | bytes 3244040 | tf_op jit(solution)/shard_map/ppermute | solution.py:31
  9.8 31.9 %collective-permute-start = (bf16[528,1024]{1,0:T(8,128)(2,1)S(1)}, bf16[528,1024]{1,0:T(8,128)(2,1)}, u32[]{:S(2)}, u32[]{:S(2)}) collective-permute-start(bf16[528,1024]{1,0:T(8,128)(2,1)S(1)} %norm_1.1.own1.refs_1_), channel_id=1, source_target_pairs={{0,1},{2,3},{4,5},{6,7},{8,9},{10,11},{12,13},{14,15},{16,17},{18,... | collective-permute-start | bytes 3244040 | tf_op jit(solution)/shard_map/ppermute | solution.py:31
  12.1 31.4 %collective-permute-start.2 = (bf16[528,1024]{1,0:T(8,128)(2,1)S(1)}, bf16[528,1024]{1,0:T(8,128)(2,1)}, u32[]{:S(2)}, u32[]{:S(2)}) collective-permute-start(bf16[528,1024]{1,0:T(8,128)(2,1)S(1)} %norm_0.1.own0.refs_0_), channel_id=1, source_target_pairs={{1,3},{3,5},{5,7},{7,9},{9,11},{11,13},{13,15},{15,17},{17,19},{19... | collective-permute-start | bytes 3244040 | tf_op jit(solution)/shard_map/ppermute | solution.py:31
  17.9 36.1 %all-to-all-start = ((bf16[128,4,1152]{2,1,0:T(4,128)(2,1)}), bf16[128,4,1152]{2,1,0:T(4,128)(2,1)S(1)}, u32[]{:S(2)}, u32[]{:S(2)}) async-start(bf16[128,4,1152]{2,1,0:T(4,128)(2,1)} %place.1), calls=%async_computation | async-start | bytes 2359296 | tf_op jit(solution)/shard_map/all_to_all | solution.py:305
  28.4 26.7 %collective-permute-start.5 = (bf16[528,1024]{1,0:T(8,128)(2,1)}, bf16[528,1024]{1,0:T(8,128)(2,1)}, u32[]{:S(2)}, u32[]{:S(2)}) collective-permute-start(bf16[528,1024]{1,0:T(8,128)(2,1)} %collective-permute-done.4.refs_2_.refs_7_), channel_id=1, source_target_pairs={{1,31},{3,1},{5,3},{7,5},{9,7},{11,9},{13,11},{15,13},{17,15},{19,... | collective-permute-start | bytes 3244040 | tf_op jit(solution)/shard_map/ppermute | solution.py:31
  30.0 25.1 %collective-permute-start.6 = (bf16[528,1024]{1,0:T(8,128)(2,1)}, bf16[528,1024]{1,0:T(8,128)(2,1)}, u32[]{:S(2)}, u32[]{:S(2)}) collective-permute-start(bf16[528,1024]{1,0:T(8,128)(2,1)} %collective-permute-done.4.refs_2_.refs_7_), channel_id=1, source_target_pairs={{1,3},{3,5},{5,7},{7,9},{9,11},{11,13},{13,15},{15,17},{17,19},{19... | collective-permute-start | bytes 3244040 | tf_op jit(solution)/shard_map/ppermute | solution.py:31
  31.8 23.6 %collective-permute-start.7 = (bf16[528,1024]{1,0:T(8,128)(2,1)}, bf16[528,1024]{1,0:T(8,128)(2,1)}, u32[]{:S(2)}, u32[]{:S(2)}) collective-permute-start(bf16[528,1024]{1,0:T(8,128)(2,1)} %collective-permute-done.3.refs_3_.refs_4_.refs_2_), channel_id=1, source_target_pairs={{0,1},{2,3},{4,5},{6,7},{8,9},{10,11},{12,13},{14,15},{16,17},{18,... | collective-permute-start | bytes 3244040 | tf_op jit(solution)/shard_map/ppermute | solution.py:31
  41.7 16.6 %collective-permute-start.1 = (bf16[528,1024]{1,0:T(8,128)(2,1)}, bf16[528,1024]{1,0:T(8,128)(2,1)}, u32[]{:S(2)}, u32[]{:S(2)}) collective-permute-start(bf16[528,1024]{1,0:T(8,128)(2,1)} %collective-permute-done.refs_5_.refs_8_), channel_id=1, source_target_pairs={{1,31},{3,1},{5,3},{7,5},{9,7},{11,9},{13,11},{15,13},{17,15},{19,... | collective-permute-start | bytes 3244040 | tf_op jit(solution)/shard_map/ppermute | solution.py:31
  55.4 0.7 copy-start.6
  56.9 17.1 %collective-permute-start.8 = (f32[1,1024]{1,0:T(1,128)S(1)}, f32[1,1024]{1,0:T(1,128)S(1)}, u32[]{:S(2)}, u32[]{:S(2)}) collective-permute-start(f32[1,1024]{1,0:T(1,128)S(1)} %slice.4), channel_id=1, source_target_pairs={{1,0},{3,2},{5,4},{7,6},{9,8},{11,10},{13,12},{15,14},{17,16},{19,... | collective-permute-start | bytes 12296 | tf_op jit(solution)/shard_map/ppermute | solution.py:31
  75.2 2.0 %collective-permute-start.10 = (f32[1,1024]{1,0:T(1,128)S(1)}, f32[1,1024]{1,0:T(1,128)S(1)}, u32[]{:S(2)}, u32[]{:S(2)}) collective-permute-start(f32[1,1024]{1,0:T(1,128)S(1)} %get-tuple-element.11), channel_id=1, source_target_pairs={{32,34},{33,35},{34,36},{35,37},{36,38},{37,39},{38,40},{39,41},{4... | collective-permute-start | bytes 12296 | tf_op jit(solution)/shard_map/ppermute | solution.py:31
  75.9 9.7 %collective-permute-start.9 = (f32[1,1024]{1,0:T(1,128)S(1)}, f32[1,1024]{1,0:T(1,128)S(1)}, u32[]{:S(2)}, u32[]{:S(2)}) collective-permute-start(f32[1,1024]{1,0:T(1,128)S(1)} %get-tuple-element.10), channel_id=1, source_target_pairs={{1,2},{3,4},{5,6},{7,8},{9,10},{11,12},{13,14},{15,16},{17,18},{19... | collective-permute-start | bytes 12296 | tf_op jit(solution)/shard_map/ppermute | solution.py:31

commit v10 on v9

--- a/solution.py
+++ b/solution.py
@@ -8,7 +8,6 @@
 CAP = 4
 LOWEST = -2.0
 EXTRA = 16
-AHEAD = 3
 BOTH = ("grp", "blk")
 OWN, PARTNER, NEAR, NEAR_PARTNER, FAR_PARTNER = range(5)
 
@@ -90,19 +89,13 @@
             name: pltpu.make_async_copy(refs[names.index(name)], buffers.at[k], sems.at[k])
             for k, name in enumerate(needed)
         }
-        started, there = set(), set()
+        for copy in copies.values():
+            copy.start()
+        for copy in copies.values():
+            copy.wait()
 
         def arrive(name):
-            if name in held:
-                return held[name]
-            if name not in there:
-                for k, other in enumerate(needed):
-                    if other not in started and k <= needed.index(name) + AHEAD:
-                        copies[other].start()
-                        started.add(other)
-                copies[name].wait()
-                there.add(name)
-            return buffers.at[needed.index(name)]
+            return held[name] if name in held else buffers.at[needed.index(name)]
 
         for (first, first_halves), (second, second_halves) in pairs:
             if core == 0:

time: 86.7 us -> 87.6 us (1.010)
  waiting for transfers between devices: 31.7 us -> 32.6 us
    ppermute x11, waiting for transfers between devices: 24.5 us -> 25.4 us  [send(): return lax.ppermute(value, BOTH, pairs)]
where the time goes in v10:
time: 87.6 us; the launch traced here: 87.1 us
  starting transfers between devices  38.8 us (44%)
  waiting for transfers between devices  32.6 us (37%)
  Pallas kernels  11.3 us (13%)
  local copies, waits for them, and re-layouts  2.98 us (3%)
    ppermute x11, starting transfers between devices, send(): return lax.ppermute(value, BOTH, pairs)  28.3 us
    ppermute x11, waiting for transfers between devices, send(): return lax.ppermute(value, BOTH, pairs)  25.4 us
    all_to_all x1, starting transfers between devices, body(): lax.all_to_all(outgoing, BOTH, split_axis=0, concat_axis=0, tiled=True)  10.5 us
    all_to_all x1, waiting for transfers between devices, body(): lax.all_to_all(outgoing, BOTH, split_axis=0, concat_axis=0, tiled=True)  7.25 us
    pallas_call x3, Pallas kernels, stage(): pl.pallas_call(run, in_specs=vmem(len(own)) + [pl.BlockSpec(memory_space=...  5.34 us
    unnamed x14, local copies, waits for them, and re-layouts  2.98 us
    pallas_call x1, Pallas kernels, body(): pl.pallas_call(within_kernel, in_specs=vmem(3), out_specs=pl.BlockSpec(me...  2.38 us
    pallas_call x1, Pallas kernels, placed_rows(): pl.pallas_call(place_kernel, in_specs=vmem(4), out_specs=pl.BlockSpec(mem...  1.76 us
  transfers between devices with their start and end apart: 12, of which 4 were waited for; matrix products, arithmetic and copies ran while one was open for 0% of the time, Pallas kernels for 11%

profile of v10, /device:TPU:0, one launch (start us, length us, event | category | flops | bytes accessed | tf_op | source)
XLA Modules:
  0.0 87.1 jit_solution(6561793271401098760)
XLA Ops:
  0.6 0.0 copy-start
  0.6 1.6 %copy-done = bf16[1,1024,1024]{2,1,0:T(8,128)(2,1)S(1)} copy-done((bf16[1,1024,1024]{2,1,0:T(8,128)(2,1)S(1)}, bf16[1,1024,1024]{2,1,0:T(8,128)(2,1)}, u32[]{:S(2)}) %copy-start) | copy-done | bytes 2097176
  2.2 0.0 copy-start.2
  2.2 0.7 copy-done.2
  2.9 0.3 norm_0.1.own0.refs_0_
  3.2 0.0 copy-start.5
  3.3 4.6 %collective-permute-start.4 = (bf16[528,1024]{1,0:T(8,128)(2,1)S(1)}, bf16[528,1024]{1,0:T(8,128)(2,1)}, u32[]{:S(2)}, u32[]{:S(2)}) collective-permute-start(bf16[528,1024]{1,0:T(8,128)(2,1)S(1)} %norm_0.1.own0.refs_0_), channel_id=1, source_target_pairs={{0,1},{2,3},{4,5},{6,7},{8,9},{10,11},{12,13},{14,15},{16,17},{18,... | collective-permute-start | bytes 3244040 | tf_op jit(solution)/shard_map/ppermute | solution.py:30
  7.9 0.3 norm_1.1.own1.refs_1_
  8.2 0.0 copy-start.1
  8.2 0.0 copy-start.3
  8.2 0.0 copy-start.4
  8.2 1.6 %collective-permute-start.3 = (bf16[528,1024]{1,0:T(8,128)(2,1)S(1)}, bf16[528,1024]{1,0:T(8,128)(2,1)}, u32[]{:S(2)}, u32[]{:S(2)}) collective-permute-start(bf16[528,1024]{1,0:T(8,128)(2,1)S(1)} %norm_1.1.own1.refs_1_), channel_id=1, source_target_pairs={{0,2},{1,3},{2,4},{3,5},{4,6},{5,7},{6,8},{7,9},{8,10},{9,11},{10,... | collective-permute-start | bytes 3244040 | tf_op jit(solution)/shard_map/ppermute | solution.py:30
  9.8 2.3 %collective-permute-start = (bf16[528,1024]{1,0:T(8,128)(2,1)S(1)}, bf16[528,1024]{1,0:T(8,128)(2,1)}, u32[]{:S(2)}, u32[]{:S(2)}) collective-permute-start(bf16[528,1024]{1,0:T(8,128)(2,1)S(1)} %norm_1.1.own1.refs_1_), channel_id=1, source_target_pairs={{0,1},{2,3},{4,5},{6,7},{8,9},{10,11},{12,13},{14,15},{16,17},{18,... | collective-permute-start | bytes 3244040 | tf_op jit(solution)/shard_map/ppermute | solution.py:30
  12.1 1.7 %collective-permute-start.2 = (bf16[528,1024]{1,0:T(8,128)(2,1)S(1)}, bf16[528,1024]{1,0:T(8,128)(2,1)}, u32[]{:S(2)}, u32[]{:S(2)}) collective-permute-start(bf16[528,1024]{1,0:T(8,128)(2,1)S(1)} %norm_0.1.own0.refs_0_), channel_id=1, source_target_pairs={{1,3},{3,5},{5,7},{7,9},{9,11},{11,13},{13,15},{15,17},{17,19},{19... | collective-permute-start | bytes 3244040 | tf_op jit(solution)/shard_map/ppermute | solution.py:30
  13.7 0.0 copy-done.5
  13.7 2.4 %within.1.refs_7_.after_ref = f32[8,1024]{1,0:T(8,128)S(1)} custom-call(bf16[528,1024]{1,0:T(8,128)(2,1)S(1)} %norm_0.1.own0.refs_0_, bf16[528,1024]{1,0:T(8,128)(2,1)S(1)} %norm_1.1.own1.refs_1_, f32[1,1024]{1,0:T(1,128)S(1)} %copy-done.5), custom_call_target="tpu_custom_call" | custom-call | flops 2147483648 | bytes 2097152 | tf_op jit(solution)/shard_map/within/pallas_call | solution.py:286
  16.1 0.0 copy-done.1
  16.1 0.0 copy-done.3
  16.1 0.0 copy-done.4
  16.1 1.8 %place.1 = bf16[128,4,1152]{2,1,0:T(4,128)(2,1)} custom-call(bf16[256,1024]{1,0:T(8,128)(2,1)S(1)} %copy-done.1, s32[1,256]{1,0:T(1,128)S(1)} %bitcast.8, s32[1,256]{1,0:T(1,128)S(1)} %bitcast.9, f32[8,1024]{1,0:T(8,128)S(1)} %within.1.refs_7_.after_ref), custom_call_target="tpu_custom_call" | custom-call | flops 268435456 | bytes 1572864 | tf_op jit(solution)/shard_map/place/pallas_call | solution.py:165
  17.9 10.5 %all-to-all-start = ((bf16[128,4,1152]{2,1,0:T(4,128)(2,1)}), bf16[128,4,1152]{2,1,0:T(4,128)(2,1)S(1)}, u32[]{:S(2)}, u32[]{:S(2)}) async-start(bf16[128,4,1152]{2,1,0:T(4,128)(2,1)} %place.1), calls=%async_computation | async-start | bytes 2359296 | tf_op jit(solution)/shard_map/all_to_all | solution.py:298
  28.4 0.0 collective-permute-done.4.refs_2_.refs_7_
  28.4 1.7 %collective-permute-start.5 = (bf16[528,1024]{1,0:T(8,128)(2,1)}, bf16[528,1024]{1,0:T(8,128)(2,1)}, u32[]{:S(2)}, u32[]{:S(2)}) collective-permute-start(bf16[528,1024]{1,0:T(8,128)(2,1)} %collective-permute-done.4.refs_2_.refs_7_), channel_id=1, source_target_pairs={{1,31},{3,1},{5,3},{7,5},{9,7},{11,9},{13,11},{15,13},{17,15},{19,... | collective-permute-start | bytes 3244040 | tf_op jit(solution)/shard_map/ppermute | solution.py:30
  30.0 1.7 %collective-permute-start.6 = (bf16[528,1024]{1,0:T(8,128)(2,1)}, bf16[528,1024]{1,0:T(8,128)(2,1)}, u32[]{:S(2)}, u32[]{:S(2)}) collective-permute-start(bf16[528,1024]{1,0:T(8,128)(2,1)} %collective-permute-done.4.refs_2_.refs_7_), channel_id=1, source_target_pairs={{1,3},{3,5},{5,7},{7,9},{9,11},{11,13},{13,15},{15,17},{17,19},{19... | collective-permute-start | bytes 3244040 | tf_op jit(solution)/shard_map/ppermute | solution.py:30
  31.8 0.0 collective-permute-done.3.refs_3_.refs_4_.refs_2_
  31.8 9.9 %collective-permute-start.7 = (bf16[528,1024]{1,0:T(8,128)(2,1)}, bf16[528,1024]{1,0:T(8,128)(2,1)}, u32[]{:S(2)}, u32[]{:S(2)}) collective-permute-start(bf16[528,1024]{1,0:T(8,128)(2,1)} %collective-permute-done.3.refs_3_.refs_4_.refs_2_), channel_id=1, source_target_pairs={{0,1},{2,3},{4,5},{6,7},{8,9},{10,11},{12,13},{14,15},{16,17},{18,... | collective-permute-start | bytes 3244040 | tf_op jit(solution)/shard_map/ppermute | solution.py:30
  41.7 0.0 collective-permute-done.refs_5_.refs_8_
  41.7 1.7 %collective-permute-start.1 = (bf16[528,1024]{1,0:T(8,128)(2,1)}, bf16[528,1024]{1,0:T(8,128)(2,1)}, u32[]{:S(2)}, u32[]{:S(2)}) collective-permute-start(bf16[528,1024]{1,0:T(8,128)(2,1)} %collective-permute-done.refs_5_.refs_8_), channel_id=1, source_target_pairs={{1,31},{3,1},{5,3},{7,5},{9,7},{11,9},{13,11},{15,13},{17,15},{19,... | collective-permute-start | bytes 3244040 | tf_op jit(solution)/shard_map/ppermute | solution.py:30
  43.3 0.1 pad_add_fusion.refs_6_.refs_9_.refs_3_
  43.4 0.0 collective-permute-done.2.refs_4_.refs_2_.refs_1_
  43.4 3.3 %cross_a.1.refs_10_ = f32[8,1024]{1,0:T(8,128)S(1)} custom-call(bf16[528,1024]{1,0:T(8,128)(2,1)S(1)} %norm_0.1.own0.refs_0_, bf16[528,1024]{1,0:T(8,128)(2,1)S(1)} %norm_1.1.own1.refs_1_, bf16[528,1024]{1,0:T(8,128)(2,1)} %collective-permute-done.4.refs_2_.refs_7_, bf16[528,1024]{1,0:T(8,128)(2,1)} %collective-permute-done.3.refs_3_.refs_4_.refs_2_, ...), custom_call_target="tpu_custom_call" | custom-call | flops 6442450944 | bytes 4325376 | tf_op jit(solution)/shard_map/cross_a/pallas_call | solution.py:233
  46.7 7.2 %all-to-all-done.in_ref = bf16[128,4,1152]{2,1,0:T(4,128)(2,1)S(1)} async-done(((bf16[128,4,1152]{2,1,0:T(4,128)(2,1)}), bf16[128,4,1152]{2,1,0:T(4,128)(2,1)S(1)}, u32[]{:S(2)}, u32[]{:S(2)}) %all-to-all-start) | async-done | bytes 1179680 | tf_op jit(solution)/shard_map/all_to_all | solution.py:298
  54.0 1.1 %split.1 = (bf16[512,1024]{1,0:T(8,128)(2,1)}, s32[1,512]{1,0:T(1,128)}) custom-call(bf16[128,4,1152]{2,1,0:T(4,128)(2,1)S(1)} %all-to-all-done.in_ref), custom_call_target="tpu_custom_call" | custom-call | bytes 2097152 | tf_op jit(solution)/shard_map/split/pallas_call | solution.py:189
  55.1 0.0 collective-permute-done.5.refs_3_
  55.1 0.0 collective-permute-done.6.refs_5_
  55.1 0.3 collective-permute-done.7.refs_6_
  55.4 0.0 copy-start.6
  55.4 0.7 copy-done.6
  56.1 0.8 cross_b.1.refs_4_
  56.9 1.3 %collective-permute-start.8 = (f32[1,1024]{1,0:T(1,128)S(1)}, f32[1,1024]{1,0:T(1,128)S(1)}, u32[]{:S(2)}, u32[]{:S(2)}) collective-permute-start(f32[1,1024]{1,0:T(1,128)S(1)} %slice.4), channel_id=1, source_target_pairs={{1,0},{3,2},{5,4},{7,6},{9,8},{11,10},{13,12},{15,14},{17,16},{19,... | collective-permute-start | bytes 12296 | tf_op jit(solution)/shard_map/ppermute | solution.py:30
  58.2 0.0 collective-permute-done.1.refs_0_
  58.2 16.7 %collective-permute-done.8.refs_5_ = f32[1,1024]{1,0:T(1,128)S(1)} collective-permute-done((f32[1,1024]{1,0:T(1,128)S(1)}, f32[1,1024]{1,0:T(1,128)S(1)}, u32[]{:S(2)}, u32[]{:S(2)}) %collective-permute-start.8) | collective-permute-done | bytes 4128 | tf_op jit(solution)/shard_map/ppermute | solution.py:30
  74.9 1.2 %cross_c.1 = (f32[1,1024]{1,0:T(1,128)S(1)}, f32[1,1024]{1,0:T(1,128)S(1)}, f32[1,1024]{1,0:T(1,128)S(1)}, f32[8,1024]{1,0:T(8,128)}) custom-call(bf16[528,1024]{1,0:T(8,128)(2,1)} %collective-permute-done.1.refs_0_, bf16[528,1024]{1,0:T(8,128)(2,1)} %collective-permute-done.2.refs_4_.refs_2_.refs_1_, ...), custom_call_target="tpu_custom_call" | custom-call | flops 1073741824 | bytes 3244032 | tf_op jit(solution)/shard_map/cross_c/pallas_call | solution.py:233
  76.1 0.7 collective-permute-start.10
  76.8 1.3 %collective-permute-start.9 = (f32[1,1024]{1,0:T(1,128)S(1)}, f32[1,1024]{1,0:T(1,128)S(1)}, u32[]{:S(2)}, u32[]{:S(2)}) collective-permute-start(f32[1,1024]{1,0:T(1,128)S(1)} %get-tuple-element.10), channel_id=1, source_target_pairs={{1,2},{3,4},{5,6},{7,8},{9,10},{11,12},{13,14},{15,16},{17,18},{19... | collective-permute-start | bytes 12296 | tf_op jit(solution)/shard_map/ppermute | solution.py:30
  78.1 0.0 collective-permute-done.10
  78.1 8.4 %collective-permute-done.9 = f32[1,1024]{1,0:T(1,128)S(1)} collective-permute-done((f32[1,1024]{1,0:T(1,128)S(1)}, f32[1,1024]{1,0:T(1,128)S(1)}, u32[]{:S(2)}, u32[]{:S(2)}) %collective-permute-start.9) | collective-permute-done | bytes 4128 | tf_op jit(solution)/shard_map/ppermute | solution.py:30
  86.5 0.6 fusion.1
  (1 shorter events, 0.0 us)
Async XLA Ops:
  0.6 1.6 %copy-start = (bf16[1,1024,1024]{2,1,0:T(8,128)(2,1)S(1)}, bf16[1,1024,1024]{2,1,0:T(8,128)(2,1)}, u32[]{:S(2)}) copy-start(bf16[1,1024,1024]{2,1,0:T(8,128)(2,1)} %param.6) | copy-start | bytes 6291460
  2.2 0.7 copy-start.2
  3.2 10.5 %copy-start.5 = (f32[1,1024]{1,0:T(1,128)S(1)}, f32[1,1024]{1,0:T(1,128)}, u32[]{:S(2)}) copy-start(f32[1,1024]{1,0:T(1,128)} %prior_ref.1) | copy-start | bytes 12292
  3.3 25.1 %collective-permute-start.4 = (bf16[528,1024]{1,0:T(8,128)(2,1)S(1)}, bf16[528,1024]{1,0:T(8,128)(2,1)}, u32[]{:S(2)}, u32[]{:S(2)}) collective-permute-start(bf16[528,1024]{1,0:T(8,128)(2,1)S(1)} %norm_0.1.own0.refs_0_), channel_id=1, source_target_pairs={{0,1},{2,3},{4,5},{6,7},{8,9},{10,11},{12,13},{14,15},{16,17},{18,... | collective-permute-start | bytes 3244040 | tf_op jit(solution)/shard_map/ppermute | solution.py:30
  8.2 7.9 %copy-start.1 = (bf16[256,1024]{1,0:T(8,128)(2,1)S(1)}, bf16[256,1024]{1,0:T(8,128)(2,1)}, u32[]{:S(2)}) copy-start(bf16[256,1024]{1,0:T(8,128)(2,1)} %rows_ref.1) | copy-start | bytes 1572868
  8.2 7.9 %copy-start.3 = (s32[256,1]{0,1:T(1,128)S(1)}, s32[256,1]{0,1:T(1,128)}, u32[]{:S(2)}) copy-start(s32[256,1]{0,1:T(1,128)} %param.11) | copy-start | bytes 3076
  8.2 7.9 %copy-start.4 = (s32[256]{0:T(256)S(1)}, s32[256]{0:T(256)}, u32[]{:S(2)}) copy-start(s32[256]{0:T(256)} %param.10) | copy-start | bytes 3076
  8.2 23.6 %collective-permute-start.3 = (bf16[528,1024]{1,0:T(8,128)(2,1)S(1)}, bf16[528,1024]{1,0:T(8,128)(2,1)}, u32[]{:S(2)}, u32[]{:S(2)}) collective-permute-start(bf16[528,1024]{1,0:T(8,128)(2,1)S(1)} %norm_1.1.own1.refs_1_), channel_id=1, source_target_pairs={{0,2},{1,3},{2,4},{3,5},{4,6},{5,7},{6,8},{7,9},{8,10},{9,11},{10,... | collective-permute-start | bytes 3244040 | tf_op jit(solution)/shard_map/ppermute | solution.py:30
  9.8 31.9 %collective-permute-start = (bf16[528,1024]{1,0:T(8,128)(2,1)S(1)}, bf16[528,1024]{1,0:T(8,128)(2,1)}, u32[]{:S(2)}, u32[]{:S(2)}) collective-permute-start(bf16[528,1024]{1,0:T(8,128)(2,1)S(1)} %norm_1.1.own1.refs_1_), channel_id=1, source_target_pairs={{0,1},{2,3},{4,5},{6,7},{8,9},{10,11},{12,13},{14,15},{16,17},{18,... | collective-permute-start | bytes 3244040 | tf_op jit(solution)/shard_map/ppermute | solution.py:30
  12.1 31.4 %collective-permute-start.2 = (bf16[528,1024]{1,0:T(8,128)(2,1)S(1)}, bf16[528,1024]{1,0:T(8,128)(2,1)}, u32[]{:S(2)}, u32[]{:S(2)}) collective-permute-start(bf16[528,1024]{1,0:T(8,128)(2,1)S(1)} %norm_0.1.own0.refs_0_), channel_id=1, source_target_pairs={{1,3},{3,5},{5,7},{7,9},{9,11},{11,13},{13,15},{15,17},{17,19},{19... | collective-permute-start | bytes 3244040 | tf_op jit(solution)/shard_map/ppermute | solution.py:30
  17.9 36.1 %all-to-all-start = ((bf16[128,4,1152]{2,1,0:T(4,128)(2,1)}), bf16[128,4,1152]{2,1,0:T(4,128)(2,1)S(1)}, u32[]{:S(2)}, u32[]{:S(2)}) async-start(bf16[128,4,1152]{2,1,0:T(4,128)(2,1)} %place.1), calls=%async_computation | async-start | bytes 2359296 | tf_op jit(solution)/shard_map/all_to_all | solution.py:298
  28.4 26.7 %collective-permute-start.5 = (bf16[528,1024]{1,0:T(8,128)(2,1)}, bf16[528,1024]{1,0:T(8,128)(2,1)}, u32[]{:S(2)}, u32[]{:S(2)}) collective-permute-start(bf16[528,1024]{1,0:T(8,128)(2,1)} %collective-permute-done.4.refs_2_.refs_7_), channel_id=1, source_target_pairs={{1,31},{3,1},{5,3},{7,5},{9,7},{11,9},{13,11},{15,13},{17,15},{19,... | collective-permute-start | bytes 3244040 | tf_op jit(solution)/shard_map/ppermute | solution.py:30
  30.0 25.1 %collective-permute-start.6 = (bf16[528,1024]{1,0:T(8,128)(2,1)}, bf16[528,1024]{1,0:T(8,128)(2,1)}, u32[]{:S(2)}, u32[]{:S(2)}) collective-permute-start(bf16[528,1024]{1,0:T(8,128)(2,1)} %collective-permute-done.4.refs_2_.refs_7_), channel_id=1, source_target_pairs={{1,3},{3,5},{5,7},{7,9},{9,11},{11,13},{13,15},{15,17},{17,19},{19... | collective-permute-start | bytes 3244040 | tf_op jit(solution)/shard_map/ppermute | solution.py:30
  31.8 23.6 %collective-permute-start.7 = (bf16[528,1024]{1,0:T(8,128)(2,1)}, bf16[528,1024]{1,0:T(8,128)(2,1)}, u32[]{:S(2)}, u32[]{:S(2)}) collective-permute-start(bf16[528,1024]{1,0:T(8,128)(2,1)} %collective-permute-done.3.refs_3_.refs_4_.refs_2_), channel_id=1, source_target_pairs={{0,1},{2,3},{4,5},{6,7},{8,9},{10,11},{12,13},{14,15},{16,17},{18,... | collective-permute-start | bytes 3244040 | tf_op jit(solution)/shard_map/ppermute | solution.py:30
  41.7 16.6 %collective-permute-start.1 = (bf16[528,1024]{1,0:T(8,128)(2,1)}, bf16[528,1024]{1,0:T(8,128)(2,1)}, u32[]{:S(2)}, u32[]{:S(2)}) collective-permute-start(bf16[528,1024]{1,0:T(8,128)(2,1)} %collective-permute-done.refs_5_.refs_8_), channel_id=1, source_target_pairs={{1,31},{3,1},{5,3},{7,5},{9,7},{11,9},{13,11},{15,13},{17,15},{19,... | collective-permute-start | bytes 3244040 | tf_op jit(solution)/shard_map/ppermute | solution.py:30
  55.4 0.7 copy-start.6
  56.9 18.0 %collective-permute-start.8 = (f32[1,1024]{1,0:T(1,128)S(1)}, f32[1,1024]{1,0:T(1,128)S(1)}, u32[]{:S(2)}, u32[]{:S(2)}) collective-permute-start(f32[1,1024]{1,0:T(1,128)S(1)} %slice.4), channel_id=1, source_target_pairs={{1,0},{3,2},{5,4},{7,6},{9,8},{11,10},{13,12},{15,14},{17,16},{19,... | collective-permute-start | bytes 12296 | tf_op jit(solution)/shard_map/ppermute | solution.py:30
  76.1 2.0 %collective-permute-start.10 = (f32[1,1024]{1,0:T(1,128)S(1)}, f32[1,1024]{1,0:T(1,128)S(1)}, u32[]{:S(2)}, u32[]{:S(2)}) collective-permute-start(f32[1,1024]{1,0:T(1,128)S(1)} %get-tuple-element.11), channel_id=1, source_target_pairs={{32,34},{33,35},{34,36},{35,37},{36,38},{37,39},{38,40},{39,41},{4... | collective-permute-start | bytes 12296 | tf_op jit(solution)/shard_map/ppermute | solution.py:30
  76.8 9.7 %collective-permute-start.9 = (f32[1,1024]{1,0:T(1,128)S(1)}, f32[1,1024]{1,0:T(1,128)S(1)}, u32[]{:S(2)}, u32[]{:S(2)}) collective-permute-start(f32[1,1024]{1,0:T(1,128)S(1)} %get-tuple-element.10), channel_id=1, source_target_pairs={{1,2},{3,4},{5,6},{7,8},{9,10},{11,12},{13,14},{15,16},{17,18},{19... | collective-permute-start | bytes 12296 | tf_op jit(solution)/shard_map/ppermute | solution.py:30

commit v11 on v9

--- a/solution.py
+++ b/solution.py
@@ -229,12 +229,14 @@
         if light_pairs:
             compare(where_ref, 0, acc_ref, held, names, inputs, buffers, sems, light_pairs)
         if last:
-            own_out, far_out, side_out = outs[:3]
-            own_row, from_partner = acc_ref[OWN : OWN + 1, :], refs[len(names) + 2][...]
-            own_out[...] = jnp.where(where_ref[1] == 0, jnp.maximum(own_row, from_partner), own_row)
-            near_partner_row = acc_ref[NEAR_PARTNER : NEAR_PARTNER + 1, :]
-            far_out[...] = jnp.where(where_ref[0] == 0, acc_ref[FAR_PARTNER : FAR_PARTNER + 1, :], near_partner_row)
-            side_out[...] = jnp.where(where_ref[1] == 1, acc_ref[NEAR : NEAR + 1, :], near_partner_row)
+            own_out, send_out = outs[:2]
+            own_row = acc_ref[OWN : OWN + 1, :]
+            from_partner, from_behind = refs[len(names) + 2][...], refs[len(names) + 3][...]
+            with_behind = jnp.where(where_ref[0] == 1, jnp.maximum(from_partner, from_behind), from_partner)
+            own_out[...] = jnp.where(where_ref[1] == 0, jnp.maximum(own_row, with_behind), own_row)
+            near_rows = slice(NEAR, NEAR + 1), slice(NEAR_PARTNER, NEAR_PARTNER + 1)
+            sent = jnp.where(where_ref[1] == 1, acc_ref[near_rows[0], :], acc_ref[near_rows[1], :])
+            send_out[...] = jnp.where(where_ref[0] == 0, acc_ref[FAR_PARTNER : FAR_PARTNER + 1, :], sent)
 
     products = sum(len(a[1]) * len(b[1]) for a, b in heavy_pairs) / 4
     return pl.pallas_call(
@@ -244,8 +246,8 @@
         + smem()
         + vmem(1)
         + ([pl.BlockSpec(memory_space=pltpu.VMEM if last else pltpu.HBM)] * len(after)),
-        out_specs=vmem(4 if last else 1),
-        out_shape=[jax.ShapeDtypeStruct((1, rows), jnp.float32)] * (3 if last else 0)
+        out_specs=vmem(3 if last else 1),
+        out_shape=[jax.ShapeDtypeStruct((1, rows), jnp.float32)] * (2 if last else 0)
         + [jax.ShapeDtypeStruct(found.shape, jnp.float32)],
         scratch_shapes=[pltpu.VMEM((len(names), size, width), jnp.bfloat16), pltpu.SemaphoreType.DMA((len(names),))],
         compiler_params=params(),
@@ -347,10 +349,11 @@
         [],
         where,
         found,
-        (next_ids,),
     )
     from_partner = send(found[PARTNER : PARTNER + 1], to_light)
-    mine, for_far, for_side, _ = stage(
+    behind = found[NEAR_PARTNER : NEAR_PARTNER + 1]
+    from_behind = send(behind, lambda core, heavy, block: block + 3 if heavy and core else None)
+    mine, for_last, _ = stage(
         "cross_c",
         (),
         {"far1": far1, "near0": near0, "near1": near1},
@@ -358,14 +361,12 @@
         [],
         where,
         found,
-        (from_partner,),
+        (from_partner, from_behind, next_ids),
         last=True,
     )
-    from_far = send(for_far, lambda core, heavy, block: block + 1 + 2 * core if heavy else None)
-    from_side = send(for_side, lambda core, heavy, block: block + 2 if core else None)
-    lowest = jnp.float32(LOWEST)
-    running = jnp.maximum(mine, jnp.where(heavy == 0, from_far, lowest))
-    running = jnp.maximum(running, jnp.where(core == 1, from_side, lowest))
+    from_last = send(for_last, lambda core, heavy, block: block + 2 if core else (block + 1 if heavy else None))
+    gets = (core == 1) | (heavy == 0)
+    running = jnp.maximum(mine, jnp.where(gets, from_last, jnp.float32(LOWEST)))
     return (running, next_rows, next_ids.reshape(-1))
 
 

time: 86.7 us -> 93.9 us (1.083)
  the two profiles are of different devices: /device:TPU:0 before, /device:TPU:1 now
where the time goes in v11:
time: 93.9 us; the launch traced here: 93.4 us
  starting transfers between devices  45 us (48%)
  Pallas kernels  27.7 us (29%)
  waiting for transfers between devices  16.1 us (17%)
  local copies, waits for them, and re-layouts  2.99 us (3%)
    ppermute x11, starting transfers between devices, send(): return lax.ppermute(value, BOTH, pairs)  31.5 us
    pallas_call x3, Pallas kernels, stage(): pl.pallas_call(run, in_specs=vmem(len(own)) + [pl.BlockSpec(memory_space=...  21.8 us
    ppermute x11, waiting for transfers between devices, send(): return lax.ppermute(value, BOTH, pairs)  16.1 us
    all_to_all x1, starting transfers between devices, body(): lax.all_to_all(outgoing, BOTH, split_axis=0, concat_axis=0, tiled=True)  13.5 us
    unnamed x14, local copies, waits for them, and re-layouts  2.98 us
    pallas_call x1, Pallas kernels, body(): pl.pallas_call(within_kernel, in_specs=vmem(3), out_specs=pl.BlockSpec(me...  2.38 us
  transfers between devices with their start and end apart: 12, of which 3 were waited for; matrix products, arithmetic and copies ran while one was open for 0% of the time, Pallas kernels for 25%

profile of v11, /device:TPU:1, one launch (start us, length us, event | category | flops | bytes accessed | tf_op | source)
XLA Modules:
  0.0 93.4 jit_solution(16014937181538930881)
XLA Ops:
  0.6 0.0 copy-start
  0.6 1.6 %copy-done = bf16[1,1024,1024]{2,1,0:T(8,128)(2,1)S(1)} copy-done((bf16[1,1024,1024]{2,1,0:T(8,128)(2,1)S(1)}, bf16[1,1024,1024]{2,1,0:T(8,128)(2,1)}, u32[]{:S(2)}) %copy-start) | copy-done | bytes 2097176
  2.2 0.0 copy-start.2
  2.2 0.7 copy-done.2
  2.9 0.3 norm_0.1.own0.refs_0_
  3.2 0.0 copy-start.5
  3.3 1.3 %collective-permute-start.4 = (bf16[528,1024]{1,0:T(8,128)(2,1)S(1)}, bf16[528,1024]{1,0:T(8,128)(2,1)}, u32[]{:S(2)}, u32[]{:S(2)}) collective-permute-start(bf16[528,1024]{1,0:T(8,128)(2,1)S(1)} %norm_0.1.own0.refs_0_), channel_id=1, source_target_pairs={{0,1},{2,3},{4,5},{6,7},{8,9},{10,11},{12,13},{14,15},{16,17},{18,... | collective-permute-start | bytes 3244040 | tf_op jit(solution)/shard_map/ppermute | solution.py:31
  4.6 0.3 norm_1.1.own1.refs_1_
  4.9 0.0 copy-start.1
  4.9 0.0 copy-start.3
  4.9 0.0 copy-start.4
  4.9 6.8 %collective-permute-start.3 = (bf16[528,1024]{1,0:T(8,128)(2,1)S(1)}, bf16[528,1024]{1,0:T(8,128)(2,1)}, u32[]{:S(2)}, u32[]{:S(2)}) collective-permute-start(bf16[528,1024]{1,0:T(8,128)(2,1)S(1)} %norm_1.1.own1.refs_1_), channel_id=1, source_target_pairs={{0,2},{1,3},{2,4},{3,5},{4,6},{5,7},{6,8},{7,9},{8,10},{9,11},{10,... | collective-permute-start | bytes 3244040 | tf_op jit(solution)/shard_map/ppermute | solution.py:31
  11.8 1.3 %collective-permute-start = (bf16[528,1024]{1,0:T(8,128)(2,1)S(1)}, bf16[528,1024]{1,0:T(8,128)(2,1)}, u32[]{:S(2)}, u32[]{:S(2)}) collective-permute-start(bf16[528,1024]{1,0:T(8,128)(2,1)S(1)} %norm_1.1.own1.refs_1_), channel_id=1, source_target_pairs={{0,1},{2,3},{4,5},{6,7},{8,9},{10,11},{12,13},{14,15},{16,17},{18,... | collective-permute-start | bytes 3244040 | tf_op jit(solution)/shard_map/ppermute | solution.py:31
  13.1 2.5 %collective-permute-start.2 = (bf16[528,1024]{1,0:T(8,128)(2,1)S(1)}, bf16[528,1024]{1,0:T(8,128)(2,1)}, u32[]{:S(2)}, u32[]{:S(2)}) collective-permute-start(bf16[528,1024]{1,0:T(8,128)(2,1)S(1)} %norm_0.1.own0.refs_0_), channel_id=1, source_target_pairs={{1,3},{3,5},{5,7},{7,9},{9,11},{11,13},{13,15},{15,17},{17,19},{19... | collective-permute-start | bytes 3244040 | tf_op jit(solution)/shard_map/ppermute | solution.py:31
  15.5 4.1 %collective-permute-done.4.refs_2_.refs_7_ = bf16[528,1024]{1,0:T(8,128)(2,1)} collective-permute-done((bf16[528,1024]{1,0:T(8,128)(2,1)S(1)}, bf16[528,1024]{1,0:T(8,128)(2,1)}, u32[]{:S(2)}, u32[]{:S(2)}) %collective-permute-start.4) | collective-permute-done | bytes 1081376 | tf_op jit(solution)/shard_map/ppermute | solution.py:31
  19.6 3.9 %collective-permute-start.5 = (bf16[528,1024]{1,0:T(8,128)(2,1)}, bf16[528,1024]{1,0:T(8,128)(2,1)}, u32[]{:S(2)}, u32[]{:S(2)}) collective-permute-start(bf16[528,1024]{1,0:T(8,128)(2,1)} %collective-permute-done.4.refs_2_.refs_7_), channel_id=1, source_target_pairs={{1,31},{3,1},{5,3},{7,5},{9,7},{11,9},{13,11},{15,13},{17,15},{19,... | collective-permute-start | bytes 3244040 | tf_op jit(solution)/shard_map/ppermute | solution.py:31
  23.5 6.7 %collective-permute-start.6 = (bf16[528,1024]{1,0:T(8,128)(2,1)}, bf16[528,1024]{1,0:T(8,128)(2,1)}, u32[]{:S(2)}, u32[]{:S(2)}) collective-permute-start(bf16[528,1024]{1,0:T(8,128)(2,1)} %collective-permute-done.4.refs_2_.refs_7_), channel_id=1, source_target_pairs={{1,3},{3,5},{5,7},{7,9},{9,11},{11,13},{13,15},{15,17},{17,19},{19... | collective-permute-start | bytes 3244040 | tf_op jit(solution)/shard_map/ppermute | solution.py:31
  30.2 0.0 collective-permute-done.3.refs_3_.refs_4_.refs_2_
  30.2 1.3 %collective-permute-start.7 = (bf16[528,1024]{1,0:T(8,128)(2,1)}, bf16[528,1024]{1,0:T(8,128)(2,1)}, u32[]{:S(2)}, u32[]{:S(2)}) collective-permute-start(bf16[528,1024]{1,0:T(8,128)(2,1)} %collective-permute-done.3.refs_3_.refs_4_.refs_2_), channel_id=1, source_target_pairs={{0,1},{2,3},{4,5},{6,7},{8,9},{10,11},{12,13},{14,15},{16,17},{18,... | collective-permute-start | bytes 3244040 | tf_op jit(solution)/shard_map/ppermute | solution.py:31
  31.5 0.0 copy-done.5
  31.5 2.4 %within.1.refs_7_.after_ref = f32[8,1024]{1,0:T(8,128)S(1)} custom-call(bf16[528,1024]{1,0:T(8,128)(2,1)S(1)} %norm_0.1.own0.refs_0_, bf16[528,1024]{1,0:T(8,128)(2,1)S(1)} %norm_1.1.own1.refs_1_, f32[1,1024]{1,0:T(1,128)S(1)} %copy-done.5), custom_call_target="tpu_custom_call" | custom-call | flops 2147483648 | bytes 2097152 | tf_op jit(solution)/shard_map/within/pallas_call | solution.py:295
  33.9 0.0 copy-done.1
  33.9 0.0 copy-done.3
  33.9 0.0 copy-done.4
  33.9 1.8 %place.1 = bf16[128,4,1152]{2,1,0:T(4,128)(2,1)} custom-call(bf16[256,1024]{1,0:T(8,128)(2,1)S(1)} %copy-done.1, s32[1,256]{1,0:T(1,128)S(1)} %bitcast.8, s32[1,256]{1,0:T(1,128)S(1)} %bitcast.9, f32[8,1024]{1,0:T(8,128)S(1)} %within.1.refs_7_.after_ref), custom_call_target="tpu_custom_call" | custom-call | flops 268435456 | bytes 1572864 | tf_op jit(solution)/shard_map/place/pallas_call | solution.py:172
  35.7 13.5 %all-to-all-start = ((bf16[128,4,1152]{2,1,0:T(4,128)(2,1)}), bf16[128,4,1152]{2,1,0:T(4,128)(2,1)S(1)}, u32[]{:S(2)}, u32[]{:S(2)}) async-start(bf16[128,4,1152]{2,1,0:T(4,128)(2,1)} %place.1), calls=%async_computation | async-start | bytes 2359296 | tf_op jit(solution)/shard_map/all_to_all | solution.py:307
  49.2 0.1 pad_add_fusion.refs_6_.refs_9_.refs_3_
  49.3 0.0 collective-permute-done.refs_5_.refs_8_
  49.3 3.3 %collective-permute-start.1 = (bf16[528,1024]{1,0:T(8,128)(2,1)}, bf16[528,1024]{1,0:T(8,128)(2,1)}, u32[]{:S(2)}, u32[]{:S(2)}) collective-permute-start(bf16[528,1024]{1,0:T(8,128)(2,1)} %collective-permute-done.refs_5_.refs_8_), channel_id=1, source_target_pairs={{1,31},{3,1},{5,3},{7,5},{9,7},{11,9},{13,11},{15,13},{17,15},{19,... | collective-permute-start | bytes 3244040 | tf_op jit(solution)/shard_map/ppermute | solution.py:31
  52.5 0.0 collective-permute-done.2.refs_4_.refs_2_.refs_1_
  52.6 9.4 %cross_a.1.refs_10_ = f32[8,1024]{1,0:T(8,128)S(1)} custom-call(bf16[528,1024]{1,0:T(8,128)(2,1)S(1)} %norm_0.1.own0.refs_0_, bf16[528,1024]{1,0:T(8,128)(2,1)S(1)} %norm_1.1.own1.refs_1_, bf16[528,1024]{1,0:T(8,128)(2,1)} %collective-permute-done.4.refs_2_.refs_7_, bf16[528,1024]{1,0:T(8,128)(2,1)} %collective-permute-done.3.refs_3_.refs_4_.refs_2_, ...), custom_call_target="tpu_custom_call" | custom-call | flops 6442450944 | bytes 4325376 | tf_op jit(solution)/shard_map/cross_a/pallas_call | solution.py:242
  61.9 0.0 collective-permute-done.5.refs_3_
  62.0 0.0 collective-permute-done.6.refs_5_
  62.0 0.0 collective-permute-done.7.refs_6_
  62.0 8.2 %cross_b.1.refs_4_ = f32[8,1024]{1,0:T(8,128)S(1)} custom-call(bf16[528,1024]{1,0:T(8,128)(2,1)S(1)} %norm_0.1.own0.refs_0_, bf16[528,1024]{1,0:T(8,128)(2,1)S(1)} %norm_1.1.own1.refs_1_, bf16[528,1024]{1,0:T(8,128)(2,1)} %collective-permute-done.2.refs_4_.refs_2_.refs_1_, bf16[528,1024]{1,0:T(8,128)(2,1)} %collective-permute-done.5.refs_3_, ...), custom_call_target="tpu_custom_call" | custom-call | flops 4294967296 | bytes 7569408 | tf_op jit(solution)/shard_map/cross_b/pallas_call | solution.py:242
  70.2 1.3 %collective-permute-start.8 = (f32[1,1024]{1,0:T(1,128)S(1)}, f32[1,1024]{1,0:T(1,128)S(1)}, u32[]{:S(2)}, u32[]{:S(2)}) collective-permute-start(f32[1,1024]{1,0:T(1,128)S(1)} %get-tuple-element.12), channel_id=1, source_target_pairs={{1,0},{3,2},{5,4},{7,6},{9,8},{11,10},{13,12},{15,14},{17,16},{19,... | collective-permute-start | bytes 12296 | tf_op jit(solution)/shard_map/ppermute | solution.py:31
  71.5 1.3 %collective-permute-start.9 = (f32[1,1024]{1,0:T(1,128)S(1)}, f32[1,1024]{1,0:T(1,128)S(1)}, u32[]{:S(2)}, u32[]{:S(2)}) collective-permute-start(f32[1,1024]{1,0:T(1,128)S(1)} %get-tuple-element.11), channel_id=1, source_target_pairs={{32,35},{34,37},{36,39},{38,41},{40,43},{42,45},{44,47},{46,49},{4... | collective-permute-start | bytes 12296 | tf_op jit(solution)/shard_map/ppermute | solution.py:31
  72.8 0.0 all-to-all-done.in_ref
  72.8 1.1 %split.1 = (bf16[512,1024]{1,0:T(8,128)(2,1)}, s32[1,512]{1,0:T(1,128)}) custom-call(bf16[128,4,1152]{2,1,0:T(4,128)(2,1)S(1)} %all-to-all-done.in_ref), custom_call_target="tpu_custom_call" | custom-call | bytes 2097152 | tf_op jit(solution)/shard_map/split/pallas_call | solution.py:196
  73.9 6.3 %collective-permute-done.1.refs_0_ = bf16[528,1024]{1,0:T(8,128)(2,1)} collective-permute-done((bf16[528,1024]{1,0:T(8,128)(2,1)}, bf16[528,1024]{1,0:T(8,128)(2,1)}, u32[]{:S(2)}, u32[]{:S(2)}) %collective-permute-start.1) | collective-permute-done | bytes 1081376 | tf_op jit(solution)/shard_map/ppermute | solution.py:31
  80.2 0.0 collective-permute-done.8.refs_5_
  80.2 0.0 collective-permute-done.9.refs_6_
  80.2 0.0 copy-start.6
  80.2 0.7 copy-done.6
  80.9 4.3 %cross_c.1 = (f32[1,1024]{1,0:T(1,128)S(1)}, f32[1,1024]{1,0:T(1,128)S(1)}, f32[8,1024]{1,0:T(8,128)}) custom-call(bf16[528,1024]{1,0:T(8,128)(2,1)} %collective-permute-done.1.refs_0_, bf16[528,1024]{1,0:T(8,128)(2,1)} %collective-permute-done.2.refs_4_.refs_2_.refs_1_, bf16[528,1024]{1,0:T(8,128)(2,1)} %collective-permute-done.3.refs_3_.refs_4_.refs_2_, ...), custom_call_target="tpu_custom_call" | custom-call | flops 1073741824 | bytes 3244032 | tf_op jit(solution)/shard_map/cross_c/pallas_call | solution.py:242
  85.2 1.9 %collective-permute-start.10 = (f32[1,1024]{1,0:T(1,128)S(1)}, f32[1,1024]{1,0:T(1,128)S(1)}, u32[]{:S(2)}, u32[]{:S(2)}) collective-permute-start(f32[1,1024]{1,0:T(1,128)S(1)} %get-tuple-element.9), channel_id=1, source_target_pairs={{1,2},{3,4},{5,6},{7,8},{9,10},{11,12},{13,14},{15,16},{17,18},{19... | collective-permute-start | bytes 12296 | tf_op jit(solution)/shard_map/ppermute | solution.py:31
  87.1 5.7 %collective-permute-done.10 = f32[1,1024]{1,0:T(1,128)S(1)} collective-permute-done((f32[1,1024]{1,0:T(1,128)S(1)}, f32[1,1024]{1,0:T(1,128)S(1)}, u32[]{:S(2)}, u32[]{:S(2)}) %collective-permute-start.10) | collective-permute-done | bytes 4128 | tf_op jit(solution)/shard_map/ppermute | solution.py:31
  92.8 0.6 fusion
  (1 shorter events, 0.0 us)
Async XLA Ops:
  0.6 1.6 %copy-start = (bf16[1,1024,1024]{2,1,0:T(8,128)(2,1)S(1)}, bf16[1,1024,1024]{2,1,0:T(8,128)(2,1)}, u32[]{:S(2)}) copy-start(bf16[1,1024,1024]{2,1,0:T(8,128)(2,1)} %param.6) | copy-start | bytes 6291460
  2.2 0.7 copy-start.2
  3.2 28.2 %copy-start.5 = (f32[1,1024]{1,0:T(1,128)S(1)}, f32[1,1024]{1,0:T(1,128)}, u32[]{:S(2)}) copy-start(f32[1,1024]{1,0:T(1,128)} %prior_ref.1) | copy-start | bytes 12292
  3.3 16.3 %collective-permute-start.4 = (bf16[528,1024]{1,0:T(8,128)(2,1)S(1)}, bf16[528,1024]{1,0:T(8,128)(2,1)}, u32[]{:S(2)}, u32[]{:S(2)}) collective-permute-start(bf16[528,1024]{1,0:T(8,128)(2,1)S(1)} %norm_0.1.own0.refs_0_), channel_id=1, source_target_pairs={{0,1},{2,3},{4,5},{6,7},{8,9},{10,11},{12,13},{14,15},{16,17},{18,... | collective-permute-start | bytes 3244040 | tf_op jit(solution)/shard_map/ppermute | solution.py:31
  4.9 29.0 %copy-start.1 = (bf16[256,1024]{1,0:T(8,128)(2,1)S(1)}, bf16[256,1024]{1,0:T(8,128)(2,1)}, u32[]{:S(2)}) copy-start(bf16[256,1024]{1,0:T(8,128)(2,1)} %rows_ref.1) | copy-start | bytes 1572868
  4.9 29.0 %copy-start.3 = (s32[256,1]{0,1:T(1,128)S(1)}, s32[256,1]{0,1:T(1,128)}, u32[]{:S(2)}) copy-start(s32[256,1]{0,1:T(1,128)} %param.11) | copy-start | bytes 3076
  4.9 29.0 %copy-start.4 = (s32[256]{0:T(256)S(1)}, s32[256]{0:T(256)}, u32[]{:S(2)}) copy-start(s32[256]{0:T(256)} %param.10) | copy-start | bytes 3076
  4.9 25.2 %collective-permute-start.3 = (bf16[528,1024]{1,0:T(8,128)(2,1)S(1)}, bf16[528,1024]{1,0:T(8,128)(2,1)}, u32[]{:S(2)}, u32[]{:S(2)}) collective-permute-start(bf16[528,1024]{1,0:T(8,128)(2,1)S(1)} %norm_1.1.own1.refs_1_), channel_id=1, source_target_pairs={{0,2},{1,3},{2,4},{3,5},{4,6},{5,7},{6,8},{7,9},{8,10},{9,11},{10,... | collective-permute-start | bytes 3244040 | tf_op jit(solution)/shard_map/ppermute | solution.py:31
  11.8 37.5 %collective-permute-start = (bf16[528,1024]{1,0:T(8,128)(2,1)S(1)}, bf16[528,1024]{1,0:T(8,128)(2,1)}, u32[]{:S(2)}, u32[]{:S(2)}) collective-permute-start(bf16[528,1024]{1,0:T(8,128)(2,1)S(1)} %norm_1.1.own1.refs_1_), channel_id=1, source_target_pairs={{0,1},{2,3},{4,5},{6,7},{8,9},{10,11},{12,13},{14,15},{16,17},{18,... | collective-permute-start | bytes 3244040 | tf_op jit(solution)/shard_map/ppermute | solution.py:31
  13.1 39.5 %collective-permute-start.2 = (bf16[528,1024]{1,0:T(8,128)(2,1)S(1)}, bf16[528,1024]{1,0:T(8,128)(2,1)}, u32[]{:S(2)}, u32[]{:S(2)}) collective-permute-start(bf16[528,1024]{1,0:T(8,128)(2,1)S(1)} %norm_0.1.own0.refs_0_), channel_id=1, source_target_pairs={{1,3},{3,5},{5,7},{7,9},{9,11},{11,13},{13,15},{15,17},{17,19},{19... | collective-permute-start | bytes 3244040 | tf_op jit(solution)/shard_map/ppermute | solution.py:31
  19.6 42.4 %collective-permute-start.5 = (bf16[528,1024]{1,0:T(8,128)(2,1)}, bf16[528,1024]{1,0:T(8,128)(2,1)}, u32[]{:S(2)}, u32[]{:S(2)}) collective-permute-start(bf16[528,1024]{1,0:T(8,128)(2,1)} %collective-permute-done.4.refs_2_.refs_7_), channel_id=1, source_target_pairs={{1,31},{3,1},{5,3},{7,5},{9,7},{11,9},{13,11},{15,13},{17,15},{19,... | collective-permute-start | bytes 3244040 | tf_op jit(solution)/shard_map/ppermute | solution.py:31
  23.5 38.5 %collective-permute-start.6 = (bf16[528,1024]{1,0:T(8,128)(2,1)}, bf16[528,1024]{1,0:T(8,128)(2,1)}, u32[]{:S(2)}, u32[]{:S(2)}) collective-permute-start(bf16[528,1024]{1,0:T(8,128)(2,1)} %collective-permute-done.4.refs_2_.refs_7_), channel_id=1, source_target_pairs={{1,3},{3,5},{5,7},{7,9},{9,11},{11,13},{13,15},{15,17},{17,19},{19... | collective-permute-start | bytes 3244040 | tf_op jit(solution)/shard_map/ppermute | solution.py:31
  30.2 31.8 %collective-permute-start.7 = (bf16[528,1024]{1,0:T(8,128)(2,1)}, bf16[528,1024]{1,0:T(8,128)(2,1)}, u32[]{:S(2)}, u32[]{:S(2)}) collective-permute-start(bf16[528,1024]{1,0:T(8,128)(2,1)} %collective-permute-done.3.refs_3_.refs_4_.refs_2_), channel_id=1, source_target_pairs={{0,1},{2,3},{4,5},{6,7},{8,9},{10,11},{12,13},{14,15},{16,17},{18,... | collective-permute-start | bytes 3244040 | tf_op jit(solution)/shard_map/ppermute | solution.py:31
  35.7 37.1 %all-to-all-start = ((bf16[128,4,1152]{2,1,0:T(4,128)(2,1)}), bf16[128,4,1152]{2,1,0:T(4,128)(2,1)S(1)}, u32[]{:S(2)}, u32[]{:S(2)}) async-start(bf16[128,4,1152]{2,1,0:T(4,128)(2,1)} %place.1), calls=%async_computation | async-start | bytes 2359296 | tf_op jit(solution)/shard_map/all_to_all | solution.py:307
  49.3 30.9 %collective-permute-start.1 = (bf16[528,1024]{1,0:T(8,128)(2,1)}, bf16[528,1024]{1,0:T(8,128)(2,1)}, u32[]{:S(2)}, u32[]{:S(2)}) collective-permute-start(bf16[528,1024]{1,0:T(8,128)(2,1)} %collective-permute-done.refs_5_.refs_8_), channel_id=1, source_target_pairs={{1,31},{3,1},{5,3},{7,5},{9,7},{11,9},{13,11},{15,13},{17,15},{19,... | collective-permute-start | bytes 3244040 | tf_op jit(solution)/shard_map/ppermute | solution.py:31
  70.2 10.0 %collective-permute-start.8 = (f32[1,1024]{1,0:T(1,128)S(1)}, f32[1,1024]{1,0:T(1,128)S(1)}, u32[]{:S(2)}, u32[]{:S(2)}) collective-permute-start(f32[1,1024]{1,0:T(1,128)S(1)} %get-tuple-element.12), channel_id=1, source_target_pairs={{1,0},{3,2},{5,4},{7,6},{9,8},{11,10},{13,12},{15,14},{17,16},{19,... | collective-permute-start | bytes 12296 | tf_op jit(solution)/shard_map/ppermute | solution.py:31
  71.5 8.7 %collective-permute-start.9 = (f32[1,1024]{1,0:T(1,128)S(1)}, f32[1,1024]{1,0:T(1,128)S(1)}, u32[]{:S(2)}, u32[]{:S(2)}) collective-permute-start(f32[1,1024]{1,0:T(1,128)S(1)} %get-tuple-element.11), channel_id=1, source_target_pairs={{32,35},{34,37},{36,39},{38,41},{40,43},{42,45},{44,47},{46,49},{4... | collective-permute-start | bytes 12296 | tf_op jit(solution)/shard_map/ppermute | solution.py:31
  80.2 0.7 copy-start.6
  85.2 7.7 %collective-permute-start.10 = (f32[1,1024]{1,0:T(1,128)S(1)}, f32[1,1024]{1,0:T(1,128)S(1)}, u32[]{:S(2)}, u32[]{:S(2)}) collective-permute-start(f32[1,1024]{1,0:T(1,128)S(1)} %get-tuple-element.9), channel_id=1, source_target_pairs={{1,2},{3,4},{5,6},{7,8},{9,10},{11,12},{13,14},{15,16},{17,18},{19... | collective-permute-start | bytes 12296 | tf_op jit(solution)/shard_map/ppermute | solution.py:31

commit v12 on v11

--- a/solution.py
+++ b/solution.py
@@ -349,6 +349,7 @@
         [],
         where,
         found,
+        (next_ids,),
     )
     from_partner = send(found[PARTNER : PARTNER + 1], to_light)
     behind = found[NEAR_PARTNER : NEAR_PARTNER + 1]
@@ -361,7 +362,7 @@
         [],
         where,
         found,
-        (from_partner, from_behind, next_ids),
+        (from_partner, from_behind),
         last=True,
     )
     from_last = send(for_last, lambda core, heavy, block: block + 2 if core else (block + 1 if heavy else None))

time: 93.9 us -> 87.4 us (0.931)
  the two profiles are of different devices: /device:TPU:1 before, /device:TPU:25 now
where the time goes in v12:
time: 87.4 us; the launch traced here: 86.9 us
  starting transfers between devices  38.8 us (44%)
  waiting for transfers between devices  32.4 us (37%)
  Pallas kernels  11.3 us (13%)
  local copies, waits for them, and re-layouts  2.99 us (3%)
    ppermute x11, starting transfers between devices, send(): return lax.ppermute(value, BOTH, pairs)  32.2 us
    ppermute x11, waiting for transfers between devices, send(): return lax.ppermute(value, BOTH, pairs)  27.6 us
    all_to_all x1, starting transfers between devices, body(): lax.all_to_all(outgoing, BOTH, split_axis=0, concat_axis=0, tiled=True)  6.64 us
    pallas_call x3, Pallas kernels, stage(): pl.pallas_call(run, in_specs=vmem(len(own)) + [pl.BlockSpec(memory_space=...  5.35 us
    all_to_all x1, waiting for transfers between devices, body(): lax.all_to_all(outgoing, BOTH, split_axis=0, concat_axis=0, tiled=True)  4.8 us
    unnamed x14, local copies, waits for them, and re-layouts  2.98 us
    pallas_call x1, Pallas kernels, body(): pl.pallas_call(within_kernel, in_specs=vmem(3), out_specs=pl.BlockSpec(me...  2.38 us
    pallas_call x1, Pallas kernels, placed_rows(): pl.pallas_call(place_kernel, in_specs=vmem(4), out_specs=pl.BlockSpec(mem...  1.76 us
  transfers between devices with their start and end apart: 12, of which 5 were waited for; matrix products, arithmetic and copies ran while one was open for 0% of the time, Pallas kernels for 11%

profile of v12, /device:TPU:25, one launch (start us, length us, event | category | flops | bytes accessed | tf_op | source)
XLA Modules:
  0.0 86.9 jit_solution(4941102495035837276)
XLA Ops:
  0.6 0.0 copy-start
  0.6 1.6 %copy-done = bf16[1,1024,1024]{2,1,0:T(8,128)(2,1)S(1)} copy-done((bf16[1,1024,1024]{2,1,0:T(8,128)(2,1)S(1)}, bf16[1,1024,1024]{2,1,0:T(8,128)(2,1)}, u32[]{:S(2)}) %copy-start) | copy-done | bytes 2097176
  2.2 0.0 copy-start.2
  2.2 0.7 copy-done.2
  2.9 0.3 norm_0.1.own0.refs_0_
  3.2 0.0 copy-start.5
  3.3 3.4 %collective-permute-start.4 = (bf16[528,1024]{1,0:T(8,128)(2,1)S(1)}, bf16[528,1024]{1,0:T(8,128)(2,1)}, u32[]{:S(2)}, u32[]{:S(2)}) collective-permute-start(bf16[528,1024]{1,0:T(8,128)(2,1)S(1)} %norm_0.1.own0.refs_0_), channel_id=1, source_target_pairs={{0,1},{2,3},{4,5},{6,7},{8,9},{10,11},{12,13},{14,15},{16,17},{18,... | collective-permute-start | bytes 3244040 | tf_op jit(solution)/shard_map/ppermute | solution.py:31
  6.7 0.3 norm_1.1.own1.refs_1_
  7.0 0.0 copy-start.1
  7.0 0.0 copy-start.3
  7.0 0.0 copy-start.4
  7.0 6.0 %collective-permute-start.3 = (bf16[528,1024]{1,0:T(8,128)(2,1)S(1)}, bf16[528,1024]{1,0:T(8,128)(2,1)}, u32[]{:S(2)}, u32[]{:S(2)}) collective-permute-start(bf16[528,1024]{1,0:T(8,128)(2,1)S(1)} %norm_1.1.own1.refs_1_), channel_id=1, source_target_pairs={{0,2},{1,3},{2,4},{3,5},{4,6},{5,7},{6,8},{7,9},{8,10},{9,11},{10,... | collective-permute-start | bytes 3244040 | tf_op jit(solution)/shard_map/ppermute | solution.py:31
  13.0 2.3 %collective-permute-start = (bf16[528,1024]{1,0:T(8,128)(2,1)S(1)}, bf16[528,1024]{1,0:T(8,128)(2,1)}, u32[]{:S(2)}, u32[]{:S(2)}) collective-permute-start(bf16[528,1024]{1,0:T(8,128)(2,1)S(1)} %norm_1.1.own1.refs_1_), channel_id=1, source_target_pairs={{0,1},{2,3},{4,5},{6,7},{8,9},{10,11},{12,13},{14,15},{16,17},{18,... | collective-permute-start | bytes 3244040 | tf_op jit(solution)/shard_map/ppermute | solution.py:31
  15.3 1.7 %collective-permute-start.2 = (bf16[528,1024]{1,0:T(8,128)(2,1)S(1)}, bf16[528,1024]{1,0:T(8,128)(2,1)}, u32[]{:S(2)}, u32[]{:S(2)}) collective-permute-start(bf16[528,1024]{1,0:T(8,128)(2,1)S(1)} %norm_0.1.own0.refs_0_), channel_id=1, source_target_pairs={{1,3},{3,5},{5,7},{7,9},{9,11},{11,13},{13,15},{15,17},{17,19},{19... | collective-permute-start | bytes 3244040 | tf_op jit(solution)/shard_map/ppermute | solution.py:31
  17.0 0.0 copy-done.5
  17.0 2.4 %within.1.refs_7_.after_ref = f32[8,1024]{1,0:T(8,128)S(1)} custom-call(bf16[528,1024]{1,0:T(8,128)(2,1)S(1)} %norm_0.1.own0.refs_0_, bf16[528,1024]{1,0:T(8,128)(2,1)S(1)} %norm_1.1.own1.refs_1_, f32[1,1024]{1,0:T(1,128)S(1)} %copy-done.5), custom_call_target="tpu_custom_call" | custom-call | flops 2147483648 | bytes 2097152 | tf_op jit(solution)/shard_map/within/pallas_call | solution.py:295
  19.4 0.0 copy-done.1
  19.4 0.0 copy-done.3
  19.4 0.0 copy-done.4
  19.4 1.8 %place.1 = bf16[128,4,1152]{2,1,0:T(4,128)(2,1)} custom-call(bf16[256,1024]{1,0:T(8,128)(2,1)S(1)} %copy-done.1, s32[1,256]{1,0:T(1,128)S(1)} %bitcast.8, s32[1,256]{1,0:T(1,128)S(1)} %bitcast.9, f32[8,1024]{1,0:T(8,128)S(1)} %within.1.refs_7_.after_ref), custom_call_target="tpu_custom_call" | custom-call | flops 268435456 | bytes 1572864 | tf_op jit(solution)/shard_map/place/pallas_call | solution.py:172
  21.2 6.6 %all-to-all-start = ((bf16[128,4,1152]{2,1,0:T(4,128)(2,1)}), bf16[128,4,1152]{2,1,0:T(4,128)(2,1)S(1)}, u32[]{:S(2)}, u32[]{:S(2)}) async-start(bf16[128,4,1152]{2,1,0:T(4,128)(2,1)} %place.1), calls=%async_computation | async-start | bytes 2359296 | tf_op jit(solution)/shard_map/all_to_all | solution.py:307
  27.8 0.0 collective-permute-done.4.refs_2_.refs_7_
  27.8 1.7 %collective-permute-start.5 = (bf16[528,1024]{1,0:T(8,128)(2,1)}, bf16[528,1024]{1,0:T(8,128)(2,1)}, u32[]{:S(2)}, u32[]{:S(2)}) collective-permute-start(bf16[528,1024]{1,0:T(8,128)(2,1)} %collective-permute-done.4.refs_2_.refs_7_), channel_id=1, source_target_pairs={{1,31},{3,1},{5,3},{7,5},{9,7},{11,9},{13,11},{15,13},{17,15},{19,... | collective-permute-start | bytes 3244040 | tf_op jit(solution)/shard_map/ppermute | solution.py:31
  29.5 1.7 %collective-permute-start.6 = (bf16[528,1024]{1,0:T(8,128)(2,1)}, bf16[528,1024]{1,0:T(8,128)(2,1)}, u32[]{:S(2)}, u32[]{:S(2)}) collective-permute-start(bf16[528,1024]{1,0:T(8,128)(2,1)} %collective-permute-done.4.refs_2_.refs_7_), channel_id=1, source_target_pairs={{1,3},{3,5},{5,7},{7,9},{9,11},{11,13},{13,15},{15,17},{17,19},{19... | collective-permute-start | bytes 3244040 | tf_op jit(solution)/shard_map/ppermute | solution.py:31
  31.2 0.0 collective-permute-done.3.refs_3_.refs_4_.refs_2_
  31.2 9.2 %collective-permute-start.7 = (bf16[528,1024]{1,0:T(8,128)(2,1)}, bf16[528,1024]{1,0:T(8,128)(2,1)}, u32[]{:S(2)}, u32[]{:S(2)}) collective-permute-start(bf16[528,1024]{1,0:T(8,128)(2,1)} %collective-permute-done.3.refs_3_.refs_4_.refs_2_), channel_id=1, source_target_pairs={{0,1},{2,3},{4,5},{6,7},{8,9},{10,11},{12,13},{14,15},{16,17},{18,... | collective-permute-start | bytes 3244040 | tf_op jit(solution)/shard_map/ppermute | solution.py:31
  40.4 0.1 pad_add_fusion.refs_6_.refs_9_.refs_3_
  40.5 0.0 collective-permute-done.refs_5_.refs_8_
  40.5 1.7 %collective-permute-start.1 = (bf16[528,1024]{1,0:T(8,128)(2,1)}, bf16[528,1024]{1,0:T(8,128)(2,1)}, u32[]{:S(2)}, u32[]{:S(2)}) collective-permute-start(bf16[528,1024]{1,0:T(8,128)(2,1)} %collective-permute-done.refs_5_.refs_8_), channel_id=1, source_target_pairs={{1,31},{3,1},{5,3},{7,5},{9,7},{11,9},{13,11},{15,13},{17,15},{19,... | collective-permute-start | bytes 3244040 | tf_op jit(solution)/shard_map/ppermute | solution.py:31
  42.2 0.0 collective-permute-done.2.refs_4_.refs_2_.refs_1_
  42.2 3.3 %cross_a.1.refs_10_ = f32[8,1024]{1,0:T(8,128)S(1)} custom-call(bf16[528,1024]{1,0:T(8,128)(2,1)S(1)} %norm_0.1.own0.refs_0_, bf16[528,1024]{1,0:T(8,128)(2,1)S(1)} %norm_1.1.own1.refs_1_, bf16[528,1024]{1,0:T(8,128)(2,1)} %collective-permute-done.4.refs_2_.refs_7_, bf16[528,1024]{1,0:T(8,128)(2,1)} %collective-permute-done.3.refs_3_.refs_4_.refs_2_, ...), custom_call_target="tpu_custom_call" | custom-call | flops 6442450944 | bytes 4325376 | tf_op jit(solution)/shard_map/cross_a/pallas_call | solution.py:242
  45.5 4.8 %all-to-all-done.in_ref = bf16[128,4,1152]{2,1,0:T(4,128)(2,1)S(1)} async-done(((bf16[128,4,1152]{2,1,0:T(4,128)(2,1)}), bf16[128,4,1152]{2,1,0:T(4,128)(2,1)S(1)}, u32[]{:S(2)}, u32[]{:S(2)}) %all-to-all-start) | async-done | bytes 1179680 | tf_op jit(solution)/shard_map/all_to_all | solution.py:307
  50.3 1.1 %split.1 = (bf16[512,1024]{1,0:T(8,128)(2,1)}, s32[1,512]{1,0:T(1,128)}) custom-call(bf16[128,4,1152]{2,1,0:T(4,128)(2,1)S(1)} %all-to-all-done.in_ref), custom_call_target="tpu_custom_call" | custom-call | bytes 2097152 | tf_op jit(solution)/shard_map/split/pallas_call | solution.py:196
  51.4 0.0 collective-permute-done.5.refs_3_
  51.4 0.0 collective-permute-done.6.refs_5_
  51.4 3.6 %collective-permute-done.7.refs_6_ = bf16[528,1024]{1,0:T(8,128)(2,1)} collective-permute-done((bf16[528,1024]{1,0:T(8,128)(2,1)}, bf16[528,1024]{1,0:T(8,128)(2,1)}, u32[]{:S(2)}, u32[]{:S(2)}) %collective-permute-start.7) | collective-permute-done | bytes 1081376 | tf_op jit(solution)/shard_map/ppermute | solution.py:31
  55.0 0.0 copy-start.6
  55.0 0.7 copy-done.6
  55.7 0.8 cross_b.1.refs_4_
  56.6 1.3 %collective-permute-start.8 = (f32[1,1024]{1,0:T(1,128)S(1)}, f32[1,1024]{1,0:T(1,128)S(1)}, u32[]{:S(2)}, u32[]{:S(2)}) collective-permute-start(f32[1,1024]{1,0:T(1,128)S(1)} %get-tuple-element.12), channel_id=1, source_target_pairs={{1,0},{3,2},{5,4},{7,6},{9,8},{11,10},{13,12},{15,14},{17,16},{19,... | collective-permute-start | bytes 12296 | tf_op jit(solution)/shard_map/ppermute | solution.py:31
  57.9 1.3 %collective-permute-start.9 = (f32[1,1024]{1,0:T(1,128)S(1)}, f32[1,1024]{1,0:T(1,128)S(1)}, u32[]{:S(2)}, u32[]{:S(2)}) collective-permute-start(f32[1,1024]{1,0:T(1,128)S(1)} %get-tuple-element.11), channel_id=1, source_target_pairs={{32,35},{34,37},{36,39},{38,41},{40,43},{42,45},{44,47},{46,49},{4... | collective-permute-start | bytes 12296 | tf_op jit(solution)/shard_map/ppermute | solution.py:31
  59.2 0.0 collective-permute-done.1.refs_0_
  59.2 12.0 %collective-permute-done.8.refs_5_ = f32[1,1024]{1,0:T(1,128)S(1)} collective-permute-done((f32[1,1024]{1,0:T(1,128)S(1)}, f32[1,1024]{1,0:T(1,128)S(1)}, u32[]{:S(2)}, u32[]{:S(2)}) %collective-permute-start.8) | collective-permute-done | bytes 4128 | tf_op jit(solution)/shard_map/ppermute | solution.py:31
  71.2 6.3 %collective-permute-done.9.refs_6_ = f32[1,1024]{1,0:T(1,128)S(1)} collective-permute-done((f32[1,1024]{1,0:T(1,128)S(1)}, f32[1,1024]{1,0:T(1,128)S(1)}, u32[]{:S(2)}, u32[]{:S(2)}) %collective-permute-start.9) | collective-permute-done | bytes 4128 | tf_op jit(solution)/shard_map/ppermute | solution.py:31
  77.5 1.2 %cross_c.1 = (f32[1,1024]{1,0:T(1,128)S(1)}, f32[1,1024]{1,0:T(1,128)S(1)}, f32[8,1024]{1,0:T(8,128)}) custom-call(bf16[528,1024]{1,0:T(8,128)(2,1)} %collective-permute-done.1.refs_0_, bf16[528,1024]{1,0:T(8,128)(2,1)} %collective-permute-done.2.refs_4_.refs_2_.refs_1_, bf16[528,1024]{1,0:T(8,128)(2,1)} %collective-permute-done.3.refs_3_.refs_4_.refs_2_, ...), custom_call_target="tpu_custom_call" | custom-call | flops 1073741824 | bytes 3244032 | tf_op jit(solution)/shard_map/cross_c/pallas_call | solution.py:242
  78.7 1.9 %collective-permute-start.10 = (f32[1,1024]{1,0:T(1,128)S(1)}, f32[1,1024]{1,0:T(1,128)S(1)}, u32[]{:S(2)}, u32[]{:S(2)}) collective-permute-start(f32[1,1024]{1,0:T(1,128)S(1)} %get-tuple-element.9), channel_id=1, source_target_pairs={{1,2},{3,4},{5,6},{7,8},{9,10},{11,12},{13,14},{15,16},{17,18},{19... | collective-permute-start | bytes 12296 | tf_op jit(solution)/shard_map/ppermute | solution.py:31
  80.6 5.7 %collective-permute-done.10 = f32[1,1024]{1,0:T(1,128)S(1)} collective-permute-done((f32[1,1024]{1,0:T(1,128)S(1)}, f32[1,1024]{1,0:T(1,128)S(1)}, u32[]{:S(2)}, u32[]{:S(2)}) %collective-permute-start.10) | collective-permute-done | bytes 4128 | tf_op jit(solution)/shard_map/ppermute | solution.py:31
  86.3 0.6 fusion
  (1 shorter events, 0.0 us)
Async XLA Ops:
  0.6 1.6 %copy-start = (bf16[1,1024,1024]{2,1,0:T(8,128)(2,1)S(1)}, bf16[1,1024,1024]{2,1,0:T(8,128)(2,1)}, u32[]{:S(2)}) copy-start(bf16[1,1024,1024]{2,1,0:T(8,128)(2,1)} %param.6) | copy-start | bytes 6291460
  2.2 0.7 copy-start.2
  3.2 13.7 %copy-start.5 = (f32[1,1024]{1,0:T(1,128)S(1)}, f32[1,1024]{1,0:T(1,128)}, u32[]{:S(2)}) copy-start(f32[1,1024]{1,0:T(1,128)} %prior_ref.1) | copy-start | bytes 12292
  3.3 24.6 %collective-permute-start.4 = (bf16[528,1024]{1,0:T(8,128)(2,1)S(1)}, bf16[528,1024]{1,0:T(8,128)(2,1)}, u32[]{:S(2)}, u32[]{:S(2)}) collective-permute-start(bf16[528,1024]{1,0:T(8,128)(2,1)S(1)} %norm_0.1.own0.refs_0_), channel_id=1, source_target_pairs={{0,1},{2,3},{4,5},{6,7},{8,9},{10,11},{12,13},{14,15},{16,17},{18,... | collective-permute-start | bytes 3244040 | tf_op jit(solution)/shard_map/ppermute | solution.py:31
  7.0 12.4 %copy-start.1 = (bf16[256,1024]{1,0:T(8,128)(2,1)S(1)}, bf16[256,1024]{1,0:T(8,128)(2,1)}, u32[]{:S(2)}) copy-start(bf16[256,1024]{1,0:T(8,128)(2,1)} %rows_ref.1) | copy-start | bytes 1572868
  7.0 12.4 %copy-start.3 = (s32[256,1]{0,1:T(1,128)S(1)}, s32[256,1]{0,1:T(1,128)}, u32[]{:S(2)}) copy-start(s32[256,1]{0,1:T(1,128)} %param.11) | copy-start | bytes 3076
  7.0 12.4 %copy-start.4 = (s32[256]{0:T(256)S(1)}, s32[256]{0:T(256)}, u32[]{:S(2)}) copy-start(s32[256]{0:T(256)} %param.10) | copy-start | bytes 3076
  7.0 24.2 %collective-permute-start.3 = (bf16[528,1024]{1,0:T(8,128)(2,1)S(1)}, bf16[528,1024]{1,0:T(8,128)(2,1)}, u32[]{:S(2)}, u32[]{:S(2)}) collective-permute-start(bf16[528,1024]{1,0:T(8,128)(2,1)S(1)} %norm_1.1.own1.refs_1_), channel_id=1, source_target_pairs={{0,2},{1,3},{2,4},{3,5},{4,6},{5,7},{6,8},{7,9},{8,10},{9,11},{10,... | collective-permute-start | bytes 3244040 | tf_op jit(solution)/shard_map/ppermute | solution.py:31
  13.0 27.5 %collective-permute-start = (bf16[528,1024]{1,0:T(8,128)(2,1)S(1)}, bf16[528,1024]{1,0:T(8,128)(2,1)}, u32[]{:S(2)}, u32[]{:S(2)}) collective-permute-start(bf16[528,1024]{1,0:T(8,128)(2,1)S(1)} %norm_1.1.own1.refs_1_), channel_id=1, source_target_pairs={{0,1},{2,3},{4,5},{6,7},{8,9},{10,11},{12,13},{14,15},{16,17},{18,... | collective-permute-start | bytes 3244040 | tf_op jit(solution)/shard_map/ppermute | solution.py:31
  15.3 26.9 %collective-permute-start.2 = (bf16[528,1024]{1,0:T(8,128)(2,1)S(1)}, bf16[528,1024]{1,0:T(8,128)(2,1)}, u32[]{:S(2)}, u32[]{:S(2)}) collective-permute-start(bf16[528,1024]{1,0:T(8,128)(2,1)S(1)} %norm_0.1.own0.refs_0_), channel_id=1, source_target_pairs={{1,3},{3,5},{5,7},{7,9},{9,11},{11,13},{13,15},{15,17},{17,19},{19... | collective-permute-start | bytes 3244040 | tf_op jit(solution)/shard_map/ppermute | solution.py:31
  21.2 29.2 %all-to-all-start = ((bf16[128,4,1152]{2,1,0:T(4,128)(2,1)}), bf16[128,4,1152]{2,1,0:T(4,128)(2,1)S(1)}, u32[]{:S(2)}, u32[]{:S(2)}) async-start(bf16[128,4,1152]{2,1,0:T(4,128)(2,1)} %place.1), calls=%async_computation | async-start | bytes 2359296 | tf_op jit(solution)/shard_map/all_to_all | solution.py:307
  27.8 23.6 %collective-permute-start.5 = (bf16[528,1024]{1,0:T(8,128)(2,1)}, bf16[528,1024]{1,0:T(8,128)(2,1)}, u32[]{:S(2)}, u32[]{:S(2)}) collective-permute-start(bf16[528,1024]{1,0:T(8,128)(2,1)} %collective-permute-done.4.refs_2_.refs_7_), channel_id=1, source_target_pairs={{1,31},{3,1},{5,3},{7,5},{9,7},{11,9},{13,11},{15,13},{17,15},{19,... | collective-permute-start | bytes 3244040 | tf_op jit(solution)/shard_map/ppermute | solution.py:31
  29.5 22.0 %collective-permute-start.6 = (bf16[528,1024]{1,0:T(8,128)(2,1)}, bf16[528,1024]{1,0:T(8,128)(2,1)}, u32[]{:S(2)}, u32[]{:S(2)}) collective-permute-start(bf16[528,1024]{1,0:T(8,128)(2,1)} %collective-permute-done.4.refs_2_.refs_7_), channel_id=1, source_target_pairs={{1,3},{3,5},{5,7},{7,9},{9,11},{11,13},{13,15},{15,17},{17,19},{19... | collective-permute-start | bytes 3244040 | tf_op jit(solution)/shard_map/ppermute | solution.py:31
  31.2 23.8 %collective-permute-start.7 = (bf16[528,1024]{1,0:T(8,128)(2,1)}, bf16[528,1024]{1,0:T(8,128)(2,1)}, u32[]{:S(2)}, u32[]{:S(2)}) collective-permute-start(bf16[528,1024]{1,0:T(8,128)(2,1)} %collective-permute-done.3.refs_3_.refs_4_.refs_2_), channel_id=1, source_target_pairs={{0,1},{2,3},{4,5},{6,7},{8,9},{10,11},{12,13},{14,15},{16,17},{18,... | collective-permute-start | bytes 3244040 | tf_op jit(solution)/shard_map/ppermute | solution.py:31
  40.5 18.6 %collective-permute-start.1 = (bf16[528,1024]{1,0:T(8,128)(2,1)}, bf16[528,1024]{1,0:T(8,128)(2,1)}, u32[]{:S(2)}, u32[]{:S(2)}) collective-permute-start(bf16[528,1024]{1,0:T(8,128)(2,1)} %collective-permute-done.refs_5_.refs_8_), channel_id=1, source_target_pairs={{1,31},{3,1},{5,3},{7,5},{9,7},{11,9},{13,11},{15,13},{17,15},{19,... | collective-permute-start | bytes 3244040 | tf_op jit(solution)/shard_map/ppermute | solution.py:31
  55.0 0.7 copy-start.6
  56.6 14.6 %collective-permute-start.8 = (f32[1,1024]{1,0:T(1,128)S(1)}, f32[1,1024]{1,0:T(1,128)S(1)}, u32[]{:S(2)}, u32[]{:S(2)}) collective-permute-start(f32[1,1024]{1,0:T(1,128)S(1)} %get-tuple-element.12), channel_id=1, source_target_pairs={{1,0},{3,2},{5,4},{7,6},{9,8},{11,10},{13,12},{15,14},{17,16},{19,... | collective-permute-start | bytes 12296 | tf_op jit(solution)/shard_map/ppermute | solution.py:31
  57.9 19.6 %collective-permute-start.9 = (f32[1,1024]{1,0:T(1,128)S(1)}, f32[1,1024]{1,0:T(1,128)S(1)}, u32[]{:S(2)}, u32[]{:S(2)}) collective-permute-start(f32[1,1024]{1,0:T(1,128)S(1)} %get-tuple-element.11), channel_id=1, source_target_pairs={{32,35},{34,37},{36,39},{38,41},{40,43},{42,45},{44,47},{46,49},{4... | collective-permute-start | bytes 12296 | tf_op jit(solution)/shard_map/ppermute | solution.py:31
  78.7 7.7 %collective-permute-start.10 = (f32[1,1024]{1,0:T(1,128)S(1)}, f32[1,1024]{1,0:T(1,128)S(1)}, u32[]{:S(2)}, u32[]{:S(2)}) collective-permute-start(f32[1,1024]{1,0:T(1,128)S(1)} %get-tuple-element.9), channel_id=1, source_target_pairs={{1,2},{3,4},{5,6},{7,8},{9,10},{11,12},{13,14},{15,16},{17,18},{19... | collective-permute-start | bytes 12296 | tf_op jit(solution)/shard_map/ppermute | solution.py:31
